TPU v7x, 32 devices: a whole 2x2x4 slice. The times are simulated.
32 devices in a mesh: gx: 4 (over z), gy: 2 (over x), gz: 4 (over y, core).
Axes of the slice: x: 2, y: 2, z: 4, core: 2. Of those that a mesh axis runs over, the one named last changes fastest.
Arguments:
- elevation: int32 [64, 512], P('gy', ('gx', 'gz')), may hold values from 0 to 499
- layer_base: float32 [64], P('gz'), may hold values from 0.6 to 1.6
- stretch: float32 [64], P('gz'), may hold values from -0.5 to 0.5
- material: int32 [64, 64, 512], P('gz', 'gy', 'gx'), may hold values from 0 to 15
- buoyancy: float32 [16], replicated, may hold values from 0.5 to 2
- lame_lambda: float32 [16], replicated, may hold values from 0.5 to 2
- shear_modulus: float32 [16], replicated, may hold values from 0.3 to 1.5
- relax_time: float32 [16], replicated, may hold values from 0.2 to 30
- anelastic_weight: float32 [16], replicated, may hold values from 0.05 to 0.5
- velocity: float32 [3, 64, 64, 512], P(None, 'gz', 'gy', 'gx'), may hold values from -6 to 6
- stress: float32 [6, 64, 64, 512], P(None, 'gz', 'gy', 'gx'), may hold values from -6 to 6
- memory: float32 [6, 64, 64, 512], P(None, 'gz', 'gy', 'gx'), may hold values from -4 to 4
Outputs:
- velocity_next: float32 [3, 64, 64, 512], P(None, 'gz', 'gy', 'gx')
- stress_next: float32 [6, 64, 64, 512], P(None, 'gz', 'gy', 'gx')
- memory_next: float32 [6, 64, 64, 512], P(None, 'gz', 'gy', 'gx')
All inputs are finite; a program needn't handle non-finite values.
Results may differ from a plain program's by a relative error of at most 0.00002.
Values sent between devices are 32-bit elements; how exact they have to be, the bound alone decides.
No kernel may reach another device: no remote copies, remote signals or barrier semaphores. Data moves between devices by JAX's collectives and lax.ppermute only.
A program may use at most 64 MiB of HBM per device.

v0:
```python
import jax
import jax.numpy as jnp
from jax import lax
from jax.sharding import PartitionSpec as P

step_size = 0.3
binomial = (1.0, 4.0, 6.0, 4.0, 1.0)


def padded_2(value, sides, width):
    for axis, dim in sides:
        size, length = (lax.axis_size(axis), value.shape[dim])
        up = [(i, (i + 1) % size) for i in range(size - 1)]
        down = [(j, i) for i, j in up]
        last = lax.slice_in_dim(value, length - width, length, axis=dim)
        leading = lax.slice_in_dim(value, 0, width, axis=dim)
        before = lax.ppermute(last, axis, up)
        after = lax.ppermute(leading, axis, down)
        value = jnp.concatenate([before, value, after], axis=dim)
    return value


def prefix(value, axis, combine, identity):
    size, mine = (lax.axis_size(axis), lax.axis_index(axis))
    everything = lax.all_gather(value, axis)
    start = jnp.broadcast_to(jnp.asarray(identity, value.dtype), value.shape)

    def step(k, before):
        reached = k < mine
        new = combine(before, everything[k])
        return jnp.where(reached, new, before)

    return lax.fori_loop(0, size, step, start)


def smooth_axis(values_in, dimension):
    length_out = values_in.shape[dimension] - 4
    summed = jnp.zeros_like(lax.slice_in_dim(values_in, 0, length_out, axis=dimension))
    for offset, weight in enumerate(binomial):
        summed = summed + weight * lax.slice_in_dim(
            values_in, offset, offset + length_out, axis=dimension
        )
    return summed / 16.0


def centred(values_in, dimension):
    length_out = values_in.shape[dimension] - 4
    closer = lax.slice_in_dim(values_in, 3, 3 + length_out, axis=dimension) - lax.slice_in_dim(
        values_in, 1, 1 + length_out, axis=dimension
    )
    farther = lax.slice_in_dim(values_in, 4, 4 + length_out, axis=dimension) - lax.slice_in_dim(
        values_in, 0, length_out, axis=dimension
    )
    return (8.0 * closer - farther) / 12.0


def combine_sum(earlier, later):
    return earlier + later


def lookup_table(material, tables):
    stacked = jnp.stack(tables)
    result = jnp.zeros((stacked.shape[0],) + material.shape, jnp.float32)
    for block_id in range(stacked.shape[1]):
        chosen = (material == block_id)[None]
        result = jnp.where(chosen, stacked[:, block_id][:, None, None, None], result)
    return result


def new_velocity(velocity, grad_x, grad_y, grad_k, metric_x, metric_y, metric_z, buoy_cell):
    accel_x = (
        grad_x[0] - metric_x * grad_k[0] + (grad_y[0] - metric_y * grad_k[3]) + metric_z * grad_k[4]
    )
    accel_y = (
        grad_x[1] - metric_x * grad_k[3] + (grad_y[1] - metric_y * grad_k[1]) + metric_z * grad_k[5]
    )
    accel_z = (
        grad_x[2] - metric_x * grad_k[4] + (grad_y[2] - metric_y * grad_k[5]) + metric_z * grad_k[2]
    )
    return velocity + step_size * buoy_cell[None] * jnp.stack([accel_x, accel_y, accel_z])


def new_stress(stress, memory, vel_x, vel_y, vel_k, metric_x, metric_y, metric_z, properties):
    along_x = vel_x - metric_x[None] * vel_k
    along_y = vel_y - metric_y[None] * vel_k
    along_z = metric_z[None] * vel_k
    lame_cell = properties[1]
    shear_cell = properties[2]
    volume_rate = along_x[0] + along_y[1] + along_z[2]
    elastic_rate = jnp.stack(
        [
            lame_cell * volume_rate + 2.0 * shear_cell * along_x[0],
            lame_cell * volume_rate + 2.0 * shear_cell * along_y[1],
            lame_cell * volume_rate + 2.0 * shear_cell * along_z[2],
            shear_cell * (along_y[0] + along_x[1]),
            shear_cell * (along_z[0] + along_x[2]),
            shear_cell * (along_z[1] + along_y[2]),
        ]
    )
    keep_factor = properties[3][None]
    memory_next = keep_factor * memory + (1.0 - keep_factor) * properties[4][None] * elastic_rate
    stress_next = stress + step_size * (elastic_rate - memory_next)
    return (stress_next, memory_next)


def local(
    elevation,
    layer_base,
    stretch,
    material,
    buoyancy,
    lame_lambda,
    shear_modulus,
    relax_time,
    anelastic_weight,
    velocity,
    stress,
    memory,
):
    height = elevation.astype(jnp.float32) / 200.0
    surface_slab = lax.all_gather(height, "gz", axis=1, tiled=True)
    rimmed = padded_2(surface_slab, (("gx", 1), ("gy", 0)), 4)
    surface = smooth_axis(smooth_axis(rimmed, 0), 1)
    slope_x = centred(surface[2:-2, :], 1)
    slope_y = centred(surface[:, 2:-2], 0)
    surface_own = surface[2:-2, 2:-2]
    thickness = layer_base[:, None, None] * jnp.exp(stretch[:, None, None] * surface_own[None])
    weighted = stretch[:, None, None] * thickness
    partial_sum = jnp.sum(weighted, axis=0)
    upper_sum = prefix(partial_sum, "gz", combine_sum, jnp.zeros_like(partial_sum))
    lift = upper_sum[None] + jnp.cumsum(weighted, axis=0) - 0.5 * weighted
    factor = (lift - 1.0) / thickness
    metric_x = slope_x[None] * factor
    metric_y = slope_y[None] * factor
    metric_z = 1.0 / thickness
    properties = lookup_table(
        material,
        (buoyancy, lame_lambda, shear_modulus, jnp.exp(-step_size / relax_time), anelastic_weight),
    )
    padded = padded_2(stress, (("gx", 3), ("gy", 2), ("gz", 1)), 2)
    stress_x = jnp.concatenate([padded[0:1], padded[3:5]])[:, 2:-2, 2:-2, :]
    stress_y = jnp.concatenate([padded[3:4], padded[1:2], padded[5:6]])[:, 2:-2, :, 2:-2]
    stress_z = padded[:, :, 2:-2, 2:-2]
    velocity_next = new_velocity(
        velocity,
        centred(stress_x, 3),
        centred(stress_y, 2),
        centred(stress_z, 1),
        metric_x,
        metric_y,
        metric_z,
        properties[0],
    )
    vel_pad = padded_2(velocity_next, (("gx", 3), ("gy", 2), ("gz", 1)), 2)
    vel_x = centred(vel_pad[:, 2:-2, 2:-2, :], 3)
    vel_y = centred(vel_pad[:, 2:-2, :, 2:-2], 2)
    vel_k = centred(vel_pad[:, :, 2:-2, 2:-2], 1)
    stress_next, memory_next = new_stress(
        stress, memory, vel_x, vel_y, vel_k, metric_x, metric_y, metric_z, properties
    )
    return (velocity_next, stress_next, memory_next)


def solution(mesh):
    return jax.shard_map(
        local,
        mesh=mesh,
        in_specs=(
            P("gy", ("gx", "gz")),
            P("gz"),
            P("gz"),
            P("gz", "gy", "gx"),
            P(),
            P(),
            P(),
            P(),
            P(),
            P(None, "gz", "gy", "gx"),
            P(None, "gz", "gy", "gx"),
            P(None, "gz", "gy", "gx"),
        ),
        out_specs=(P(None, "gz", "gy", "gx"), P(None, "gz", "gy", "gx"), P(None, "gz", "gy", "gx")),
        check_vma=False,
    )
```

profile of v0, /device:TPU:20, one launch (start us, length us, event | category | flops | bytes accessed | tf_op | source)
XLA Modules:
  0.0 134.9 jit_solution(15328119935692131838)
XLA Ops:
  0.6 2.6 %fusion.97 = (f32[6,16,32,2]{3,2,1,0:T(8,128)S(1)}, f32[6,16,32,2]{3,2,1,0:T(8,128)S(1)}) fusion(f32[6,16,32,128]{3,2,1,0:T(8,128)} %param.24), kind=kLoop, calls=%fused_computation.263 | loop fusion | bytes 98304 | tf_op jit(solution)/shard_map/slice | solution.py:15
  3.2 0.6 copy.46
  3.9 3.6 %collective-permute-start = (f32[6,16,32,2]{2,1,3,0:T(8,128)S(1)}, f32[6,16,32,2]{2,1,3,0:T(8,128)}, u32[]{:S(2)}, u32[]{:S(2)}) collective-permute-start(f32[6,16,32,2]{2,1,3,0:T(8,128)S(1)} %copy.46), channel_id=1, source_target_pairs={{0,8},{8,16},{16,24},{1,9},{9,17},{17,25},{2,10},{10,18},{18,26},{... | collective-permute-start | bytes 73736 | tf_op jit(solution)/shard_map/ppermute | solution.py:17
  7.5 1.3 copy.47
  8.8 2.3 %collective-permute-start.1 = (f32[6,16,32,2]{2,1,3,0:T(8,128)}, f32[6,16,32,2]{2,1,3,0:T(8,128)}, u32[]{:S(2)}, u32[]{:S(2)}) collective-permute-start(f32[6,16,32,2]{2,1,3,0:T(8,128)} %copy.47), channel_id=1, source_target_pairs={{8,0},{16,8},{24,16},{9,1},{17,9},{25,17},{10,2},{18,10},{26,18},{... | collective-permute-start | bytes 73736 | tf_op jit(solution)/shard_map/ppermute | solution.py:18
  11.3 5.2 %all_gather.9 = f32[32,128]{0,1:T(8,128)S(1)} all-gather(f32[32,32]{0,1:T(8,128)S(1)} %convert_multiply_fusion), channel_id=1, replica_groups=mesh['gx'=4,'gy'=2,'gz'=4] {'gz'}, dimensions={1}, use_global_device_ids=true | all-gather | bytes 20480 | tf_op jit(solution)/shard_map/all_gather | solution.py:121
  16.5 4.1 %collective-permute-start.6 = (f32[32,4]{0,1:T(4,128)S(1)}, f32[32,4]{0,1:T(4,128)S(1)}, u32[]{:S(2)}, u32[]{:S(2)}) collective-permute-start(f32[32,4]{0,1:T(4,128)S(1)} %get-tuple-element.161), channel_id=1, source_target_pairs={{0,8},{8,16},{16,24},{1,9},{9,17},{17,25},{2,10},{10,18},{18,26},{... | collective-permute-start | bytes 1544 | tf_op jit(solution)/shard_map/ppermute | solution.py:17
  20.6 1.9 %collective-permute-start.7 = (f32[32,4]{0,1:T(4,128)S(1)}, f32[32,4]{0,1:T(4,128)S(1)}, u32[]{:S(2)}, u32[]{:S(2)}) collective-permute-start(f32[32,4]{0,1:T(4,128)S(1)} %get-tuple-element.162), channel_id=1, source_target_pairs={{8,0},{16,8},{24,16},{9,1},{17,9},{25,17},{10,2},{18,10},{26,18},{... | collective-permute-start | bytes 1544 | tf_op jit(solution)/shard_map/ppermute | solution.py:18
  22.5 0.7 broadcast_compare_fusion.15
  23.3 0.4 slice_reduce_fusion.15
  23.7 1.8 %select_select_fusion = f32[5,16,32,128]{3,2,1,0:T(8,128)S(1)} fusion(f32[5]{0:T(128)S(1)} %get-tuple-element.99, f32[5]{0:T(128)S(1)} %get-tuple-element.100, f32[5]{0:T(128)S(1)} %get-tuple-element.101, f32[5]{0:T(128)S(1)} %get-tuple-element.102, f32[5]{0:T(128)S(1)} %get-tuple-element.103, f32[5]{0:T(128)S(1)} %get-tuple-element.104, ...), kind=kLoop, calls=%fused_computation.83 | loop fusion | flops 5242880 | bytes 2359616 | tf_op jit(solution)/shard_map/jit(_where)/select_n | solution.py:66
  25.7 0.4 collective-permute-done.7
  26.2 3.4 %collective-permute-start.8 = (f32[4,136]{1,0:T(4,128)S(1)}, f32[4,136]{1,0:T(4,128)S(1)}, u32[]{:S(2)}, u32[]{:S(2)}) collective-permute-start(f32[4,136]{1,0:T(4,128)S(1)} %get-tuple-element.163), channel_id=1, source_target_pairs={{0,4},{1,5},{2,6},{3,7},{8,12},{9,13},{10,14},{11,15},{16,20},{17,... | collective-permute-start | bytes 6536 | tf_op jit(solution)/shard_map/ppermute | solution.py:17
  29.6 1.3 collective-permute-start.9
  30.9 0.7 fusion.70
  31.7 3.5 %collective-permute-done.9 = f32[4,136]{1,0:T(4,128)S(1)} collective-permute-done((f32[4,136]{1,0:T(4,128)S(1)}, f32[4,136]{1,0:T(4,128)S(1)}, u32[]{:S(2)}, u32[]{:S(2)}) %collective-permute-start.9) | collective-permute-done | bytes 2208 | tf_op jit(solution)/shard_map/ppermute | solution.py:18
  35.5 0.7 fusion.95
  36.2 1.6 %copy.34 = f32[6,16,32,2]{3,2,1,0:T(8,128)S(1)} copy(f32[6,16,32,2]{2,1,3,0:T(8,128)} %collective-permute-done) | data formatting | bytes 49152 | tf_op jit(solution)/shard_map/ppermute | solution.py:17
  37.8 2.7 %copy.35 = f32[6,16,32,2]{3,2,1,0:T(8,128)} copy(f32[6,16,32,2]{2,1,3,0:T(8,128)} %collective-permute-done.1) | data formatting | bytes 49152 | tf_op jit(solution)/shard_map/ppermute | solution.py:18
  40.5 1.9 %pad_maximum_fusion.41 = (f32[6,16,2,132]{3,2,1,0:T(2,128)S(1)}, f32[6,16,2,132]{3,2,1,0:T(2,128)S(1)}) fusion(f32[6,16,32,2]{3,2,1,0:T(8,128)} %copy.35, f32[6,16,32,128]{3,2,1,0:T(8,128)S(1)} %copy-done, f32[6,16,32,2]{3,2,1,0:T(8,128)S(1)} %copy.34), kind=kLoop, calls=%fused_computation.192 | loop fusion | flops 101376 | bytes 1824768 | tf_op jit(solution)/shard_map/slice | solution.py:15
  42.4 1.7 %collective-permute-start.2 = (f32[6,16,2,132]{3,2,1,0:T(2,128)S(1)}, f32[6,16,2,132]{3,2,1,0:T(2,128)S(1)}, u32[]{:S(2)}, u32[]{:S(2)}) collective-permute-start(f32[6,16,2,132]{3,2,1,0:T(2,128)S(1)} %get-tuple-element.128), channel_id=1, source_target_pairs={{0,4},{1,5},{2,6},{3,7},{8,12},{9,13},{10,14},{11,15},{16,20},{17,... | collective-permute-start | bytes 304136 | tf_op jit(solution)/shard_map/ppermute | solution.py:17
  44.1 1.3 collective-permute-start.3
  45.6 5.7 %all-gather = f32[128,128]{1,0:T(8,128)} all-gather(f32[32,128]{1,0:T(8,128)S(1)} %fusion.78), channel_id=2, replica_groups=mesh['gx'=4,'gy'=2,'gz'=4] {'gz'}, dimensions={0}, use_global_device_ids=true | all-gather | bytes 81920 | tf_op jit(solution)/shard_map/all_gather | solution.py:25
  51.3 0.4 collective-permute-done.3
  51.7 1.4 %pad_maximum_fusion.29 = (f32[6,2,36,132]{3,2,1,0:T(8,128)}, f32[6,2,36,132]{3,2,1,0:T(8,128)}) fusion(f32[6,16,2,132]{3,2,1,0:T(2,128)S(1)} %collective-permute-done.3, f32[6,16,2,132]{3,2,1,0:T(2,128)S(1)} %collective-permute-done.2, f32[6,16,32,2]{3,2,1,0:T(8,128)S(1)} %copy-done.1, f32[6,16,32,128]{3,2,1,0:T(8,128)S(1)} %copy-done, ...), kind=kLoop, calls=%fused_computation.132 | loop fusion | flops 456192 | bytes 2280960 | tf_op jit(solution)/shard_map/concatenate | solution.py:19
  53.1 1.9 %collective-permute-start.4 = (f32[6,2,36,132]{3,2,1,0:T(8,128)}, f32[6,2,36,132]{3,2,1,0:T(8,128)}, u32[]{:S(2)}, u32[]{:S(2)}) collective-permute-start(f32[6,2,36,132]{3,2,1,0:T(8,128)} %get-tuple-element.127), channel_id=1, source_target_pairs={{0,1},{1,2},{2,3},{4,5},{5,6},{6,7},{8,9},{9,10},{10,11},{12,13},{... | collective-permute-start | bytes 684296 | tf_op jit(solution)/shard_map/ppermute | solution.py:17
  55.0 3.8 %collective-permute-start.5 = (f32[6,2,36,132]{3,2,1,0:T(8,128)}, f32[6,2,36,132]{3,2,1,0:T(8,128)}, u32[]{:S(2)}, u32[]{:S(2)}) collective-permute-start(f32[6,2,36,132]{3,2,1,0:T(8,128)} %get-tuple-element.126), channel_id=1, source_target_pairs={{1,0},{2,1},{3,2},{5,4},{6,5},{7,6},{9,8},{10,9},{11,10},{13,12},{... | collective-permute-start | bytes 684296 | tf_op jit(solution)/shard_map/ppermute | solution.py:18
  58.8 2.9 %while.14 = (s32[]{:T(128)}, f32[32,128]{1,0:T(8,128)S(1)}, s32[]{:T(128)}, f32[4,32,128]{2,1,0:T(8,128)}, s32[]{:T(128)}, /*index=5*/s32[]{:T(128)}) while((s32[]{:T(128)}, f32[32,128]{1,0:T(8,128)S(1)}, s32[]{:T(128)}, f32[4,32,128]{2,1,0:T(8,128)}, s32[]{:T(128)}, /*index=5*/s32[]{:T(128)}) %tuple.88), condition=%wide.region_2.3_spmd.clone, body=%wide.region_1.2_spmd.clone.sunk | while | flops 12292 | bytes 49245 | solution.py:33
  58.9 0.7 add_select_fusion.2
  59.6 0.7 add_select_fusion.2
  60.3 0.7 add_select_fusion.2
  61.0 0.7 add_select_fusion.2
  61.8 1.8 %collective-permute-done.4 = f32[6,2,36,132]{3,2,1,0:T(8,128)} collective-permute-done((f32[6,2,36,132]{3,2,1,0:T(8,128)}, f32[6,2,36,132]{3,2,1,0:T(8,128)}, u32[]{:S(2)}, u32[]{:S(2)}) %collective-permute-start.4) | collective-permute-done | bytes 228128 | tf_op jit(solution)/shard_map/ppermute | solution.py:17
  63.5 1.8 %collective-permute-done.5 = f32[6,2,36,132]{3,2,1,0:T(8,128)} collective-permute-done((f32[6,2,36,132]{3,2,1,0:T(8,128)}, f32[6,2,36,132]{3,2,1,0:T(8,128)}, u32[]{:S(2)}, u32[]{:S(2)}) %collective-permute-start.5) | collective-permute-done | bytes 228128 | tf_op jit(solution)/shard_map/ppermute | solution.py:18
  65.3 3.4 %pad_maximum_fusion = f32[6,20,36,132]{3,2,1,0:T(8,128)S(1)} fusion(f32[6,2,36,132]{3,2,1,0:T(8,128)} %collective-permute-done.5, f32[6,16,2,132]{3,2,1,0:T(2,128)S(1)} %collective-permute-done.3, f32[6,16,32,2]{3,2,1,0:T(8,128)} %copy.35, f32[6,16,32,128]{3,2,1,0:T(8,128)S(1)} %copy-done, f32[6,16,32,2]{3,2,1,0:T(8,128)S(1)} %copy.34, ...), kind=kLoop, calls=%fused_computation.1 | loop fusion | flops 3421440 | bytes 4561920 | tf_op jit(solution)/shard_map/concatenate | solution.py:19
  68.9 1.3 copy-done.2
  70.1 5.3 %fusion.14 = f32[3,20,36,132]{3,2,1,0:T(8,128)S(1)} fusion(f32[6,16,32,2]{3,2,1,0:T(8,128)S(1)} %copy.34, f32[6,16,32,128]{3,2,1,0:T(8,128)S(1)} %copy-done, f32[6,16,32,2]{3,2,1,0:T(8,128)S(1)} %copy-done.2, f32[6,2,36,132]{3,2,1,0:T(8,128)} %collective-permute-done.4, f32[6,2,36,132]{3,2,1,0:T(8,128)} %collective-permute-done.5, ...), kind=kLoop, calls=%fused_computation.46 | loop fusion | flops 13115520 | bytes 3421440 | tf_op jit(solution)/shard_map/concatenate | solution.py:142
  75.4 1.7 %fusion.6 = f32[3,20,36,132]{3,2,1,0:T(8,128)S(1)} fusion(f32[6,16,32,2]{3,2,1,0:T(8,128)S(1)} %copy.34, f32[6,16,32,128]{3,2,1,0:T(8,128)S(1)} %copy-done, f32[6,16,32,2]{3,2,1,0:T(8,128)S(1)} %copy-done.2, f32[6,2,36,132]{3,2,1,0:T(8,128)} %collective-permute-done.4, f32[6,2,36,132]{3,2,1,0:T(8,128)} %collective-permute-done.5, ...), kind=kLoop, calls=%fused_computation.38 | loop fusion | flops 4276800 | bytes 4181760 | tf_op jit(solution)/shard_map/concatenate | solution.py:141
  77.2 1.5 %fusion.49 = (f32[3,16,32,128]{3,2,1,0:T(8,128)S(1)}, f32[3,16,32,128]{3,2,1,0:T(8,128)S(1)}) fusion(f32[3,20,36,132]{3,2,1,0:T(8,128)S(1)} %fusion.14, f32[3,20,36,132]{3,2,1,0:T(8,128)S(1)} %fusion.6), kind=kLoop, calls=%fused_computation.122 | loop fusion | flops 1966080 | bytes 7864320 | tf_op jit(solution)/shard_map/div | solution.py:54
  78.7 4.6 %fusion.30 = f32[6,16,32,128]{3,2,1,0:T(8,128)S(1)} fusion(f32[6,2,36,132]{3,2,1,0:T(8,128)} %collective-permute-done.4, f32[6,16,2,132]{3,2,1,0:T(2,128)S(1)} %collective-permute-done.3, f32[6,16,2,132]{3,2,1,0:T(2,128)S(1)} %collective-permute-done.2, f32[6,16,32,2]{3,2,1,0:T(8,128)S(1)} %copy-done.2, f32[6,16,32,128]{3,2,1,0:T(8,128)S(1)} %copy-done, ...), kind=kLoop, calls=%fused_computation.65 | loop fusion | flops 9830400 | bytes 3853824 | tf_op jit(solution)/shard_map/div | solution.py:54
  83.3 0.4 fusion.68
  84.0 0.7 copy-done.8
  85.1 1.2 fusion.98
  86.3 1.5 %copy.40 = f32[3,16,32,2]{2,1,3,0:T(8,128)S(1)} copy(f32[3,16,32,2]{3,2,1,0:T(8,128)} %get-tuple-element.141) | data formatting | bytes 24576 | tf_op jit(solution)/shard_map/slice | solution.py:16
  87.7 2.4 %collective-permute-start.10 = (f32[3,16,32,2]{2,1,3,0:T(8,128)S(1)}, f32[3,16,32,2]{2,1,3,0:T(8,128)S(1)}, u32[]{:S(2)}, u32[]{:S(2)}) collective-permute-start(f32[3,16,32,2]{2,1,3,0:T(8,128)S(1)} %copy.40), channel_id=1, source_target_pairs={{8,0},{16,8},{24,16},{9,1},{17,9},{25,17},{10,2},{18,10},{26,18},{... | collective-permute-start | bytes 36872 | tf_op jit(solution)/shard_map/ppermute | solution.py:18
  90.2 1.0 copy.42
  91.1 3.4 %collective-permute-start.11 = (f32[3,16,32,2]{2,1,3,0:T(8,128)}, f32[3,16,32,2]{2,1,3,0:T(8,128)}, u32[]{:S(2)}, u32[]{:S(2)}) collective-permute-start(f32[3,16,32,2]{2,1,3,0:T(8,128)} %copy.42), channel_id=1, source_target_pairs={{0,8},{8,16},{16,24},{1,9},{9,17},{17,25},{2,10},{10,18},{18,26},{... | collective-permute-start | bytes 36872 | tf_op jit(solution)/shard_map/ppermute | solution.py:17
  94.6 0.4 copy.41
  94.9 2.5 %collective-permute-done.11 = f32[3,16,32,2]{2,1,3,0:T(8,128)} collective-permute-done((f32[3,16,32,2]{2,1,3,0:T(8,128)}, f32[3,16,32,2]{2,1,3,0:T(8,128)}, u32[]{:S(2)}, u32[]{:S(2)}) %collective-permute-start.11) | collective-permute-done | bytes 12320 | tf_op jit(solution)/shard_map/ppermute | solution.py:17
  97.4 2.0 %copy.43 = f32[3,16,32,2]{3,2,1,0:T(8,128)} copy(f32[3,16,32,2]{2,1,3,0:T(8,128)} %collective-permute-done.11) | data formatting | bytes 24576 | tf_op jit(solution)/shard_map/ppermute | solution.py:17
  99.5 1.5 %pad_maximum_fusion.44 = (f32[3,16,2,132]{3,2,1,0:T(2,128)S(1)}, f32[3,16,2,132]{3,2,1,0:T(2,128)S(1)}) fusion(f32[3,16,32,2]{3,2,1,0:T(8,128)S(1)} %copy.41, f32[3,16,32,128]{3,2,1,0:T(8,128)S(1)} %fusion.54, f32[3,16,32,2]{3,2,1,0:T(8,128)} %copy.43), kind=kLoop, calls=%fused_computation.214 | loop fusion | flops 50688 | bytes 912384 | tf_op jit(solution)/shard_map/slice | solution.py:15
  101.0 4.3 %collective-permute-start.12 = (f32[3,16,2,132]{3,2,1,0:T(2,128)S(1)}, f32[3,16,2,132]{3,2,1,0:T(2,128)S(1)}, u32[]{:S(2)}, u32[]{:S(2)}) collective-permute-start(f32[3,16,2,132]{3,2,1,0:T(2,128)S(1)} %get-tuple-element.134), channel_id=1, source_target_pairs={{0,4},{1,5},{2,6},{3,7},{8,12},{9,13},{10,14},{11,15},{16,20},{17,... | collective-permute-start | bytes 152072 | tf_op jit(solution)/shard_map/ppermute | solution.py:17
  105.3 1.3 collective-permute-start.13
  106.6 0.9 collective-permute-done.12
  107.5 4.3 %collective-permute-done.13 = f32[3,16,2,132]{3,2,1,0:T(2,128)S(1)} collective-permute-done((f32[3,16,2,132]{3,2,1,0:T(2,128)S(1)}, f32[3,16,2,132]{3,2,1,0:T(2,128)S(1)}, u32[]{:S(2)}, u32[]{:S(2)}) %collective-permute-start.13) | collective-permute-done | bytes 50720 | tf_op jit(solution)/shard_map/ppermute | solution.py:18
  112.1 1.9 %collective-permute-start.14 = (f32[3,2,36,132]{3,2,1,0:T(8,128)S(1)}, f32[3,2,36,132]{3,2,1,0:T(8,128)S(1)}, u32[]{:S(2)}, u32[]{:S(2)}) collective-permute-start(f32[3,2,36,132]{3,2,1,0:T(8,128)S(1)} %get-tuple-element.132), channel_id=1, source_target_pairs={{1,0},{2,1},{3,2},{5,4},{6,5},{7,6},{9,8},{10,9},{11,10},{13,12},{... | collective-permute-start | bytes 342152 | tf_op jit(solution)/shard_map/ppermute | solution.py:18
  114.0 2.6 %collective-permute-start.15 = (f32[3,2,36,132]{3,2,1,0:T(8,128)S(1)}, f32[3,2,36,132]{3,2,1,0:T(8,128)S(1)}, u32[]{:S(2)}, u32[]{:S(2)}) collective-permute-start(f32[3,2,36,132]{3,2,1,0:T(8,128)S(1)} %get-tuple-element.133), channel_id=1, source_target_pairs={{0,1},{1,2},{2,3},{4,5},{5,6},{6,7},{8,9},{9,10},{10,11},{12,13},{... | collective-permute-start | bytes 342152 | tf_op jit(solution)/shard_map/ppermute | solution.py:17
  116.9 0.8 collective-permute-done.14
  117.7 3.8 %collective-permute-done.15 = f32[3,2,36,132]{3,2,1,0:T(8,128)S(1)} collective-permute-done((f32[3,2,36,132]{3,2,1,0:T(8,128)S(1)}, f32[3,2,36,132]{3,2,1,0:T(8,128)S(1)}, u32[]{:S(2)}, u32[]{:S(2)}) %collective-permute-start.15) | collective-permute-done | bytes 114080 | tf_op jit(solution)/shard_map/ppermute | solution.py:17
  121.5 4.1 %fusion.42 = f32[3,16,32,128]{3,2,1,0:T(8,128)S(1)} fusion(f32[3,16,2,132]{3,2,1,0:T(2,128)S(1)} %collective-permute-done.12, f32[3,16,32,2]{3,2,1,0:T(8,128)S(1)} %copy.41, f32[3,16,32,128]{3,2,1,0:T(8,128)S(1)} %fusion.54, f32[3,16,32,2]{3,2,1,0:T(8,128)S(1)} %copy-done.4, f32[3,16,2,132]{3,2,1,0:T(2,128)S(1)} %collective-permute-done.13, ...), kind=kLoop, calls=%fused_computation.95 | loop fusion | flops 8454144 | bytes 2189056 | tf_op jit(solution)/shard_map/sub | solution.py:85
  125.6 1.1 broadcast_multiply_fusion
  126.7 4.0 %fusion.37 = f32[3,16,32,128]{3,2,1,0:T(8,128)S(1)} fusion(f32[3,16,32,2]{3,2,1,0:T(8,128)S(1)} %copy-done.4, f32[3,16,32,128]{3,2,1,0:T(8,128)S(1)} %fusion.54, f32[3,16,32,2]{3,2,1,0:T(8,128)S(1)} %copy.41, f32[16,32,128]{2,1,0:T(8,128)S(1)} %get-tuple-element.144, f32[3,16,2,132]{3,2,1,0:T(2,128)S(1)} %collective-permute-done.13, ...), kind=kLoop, calls=%fused_computation.89 | loop fusion | flops 6881280 | bytes 2189056 | tf_op jit(solution)/shard_map/sub | solution.py:84
  131.2 1.2 copy-done.7
  132.4 2.5 %multiply_add_fusion = (f32[6,16,32,128]{3,2,1,0:T(8,128)}, f32[6,16,32,128]{3,2,1,0:T(8,128)}) fusion(f32[6,16,32,128]{3,2,1,0:T(8,128)S(1)} %copy-done, f32[6,16,32,128]{3,2,1,0:T(8,128)S(1)} %fusion.57, f32[16,32,128]{2,1,0:T(8,128)S(1)} %get-tuple-element.140, f32[6,16,32,128]{3,2,1,0:T(8,128)S(1)} %copy-done.7, f32[16,32,128]{2,1,0:T(8,128)S(1)} %get-tuple-element.138), kind=kLoop, calls=%fused_computation.81 | loop fusion | flops 2359296 | bytes 8388608 | tf_op jit(solution)/shard_map/add | solution.py:102
  (88 shorter events, 2.8 us)
Async XLA Ops:
  3.2 8.0 %copy-start.18 = (s32[32,32]{1,0:T(8,128)S(1)}, s32[32,32]{1,0:T(8,128)}, u32[]{:S(2)}) copy-start(s32[32,32]{1,0:T(8,128)} %param.14) | copy-start | bytes 12292
  3.2 19.3 %copy-start.17 = (s32[16,32,128]{2,1,0:T(8,128)S(1)}, s32[16,32,128]{2,1,0:T(8,128)}, u32[]{:S(2)}) copy-start(s32[16,32,128]{2,1,0:T(8,128)} %param.17) | copy-start | bytes 786436
  3.9 19.4 %copy-start.29 = (f32[16]{0:T(128)S(1)}, f32[16]{0:T(128)}, u32[]{:S(2)}) copy-start(f32[16]{0:T(128)} %param.21) | copy-start | bytes 196
  3.9 32.3 %collective-permute-start = (f32[6,16,32,2]{2,1,3,0:T(8,128)S(1)}, f32[6,16,32,2]{2,1,3,0:T(8,128)}, u32[]{:S(2)}, u32[]{:S(2)}) collective-permute-start(f32[6,16,32,2]{2,1,3,0:T(8,128)S(1)} %copy.46), channel_id=1, source_target_pairs={{0,8},{8,16},{16,24},{1,9},{9,17},{17,25},{2,10},{10,18},{18,26},{... | collective-permute-start | bytes 73736 | tf_op jit(solution)/shard_map/ppermute | solution.py:17
  7.5 15.7 %copy-start.25 = (f32[16]{0:T(128)S(1)}, f32[16]{0:T(128)}, u32[]{:S(2)}) copy-start(f32[16]{0:T(128)} %param.18) | copy-start | bytes 196
  7.5 15.7 %copy-start.26 = (f32[16]{0:T(128)S(1)}, f32[16]{0:T(128)}, u32[]{:S(2)}) copy-start(f32[16]{0:T(128)} %param.19) | copy-start | bytes 196
  7.5 15.7 %copy-start.27 = (f32[16]{0:T(128)S(1)}, f32[16]{0:T(128)}, u32[]{:S(2)}) copy-start(f32[16]{0:T(128)} %param.20) | copy-start | bytes 196
  7.5 15.7 %copy-start.28 = (f32[16]{0:T(128)S(1)}, f32[16]{0:T(128)}, u32[]{:S(2)}) copy-start(f32[16]{0:T(128)} %param.22) | copy-start | bytes 196
  8.8 29.0 %collective-permute-start.1 = (f32[6,16,32,2]{2,1,3,0:T(8,128)}, f32[6,16,32,2]{2,1,3,0:T(8,128)}, u32[]{:S(2)}, u32[]{:S(2)}) collective-permute-start(f32[6,16,32,2]{2,1,3,0:T(8,128)} %copy.47), channel_id=1, source_target_pairs={{8,0},{16,8},{24,16},{9,1},{17,9},{25,17},{10,2},{18,10},{26,18},{... | collective-permute-start | bytes 73736 | tf_op jit(solution)/shard_map/ppermute | solution.py:18
  16.5 9.1 %collective-permute-start.6 = (f32[32,4]{0,1:T(4,128)S(1)}, f32[32,4]{0,1:T(4,128)S(1)}, u32[]{:S(2)}, u32[]{:S(2)}) collective-permute-start(f32[32,4]{0,1:T(4,128)S(1)} %get-tuple-element.161), channel_id=1, source_target_pairs={{0,8},{8,16},{16,24},{1,9},{9,17},{17,25},{2,10},{10,18},{18,26},{... | collective-permute-start | bytes 1544 | tf_op jit(solution)/shard_map/ppermute | solution.py:17
  20.6 5.5 %collective-permute-start.7 = (f32[32,4]{0,1:T(4,128)S(1)}, f32[32,4]{0,1:T(4,128)S(1)}, u32[]{:S(2)}, u32[]{:S(2)}) collective-permute-start(f32[32,4]{0,1:T(4,128)S(1)} %get-tuple-element.162), channel_id=1, source_target_pairs={{8,0},{16,8},{24,16},{9,1},{17,9},{25,17},{10,2},{18,10},{26,18},{... | collective-permute-start | bytes 1544 | tf_op jit(solution)/shard_map/ppermute | solution.py:18
  25.5 9.9 %copy-start.5 = (f32[5,16,32,128]{3,2,1,0:T(8,128)}, f32[5,16,32,128]{3,2,1,0:T(8,128)S(1)}, u32[]{:S(2)}) copy-start(f32[5,16,32,128]{3,2,1,0:T(8,128)S(1)} %select_select_fusion) | copy-start | bytes 3932164
  26.2 5.4 %collective-permute-start.8 = (f32[4,136]{1,0:T(4,128)S(1)}, f32[4,136]{1,0:T(4,128)S(1)}, u32[]{:S(2)}, u32[]{:S(2)}) collective-permute-start(f32[4,136]{1,0:T(4,128)S(1)} %get-tuple-element.163), channel_id=1, source_target_pairs={{0,4},{1,5},{2,6},{3,7},{8,12},{9,13},{10,14},{11,15},{16,20},{17,... | collective-permute-start | bytes 6536 | tf_op jit(solution)/shard_map/ppermute | solution.py:17
  29.6 5.5 %collective-permute-start.9 = (f32[4,136]{1,0:T(4,128)S(1)}, f32[4,136]{1,0:T(4,128)S(1)}, u32[]{:S(2)}, u32[]{:S(2)}) collective-permute-start(f32[4,136]{1,0:T(4,128)S(1)} %get-tuple-element.164), channel_id=1, source_target_pairs={{4,0},{5,1},{6,2},{7,3},{12,8},{13,9},{14,10},{15,11},{20,16},{21,... | collective-permute-start | bytes 6536 | tf_op jit(solution)/shard_map/ppermute | solution.py:18
  36.2 4.3 %copy-start = (f32[6,16,32,128]{3,2,1,0:T(8,128)S(1)}, f32[6,16,32,128]{3,2,1,0:T(8,128)}, u32[]{:S(2)}) copy-start(f32[6,16,32,128]{3,2,1,0:T(8,128)} %param.24) | copy-start | bytes 4718596
  40.5 4.9 %copy-start.10 = (f32[32,128]{1,0:T(8,128)S(1)}, f32[32,128]{1,0:T(8,128)}, u32[]{:S(2)}) copy-start(f32[32,128]{1,0:T(8,128)} %get-tuple-element.167) | copy-start | bytes 49156
  40.5 4.9 %copy-start.19 = (f32[16]{0:T(128)S(1)}, f32[16]{0:T(128)}, u32[]{:S(2)}) copy-start(f32[16]{0:T(128)} %param.16) | copy-start | bytes 196
  40.5 4.9 %copy-start.22 = (f32[16]{0:T(128)S(1)}, f32[16]{0:T(128)}, u32[]{:S(2)}) copy-start(f32[16]{0:T(128)} %param.15) | copy-start | bytes 196
  40.5 11.2 %copy-start.1 = (f32[6,16,32,2]{3,2,1,0:T(8,128)S(1)}, f32[6,16,32,2]{3,2,1,0:T(8,128)}, u32[]{:S(2)}) copy-start(f32[6,16,32,2]{3,2,1,0:T(8,128)} %copy.35) | copy-start | bytes 73732
  42.4 8.8 %collective-permute-start.2 = (f32[6,16,2,132]{3,2,1,0:T(2,128)S(1)}, f32[6,16,2,132]{3,2,1,0:T(2,128)S(1)}, u32[]{:S(2)}, u32[]{:S(2)}) collective-permute-start(f32[6,16,2,132]{3,2,1,0:T(2,128)S(1)} %get-tuple-element.128), channel_id=1, source_target_pairs={{0,4},{1,5},{2,6},{3,7},{8,12},{9,13},{10,14},{11,15},{16,20},{17,... | collective-permute-start | bytes 304136 | tf_op jit(solution)/shard_map/ppermute | solution.py:17
  44.1 7.6 %collective-permute-start.3 = (f32[6,16,2,132]{3,2,1,0:T(2,128)S(1)}, f32[6,16,2,132]{3,2,1,0:T(2,128)S(1)}, u32[]{:S(2)}, u32[]{:S(2)}) collective-permute-start(f32[6,16,2,132]{3,2,1,0:T(2,128)S(1)} %get-tuple-element.129), channel_id=1, source_target_pairs={{4,0},{5,1},{6,2},{7,3},{12,8},{13,9},{14,10},{15,11},{20,16},{21,... | collective-permute-start | bytes 304136 | tf_op jit(solution)/shard_map/ppermute | solution.py:18
  53.1 10.5 %collective-permute-start.4 = (f32[6,2,36,132]{3,2,1,0:T(8,128)}, f32[6,2,36,132]{3,2,1,0:T(8,128)}, u32[]{:S(2)}, u32[]{:S(2)}) collective-permute-start(f32[6,2,36,132]{3,2,1,0:T(8,128)} %get-tuple-element.127), channel_id=1, source_target_pairs={{0,1},{1,2},{2,3},{4,5},{5,6},{6,7},{8,9},{9,10},{10,11},{12,13},{... | collective-permute-start | bytes 684296 | tf_op jit(solution)/shard_map/ppermute | solution.py:17
  55.0 10.3 %collective-permute-start.5 = (f32[6,2,36,132]{3,2,1,0:T(8,128)}, f32[6,2,36,132]{3,2,1,0:T(8,128)}, u32[]{:S(2)}, u32[]{:S(2)}) collective-permute-start(f32[6,2,36,132]{3,2,1,0:T(8,128)} %get-tuple-element.126), channel_id=1, source_target_pairs={{1,0},{2,1},{3,2},{5,4},{6,5},{7,6},{9,8},{10,9},{11,10},{13,12},{... | collective-permute-start | bytes 684296 | tf_op jit(solution)/shard_map/ppermute | solution.py:18
  68.7 1.4 %copy-start.2 = (f32[6,16,32,2]{3,2,1,0:T(8,128)S(1)}, f32[6,16,32,2]{3,2,1,0:T(8,128)}, u32[]{:S(2)}) copy-start(f32[6,16,32,2]{3,2,1,0:T(8,128)} %copy.35) | copy-start | bytes 73732
  78.6 4.6 %copy-start.11 = (f32[32,128]{1,0:T(8,128)S(1)}, f32[32,128]{1,0:T(8,128)}, u32[]{:S(2)}) copy-start(f32[32,128]{1,0:T(8,128)} %get-tuple-element.167) | copy-start | bytes 49156
  78.7 4.6 %copy-start.13 = (f32[32,128]{1,0:T(8,128)S(1)}, f32[32,128]{1,0:T(8,128)}, u32[]{:S(2)}) copy-start(f32[32,128]{1,0:T(8,128)} %get-tuple-element.165) | copy-start | bytes 49156
  78.7 4.6 %copy-start.15 = (f32[32,128]{1,0:T(8,128)S(1)}, f32[32,128]{1,0:T(8,128)}, u32[]{:S(2)}) copy-start(f32[32,128]{1,0:T(8,128)} %get-tuple-element.166) | copy-start | bytes 49156
  78.7 4.6 %copy-start.20 = (f32[16]{0:T(128)S(1)}, f32[16]{0:T(128)}, u32[]{:S(2)}) copy-start(f32[16]{0:T(128)} %param.16) | copy-start | bytes 196
  78.7 4.6 %copy-start.23 = (f32[16]{0:T(128)S(1)}, f32[16]{0:T(128)}, u32[]{:S(2)}) copy-start(f32[16]{0:T(128)} %param.15) | copy-start | bytes 196
  83.7 1.0 copy-start.8
  83.7 1.2 copy-start.9
  85.1 41.6 %copy-start.3 = (f32[3,16,32,128]{3,2,1,0:T(8,128)}, f32[3,16,32,128]{3,2,1,0:T(8,128)S(1)}, u32[]{:S(2)}) copy-start(f32[3,16,32,128]{3,2,1,0:T(8,128)S(1)} %fusion.54) | copy-start | bytes 2359300
  87.7 6.8 %collective-permute-start.10 = (f32[3,16,32,2]{2,1,3,0:T(8,128)S(1)}, f32[3,16,32,2]{2,1,3,0:T(8,128)S(1)}, u32[]{:S(2)}, u32[]{:S(2)}) collective-permute-start(f32[3,16,32,2]{2,1,3,0:T(8,128)S(1)} %copy.40), channel_id=1, source_target_pairs={{8,0},{16,8},{24,16},{9,1},{17,9},{25,17},{10,2},{18,10},{26,18},{... | collective-permute-start | bytes 36872 | tf_op jit(solution)/shard_map/ppermute | solution.py:18
  91.1 6.3 %collective-permute-start.11 = (f32[3,16,32,2]{2,1,3,0:T(8,128)}, f32[3,16,32,2]{2,1,3,0:T(8,128)}, u32[]{:S(2)}, u32[]{:S(2)}) collective-permute-start(f32[3,16,32,2]{2,1,3,0:T(8,128)} %copy.42), channel_id=1, source_target_pairs={{0,8},{8,16},{16,24},{1,9},{9,17},{17,25},{2,10},{10,18},{18,26},{... | collective-permute-start | bytes 36872 | tf_op jit(solution)/shard_map/ppermute | solution.py:17
  99.5 12.3 %copy-start.4 = (f32[3,16,32,2]{3,2,1,0:T(8,128)S(1)}, f32[3,16,32,2]{3,2,1,0:T(8,128)}, u32[]{:S(2)}) copy-start(f32[3,16,32,2]{3,2,1,0:T(8,128)} %copy.43) | copy-start | bytes 36868
  100.9 15.7 %copy-start.12 = (f32[32,128]{1,0:T(8,128)S(1)}, f32[32,128]{1,0:T(8,128)}, u32[]{:S(2)}) copy-start(f32[32,128]{1,0:T(8,128)} %get-tuple-element.167) | copy-start | bytes 49156
  100.9 15.7 %copy-start.14 = (f32[32,128]{1,0:T(8,128)S(1)}, f32[32,128]{1,0:T(8,128)}, u32[]{:S(2)}) copy-start(f32[32,128]{1,0:T(8,128)} %get-tuple-element.165) | copy-start | bytes 49156
  101.0 15.7 %copy-start.16 = (f32[32,128]{1,0:T(8,128)S(1)}, f32[32,128]{1,0:T(8,128)}, u32[]{:S(2)}) copy-start(f32[32,128]{1,0:T(8,128)} %get-tuple-element.166) | copy-start | bytes 49156
  101.0 15.7 %copy-start.21 = (f32[16]{0:T(128)S(1)}, f32[16]{0:T(128)}, u32[]{:S(2)}) copy-start(f32[16]{0:T(128)} %param.16) | copy-start | bytes 196
  101.0 15.7 %copy-start.24 = (f32[16]{0:T(128)S(1)}, f32[16]{0:T(128)}, u32[]{:S(2)}) copy-start(f32[16]{0:T(128)} %param.15) | copy-start | bytes 196
  101.0 6.5 %collective-permute-start.12 = (f32[3,16,2,132]{3,2,1,0:T(2,128)S(1)}, f32[3,16,2,132]{3,2,1,0:T(2,128)S(1)}, u32[]{:S(2)}, u32[]{:S(2)}) collective-permute-start(f32[3,16,2,132]{3,2,1,0:T(2,128)S(1)} %get-tuple-element.134), channel_id=1, source_target_pairs={{0,4},{1,5},{2,6},{3,7},{8,12},{9,13},{10,14},{11,15},{16,20},{17,... | collective-permute-start | bytes 152072 | tf_op jit(solution)/shard_map/ppermute | solution.py:17
  105.3 6.5 %collective-permute-start.13 = (f32[3,16,2,132]{3,2,1,0:T(2,128)S(1)}, f32[3,16,2,132]{3,2,1,0:T(2,128)S(1)}, u32[]{:S(2)}, u32[]{:S(2)}) collective-permute-start(f32[3,16,2,132]{3,2,1,0:T(2,128)S(1)} %get-tuple-element.135), channel_id=1, source_target_pairs={{4,0},{5,1},{6,2},{7,3},{12,8},{13,9},{14,10},{15,11},{20,16},{21,... | collective-permute-start | bytes 152072 | tf_op jit(solution)/shard_map/ppermute | solution.py:18
  112.1 5.6 %collective-permute-start.14 = (f32[3,2,36,132]{3,2,1,0:T(8,128)S(1)}, f32[3,2,36,132]{3,2,1,0:T(8,128)S(1)}, u32[]{:S(2)}, u32[]{:S(2)}) collective-permute-start(f32[3,2,36,132]{3,2,1,0:T(8,128)S(1)} %get-tuple-element.132), channel_id=1, source_target_pairs={{1,0},{2,1},{3,2},{5,4},{6,5},{7,6},{9,8},{10,9},{11,10},{13,12},{... | collective-permute-start | bytes 342152 | tf_op jit(solution)/shard_map/ppermute | solution.py:18
  114.0 7.5 %collective-permute-start.15 = (f32[3,2,36,132]{3,2,1,0:T(8,128)S(1)}, f32[3,2,36,132]{3,2,1,0:T(8,128)S(1)}, u32[]{:S(2)}, u32[]{:S(2)}) collective-permute-start(f32[3,2,36,132]{3,2,1,0:T(8,128)S(1)} %get-tuple-element.133), channel_id=1, source_target_pairs={{0,1},{1,2},{2,3},{4,5},{5,6},{6,7},{8,9},{9,10},{10,11},{12,13},{... | collective-permute-start | bytes 342152 | tf_op jit(solution)/shard_map/ppermute | solution.py:17
  126.7 4.0 %copy-start.6 = (f32[5,16,32,128]{3,2,1,0:T(8,128)S(1)}, f32[5,16,32,128]{3,2,1,0:T(8,128)}, u32[]{:S(2)}) copy-start(f32[5,16,32,128]{3,2,1,0:T(8,128)} %copy-done.5) | copy-start | bytes 3932164
  131.0 1.4 %copy-start.7 = (f32[6,16,32,128]{3,2,1,0:T(8,128)S(1)}, f32[6,16,32,128]{3,2,1,0:T(8,128)}, u32[]{:S(2)}) copy-start(f32[6,16,32,128]{3,2,1,0:T(8,128)} %param.25) | copy-start | bytes 4718596
where the time goes:
time: 136 us; the launch traced here: 135 us
  other arithmetic  41.9 us (31%)
  starting transfers between devices  41.3 us (30%)
  waiting for transfers between devices  20.1 us (15%)
  local copies, waits for them, and re-layouts  19.2 us (14%)
  blocking collectives  10.9 us (8%)
  between operations  1.36 us (1%)
    ppermute x8, starting transfers between devices, padded_2(): before = lax.ppermute(last, axis, up)  25 us
    ppermute x8, starting transfers between devices, padded_2(): after = lax.ppermute(leading, axis, down)  16.3 us
    ppermute x8, waiting for transfers between devices, padded_2(): after = lax.ppermute(leading, axis, down)  11.1 us
    ppermute x8, waiting for transfers between devices, padded_2(): before = lax.ppermute(last, axis, up)  9 us
    div x3, other arithmetic, centred(): return (8.0 * closer - farther) / 12.0  6.76 us
    all_gather x1, blocking collectives, prefix(): everything = lax.all_gather(value, axis)  5.69 us
    unnamed x63, local copies, waits for them, and re-layouts  5.54 us
    concatenate x1, other arithmetic, local(): jnp.concatenate([padded[3:4], padded[1:2], padded[5:6]])[:, 2:-2, :, 2:-2]  5.29 us
  transfers between devices with their start and end apart: 16, of which 10 were waited for; matrix products, arithmetic and copies ran while one was open for 9% of the time, Pallas kernels for 0%

commit v1 on v0

v1 whole, which is shorter than its diff:
```python
import functools
import jax
import jax.numpy as jnp
from jax import lax
from jax.experimental import pallas as pl
from jax.experimental.pallas import tpu as pltpu
from jax.sharding import PartitionSpec as P

step_size = 0.3
SUB = 8
PAD = 8
F32 = jnp.float32
params = functools.partial(pltpu.CompilerParams, vmem_limit_bytes=48 * 1024 * 1024)
VM = pl.BlockSpec(memory_space=pltpu.VMEM)
SM = pl.BlockSpec(memory_space=pltpu.SMEM)


def ring(n, step):
    return [(i, (i + step) % n) for i in range(n)]


def exchange(axis, n, to_after, to_before):
    if n == 1:
        return to_after, to_before
    if n == 2:
        mine = lax.axis_index(axis)
        got = lax.ppermute(jnp.where(mine == 0, to_after, to_before), axis, ring(2, 1))
        return got, got
    return lax.ppermute(to_after, axis, ring(n, 1)), lax.ppermute(to_before, axis, ring(n, -1))


def lanes_of(shape):
    return lax.broadcasted_iota(jnp.int32, shape, len(shape) - 1)


def terrain_piece_kernel(gz_axis, elev_ref, base_ref, stretch_ref, out_ref):
    mine = lax.axis_index(gz_axis)
    ny, width = elev_ref.shape
    nx = out_ref.shape[1]
    nz = base_ref.shape[1]
    height = elev_ref[...].astype(F32) / 200.0
    wide = jnp.concatenate([height, jnp.zeros((ny, nx - width), F32)], axis=1)
    out_ref[:ny, :] = pltpu.roll(wide, mine * width, 1)
    row = lax.broadcasted_iota(jnp.int32, (SUB, nx), 0)
    fill = jnp.zeros((1, nx - nz), F32)
    base = jnp.concatenate([base_ref[...], fill], axis=1)
    stretch = jnp.concatenate([stretch_ref[...], fill], axis=1)
    both = jnp.where(row == 0, base, jnp.where(row == 1, stretch, 0.0))
    out_ref[ny:, :] = pltpu.roll(both, mine * nz, 1)


def pack_sides(field, nz, ny, nx):
    tiles = ny // SUB
    lane2 = lanes_of((SUB, nx)) // 2
    low, high = [], []
    for c in range(3):
        lo = jnp.zeros((SUB, nx), F32)
        hi = jnp.zeros((SUB, nx), F32)
        for k in range(nz):
            for t in range(tiles):
                m = k * tiles + t
                turned = pltpu.roll(field(c, k, t), (2 * m + 2) % nx, 1)
                hi = jnp.where(lane2 == m, turned, hi)
                lo = jnp.where(lane2 == (m + 1) % (nx // 2), turned, lo)
        low.append(lo)
        high.append(hi)
    return low, high


def pack_kernel(rows_out, stress_ref, low_ref, high_ref, *y_refs):
    _, nz, ny, nx = stress_ref.shape
    of_x = (0, 3, 4)
    of_y = (3, 1, 5)
    low, high = pack_sides(
        lambda c, k, t: stress_ref[of_x[c], k, SUB * t : SUB * t + SUB, :], nz, ny, nx
    )
    for c in range(3):
        low_ref[SUB * c : SUB * c + SUB, :] = low[c]
        high_ref[SUB * c : SUB * c + SUB, :] = high[c]
    for c in range(3):
        for k in range(nz):
            j = 2 * (c * nz + k)
            y_refs[0][j : j + 2, :] = stress_ref[of_y[c], k, ny - 2 : ny, :]
            y_refs[1][j : j + 2, :] = stress_ref[of_y[c], k, 0:2, :]


def y_terrain_kernel(sizes, slab_ref, left_ref, right_ref, after_ref, before_ref):
    n = sizes[0]
    mine = lax.axis_index("gx")
    nx = slab_ref.shape[1]
    ny = slab_ref.shape[0] - SUB
    lane = lanes_of((4, nx))
    for ref, start in ((after_ref, ny - 4), (before_ref, 0)):
        left = jnp.where(mine > 0, left_ref[start : start + 4, :], 0.0)
        right = jnp.where(mine < n - 1, right_ref[start : start + 4, :], 0.0)
        ref[0:4, :] = slab_ref[start : start + 4, :]
        ref[4:8, :] = jnp.where(lane < nx // 2, right, left)


def binomial(at):
    return (at(-2) + at(2) + 4.0 * (at(-1) + at(1)) + 6.0 * at(0)) / 16.0


def centred12(at):
    return 8.0 * (at(1) - at(-1)) - (at(2) - at(-2))


def metric_kernel(
    sizes, layers_ref, slab_ref, left_ref, right_ref, yb_ref, ya_ref, factor_ref, mz_ref, slope_ref,
    own, rim, sown,
):
    n_gx, n_gy = sizes
    gx, gy, gz = lax.axis_index("gx"), lax.axis_index("gy"), lax.axis_index("gz")
    nz, ny, nx = factor_ref.shape
    lane = lanes_of((ny, nx))
    own[PAD : PAD + ny, :] = slab_ref[:ny, :]
    left = jnp.where(gx > 0, left_ref[...], 0.0)
    right = jnp.where(gx < n_gx - 1, right_ref[...], 0.0)
    rim[PAD : PAD + ny, :] = jnp.where(lane < nx // 2, right, left)
    for ref, at in ((own, 0), (rim, 4)):
        ref[PAD - 4 : PAD, :] = jnp.where(gy > 0, yb_ref[at : at + 4, :], 0.0)
        ref[PAD + ny : PAD + ny + 4, :] = jnp.where(gy < n_gy - 1, ya_ref[at : at + 4, :], 0.0)
    rows = ny + 4
    tall_own = binomial(lambda s: own[PAD - 2 + s : PAD - 2 + s + rows, :])
    tall_rim = binomial(lambda s: rim[PAD - 2 + s : PAD - 2 + s + rows, :])

    def shifted(a, b, s):
        ln = lanes_of(a.shape)
        cut = (ln < s) if s > 0 else (ln >= nx + s)
        if s > 0:
            mixed_a, mixed_b = jnp.where(cut, b, a), jnp.where(cut, a, b)
        elif s < 0:
            mixed_a, mixed_b = jnp.where(cut, b, a), jnp.where(cut, a, b)
        else:
            return a, b
        return pltpu.roll(mixed_a, (-s) % nx, 1), pltpu.roll(mixed_b, (-s) % nx, 1)

    def padded_rows(a):
        return jnp.concatenate([a, jnp.zeros((SUB - rows % SUB, nx), F32)], axis=0)

    tall_own, tall_rim = padded_rows(tall_own), padded_rows(tall_rim)
    pairs = {s: shifted(tall_own, tall_rim, s) for s in (-2, -1, 0, 1, 2)}
    surf_own = binomial(lambda s: pairs[s][0])
    surf_rim = binomial(lambda s: pairs[s][1])
    sown[...] = surf_own
    slope_ref[1] = centred12(lambda s: sown[2 + s : 2 + s + ny, :]) / 12.0
    pairs2 = {s: shifted(surf_own, surf_rim, s)[0] for s in (-2, -1, 1, 2)}
    along = centred12(lambda s: pairs2[s]) / 12.0
    surface = sown[2 : 2 + ny, :]
    sown[...] = along
    slope_ref[0] = sown[2 : 2 + ny, :]

    def above(k, total):
        s = layers_ref[1, k]
        return total + (s * layers_ref[0, k]) * jnp.exp(s * surface)

    total = lax.fori_loop(0, gz * nz, above, jnp.zeros((ny, nx), F32))
    for k in range(nz):
        s = layers_ref[1, gz * nz + k]
        thickness = layers_ref[0, gz * nz + k] * jnp.exp(s * surface)
        weighted = s * thickness
        mz = 1.0 / thickness
        lift = total + 0.5 * weighted
        total = total + weighted
        mz_ref[k] = mz
        factor_ref[k] = (lift - 1.0) * mz


def edge_terms(got_left, got_right, low, high):
    dl = got_left - high
    dr = got_right - low
    nx = dl.shape[-1]
    lane = lanes_of(dl.shape)
    even = lane % 2 == 0
    dl = pltpu.roll(dl, 2, 1)
    dr = pltpu.roll(dr, nx - 2, 1)
    to_low = jnp.where(even, dl - 8.0 * pltpu.roll(dl, nx - 1, 1), dl)
    to_high = jnp.where(even, -dr, 8.0 * pltpu.roll(dr, 1, 1) - dr)
    second = (lane // 2) % 2 == 1
    return jnp.where(second, to_low, to_high), jnp.where(second, to_high, to_low)


def along_x(tile, edges, m, lane):
    nx = tile.shape[-1]
    e = pltpu.roll(edges, (2 * nx - 2 - 2 * m) % nx if isinstance(m, int) else 2 * nx - 2 - 2 * m, 1)
    d = 8.0 * (pltpu.roll(tile, nx - 1, 1) - pltpu.roll(tile, 1, 1)) - (
        pltpu.roll(tile, nx - 2, 1) - pltpu.roll(tile, 2, 1)
    )
    return d + jnp.where((lane < 2) | (lane >= nx - 2), e, 0.0)


def lookup(row, tile):
    table = jnp.broadcast_to(row, tile.shape)
    return jnp.take_along_axis(table, tile, axis=1, mode="promise_in_bounds")


def table_rows(refs, nx):
    n = refs[0].shape[1]
    return [jnp.concatenate([r, jnp.zeros((1, nx - n), F32)], axis=1) for r in refs]


def fill_edges(n_gx, edge_ref, got_left_ref, got_right_ref, low_ref, high_ref):
    gx = lax.axis_index("gx")
    for c in range(3):
        at = slice(SUB * c, SUB * c + SUB)
        left = jnp.where(gx > 0, got_left_ref[at, :], 0.0)
        right = jnp.where(gx < n_gx - 1, got_right_ref[at, :], 0.0)
        first, second = edge_terms(left, right, low_ref[at, :], high_ref[at, :])
        edge_ref[c, 0] = first
        edge_ref[c, 1] = second


def fill_rows(n_gy, tall, field, yb_ref, ya_ref, nz, ny):
    gy = lax.axis_index("gy")
    for c in range(3):
        for k in range(nz):
            j = 2 * (c * nz + k)
            tall[c, k, PAD : PAD + ny, :] = field(c, k)
            tall[c, k, PAD - 2 : PAD, :] = jnp.where(gy > 0, yb_ref[j : j + 2, :], 0.0)
            tall[c, k, PAD + ny : PAD + ny + 2, :] = jnp.where(
                gy < n_gy - 1, ya_ref[j : j + 2, :], 0.0
            )


def depth_halos(n_gz, zb, za, zb_ref, za_ref):
    gz = lax.axis_index("gz")
    zb[...] = jnp.where(gz > 0, zb_ref[...], 0.0)
    za[...] = jnp.where(gz < n_gz - 1, za_ref[...], 0.0)


def over_layers(nz, layer):
    for k in (0, 1):
        layer(k)

    @pl.loop(2, nz - 2)
    def _(k):
        layer(k)

    for k in (nz - 2, nz - 1):
        layer(k)


def velocity_kernel(
    sizes, velocity_ref, stress_ref, material_ref, buoy_ref, factor_ref, mz_ref, slope_ref,
    got_left_ref, got_right_ref, low_ref, high_ref, yb_ref, ya_ref, zb_ref, za_ref,
    out_ref, vlow_ref, vhigh_ref, vya_ref, vyb_ref, vza_ref, vzb_ref,
    edge, tall, zb, za,
):
    n_gx, n_gy, n_gz = sizes
    _, nz, ny, nx = velocity_ref.shape
    tiles = ny // SUB
    lane = lanes_of((SUB, nx))
    fill_edges(n_gx, edge, got_left_ref, got_right_ref, low_ref, high_ref)
    of_y = (3, 1, 5)
    fill_rows(n_gy, tall, lambda c, k: stress_ref[of_y[c], k], yb_ref, ya_ref, nz, ny)
    depth_halos(n_gz, zb, za, zb_ref, za_ref)
    (buoy_row,) = table_rows([buoy_ref[...] * (step_size / 12.0)], nx)

    def layer(k):
        def depth(c, t):
            rows = slice(SUB * t, SUB * t + SUB)

            def at(s):
                if isinstance(k, int) and k + s < 0:
                    return zb[c, k + s + 2, rows, :]
                if isinstance(k, int) and k + s >= nz:
                    return za[c, k + s - nz, rows, :]
                return stress_ref[c, k + s, rows, :]

            return centred12(at)

        for t in range(tiles):
            rows = slice(SUB * t, SUB * t + SUB)
            m = k * tiles + t

            def gx_of(c, comp):
                return along_x(stress_ref[comp, k, rows, :], edge[c, t % 2], m, lane)

            def gy_of(c):
                return centred12(
                    lambda s: tall[c, k, PAD + SUB * t + s : PAD + SUB * t + s + SUB, :]
                )

            b = lookup(buoy_row, material_ref[k, rows, :])
            factor = factor_ref[k, rows, :]
            mz = mz_ref[k, rows, :]
            mx = slope_ref[0, rows, :] * factor
            my = slope_ref[1, rows, :] * factor
            gk = [depth(c, t) for c in range(6)]
            accel = (
                gx_of(0, 0) + gy_of(0) - mx * gk[0] - my * gk[3] + mz * gk[4],
                gx_of(1, 3) + gy_of(1) - mx * gk[3] - my * gk[1] + mz * gk[5],
                gx_of(2, 4) + gy_of(2) - mx * gk[4] - my * gk[5] + mz * gk[2],
            )
            for c in range(3):
                out_ref[c, k, rows, :] = velocity_ref[c, k, rows, :] + b * accel[c]

    over_layers(nz, layer)
    low, high = pack_sides(lambda c, k, t: out_ref[c, k, SUB * t : SUB * t + SUB, :], nz, ny, nx)
    for c in range(3):
        vlow_ref[SUB * c : SUB * c + SUB, :] = low[c]
        vhigh_ref[SUB * c : SUB * c + SUB, :] = high[c]
        for k in range(nz):
            j = 2 * (c * nz + k)
            vya_ref[j : j + 2, :] = out_ref[c, k, ny - 2 : ny, :]
            vyb_ref[j : j + 2, :] = out_ref[c, k, 0:2, :]
    vza_ref[...] = out_ref[:, nz - 2 : nz]
    vzb_ref[...] = out_ref[:, 0:2]


def stress_kernel(
    sizes, vel_ref, stress_ref, memory_ref, material_ref, lam_ref, mu_ref, relax_ref, weight_ref,
    factor_ref, mz_ref, slope_ref, got_left_ref, got_right_ref, low_ref, high_ref, yb_ref, ya_ref, zb_ref, za_ref,
    stress_out, memory_out, edge, tall, zb, za,
):
    n_gx, n_gy, n_gz = sizes
    _, nz, ny, nx = vel_ref.shape
    tiles = ny // SUB
    lane = lanes_of((SUB, nx))
    fill_edges(n_gx, edge, got_left_ref, got_right_ref, low_ref, high_ref)
    fill_rows(n_gy, tall, lambda c, k: vel_ref[c, k], yb_ref, ya_ref, nz, ny)
    depth_halos(n_gz, zb, za, zb_ref, za_ref)
    keep1 = jnp.exp(-step_size / relax_ref[...])
    lam_row, mu_row, keep_row, gain_row = table_rows(
        [lam_ref[...] / 12.0, mu_ref[...] / 12.0, keep1, (1.0 - keep1) * weight_ref[...]], nx
    )

    def layer(k):
        for t in range(tiles):
            rows = slice(SUB * t, SUB * t + SUB)
            m = k * tiles + t
            kind = material_ref[k, rows, :]
            factor = factor_ref[k, rows, :]
            mz = mz_ref[k, rows, :]
            mx = slope_ref[0, rows, :] * factor
            my = slope_ref[1, rows, :] * factor

            def depth(c):
                def at(s):
                    if isinstance(k, int) and k + s < 0:
                        return zb[c, k + s + 2, rows, :]
                    if isinstance(k, int) and k + s >= nz:
                        return za[c, k + s - nz, rows, :]
                    return vel_ref[c, k + s, rows, :]

                return centred12(at)

            dk = [depth(c) for c in range(3)]
            dx = [
                along_x(vel_ref[c, k, rows, :], edge[c, t % 2], m, lane) - mx * dk[c]
                for c in range(3)
            ]
            dy = [
                centred12(lambda s: tall[c, k, PAD + SUB * t + s : PAD + SUB * t + s + SUB, :])
                - my * dk[c]
                for c in range(3)
            ]
            dz = [mz * dk[c] for c in range(3)]
            lam = lookup(lam_row, kind)
            mu = lookup(mu_row, kind)
            keep = lookup(keep_row, kind)
            gain = lookup(gain_row, kind)
            volume = lam * (dx[0] + dy[1] + dz[2])
            mu2 = mu + mu
            rates = (
                volume + mu2 * dx[0],
                volume + mu2 * dy[1],
                volume + mu2 * dz[2],
                mu * (dy[0] + dx[1]),
                mu * (dz[0] + dx[2]),
                mu * (dz[1] + dy[2]),
            )
            for c in range(6):
                kept = keep * memory_ref[c, k, rows, :] + gain * rates[c]
                memory_out[c, k, rows, :] = kept
                stress_out[c, k, rows, :] = stress_ref[c, k, rows, :] + step_size * (
                    rates[c] - kept
                )

    over_layers(nz, layer)


def call(kernel, outs, in_specs, scratch=(), name=None):
    return pl.pallas_call(
        kernel,
        out_shape=[jax.ShapeDtypeStruct(s, F32) for s in outs],
        in_specs=in_specs,
        out_specs=[VM] * len(outs),
        scratch_shapes=list(scratch),
        compiler_params=params(),
        name=name,
    )


def local(
    n_gx, n_gy, n_gz, elevation, layer_base, stretch, material, buoyancy, lame_lambda, shear_modulus,
    relax_time, anelastic_weight, velocity, stress, memory,
):
    _, nz, ny, nx = velocity.shape
    rows = ny + SUB
    slab = call(
        functools.partial(terrain_piece_kernel, "gz"), [(rows, nx)], [VM] * 3, name="terrain_piece"
    )(elevation, layer_base[None], stretch[None])[0]
    faces = 2 * 3 * nz
    low, high, y_up, y_down = call(
        functools.partial(pack_kernel, faces),
        [(3 * SUB, nx), (3 * SUB, nx), (faces, nx), (faces, nx)],
        [VM],
        name="pack_stress",
    )(stress)
    if n_gz & (n_gz - 1):
        slab = lax.psum(slab, "gz")
    else:
        bit = 1
        while bit < n_gz:
            slab = slab + lax.ppermute(slab, "gz", [(i, i ^ bit) for i in range(n_gz)])
            bit *= 2
    height = slab[:ny]
    from_left, from_right = exchange(
        "gx", n_gx, jnp.concatenate([high, height]), jnp.concatenate([low, height])
    )
    zb, za = exchange("gz", n_gz, stress[:, nz - 2 :], stress[:, :2])
    xs = 3 * SUB
    left_slab, right_slab = from_left[xs:], from_right[xs:]
    t_after, t_before = call(
        functools.partial(y_terrain_kernel, (n_gx,)),
        [(SUB, nx), (SUB, nx)],
        [VM] * 3,
        name="y_terrain",
    )(slab, left_slab, right_slab)
    from_b, from_a = exchange(
        "gy", n_gy, jnp.concatenate([y_up, t_after]), jnp.concatenate([y_down, t_before])
    )
    factor, mz, slope = call(
        functools.partial(metric_kernel, (n_gx, n_gy)),
        [(nz, ny, nx), (nz, ny, nx), (2, ny, nx)],
        [SM] + [VM] * 5,
        [
            pltpu.VMEM((ny + 2 * PAD, nx), F32),
            pltpu.VMEM((ny + 2 * PAD, nx), F32),
            pltpu.VMEM((ny + PAD, nx), F32),
        ],
        name="metrics",
    )(slab[ny:], slab, left_slab, right_slab, from_b[faces:], from_a[faces:])
    sizes = (n_gx, n_gy, n_gz)

    def scratch(comps):
        return [
            pltpu.VMEM((3, 2, SUB, nx), F32),
            pltpu.VMEM((3, nz, ny + 2 * PAD, nx), F32),
            pltpu.VMEM((comps, 2, ny, nx), F32),
            pltpu.VMEM((comps, 2, ny, nx), F32),
        ]

    vel, vlow, vhigh, vya, vyb, vza, vzb = call(
        functools.partial(velocity_kernel, sizes),
        [velocity.shape, (xs, nx), (xs, nx), (faces, nx), (faces, nx), (3, 2, ny, nx), (3, 2, ny, nx)],
        [VM] * 15,
        scratch(6),
        name="velocity",
    )(
        velocity, stress, material, buoyancy[None], factor, mz, slope, from_left, from_right, low, high,
        from_b, from_a, zb, za,
    )
    v_left, v_right = exchange("gx", n_gx, vhigh, vlow)
    v_zb, v_za = exchange("gz", n_gz, vza, vzb)
    v_yb, v_ya = exchange("gy", n_gy, vya, vyb)
    stress_next, memory_next = call(
        functools.partial(stress_kernel, sizes),
        [stress.shape, stress.shape],
        [VM] * 19,
        scratch(3),
        name="stress",
    )(
        vel, stress, memory, material, lame_lambda[None], shear_modulus[None], relax_time[None],
        anelastic_weight[None], factor, mz, slope, v_left, v_right, vlow, vhigh, v_yb, v_ya, v_zb, v_za,
    )
    return vel, stress_next, memory_next


def solution(mesh):
    sizes = mesh.shape
    field = P(None, "gz", "gy", "gx")
    return jax.shard_map(
        functools.partial(local, sizes["gx"], sizes["gy"], sizes["gz"]),
        mesh=mesh,
        in_specs=(
            P("gy", ("gx", "gz")), P("gz"), P("gz"), P("gz", "gy", "gx"),
            P(), P(), P(), P(), P(), field, field, field,
        ),
        out_specs=(field, field, field),
        check_vma=False,
    )
```

time: 136 us -> 44.5 us (0.33)
  the two profiles are of different devices: /device:TPU:20 before, /device:TPU:0 now
where the time goes in v1:
time: 44.5 us; the launch traced here: 44.2 us
  starting transfers between devices  16.1 us (36%)
  waiting for transfers between devices  11 us (25%)
  Pallas kernels  9.34 us (21%)
  local copies, waits for them, and re-layouts  6.82 us (15%)
  between operations  0.85 us (2%)
    ppermute x4, starting transfers between devices, exchange(): lax.ppermute(to_before, axis, ring(n, -1))  9.28 us
    ppermute x4, waiting for transfers between devices, exchange(): lax.ppermute(to_after, axis, ring(n, 1))  5.96 us
    unnamed x28, local copies, waits for them, and re-layouts  5.76 us
    pallas_call x1, Pallas kernels, local(): call(functools.partial(stress_kernel, sizes), [stress.shape, stress.shape...  4.55 us
    pallas_call x1, Pallas kernels, local(): call(functools.partial(velocity_kernel, sizes), [velocity.shape, (xs, nx)...  3.49 us
    ppermute x2, starting transfers between devices, local(): slab = slab + lax.ppermute(slab, 'gz', [(i, i ^ bit) for i in range(n_gz)])  3.32 us
    ppermute x2, starting transfers between devices, exchange(): lax.ppermute(jnp.where(mine == 0, to_after, to_before), axis, ring(2, 1))  3.05 us
    ppermute x2, waiting for transfers between devices, exchange(): lax.ppermute(jnp.where(mine == 0, to_after, to_before), axis, ring(2, 1))  2.64 us
  transfers between devices with their start and end apart: 12, of which 5 were waited for; matrix products, arithmetic and copies ran while one was open for 2% of the time, Pallas kernels for 3%

profile of v1, /device:TPU:0, one launch (start us, length us, event | category | flops | bytes accessed | tf_op | source)
XLA Modules:
  0.0 44.2 jit_solution(12964637898007167061)
XLA Ops:
  0.6 0.0 copy-start.3
  0.6 0.0 copy-start.6
  0.7 0.8 %copy-done.6 = s32[32,32]{1,0:T(8,128)S(1)} copy-done((s32[32,32]{1,0:T(8,128)S(1)}, s32[32,32]{1,0:T(8,128)}, u32[]{:S(2)}) %copy-start.6) | copy-done | bytes 4120
  1.4 0.0 copy-start.7
  1.4 0.7 %copy-done.7 = f32[16]{0:T(128)S(1)} copy-done((f32[16]{0:T(128)S(1)}, f32[16]{0:T(128)}, u32[]{:S(2)}) %copy-start.7) | copy-done | bytes 88
  2.1 0.0 copy-start.8
  2.1 0.7 %copy-done.8 = f32[16]{0:T(128)S(1)} copy-done((f32[16]{0:T(128)S(1)}, f32[16]{0:T(128)}, u32[]{:S(2)}) %copy-start.8) | copy-done | bytes 88
  2.7 0.0 copy-start.13
  2.7 0.1 terrain_piece.1
  2.8 0.5 %collective-permute-start = (f32[40,128]{1,0:T(8,128)S(1)}, f32[40,128]{1,0:T(8,128)S(1)}, u32[]{:S(2)}, u32[]{:S(2)}) collective-permute-start(f32[40,128]{1,0:T(8,128)S(1)} %terrain_piece.1), channel_id=1, source_target_pairs={{0,1},{1,0},{2,3},{3,2},{4,5},{5,4},{6,7},{7,6},{8,9},{9,8},{10,11... | collective-permute-start | bytes 61448 | tf_op jit(solution)/shard_map/ppermute | solution.py:416
  3.2 0.8 %collective-permute-done = f32[40,128]{1,0:T(8,128)S(1)} collective-permute-done((f32[40,128]{1,0:T(8,128)S(1)}, f32[40,128]{1,0:T(8,128)S(1)}, u32[]{:S(2)}, u32[]{:S(2)}) %collective-permute-start) | collective-permute-done | bytes 20512 | tf_op jit(solution)/shard_map/ppermute | solution.py:416
  4.1 2.9 %collective-permute-start.1 = (f32[40,128]{1,0:T(8,128)S(1)}, f32[40,128]{1,0:T(8,128)S(1)}, u32[]{:S(2)}, u32[]{:S(2)}) collective-permute-start(f32[40,128]{1,0:T(8,128)S(1)} %add.6), channel_id=1, source_target_pairs={{0,2},{1,3},{2,0},{3,1},{4,6},{5,7},{6,4},{7,5},{8,10},{9,11},{10,... | collective-permute-start | bytes 61448 | tf_op jit(solution)/shard_map/ppermute | solution.py:416
  7.0 1.0 %fusion = (f32[6,2,32,128]{3,2,1,0:T(8,128)S(1)}, f32[6,2,32,128]{3,2,1,0:T(8,128)S(1)}) fusion(f32[6,16,32,128]{3,2,1,0:T(8,128)} %stress_ref.5), kind=kLoop, calls=%fused_computation.4 | loop fusion | bytes 786432 | tf_op jit(solution)/shard_map/slice | solution.py:422
  8.0 0.1 collective-permute-start.6
  8.1 0.5 %collective-permute-start.5 = (f32[6,2,32,128]{3,2,1,0:T(8,128)S(1)}, f32[6,2,32,128]{3,2,1,0:T(8,128)S(1)}, u32[]{:S(2)}, u32[]{:S(2)}) collective-permute-start(f32[6,2,32,128]{3,2,1,0:T(8,128)S(1)} %get-tuple-element.40), channel_id=1, source_target_pairs={{0,1},{1,2},{2,3},{3,0},{4,5},{5,6},{6,7},{7,4},{8,9},{9,10},{10,1... | collective-permute-start | bytes 589832 | tf_op jit(solution)/shard_map/ppermute | solution.py:29
  8.6 0.0 copy-start
  8.6 1.4 %copy-done = f32[6,16,32,128]{3,2,1,0:T(8,128)S(1)} copy-done((f32[6,16,32,128]{3,2,1,0:T(8,128)S(1)}, f32[6,16,32,128]{3,2,1,0:T(8,128)}, u32[]{:S(2)}) %copy-start) | copy-done | bytes 1572888
  10.0 0.0 copy-start.1
  10.0 0.3 pack_stress.1
  10.3 0.0 collective-permute-done.1
  10.3 3.7 %collective-permute-start.3 = (f32[56,128]{1,0:T(8,128)S(1)}, f32[56,128]{1,0:T(8,128)S(1)}, u32[]{:S(2)}, u32[]{:S(2)}) collective-permute-start(f32[56,128]{1,0:T(8,128)S(1)} %get-tuple-element.41), channel_id=1, source_target_pairs={{0,24},{8,0},{16,8},{24,16},{1,25},{9,1},{17,9},{25,17},{2,26},{10... | collective-permute-start | bytes 86024 | tf_op jit(solution)/shard_map/ppermute | solution.py:29
  14.0 0.0 collective-permute-start.2
  14.0 1.6 %collective-permute-done.3.got_right_ref = f32[56,128]{1,0:T(8,128)S(1)} collective-permute-done((f32[56,128]{1,0:T(8,128)S(1)}, f32[56,128]{1,0:T(8,128)S(1)}, u32[]{:S(2)}, u32[]{:S(2)}) %collective-permute-start.3) | collective-permute-done | bytes 28704 | tf_op jit(solution)/shard_map/ppermute | solution.py:29
  15.5 4.3 %collective-permute-done.2.got_left_ref = f32[56,128]{1,0:T(8,128)S(1)} collective-permute-done((f32[56,128]{1,0:T(8,128)S(1)}, f32[56,128]{1,0:T(8,128)S(1)}, u32[]{:S(2)}, u32[]{:S(2)}) %collective-permute-start.2) | collective-permute-done | bytes 28704 | tf_op jit(solution)/shard_map/ppermute | solution.py:29
  19.8 1.6 %collective-permute-start.4 = (f32[104,128]{1,0:T(8,128)S(1)}, f32[104,128]{1,0:T(8,128)S(1)}, u32[]{:S(2)}, u32[]{:S(2)}) collective-permute-start(f32[104,128]{1,0:T(8,128)S(1)} %maximum_select_fusion), channel_id=1, source_target_pairs={{0,4},{4,0},{1,5},{5,1},{2,6},{6,2},{3,7},{7,3},{8,12},{12,8},{9,1... | collective-permute-start | bytes 159752 | tf_op jit(solution)/shard_map/ppermute | solution.py:27
  21.4 2.6 %collective-permute-done.4.yb_ref.ya_ref = f32[104,128]{1,0:T(8,128)S(1)} collective-permute-done((f32[104,128]{1,0:T(8,128)S(1)}, f32[104,128]{1,0:T(8,128)S(1)}, u32[]{:S(2)}, u32[]{:S(2)}) %collective-permute-start.4) | collective-permute-done | bytes 53280 | tf_op jit(solution)/shard_map/ppermute | solution.py:27
  24.0 0.9 %metrics.1 = (f32[16,32,128]{2,1,0:T(8,128)S(1)}, f32[16,32,128]{2,1,0:T(8,128)S(1)}, f32[2,32,128]{2,1,0:T(8,128)S(1)}) custom-call(f32[8,128]{1,0:T(8,128)S(1)} %slice.29.layers_ref, f32[40,128]{1,0:T(8,128)S(1)} %add.7.slab_ref, f32[32,128]{1,0:T(8,128)S(1)} %slice.31.left_ref, f32[32,128]{1,0:T(8,128)S(1)} %slice.32.right_ref, ...), custom_call_target="tpu_custom_call" | custom-call | tf_op jit(solution)/shard_map/metrics/pallas_call | solution.py:434
  25.0 0.0 collective-permute-done.6.za_ref
  25.0 0.0 collective-permute-done.5.zb_ref
  25.0 0.0 copy-done.3
  25.0 0.0 copy-done.13
  25.0 0.0 copy-done.1
  25.0 0.0 copy-start.5
  25.1 1.1 %copy-done.5 = f32[3,16,32,128]{3,2,1,0:T(8,128)S(1)} copy-done((f32[3,16,32,128]{3,2,1,0:T(8,128)S(1)}, f32[3,16,32,128]{3,2,1,0:T(8,128)}, u32[]{:S(2)}) %copy-start.5) | copy-done | bytes 786456
  26.2 0.0 copy-start.2
  26.2 0.0 copy-start.9
  26.2 0.0 copy-start.10
  26.2 0.0 copy-start.11
  26.2 0.0 copy-start.12
  26.2 3.5 %velocity.1 = (f32[3,16,32,128]{3,2,1,0:T(8,128)}, f32[24,128]{1,0:T(8,128)S(1)}, f32[24,128]{1,0:T(8,128)S(1)}, f32[96,128]{1,0:T(8,128)S(1)}, f32[96,128]{1,0:...) custom-call(f32[3,16,32,128]{3,2,1,0:T(8,128)S(1)} %copy-done.5, ...), custom_call_target="tpu_custom_call" | custom-call | tf_op jit(solution)/shard_map/velocity/pallas_call | solution.py:455
  29.7 0.0 collective-permute-start.10
  29.7 1.7 %collective-permute-start.11 = (f32[3,2,32,128]{3,2,1,0:T(8,128)S(1)}, f32[3,2,32,128]{3,2,1,0:T(8,128)S(1)}, u32[]{:S(2)}, u32[]{:S(2)}) collective-permute-start(f32[3,2,32,128]{3,2,1,0:T(8,128)S(1)} %get-tuple-element.36), channel_id=1, source_target_pairs={{0,3},{1,0},{2,1},{3,2},{4,7},{5,4},{6,5},{7,6},{8,11},{9,8},{10,9... | collective-permute-start | bytes 294920 | tf_op jit(solution)/shard_map/ppermute | solution.py:29
  31.4 1.5 %collective-permute-start.9 = (f32[96,128]{1,0:T(8,128)S(1)}, f32[96,128]{1,0:T(8,128)S(1)}, u32[]{:S(2)}, u32[]{:S(2)}) collective-permute-start(f32[96,128]{1,0:T(8,128)S(1)} %broadcast_select_fusion), channel_id=1, source_target_pairs={{0,4},{4,0},{1,5},{5,1},{2,6},{6,2},{3,7},{7,3},{8,12},{12,8},{9,1... | collective-permute-start | bytes 147464 | tf_op jit(solution)/shard_map/ppermute | solution.py:27
  32.9 0.0 collective-permute-start.7
  32.9 3.8 %collective-permute-start.8 = (f32[24,128]{1,0:T(8,128)S(1)}, f32[24,128]{1,0:T(8,128)S(1)}, u32[]{:S(2)}, u32[]{:S(2)}) collective-permute-start(f32[24,128]{1,0:T(8,128)S(1)} %get-tuple-element.32.low_ref), channel_id=1, source_target_pairs={{0,24},{8,0},{16,8},{24,16},{1,25},{9,1},{17,9},{25,17},{2,26},{10... | collective-permute-start | bytes 36872 | tf_op jit(solution)/shard_map/ppermute | solution.py:29
  36.8 1.7 %collective-permute-done.7.got_left_ref = f32[24,128]{1,0:T(8,128)S(1)} collective-permute-done((f32[24,128]{1,0:T(8,128)S(1)}, f32[24,128]{1,0:T(8,128)S(1)}, u32[]{:S(2)}, u32[]{:S(2)}) %collective-permute-start.7) | collective-permute-done | bytes 12320 | tf_op jit(solution)/shard_map/ppermute | solution.py:29
  38.4 0.0 collective-permute-done.8.got_right_ref
  38.4 0.0 collective-permute-done.9.yb_ref.ya_ref
  38.4 0.0 collective-permute-done.10.zb_ref
  38.4 0.0 collective-permute-done.11.za_ref
  38.5 0.0 copy-done.2
  38.5 0.0 copy-done.9
  38.5 0.0 copy-done.10
  38.5 0.0 copy-done.11
  38.5 0.0 copy-done.12
  38.5 0.0 copy-start.4
  38.5 1.1 %copy-done.4 = f32[3,16,32,128]{3,2,1,0:T(8,128)S(1)} copy-done((f32[3,16,32,128]{3,2,1,0:T(8,128)S(1)}, f32[3,16,32,128]{3,2,1,0:T(8,128)}, u32[]{:S(2)}) %copy-start.4) | copy-done | bytes 786456
  39.6 4.6 %stress.1 = (f32[6,16,32,128]{3,2,1,0:T(8,128)}, f32[6,16,32,128]{3,2,1,0:T(8,128)}) custom-call(f32[3,16,32,128]{3,2,1,0:T(8,128)S(1)} %copy-done.4, f32[6,16,32,128]{3,2,1,0:T(8,128)S(1)} %copy-done.1, f32[6,16,32,128]{3,2,1,0:T(8,128)S(1)} %copy-done.2, s32[16,32,128]{2,1,0:T(8,128)S(1)} %copy-done.3, f32[1,16]{1,0:T(1,128)S(1)} %bitcast.9, ...), custom_call_target="tpu_custom_call" | custom-call | tf_op jit(solution)/shard_map/stress/pallas_call | solution.py:468
  (11 shorter events, 0.1 us)
Async XLA Ops:
  0.6 24.4 %copy-start.3 = (s32[16,32,128]{2,1,0:T(8,128)S(1)}, s32[16,32,128]{2,1,0:T(8,128)}, u32[]{:S(2)}) copy-start(s32[16,32,128]{2,1,0:T(8,128)} %material_ref.3) | copy-start | bytes 786436
  0.6 0.8 %copy-start.6 = (s32[32,32]{1,0:T(8,128)S(1)}, s32[32,32]{1,0:T(8,128)}, u32[]{:S(2)}) copy-start(s32[32,32]{1,0:T(8,128)} %elev_ref.1) | copy-start | bytes 12292
  1.4 0.7 %copy-start.7 = (f32[16]{0:T(128)S(1)}, f32[16]{0:T(128)}, u32[]{:S(2)}) copy-start(f32[16]{0:T(128)} %param.13) | copy-start | bytes 196
  2.1 0.7 %copy-start.8 = (f32[16]{0:T(128)S(1)}, f32[16]{0:T(128)}, u32[]{:S(2)}) copy-start(f32[16]{0:T(128)} %param.14) | copy-start | bytes 196
  2.7 22.3 %copy-start.13 = (f32[16]{0:T(128)S(1)}, f32[16]{0:T(128)}, u32[]{:S(2)}) copy-start(f32[16]{0:T(128)} %param.16) | copy-start | bytes 196
  2.8 1.3 %collective-permute-start = (f32[40,128]{1,0:T(8,128)S(1)}, f32[40,128]{1,0:T(8,128)S(1)}, u32[]{:S(2)}, u32[]{:S(2)}) collective-permute-start(f32[40,128]{1,0:T(8,128)S(1)} %terrain_piece.1), channel_id=1, source_target_pairs={{0,1},{1,0},{2,3},{3,2},{4,5},{5,4},{6,7},{7,6},{8,9},{9,8},{10,11... | collective-permute-start | bytes 61448 | tf_op jit(solution)/shard_map/ppermute | solution.py:416
  4.1 6.2 %collective-permute-start.1 = (f32[40,128]{1,0:T(8,128)S(1)}, f32[40,128]{1,0:T(8,128)S(1)}, u32[]{:S(2)}, u32[]{:S(2)}) collective-permute-start(f32[40,128]{1,0:T(8,128)S(1)} %add.6), channel_id=1, source_target_pairs={{0,2},{1,3},{2,0},{3,1},{4,6},{5,7},{6,4},{7,5},{8,10},{9,11},{10,... | collective-permute-start | bytes 61448 | tf_op jit(solution)/shard_map/ppermute | solution.py:416
  8.0 17.0 %collective-permute-start.6 = (f32[6,2,32,128]{3,2,1,0:T(8,128)S(1)}, f32[6,2,32,128]{3,2,1,0:T(8,128)S(1)}, u32[]{:S(2)}, u32[]{:S(2)}) collective-permute-start(f32[6,2,32,128]{3,2,1,0:T(8,128)S(1)} %get-tuple-element.39), channel_id=1, source_target_pairs={{0,3},{1,0},{2,1},{3,2},{4,7},{5,4},{6,5},{7,6},{8,11},{9,8},{10,9... | collective-permute-start | bytes 589832 | tf_op jit(solution)/shard_map/ppermute | solution.py:29
  8.1 16.9 %collective-permute-start.5 = (f32[6,2,32,128]{3,2,1,0:T(8,128)S(1)}, f32[6,2,32,128]{3,2,1,0:T(8,128)S(1)}, u32[]{:S(2)}, u32[]{:S(2)}) collective-permute-start(f32[6,2,32,128]{3,2,1,0:T(8,128)S(1)} %get-tuple-element.40), channel_id=1, source_target_pairs={{0,1},{1,2},{2,3},{3,0},{4,5},{5,6},{6,7},{7,4},{8,9},{9,10},{10,1... | collective-permute-start | bytes 589832 | tf_op jit(solution)/shard_map/ppermute | solution.py:29
  8.6 1.4 %copy-start = (f32[6,16,32,128]{3,2,1,0:T(8,128)S(1)}, f32[6,16,32,128]{3,2,1,0:T(8,128)}, u32[]{:S(2)}) copy-start(f32[6,16,32,128]{3,2,1,0:T(8,128)} %stress_ref.5) | copy-start | bytes 4718596
  10.0 15.1 %copy-start.1 = (f32[6,16,32,128]{3,2,1,0:T(8,128)S(1)}, f32[6,16,32,128]{3,2,1,0:T(8,128)}, u32[]{:S(2)}) copy-start(f32[6,16,32,128]{3,2,1,0:T(8,128)} %stress_ref.5) | copy-start | bytes 4718596
  10.3 5.2 %collective-permute-start.3 = (f32[56,128]{1,0:T(8,128)S(1)}, f32[56,128]{1,0:T(8,128)S(1)}, u32[]{:S(2)}, u32[]{:S(2)}) collective-permute-start(f32[56,128]{1,0:T(8,128)S(1)} %get-tuple-element.41), channel_id=1, source_target_pairs={{0,24},{8,0},{16,8},{24,16},{1,25},{9,1},{17,9},{25,17},{2,26},{10... | collective-permute-start | bytes 86024 | tf_op jit(solution)/shard_map/ppermute | solution.py:29
  14.0 5.8 %collective-permute-start.2 = (f32[56,128]{1,0:T(8,128)S(1)}, f32[56,128]{1,0:T(8,128)S(1)}, u32[]{:S(2)}, u32[]{:S(2)}) collective-permute-start(f32[56,128]{1,0:T(8,128)S(1)} %get-tuple-element.42), channel_id=1, source_target_pairs={{0,8},{8,16},{16,24},{24,0},{1,9},{9,17},{17,25},{25,1},{2,10},{10... | collective-permute-start | bytes 86024 | tf_op jit(solution)/shard_map/ppermute | solution.py:29
  19.8 4.2 %collective-permute-start.4 = (f32[104,128]{1,0:T(8,128)S(1)}, f32[104,128]{1,0:T(8,128)S(1)}, u32[]{:S(2)}, u32[]{:S(2)}) collective-permute-start(f32[104,128]{1,0:T(8,128)S(1)} %maximum_select_fusion), channel_id=1, source_target_pairs={{0,4},{4,0},{1,5},{5,1},{2,6},{6,2},{3,7},{7,3},{8,12},{12,8},{9,1... | collective-permute-start | bytes 159752 | tf_op jit(solution)/shard_map/ppermute | solution.py:27
  25.0 1.1 %copy-start.5 = (f32[3,16,32,128]{3,2,1,0:T(8,128)S(1)}, f32[3,16,32,128]{3,2,1,0:T(8,128)}, u32[]{:S(2)}) copy-start(f32[3,16,32,128]{3,2,1,0:T(8,128)} %velocity_ref.1) | copy-start | bytes 2359300
  26.2 12.3 %copy-start.2 = (f32[6,16,32,128]{3,2,1,0:T(8,128)S(1)}, f32[6,16,32,128]{3,2,1,0:T(8,128)}, u32[]{:S(2)}) copy-start(f32[6,16,32,128]{3,2,1,0:T(8,128)} %memory_ref.1) | copy-start | bytes 4718596
  26.2 12.3 %copy-start.9 = (f32[16]{0:T(128)S(1)}, f32[16]{0:T(128)}, u32[]{:S(2)}) copy-start(f32[16]{0:T(128)} %param.17) | copy-start | bytes 196
  26.2 12.3 %copy-start.10 = (f32[16]{0:T(128)S(1)}, f32[16]{0:T(128)}, u32[]{:S(2)}) copy-start(f32[16]{0:T(128)} %param.18) | copy-start | bytes 196
  26.2 12.3 %copy-start.11 = (f32[16]{0:T(128)S(1)}, f32[16]{0:T(128)}, u32[]{:S(2)}) copy-start(f32[16]{0:T(128)} %param.19) | copy-start | bytes 196
  26.2 12.3 %copy-start.12 = (f32[16]{0:T(128)S(1)}, f32[16]{0:T(128)}, u32[]{:S(2)}) copy-start(f32[16]{0:T(128)} %param.20) | copy-start | bytes 196
  29.7 8.7 %collective-permute-start.10 = (f32[3,2,32,128]{3,2,1,0:T(8,128)S(1)}, f32[3,2,32,128]{3,2,1,0:T(8,128)S(1)}, u32[]{:S(2)}, u32[]{:S(2)}) collective-permute-start(f32[3,2,32,128]{3,2,1,0:T(8,128)S(1)} %get-tuple-element.35), channel_id=1, source_target_pairs={{0,1},{1,2},{2,3},{3,0},{4,5},{5,6},{6,7},{7,4},{8,9},{9,10},{10,1... | collective-permute-start | bytes 294920 | tf_op jit(solution)/shard_map/ppermute | solution.py:29
  29.7 8.8 %collective-permute-start.11 = (f32[3,2,32,128]{3,2,1,0:T(8,128)S(1)}, f32[3,2,32,128]{3,2,1,0:T(8,128)S(1)}, u32[]{:S(2)}, u32[]{:S(2)}) collective-permute-start(f32[3,2,32,128]{3,2,1,0:T(8,128)S(1)} %get-tuple-element.36), channel_id=1, source_target_pairs={{0,3},{1,0},{2,1},{3,2},{4,7},{5,4},{6,5},{7,6},{8,11},{9,8},{10,9... | collective-permute-start | bytes 294920 | tf_op jit(solution)/shard_map/ppermute | solution.py:29
  31.4 7.0 %collective-permute-start.9 = (f32[96,128]{1,0:T(8,128)S(1)}, f32[96,128]{1,0:T(8,128)S(1)}, u32[]{:S(2)}, u32[]{:S(2)}) collective-permute-start(f32[96,128]{1,0:T(8,128)S(1)} %broadcast_select_fusion), channel_id=1, source_target_pairs={{0,4},{4,0},{1,5},{5,1},{2,6},{6,2},{3,7},{7,3},{8,12},{12,8},{9,1... | collective-permute-start | bytes 147464 | tf_op jit(solution)/shard_map/ppermute | solution.py:27
  32.9 5.5 %collective-permute-start.7 = (f32[24,128]{1,0:T(8,128)S(1)}, f32[24,128]{1,0:T(8,128)S(1)}, u32[]{:S(2)}, u32[]{:S(2)}) collective-permute-start(f32[24,128]{1,0:T(8,128)S(1)} %get-tuple-element.31.high_ref), channel_id=1, source_target_pairs={{0,8},{8,16},{16,24},{24,0},{1,9},{9,17},{17,25},{25,1},{2,10},{10... | collective-permute-start | bytes 36872 | tf_op jit(solution)/shard_map/ppermute | solution.py:29
  32.9 5.5 %collective-permute-start.8 = (f32[24,128]{1,0:T(8,128)S(1)}, f32[24,128]{1,0:T(8,128)S(1)}, u32[]{:S(2)}, u32[]{:S(2)}) collective-permute-start(f32[24,128]{1,0:T(8,128)S(1)} %get-tuple-element.32.low_ref), channel_id=1, source_target_pairs={{0,24},{8,0},{16,8},{24,16},{1,25},{9,1},{17,9},{25,17},{2,26},{10... | collective-permute-start | bytes 36872 | tf_op jit(solution)/shard_map/ppermute | solution.py:29
  38.5 1.1 %copy-start.4 = (f32[3,16,32,128]{3,2,1,0:T(8,128)S(1)}, f32[3,16,32,128]{3,2,1,0:T(8,128)}, u32[]{:S(2)}) copy-start(f32[3,16,32,128]{3,2,1,0:T(8,128)} %get-tuple-element.18.vel_ref) | copy-start | bytes 2359300

commit v2 on v1

v2 whole, which is shorter than its diff:
```python
import functools
import jax
import jax.numpy as jnp
import numpy as np
from jax import lax
from jax.experimental import pallas as pl
from jax.experimental.pallas import tpu as pltpu
from jax.sharding import PartitionSpec as P

step_size = 0.3
SUB = 8
PAD = 8
F32 = jnp.float32
params = functools.partial(pltpu.CompilerParams, vmem_limit_bytes=48 * 1024 * 1024)
VM = pl.BlockSpec(memory_space=pltpu.VMEM)
SM = pl.BlockSpec(memory_space=pltpu.SMEM)
HB = pl.BlockSpec(memory_space=pltpu.HBM)
DMA = pltpu.SemaphoreType.DMA


def pair_swaps(sizes, axis):
    names = tuple(sizes)
    shape = tuple(sizes.values())
    index = names.index(axis)
    n = shape[index]
    others = [d for d in (2, 1, 0) if d != index and shape[d] % 2 == 0]
    rounds = []
    for first in (0, 1)[: max(0, min(2, n - 1))]:
        table = []
        for spot in np.ndindex(*shape):
            mate = spot[index] + 1 if spot[index] % 2 == first else spot[index] - 1
            target = list(spot)
            if 0 <= mate < n:
                target[index] = mate
            elif others:
                target[others[0]] ^= 1
            else:
                continue
            table.append((int(np.ravel_multi_index(spot, shape)), int(np.ravel_multi_index(tuple(target), shape))))
        rounds.append(table)
    return rounds


def exchange(sizes, axis, first, second):
    rounds = pair_swaps(sizes, axis)
    got = [lax.ppermute(v, tuple(sizes), r) for v, r in zip((first, second), rounds)]
    return (got[0], got[-1]) if got else (first, second)


def even(axis):
    return lax.axis_index(axis) % 2 == 0


def from_before(axis, got):
    value = jnp.where(even(axis), got[1], got[0])
    return jnp.where(lax.axis_index(axis) > 0, value, 0.0)


def from_after(axis, n, got):
    value = jnp.where(even(axis), got[0], got[1])
    return jnp.where(lax.axis_index(axis) < n - 1, value, 0.0)


def order(axis, to_after, to_before):
    e = even(axis)
    return jnp.where(e, to_after, to_before), jnp.where(e, to_before, to_after)


def lanes_of(shape):
    return lax.broadcasted_iota(jnp.int32, shape, len(shape) - 1)


def terrain_piece_kernel(elev_hbm, base_hbm, stretch_hbm, out_ref, elev_ref, base_ref, stretch_ref, sems):
    mine = lax.axis_index("gz")
    pairs = ((elev_hbm, elev_ref), (base_hbm, base_ref), (stretch_hbm, stretch_ref))
    copies = [pltpu.make_async_copy(a, b, sems.at[i]) for i, (a, b) in enumerate(pairs)]
    for copy in copies:
        copy.start()
    for copy in copies:
        copy.wait()
    ny, width = elev_ref.shape
    nx = out_ref.shape[1]
    nz = base_ref.shape[1]
    height = elev_ref[...].astype(F32) / 200.0
    wide = jnp.concatenate([height, jnp.zeros((ny, nx - width), F32)], axis=1)
    out_ref[:ny, :] = pltpu.roll(wide, mine * width, 1)
    row = lax.broadcasted_iota(jnp.int32, (SUB, nx), 0)
    fill = jnp.zeros((1, nx - nz), F32)
    base = jnp.concatenate([base_ref[...], fill], axis=1)
    stretch = jnp.concatenate([stretch_ref[...], fill], axis=1)
    both = jnp.where(row == 0, base, jnp.where(row == 1, stretch, 0.0))
    out_ref[ny:, :] = pltpu.roll(both, mine * nz, 1)


def pack_sides(field, nz, ny, nx, low_ref, high_ref, out1_ref, out2_ref):
    tiles = ny // SUB
    lane2 = lanes_of((SUB, nx)) // 2
    for c in range(3):
        lo = jnp.zeros((SUB, nx), F32)
        hi = jnp.zeros((SUB, nx), F32)
        for k in range(nz):
            for t in range(tiles):
                m = k * tiles + t
                turned = pltpu.roll(field(c, k, t), (2 * m + 2) % nx, 1)
                hi = jnp.where(lane2 == m, turned, hi)
                lo = jnp.where(lane2 == (m + 1) % (nx // 2), turned, lo)
        at = slice(SUB * c, SUB * c + SUB)
        low_ref[at, :] = lo
        high_ref[at, :] = hi
        out1_ref[at, :], out2_ref[at, :] = order("gx", hi, lo)


def pack_rows(field, nz, ny, y1_ref, y2_ref):
    for c in range(3):
        for k in range(nz):
            j = 2 * (c * nz + k)
            one, two = order("gy", field(c, k, slice(ny - 2, ny)), field(c, k, slice(0, 2)))
            y1_ref[j : j + 2, :] = one
            y2_ref[j : j + 2, :] = two


def pack_kernel(
    stress_hbm, stress_ref, low_ref, high_ref, out1_ref, out2_ref, y1_ref, y2_ref, z1_ref, z2_ref, sems
):
    comps, nz, ny, nx = stress_ref.shape
    copies = [
        pltpu.make_async_copy(stress_hbm.at[c], stress_ref.at[c], sems.at[c]) for c in range(comps)
    ]
    z_even = even("gz")
    z1_at = jnp.where(z_even, nz - 2, 0)
    z2_at = jnp.where(z_even, 0, nz - 2)
    z_copies = [
        pltpu.make_async_copy(stress_hbm.at[:, pl.ds(z1_at, 2)], z1_ref, sems.at[comps]),
        pltpu.make_async_copy(stress_hbm.at[:, pl.ds(z2_at, 2)], z2_ref, sems.at[comps + 1]),
    ]
    of_x = (0, 3, 4)
    of_y = (3, 1, 5)
    loading = (0, 3, 4, 1, 5, 2)
    for c in loading[:5]:
        copies[c].start()
    for copy in z_copies:
        copy.start()
    copies[2].start()
    for c in of_x:
        copies[c].wait()
    x_even = even("gx")
    pack_sides(
        lambda c, k, t: stress_ref[of_x[c], k, SUB * t : SUB * t + SUB, :],
        nz, ny, nx, low_ref, high_ref, out1_ref, out2_ref,
    )
    copies[1].wait()
    copies[5].wait()
    pack_rows(lambda c, k, rows: stress_ref[of_y[c], k, rows, :], nz, ny, y1_ref, y2_ref)
    copies[2].wait()
    for copy in z_copies:
        copy.wait()


def y_terrain_kernel(n_gx, slab_ref, got1_ref, got2_ref, one_ref, two_ref):
    nx = slab_ref.shape[1]
    ny = slab_ref.shape[0] - SUB
    lane = lanes_of((4, nx))
    sent = []
    for start in (ny - 4, 0):
        rows = slice(start, start + 4)
        got = (got1_ref[rows, :], got2_ref[rows, :])
        rim = jnp.where(lane < nx // 2, from_after("gx", n_gx, got), from_before("gx", got))
        sent.append((slab_ref[rows, :], rim))
    for i in range(2):
        one_ref[4 * i : 4 * i + 4, :], two_ref[4 * i : 4 * i + 4, :] = order(
            "gy", sent[0][i], sent[1][i]
        )


def binomial(at):
    return (at(-2) + at(2) + 4.0 * (at(-1) + at(1)) + 6.0 * at(0)) / 16.0


def centred12(at):
    return 8.0 * (at(1) - at(-1)) - (at(2) - at(-2))


def metric_kernel(
    sizes, layers_ref, slab_ref, x1_ref, x2_ref, y1_ref, y2_ref, velocity_hbm, factor_ref, mz_ref, slope_ref,
    velocity_ref, own, rim, sown, sem,
):
    n_gx, n_gy, _ = sizes
    load = pltpu.make_async_copy(velocity_hbm, velocity_ref, sem)
    load.start()
    gz = lax.axis_index("gz")
    nz, ny, nx = factor_ref.shape
    lane = lanes_of((ny, nx))
    own[PAD : PAD + ny, :] = slab_ref[:ny, :]
    got = (x1_ref[...], x2_ref[...])
    rim[PAD : PAD + ny, :] = jnp.where(
        lane < nx // 2, from_after("gx", n_gx, got), from_before("gx", got)
    )
    for ref, at in ((own, 0), (rim, 4)):
        got = (y1_ref[at : at + 4, :], y2_ref[at : at + 4, :])
        ref[PAD - 4 : PAD, :] = from_before("gy", got)
        ref[PAD + ny : PAD + ny + 4, :] = from_after("gy", n_gy, got)
    rows = ny + 4
    tall_own = binomial(lambda s: own[PAD - 2 + s : PAD - 2 + s + rows, :])
    tall_rim = binomial(lambda s: rim[PAD - 2 + s : PAD - 2 + s + rows, :])

    def shifted(a, b, s):
        ln = lanes_of(a.shape)
        cut = (ln < s) if s > 0 else (ln >= nx + s)
        if s > 0:
            mixed_a, mixed_b = jnp.where(cut, b, a), jnp.where(cut, a, b)
        elif s < 0:
            mixed_a, mixed_b = jnp.where(cut, b, a), jnp.where(cut, a, b)
        else:
            return a, b
        return pltpu.roll(mixed_a, (-s) % nx, 1), pltpu.roll(mixed_b, (-s) % nx, 1)

    def padded_rows(a):
        return jnp.concatenate([a, jnp.zeros((SUB - rows % SUB, nx), F32)], axis=0)

    tall_own, tall_rim = padded_rows(tall_own), padded_rows(tall_rim)
    pairs = {s: shifted(tall_own, tall_rim, s) for s in (-2, -1, 0, 1, 2)}
    surf_own = binomial(lambda s: pairs[s][0])
    surf_rim = binomial(lambda s: pairs[s][1])
    sown[...] = surf_own
    slope_ref[1] = centred12(lambda s: sown[2 + s : 2 + s + ny, :]) / 12.0
    pairs2 = {s: shifted(surf_own, surf_rim, s)[0] for s in (-2, -1, 1, 2)}
    along = centred12(lambda s: pairs2[s]) / 12.0
    surface = sown[2 : 2 + ny, :]
    sown[...] = along
    slope_ref[0] = sown[2 : 2 + ny, :]

    def above(k, total):
        s = layers_ref[1, k]
        return total + (s * layers_ref[0, k]) * jnp.exp(s * surface)

    total = lax.fori_loop(0, gz * nz, above, jnp.zeros((ny, nx), F32))
    for k in range(nz):
        s = layers_ref[1, gz * nz + k]
        thickness = layers_ref[0, gz * nz + k] * jnp.exp(s * surface)
        weighted = s * thickness
        mz = 1.0 / thickness
        lift = total + 0.5 * weighted
        total = total + weighted
        mz_ref[k] = mz
        factor_ref[k] = (lift - 1.0) * mz
    load.wait()


def edge_terms(got_left, got_right, low, high):
    dl = got_left - high
    dr = got_right - low
    nx = dl.shape[-1]
    lane = lanes_of(dl.shape)
    even = lane % 2 == 0
    dl = pltpu.roll(dl, 2, 1)
    dr = pltpu.roll(dr, nx - 2, 1)
    to_low = jnp.where(even, dl - 8.0 * pltpu.roll(dl, nx - 1, 1), dl)
    to_high = jnp.where(even, -dr, 8.0 * pltpu.roll(dr, 1, 1) - dr)
    second = (lane // 2) % 2 == 1
    return jnp.where(second, to_low, to_high), jnp.where(second, to_high, to_low)


def along_x(tile, edges, m, lane):
    nx = tile.shape[-1]
    e = pltpu.roll(edges, (2 * nx - 2 - 2 * m) % nx if isinstance(m, int) else 2 * nx - 2 - 2 * m, 1)
    d = 8.0 * (pltpu.roll(tile, nx - 1, 1) - pltpu.roll(tile, 1, 1)) - (
        pltpu.roll(tile, nx - 2, 1) - pltpu.roll(tile, 2, 1)
    )
    return d + jnp.where((lane < 2) | (lane >= nx - 2), e, 0.0)


def lookup(row, tile):
    table = jnp.broadcast_to(row, tile.shape)
    return jnp.take_along_axis(table, tile, axis=1, mode="promise_in_bounds")


def table_rows(refs, nx):
    n = refs[0].shape[1]
    return [jnp.concatenate([r, jnp.zeros((1, nx - n), F32)], axis=1) for r in refs]


def fill_edges(n_gx, edge_ref, x1_ref, x2_ref, low_ref, high_ref):
    for c in range(3):
        at = slice(SUB * c, SUB * c + SUB)
        got = (x1_ref[at, :], x2_ref[at, :])
        first, second = edge_terms(
            from_before("gx", got), from_after("gx", n_gx, got), low_ref[at, :], high_ref[at, :]
        )
        edge_ref[c, 0] = first
        edge_ref[c, 1] = second


def fill_rows(n_gy, tall, field, y1_ref, y2_ref, nz, ny):
    for c in range(3):
        for k in range(nz):
            j = 2 * (c * nz + k)
            got = (y1_ref[j : j + 2, :], y2_ref[j : j + 2, :])
            tall[c, k, PAD : PAD + ny, :] = field(c, k)
            tall[c, k, PAD - 2 : PAD, :] = from_before("gy", got)
            tall[c, k, PAD + ny : PAD + ny + 2, :] = from_after("gy", n_gy, got)


def depth_halos(n_gz, zb, za, z1_ref, z2_ref):
    got = (z1_ref[...], z2_ref[...])
    zb[...] = from_before("gz", got)
    za[...] = from_after("gz", n_gz, got)


def over_layers(nz, layer):
    for k in (0, 1):
        layer(k)

    @pl.loop(2, nz - 2)
    def _(k):
        layer(k)

    for k in (nz - 2, nz - 1):
        layer(k)


def velocity_kernel(
    sizes, velocity_ref, stress_ref, material_ref, buoy_ref, factor_ref, mz_ref, slope_ref,
    x1_ref, x2_ref, low_ref, high_ref, y1_ref, y2_ref, z1_ref, z2_ref,
    out_ref, vlow_ref, vhigh_ref, vx1_ref, vx2_ref, vy1_ref, vy2_ref, vz1_ref, vz2_ref,
    edge, tall, zb, za,
):
    n_gx, n_gy, n_gz = sizes
    _, nz, ny, nx = velocity_ref.shape
    tiles = ny // SUB
    lane = lanes_of((SUB, nx))
    fill_edges(n_gx, edge, x1_ref, x2_ref, low_ref, high_ref)
    of_y = (3, 1, 5)
    fill_rows(n_gy, tall, lambda c, k: stress_ref[of_y[c], k], y1_ref, y2_ref, nz, ny)
    depth_halos(n_gz, zb, za, z1_ref, z2_ref)
    (buoy_row,) = table_rows([buoy_ref[...] * (step_size / 12.0)], nx)

    def layer(k):
        def depth(c, t):
            rows = slice(SUB * t, SUB * t + SUB)

            def at(s):
                if isinstance(k, int) and k + s < 0:
                    return zb[c, k + s + 2, rows, :]
                if isinstance(k, int) and k + s >= nz:
                    return za[c, k + s - nz, rows, :]
                return stress_ref[c, k + s, rows, :]

            return centred12(at)

        for t in range(tiles):
            rows = slice(SUB * t, SUB * t + SUB)
            m = k * tiles + t

            def gx_of(c, comp):
                return along_x(stress_ref[comp, k, rows, :], edge[c, t % 2], m, lane)

            def gy_of(c):
                return centred12(
                    lambda s: tall[c, k, PAD + SUB * t + s : PAD + SUB * t + s + SUB, :]
                )

            b = lookup(buoy_row, material_ref[k, rows, :])
            factor = factor_ref[k, rows, :]
            mz = mz_ref[k, rows, :]
            mx = slope_ref[0, rows, :] * factor
            my = slope_ref[1, rows, :] * factor
            gk = [depth(c, t) for c in range(6)]
            accel = (
                gx_of(0, 0) + gy_of(0) - mx * gk[0] - my * gk[3] + mz * gk[4],
                gx_of(1, 3) + gy_of(1) - mx * gk[3] - my * gk[1] + mz * gk[5],
                gx_of(2, 4) + gy_of(2) - mx * gk[4] - my * gk[5] + mz * gk[2],
            )
            for c in range(3):
                out_ref[c, k, rows, :] = velocity_ref[c, k, rows, :] + b * accel[c]

    over_layers(nz, layer)
    pack_sides(
        lambda c, k, t: out_ref[c, k, SUB * t : SUB * t + SUB, :],
        nz, ny, nx, vlow_ref, vhigh_ref, vx1_ref, vx2_ref,
    )
    pack_rows(lambda c, k, rows: out_ref[c, k, rows, :], nz, ny, vy1_ref, vy2_ref)
    vz1_ref[...], vz2_ref[...] = order("gz", out_ref[:, nz - 2 : nz], out_ref[:, 0:2])


def stress_kernel(
    sizes, vel_ref, stress_ref, memory_ref, material_ref, lam_ref, mu_ref, relax_ref, weight_ref,
    factor_ref, mz_ref, slope_ref, x1_ref, x2_ref, low_ref, high_ref, y1_ref, y2_ref, z1_ref, z2_ref,
    vel_hbm, stress_hbm, memory_hbm, edge, tall, zb, za, stress_out, memory_out, sems,
):
    n_gx, n_gy, n_gz = sizes
    _, nz, ny, nx = vel_ref.shape
    vel_copy = pltpu.make_async_copy(vel_ref, vel_hbm, sems.at[0, 0])
    vel_copy.start()

    def out_copies(first, count, spot):
        layers = pl.ds(first, count)
        return [
            pltpu.make_async_copy(a.at[:, layers], b.at[:, layers], sems.at[i, spot])
            for i, (a, b) in enumerate(((stress_out, stress_hbm), (memory_out, memory_hbm)))
        ]

    tiles = ny // SUB
    lane = lanes_of((SUB, nx))
    fill_edges(n_gx, edge, x1_ref, x2_ref, low_ref, high_ref)
    fill_rows(n_gy, tall, lambda c, k: vel_ref[c, k], y1_ref, y2_ref, nz, ny)
    depth_halos(n_gz, zb, za, z1_ref, z2_ref)
    keep1 = jnp.exp(-step_size / relax_ref[...])
    lam_row, mu_row, keep_row, gain_row = table_rows(
        [lam_ref[...] / 12.0, mu_ref[...] / 12.0, keep1, (1.0 - keep1) * weight_ref[...]], nx
    )

    def layer(k):
        for t in range(tiles):
            rows = slice(SUB * t, SUB * t + SUB)
            m = k * tiles + t
            kind = material_ref[k, rows, :]
            factor = factor_ref[k, rows, :]
            mz = mz_ref[k, rows, :]
            mx = slope_ref[0, rows, :] * factor
            my = slope_ref[1, rows, :] * factor

            def depth(c):
                def at(s):
                    if isinstance(k, int) and k + s < 0:
                        return zb[c, k + s + 2, rows, :]
                    if isinstance(k, int) and k + s >= nz:
                        return za[c, k + s - nz, rows, :]
                    return vel_ref[c, k + s, rows, :]

                return centred12(at)

            dk = [depth(c) for c in range(3)]
            dx = [
                along_x(vel_ref[c, k, rows, :], edge[c, t % 2], m, lane) - mx * dk[c]
                for c in range(3)
            ]
            dy = [
                centred12(lambda s: tall[c, k, PAD + SUB * t + s : PAD + SUB * t + s + SUB, :])
                - my * dk[c]
                for c in range(3)
            ]
            dz = [mz * dk[c] for c in range(3)]
            lam = lookup(lam_row, kind)
            mu = lookup(mu_row, kind)
            keep = lookup(keep_row, kind)
            gain = lookup(gain_row, kind)
            volume = lam * (dx[0] + dy[1] + dz[2])
            mu2 = mu + mu
            rates = (
                volume + mu2 * dx[0],
                volume + mu2 * dy[1],
                volume + mu2 * dz[2],
                mu * (dy[0] + dx[1]),
                mu * (dz[0] + dx[2]),
                mu * (dz[1] + dy[2]),
            )
            for c in range(6):
                kept = keep * memory_ref[c, k, rows, :] + gain * rates[c]
                memory_out[c, k, rows, :] = kept
                stress_out[c, k, rows, :] = stress_ref[c, k, rows, :] + step_size * (
                    rates[c] - kept
                )

    inner = nz - 4
    step = next(d for d in (4, 3, 2, 1) if inner % d == 0)
    chunks = inner // step
    layer(0)
    layer(1)
    for copy in out_copies(0, 2, 1):
        copy.start()

    @pl.loop(0, chunks)
    def _(j):
        @pl.loop(0, step)
        def _(k):
            layer(2 + j * step + k)

        for copy in out_copies(2 + j * step, step, 2 + j):
            copy.start()

    layer(nz - 2)
    layer(nz - 1)
    for copy in out_copies(nz - 2, 2, 2 + chunks):
        copy.start()
    vel_copy.wait()
    for copy in out_copies(0, 2, 1) + out_copies(nz - 2, 2, 2 + chunks):
        copy.wait()

    @pl.loop(0, chunks)
    def _(j):
        for copy in out_copies(2 + j * step, step, 2 + j):
            copy.wait()


def call(kernel, outs, in_specs, scratch=(), name=None, out_specs=None):
    return pl.pallas_call(
        kernel,
        out_shape=[jax.ShapeDtypeStruct(s, F32) for s in outs],
        in_specs=in_specs,
        out_specs=out_specs or [VM] * len(outs),
        scratch_shapes=list(scratch),
        compiler_params=params(),
        name=name,
    )


def local(
    sizes, elevation, layer_base, stretch, material, buoyancy, lame_lambda, shear_modulus,
    relax_time, anelastic_weight, velocity, stress, memory,
):
    n_gx, n_gy, n_gz = counts = tuple(sizes[a] for a in ("gx", "gy", "gz"))
    _, nz, ny, nx = velocity.shape
    rows = ny + SUB
    slab = call(
        terrain_piece_kernel,
        [(rows, nx)],
        [HB] * 3,
        [
            pltpu.VMEM(elevation.shape, jnp.int32),
            pltpu.VMEM((1, nz), F32),
            pltpu.VMEM((1, nz), F32),
            DMA((3,)),
        ],
        name="terrain_piece",
    )(elevation, layer_base[None], stretch[None])[0]
    faces = 2 * 3 * nz
    xs = 3 * SUB
    z_face = (6, 2, ny, nx)
    stress_vm, low, high, x1, x2, y1, y2, z1, z2 = call(
        pack_kernel,
        [stress.shape] + [(xs, nx)] * 4 + [(faces, nx)] * 2 + [z_face] * 2,
        [HB],
        [DMA((8,))],
        name="pack_stress",
    )(stress)
    if n_gz & (n_gz - 1):
        slab = lax.psum(slab, "gz")
    else:
        bit = 1
        while bit < n_gz:
            slab = slab + lax.ppermute(slab, "gz", [(i, i ^ bit) for i in range(n_gz)])
            bit *= 2
    height = slab[:ny]
    z1, z2 = exchange(sizes, "gz", z1, z2)
    x1, x2 = exchange(sizes, "gx", jnp.concatenate([x1, height]), jnp.concatenate([x2, height]))
    t1, t2 = call(
        functools.partial(y_terrain_kernel, n_gx),
        [(SUB, nx), (SUB, nx)],
        [VM] * 3,
        name="y_terrain",
    )(slab, x1[xs:], x2[xs:])
    y1, y2 = exchange(sizes, "gy", jnp.concatenate([y1, t1]), jnp.concatenate([y2, t2]))
    factor, mz, slope, velocity_vm = call(
        functools.partial(metric_kernel, counts),
        [(nz, ny, nx), (nz, ny, nx), (2, ny, nx), velocity.shape],
        [SM] + [VM] * 5 + [HB],
        [
            pltpu.VMEM((ny + 2 * PAD, nx), F32),
            pltpu.VMEM((ny + 2 * PAD, nx), F32),
            pltpu.VMEM((ny + PAD, nx), F32),
            DMA,
        ],
        name="metrics",
    )(slab[ny:], slab, x1[xs:], x2[xs:], y1[faces:], y2[faces:], velocity)

    def scratch(comps):
        return [
            pltpu.VMEM((3, 2, SUB, nx), F32),
            pltpu.VMEM((3, nz, ny + 2 * PAD, nx), F32),
            pltpu.VMEM((comps, 2, ny, nx), F32),
            pltpu.VMEM((comps, 2, ny, nx), F32),
        ]

    vel, vlow, vhigh, vx1, vx2, vy1, vy2, vz1, vz2 = call(
        functools.partial(velocity_kernel, counts),
        [velocity.shape] + [(xs, nx)] * 4 + [(faces, nx)] * 2 + [(3, 2, ny, nx)] * 2,
        [VM] * 15,
        scratch(6),
        name="velocity",
    )(
        velocity_vm, stress_vm, material, buoyancy[None], factor, mz, slope, x1, x2, low, high,
        y1, y2, z1, z2,
    )
    vx1, vx2 = exchange(sizes, "gx", vx1, vx2)
    vy1, vy2 = exchange(sizes, "gy", vy1, vy2)
    vz1, vz2 = exchange(sizes, "gz", vz1, vz2)
    return call(
        functools.partial(stress_kernel, counts),
        [velocity.shape, stress.shape, stress.shape],
        [VM] * 19,
        scratch(3) + [pltpu.VMEM(stress.shape, F32), pltpu.VMEM(stress.shape, F32), DMA((2, nz))],
        name="stress",
        out_specs=[HB] * 3,
    )(
        vel, stress_vm, memory, material, lame_lambda[None], shear_modulus[None], relax_time[None],
        anelastic_weight[None], factor, mz, slope, vx1, vx2, vlow, vhigh, vy1, vy2, vz1, vz2,
    )


def solution(mesh):
    sizes = {a: mesh.shape[a] for a in ("gx", "gy", "gz")}
    field = P(None, "gz", "gy", "gx")
    return jax.shard_map(
        functools.partial(local, sizes),
        mesh=mesh,
        in_specs=(
            P("gy", ("gx", "gz")), P("gz"), P("gz"), P("gz", "gy", "gx"),
            P(), P(), P(), P(), P(), field, field, field,
        ),
        out_specs=(field, field, field),
        check_vma=False,
    )
```

time: 44.5 us -> 35.5 us (0.80)
  local copies, waits for them, and re-layouts: 6.82 us -> 3.49 us
  starting transfers between devices: 16.1 us -> 12.9 us
  waiting for transfers between devices: 11 us -> 7.91 us
  Pallas kernels: 9.34 us -> 10.1 us
    ppermute x10, starting transfers between devices: 12.8 us -> 9.48 us  [exchange(): lax.ppermute(v, tuple(sizes), r)]
    ppermute x10, waiting for transfers between devices: 10.2 us -> 7.07 us  [exchange(): lax.ppermute(v, tuple(sizes), r)]
    unnamed x28 -> x24, local copies, waits for them, and re-layouts: 5.76 us -> 3.48 us
    slice x4 -> x3, local copies, waits for them, and re-layouts: 1.05 us -> 0.01 us  [the longest x1 0.01 us: local(): x1[xs:]]
    pallas_call x6, Pallas kernels: 9.34 us -> 10.1 us  [the longest x1 3.92 us: local(): call(functools.partial(stress_kernel, counts), [velocity.shape, stress.sh...]
  transfers between devices with their start and end apart: 12 -> 12, of which waited for: 5 -> 4; matrix products, arithmetic and copies ran while one was open for 2% -> 0% of each run, Pallas kernels for 3% -> 8%
where the time goes in v2:
time: 35.5 us; the launch traced here: 35.3 us
  starting transfers between devices  12.9 us (36%)
  Pallas kernels  10.1 us (28%)
  waiting for transfers between devices  7.91 us (22%)
  local copies, waits for them, and re-layouts  3.49 us (10%)
  between operations  0.84 us (2%)
    ppermute x10, starting transfers between devices, exchange(): lax.ppermute(v, tuple(sizes), r)  9.48 us
    ppermute x10, waiting for transfers between devices, exchange(): lax.ppermute(v, tuple(sizes), r)  7.07 us
    pallas_call x1, Pallas kernels, local(): call(functools.partial(stress_kernel, counts), [velocity.shape, stress.sh...  3.92 us
    unnamed x24, local copies, waits for them, and re-layouts  3.48 us
    ppermute x2, starting transfers between devices, local(): slab = slab + lax.ppermute(slab, 'gz', [(i, i ^ bit) for i in range(n_gz)])  3.38 us
    pallas_call x1, Pallas kernels, local(): call(functools.partial(velocity_kernel, counts), [velocity.shape] + [(xs,...  3.28 us
    pallas_call x1, Pallas kernels, local(): call(pack_kernel, [stress.shape] + [(xs, nx)] * 4 + [(faces, nx)] * 2 + [...  1.2 us
    pallas_call x1, Pallas kernels, local(): call(functools.partial(metric_kernel, counts), [(nz, ny, nx), (nz, ny, nx...  1.02 us
  transfers between devices with their start and end apart: 12, of which 4 were waited for; matrix products, arithmetic and copies ran while one was open for 0% of the time, Pallas kernels for 8%

profile of v2, /device:TPU:0, one launch (start us, length us, event | category | flops | bytes accessed | tf_op | source)
XLA Modules:
  0.0 35.3 jit_solution(3897736579883851967)
XLA Ops:
  0.6 0.0 copy-start.11
  0.6 0.0 copy-start.4
  0.7 0.7 %copy-done.4 = s32[32,32]{1,0:T(8,128)S(1)} copy-done((s32[32,32]{1,0:T(8,128)S(1)}, s32[32,32]{1,0:T(8,128)}, u32[]{:S(2)}) %copy-start.4) | copy-done | bytes 4120
  1.4 0.0 copy-start.5
  1.4 0.7 %copy-done.5 = f32[16]{0:T(128)S(1)} copy-done((f32[16]{0:T(128)S(1)}, f32[16]{0:T(128)}, u32[]{:S(2)}) %copy-start.5) | copy-done | bytes 88
  2.0 0.0 copy-start.6
  2.0 0.7 %copy-done.6 = f32[16]{0:T(128)S(1)} copy-done((f32[16]{0:T(128)S(1)}, f32[16]{0:T(128)}, u32[]{:S(2)}) %copy-start.6) | copy-done | bytes 88
  2.7 0.1 terrain_piece.1
  2.8 0.5 %collective-permute-start = (f32[40,128]{1,0:T(8,128)S(1)}, f32[40,128]{1,0:T(8,128)S(1)}, u32[]{:S(2)}, u32[]{:S(2)}) collective-permute-start(f32[40,128]{1,0:T(8,128)S(1)} %terrain_piece.1), channel_id=1, source_target_pairs={{0,1},{1,0},{2,3},{3,2},{4,5},{5,4},{6,7},{7,6},{8,9},{9,8},{10,11... | collective-permute-start | bytes 61448 | tf_op jit(solution)/shard_map/ppermute | solution.py:541
  3.3 0.8 %collective-permute-done = f32[40,128]{1,0:T(8,128)S(1)} collective-permute-done((f32[40,128]{1,0:T(8,128)S(1)}, f32[40,128]{1,0:T(8,128)S(1)}, u32[]{:S(2)}, u32[]{:S(2)}) %collective-permute-start) | collective-permute-done | bytes 20512 | tf_op jit(solution)/shard_map/ppermute | solution.py:541
  4.2 2.9 %collective-permute-start.1 = (f32[40,128]{1,0:T(8,128)S(1)}, f32[40,128]{1,0:T(8,128)S(1)}, u32[]{:S(2)}, u32[]{:S(2)}) collective-permute-start(f32[40,128]{1,0:T(8,128)S(1)} %add.6), channel_id=1, source_target_pairs={{0,2},{1,3},{2,0},{3,1},{4,6},{5,7},{6,4},{7,5},{8,10},{9,11},{10,... | collective-permute-start | bytes 61448 | tf_op jit(solution)/shard_map/ppermute | solution.py:541
  7.0 0.0 copy-start
  7.0 1.4 %copy-done = f32[6,16,32,128]{3,2,1,0:T(8,128)S(1)} copy-done((f32[6,16,32,128]{3,2,1,0:T(8,128)S(1)}, f32[6,16,32,128]{3,2,1,0:T(8,128)}, u32[]{:S(2)}) %copy-start) | copy-done | bytes 1572888
  8.4 0.0 copy-start.3
  8.4 0.0 copy-start.2
  8.4 1.2 %pack_stress.1 = (f32[6,16,32,128]{3,2,1,0:T(8,128)S(1)}, f32[24,128]{1,0:T(8,128)S(1)}, f32[24,128]{1,0:T(8,128)S(1)}, f32[24,128]{1,0:T(8,128)S(1)}, f32[24,12...) custom-call(f32[6,16,32,128]{3,2,1,0:T(8,128)S(1)} %copy-done), custom_call_target="tpu_custom_call" | custom-call | tf_op jit(solution)/shard_map/pack_stress/pallas_call | solution.py:529
  9.6 0.1 collective-permute-start.5
  9.7 1.6 %collective-permute-start.6 = (f32[6,2,32,128]{3,2,1,0:T(8,128)S(1)}, f32[6,2,32,128]{3,2,1,0:T(8,128)S(1)}, u32[]{:S(2)}, u32[]{:S(2)}) collective-permute-start(f32[6,2,32,128]{3,2,1,0:T(8,128)S(1)} %get-tuple-element.36), channel_id=1, source_target_pairs={{0,4},{1,2},{2,1},{3,7},{4,0},{5,6},{6,5},{7,3},{8,12},{9,10},{10,... | collective-permute-start | bytes 589832 | tf_op jit(solution)/shard_map/ppermute | solution.py:46
  11.3 0.0 collective-permute-done.1
  11.3 0.1 collective-permute-start.3
  11.4 3.1 %collective-permute-start.2 = (f32[56,128]{1,0:T(8,128)S(1)}, f32[56,128]{1,0:T(8,128)S(1)}, u32[]{:S(2)}, u32[]{:S(2)}) collective-permute-start(f32[56,128]{1,0:T(8,128)S(1)} %get-tuple-element.46), channel_id=1, source_target_pairs={{0,8},{1,9},{2,10},{3,11},{4,12},{5,13},{6,14},{7,15},{8,0},{9,1},... | collective-permute-start | bytes 86024 | tf_op jit(solution)/shard_map/ppermute | solution.py:46
  14.5 0.0 collective-permute-done.3.x2_ref
  14.5 1.8 %collective-permute-done.2.x1_ref = f32[56,128]{1,0:T(8,128)S(1)} collective-permute-done((f32[56,128]{1,0:T(8,128)S(1)}, f32[56,128]{1,0:T(8,128)S(1)}, u32[]{:S(2)}, u32[]{:S(2)}) %collective-permute-start.2) | collective-permute-done | bytes 28704 | tf_op jit(solution)/shard_map/ppermute | solution.py:46
  16.4 0.6 %y_terrain.1 = (f32[8,128]{1,0:T(8,128)S(1)}, f32[8,128]{1,0:T(8,128)}) custom-call(f32[40,128]{1,0:T(8,128)S(1)} %add.7.slab_ref, f32[32,128]{1,0:T(8,128)S(1)} %slice.25.got1_ref.x1_ref, f32[32,128]{1,0:T(8,128)S(1)} %slice.26.got2_ref.x2_ref), custom_call_target="tpu_custom_call" | custom-call | tf_op jit(solution)/shard_map/y_terrain/pallas_call | solution.py:546
  17.0 0.5 %collective-permute-start.4 = (f32[104,128]{1,0:T(8,128)S(1)}, f32[104,128]{1,0:T(8,128)S(1)}, u32[]{:S(2)}, u32[]{:S(2)}) collective-permute-start(f32[104,128]{1,0:T(8,128)S(1)} %pad_maximum_fusion), channel_id=1, source_target_pairs={{0,4},{1,5},{2,6},{3,7},{4,0},{5,1},{6,2},{7,3},{8,12},{9,13},{10,... | collective-permute-start | bytes 159752 | tf_op jit(solution)/shard_map/ppermute | solution.py:46
  17.5 3.6 %collective-permute-done.4.y1_ref.y2_ref = f32[104,128]{1,0:T(8,128)S(1)} collective-permute-done((f32[104,128]{1,0:T(8,128)S(1)}, f32[104,128]{1,0:T(8,128)S(1)}, u32[]{:S(2)}, u32[]{:S(2)}) %collective-permute-start.4) | collective-permute-done | bytes 53280 | tf_op jit(solution)/shard_map/ppermute | solution.py:46
  21.1 0.0 copy-done.3
  21.1 1.0 %metrics.1 = (f32[16,32,128]{2,1,0:T(8,128)S(1)}, f32[16,32,128]{2,1,0:T(8,128)S(1)}, f32[2,32,128]{2,1,0:T(8,128)S(1)}, f32[3,16,32,128]{3,2,1,0:T(8,128)S(1)}) custom-call(f32[8,128]{1,0:T(8,128)S(1)} %slice.23.layers_ref, f32[40,128]{1,0:T(8,128)S(1)} %add.7.slab_ref, f32[32,128]{1,0:T(8,128)S(1)} %slice.25.got1_ref.x1_ref, ...), custom_call_target="tpu_custom_call" | custom-call | tf_op jit(solution)/shard_map/metrics/pallas_call | solution.py:553
  22.2 0.0 collective-permute-done.5.z1_ref
  22.2 0.0 collective-permute-done.6.z2_ref
  22.2 0.0 copy-done.11
  22.2 0.0 copy-done.2
  22.2 0.0 copy-start.1
  22.2 0.0 copy-start.7
  22.2 0.0 copy-start.8
  22.2 0.0 copy-start.9
  22.2 0.0 copy-start.10
  22.3 3.3 %velocity.1 = (f32[3,16,32,128]{3,2,1,0:T(8,128)S(1)}, f32[24,128]{1,0:T(8,128)S(1)}, f32[24,128]{1,0:T(8,128)S(1)}, f32[24,128]{1,0:T(8,128)S(1)}, f32[24,128]{...) custom-call(f32[3,16,32,128]{3,2,1,0:T(8,128)S(1)} %get-tuple-elemen, ...), custom_call_target="tpu_custom_call" | custom-call | tf_op jit(solution)/shard_map/velocity/pallas_call | solution.py:574
  25.5 0.0 collective-permute-start.10
  25.5 0.5 %collective-permute-start.11 = (f32[3,2,32,128]{3,2,1,0:T(8,128)S(1)}, f32[3,2,32,128]{3,2,1,0:T(8,128)S(1)}, u32[]{:S(2)}, u32[]{:S(2)}) collective-permute-start(f32[3,2,32,128]{3,2,1,0:T(8,128)S(1)} %get-tuple-element.44), channel_id=1, source_target_pairs={{0,4},{1,2},{2,1},{3,7},{4,0},{5,6},{6,5},{7,3},{8,12},{9,10},{10,... | collective-permute-start | bytes 294920 | tf_op jit(solution)/shard_map/ppermute | solution.py:46
  26.1 1.5 %collective-permute-start.9 = (f32[96,128]{1,0:T(8,128)S(1)}, f32[96,128]{1,0:T(8,128)S(1)}, u32[]{:S(2)}, u32[]{:S(2)}) collective-permute-start(f32[96,128]{1,0:T(8,128)S(1)} %get-tuple-element.42), channel_id=1, source_target_pairs={{0,4},{1,5},{2,6},{3,7},{4,0},{5,1},{6,2},{7,3},{8,12},{9,13},{10,... | collective-permute-start | bytes 147464 | tf_op jit(solution)/shard_map/ppermute | solution.py:46
  27.6 2.0 %collective-permute-start.7 = (f32[24,128]{1,0:T(8,128)S(1)}, f32[24,128]{1,0:T(8,128)S(1)}, u32[]{:S(2)}, u32[]{:S(2)}) collective-permute-start(f32[24,128]{1,0:T(8,128)S(1)} %get-tuple-element.38), channel_id=1, source_target_pairs={{0,8},{1,9},{2,10},{3,11},{4,12},{5,13},{6,14},{7,15},{8,0},{9,1},... | collective-permute-start | bytes 36872 | tf_op jit(solution)/shard_map/ppermute | solution.py:46
  29.6 0.1 collective-permute-start.8
  29.7 1.6 %collective-permute-done.7.x1_ref = f32[24,128]{1,0:T(8,128)S(1)} collective-permute-done((f32[24,128]{1,0:T(8,128)S(1)}, f32[24,128]{1,0:T(8,128)S(1)}, u32[]{:S(2)}, u32[]{:S(2)}) %collective-permute-start.7) | collective-permute-done | bytes 12320 | tf_op jit(solution)/shard_map/ppermute | solution.py:46
  31.3 0.0 collective-permute-done.8.x2_ref
  31.3 0.0 collective-permute-done.9.y1_ref.y2_ref
  31.3 0.0 collective-permute-done.10.z1_ref
  31.3 0.0 collective-permute-done.11.z2_ref
  31.3 0.0 copy-done.1
  31.3 0.0 copy-done.7
  31.3 0.0 copy-done.8
  31.3 0.0 copy-done.9
  31.3 0.0 copy-done.10
  31.3 3.9 %stress.1 = (f32[3,16,32,128]{3,2,1,0:T(8,128)}, f32[6,16,32,128]{3,2,1,0:T(8,128)}, f32[6,16,32,128]{3,2,1,0:T(8,128)}) custom-call(f32[3,16,32,128]{3,2,1,0:T(8,128)S(1)} %get-tuple-element.37.vel_ref, f32[6,16,32,128]{3,2,1,0:T(8,128)S(1)} %get-tuple-element.29.stress_ref, f32[6,16,32,128]{3,2,1,0:T(8,128)S(1)} %copy-done.1, ...), custom_call_target="tpu_custom_call" | custom-call | tf_op jit(solution)/shard_map/stress/pallas_call | solution.py:587
  (9 shorter events, 0.0 us)
Async XLA Ops:
  0.6 21.5 %copy-start.11 = (f32[16]{0:T(128)S(1)}, f32[16]{0:T(128)}, u32[]{:S(2)}) copy-start(f32[16]{0:T(128)} %param.16) | copy-start | bytes 196
  0.6 0.7 %copy-start.4 = (s32[32,32]{1,0:T(8,128)S(1)}, s32[32,32]{1,0:T(8,128)}, u32[]{:S(2)}) copy-start(s32[32,32]{1,0:T(8,128)} %elev_hbm.1) | copy-start | bytes 12292
  1.4 0.7 %copy-start.5 = (f32[16]{0:T(128)S(1)}, f32[16]{0:T(128)}, u32[]{:S(2)}) copy-start(f32[16]{0:T(128)} %param.13) | copy-start | bytes 196
  2.0 0.7 %copy-start.6 = (f32[16]{0:T(128)S(1)}, f32[16]{0:T(128)}, u32[]{:S(2)}) copy-start(f32[16]{0:T(128)} %param.14) | copy-start | bytes 196
  2.8 1.4 %collective-permute-start = (f32[40,128]{1,0:T(8,128)S(1)}, f32[40,128]{1,0:T(8,128)S(1)}, u32[]{:S(2)}, u32[]{:S(2)}) collective-permute-start(f32[40,128]{1,0:T(8,128)S(1)} %terrain_piece.1), channel_id=1, source_target_pairs={{0,1},{1,0},{2,3},{3,2},{4,5},{5,4},{6,7},{7,6},{8,9},{9,8},{10,11... | collective-permute-start | bytes 61448 | tf_op jit(solution)/shard_map/ppermute | solution.py:541
  4.2 7.1 %collective-permute-start.1 = (f32[40,128]{1,0:T(8,128)S(1)}, f32[40,128]{1,0:T(8,128)S(1)}, u32[]{:S(2)}, u32[]{:S(2)}) collective-permute-start(f32[40,128]{1,0:T(8,128)S(1)} %add.6), channel_id=1, source_target_pairs={{0,2},{1,3},{2,0},{3,1},{4,6},{5,7},{6,4},{7,5},{8,10},{9,11},{10,... | collective-permute-start | bytes 61448 | tf_op jit(solution)/shard_map/ppermute | solution.py:541
  7.0 1.4 %copy-start = (f32[6,16,32,128]{3,2,1,0:T(8,128)S(1)}, f32[6,16,32,128]{3,2,1,0:T(8,128)}, u32[]{:S(2)}) copy-start(f32[6,16,32,128]{3,2,1,0:T(8,128)} %stress_hbm.1) | copy-start | bytes 4718596
  8.4 12.7 %copy-start.3 = (f32[3,16,32,128]{3,2,1,0:T(8,128)S(1)}, f32[3,16,32,128]{3,2,1,0:T(8,128)}, u32[]{:S(2)}) copy-start(f32[3,16,32,128]{3,2,1,0:T(8,128)} %velocity_hbm.1) | copy-start | bytes 2359300
  8.4 13.8 %copy-start.2 = (s32[16,32,128]{2,1,0:T(8,128)S(1)}, s32[16,32,128]{2,1,0:T(8,128)}, u32[]{:S(2)}) copy-start(s32[16,32,128]{2,1,0:T(8,128)} %material_ref.3) | copy-start | bytes 786436
  9.6 12.5 %collective-permute-start.5 = (f32[6,2,32,128]{3,2,1,0:T(8,128)S(1)}, f32[6,2,32,128]{3,2,1,0:T(8,128)S(1)}, u32[]{:S(2)}, u32[]{:S(2)}) collective-permute-start(f32[6,2,32,128]{3,2,1,0:T(8,128)S(1)} %get-tuple-element.35), channel_id=1, source_target_pairs={{0,1},{1,0},{2,3},{3,2},{4,5},{5,4},{6,7},{7,6},{8,9},{9,8},{10,11... | collective-permute-start | bytes 589832 | tf_op jit(solution)/shard_map/ppermute | solution.py:46
  9.7 12.4 %collective-permute-start.6 = (f32[6,2,32,128]{3,2,1,0:T(8,128)S(1)}, f32[6,2,32,128]{3,2,1,0:T(8,128)S(1)}, u32[]{:S(2)}, u32[]{:S(2)}) collective-permute-start(f32[6,2,32,128]{3,2,1,0:T(8,128)S(1)} %get-tuple-element.36), channel_id=1, source_target_pairs={{0,4},{1,2},{2,1},{3,7},{4,0},{5,6},{6,5},{7,3},{8,12},{9,10},{10,... | collective-permute-start | bytes 589832 | tf_op jit(solution)/shard_map/ppermute | solution.py:46
  11.3 3.2 %collective-permute-start.3 = (f32[56,128]{1,0:T(8,128)S(1)}, f32[56,128]{1,0:T(8,128)S(1)}, u32[]{:S(2)}, u32[]{:S(2)}) collective-permute-start(f32[56,128]{1,0:T(8,128)S(1)} %get-tuple-element.45), channel_id=1, source_target_pairs={{0,1},{1,0},{2,3},{3,2},{4,5},{5,4},{6,7},{7,6},{8,16},{9,17},{10,... | collective-permute-start | bytes 86024 | tf_op jit(solution)/shard_map/ppermute | solution.py:46
  11.4 5.0 %collective-permute-start.2 = (f32[56,128]{1,0:T(8,128)S(1)}, f32[56,128]{1,0:T(8,128)S(1)}, u32[]{:S(2)}, u32[]{:S(2)}) collective-permute-start(f32[56,128]{1,0:T(8,128)S(1)} %get-tuple-element.46), channel_id=1, source_target_pairs={{0,8},{1,9},{2,10},{3,11},{4,12},{5,13},{6,14},{7,15},{8,0},{9,1},... | collective-permute-start | bytes 86024 | tf_op jit(solution)/shard_map/ppermute | solution.py:46
  17.0 4.1 %collective-permute-start.4 = (f32[104,128]{1,0:T(8,128)S(1)}, f32[104,128]{1,0:T(8,128)S(1)}, u32[]{:S(2)}, u32[]{:S(2)}) collective-permute-start(f32[104,128]{1,0:T(8,128)S(1)} %pad_maximum_fusion), channel_id=1, source_target_pairs={{0,4},{1,5},{2,6},{3,7},{4,0},{5,1},{6,2},{7,3},{8,12},{9,13},{10,... | collective-permute-start | bytes 159752 | tf_op jit(solution)/shard_map/ppermute | solution.py:46
  22.2 9.1 %copy-start.1 = (f32[6,16,32,128]{3,2,1,0:T(8,128)S(1)}, f32[6,16,32,128]{3,2,1,0:T(8,128)}, u32[]{:S(2)}) copy-start(f32[6,16,32,128]{3,2,1,0:T(8,128)} %memory_ref.1) | copy-start | bytes 4718596
  22.2 9.1 %copy-start.7 = (f32[16]{0:T(128)S(1)}, f32[16]{0:T(128)}, u32[]{:S(2)}) copy-start(f32[16]{0:T(128)} %param.17) | copy-start | bytes 196
  22.2 9.1 %copy-start.8 = (f32[16]{0:T(128)S(1)}, f32[16]{0:T(128)}, u32[]{:S(2)}) copy-start(f32[16]{0:T(128)} %param.18) | copy-start | bytes 196
  22.2 9.1 %copy-start.9 = (f32[16]{0:T(128)S(1)}, f32[16]{0:T(128)}, u32[]{:S(2)}) copy-start(f32[16]{0:T(128)} %param.19) | copy-start | bytes 196
  22.2 9.1 %copy-start.10 = (f32[16]{0:T(128)S(1)}, f32[16]{0:T(128)}, u32[]{:S(2)}) copy-start(f32[16]{0:T(128)} %param.20) | copy-start | bytes 196
  25.5 5.7 %collective-permute-start.10 = (f32[3,2,32,128]{3,2,1,0:T(8,128)S(1)}, f32[3,2,32,128]{3,2,1,0:T(8,128)S(1)}, u32[]{:S(2)}, u32[]{:S(2)}) collective-permute-start(f32[3,2,32,128]{3,2,1,0:T(8,128)S(1)} %get-tuple-element.43), channel_id=1, source_target_pairs={{0,1},{1,0},{2,3},{3,2},{4,5},{5,4},{6,7},{7,6},{8,9},{9,8},{10,11... | collective-permute-start | bytes 294920 | tf_op jit(solution)/shard_map/ppermute | solution.py:46
  25.5 5.7 %collective-permute-start.11 = (f32[3,2,32,128]{3,2,1,0:T(8,128)S(1)}, f32[3,2,32,128]{3,2,1,0:T(8,128)S(1)}, u32[]{:S(2)}, u32[]{:S(2)}) collective-permute-start(f32[3,2,32,128]{3,2,1,0:T(8,128)S(1)} %get-tuple-element.44), channel_id=1, source_target_pairs={{0,4},{1,2},{2,1},{3,7},{4,0},{5,6},{6,5},{7,3},{8,12},{9,10},{10,... | collective-permute-start | bytes 294920 | tf_op jit(solution)/shard_map/ppermute | solution.py:46
  26.1 5.2 %collective-permute-start.9 = (f32[96,128]{1,0:T(8,128)S(1)}, f32[96,128]{1,0:T(8,128)S(1)}, u32[]{:S(2)}, u32[]{:S(2)}) collective-permute-start(f32[96,128]{1,0:T(8,128)S(1)} %get-tuple-element.42), channel_id=1, source_target_pairs={{0,4},{1,5},{2,6},{3,7},{4,0},{5,1},{6,2},{7,3},{8,12},{9,13},{10,... | collective-permute-start | bytes 147464 | tf_op jit(solution)/shard_map/ppermute | solution.py:46
  27.6 3.7 %collective-permute-start.7 = (f32[24,128]{1,0:T(8,128)S(1)}, f32[24,128]{1,0:T(8,128)S(1)}, u32[]{:S(2)}, u32[]{:S(2)}) collective-permute-start(f32[24,128]{1,0:T(8,128)S(1)} %get-tuple-element.38), channel_id=1, source_target_pairs={{0,8},{1,9},{2,10},{3,11},{4,12},{5,13},{6,14},{7,15},{8,0},{9,1},... | collective-permute-start | bytes 36872 | tf_op jit(solution)/shard_map/ppermute | solution.py:46
  29.6 1.7 %collective-permute-start.8 = (f32[24,128]{1,0:T(8,128)S(1)}, f32[24,128]{1,0:T(8,128)S(1)}, u32[]{:S(2)}, u32[]{:S(2)}) collective-permute-start(f32[24,128]{1,0:T(8,128)S(1)} %get-tuple-element.39), channel_id=1, source_target_pairs={{0,1},{1,0},{2,3},{3,2},{4,5},{5,4},{6,7},{7,6},{8,16},{9,17},{10,... | collective-permute-start | bytes 36872 | tf_op jit(solution)/shard_map/ppermute | solution.py:46

commit v3 on v2

v3 whole, which is shorter than its diff:
```python
import functools
import jax
import jax.numpy as jnp
import numpy as np
from jax import lax
from jax.experimental import pallas as pl
from jax.experimental.pallas import tpu as pltpu
from jax.sharding import PartitionSpec as P

step_size = 0.3
SUB = 8
PAD = 8
F32 = jnp.float32
params = functools.partial(pltpu.CompilerParams, vmem_limit_bytes=20 * 1024 * 1024)
VM = pl.BlockSpec(memory_space=pltpu.VMEM)
SM = pl.BlockSpec(memory_space=pltpu.SMEM)
HB = pl.BlockSpec(memory_space=pltpu.HBM)
DMA = pltpu.SemaphoreType.DMA


def pair_swaps(sizes, axis):
    names = tuple(sizes)
    shape = tuple(sizes.values())
    index = names.index(axis)
    n = shape[index]
    others = [d for d in (2, 1, 0) if d != index and shape[d] % 2 == 0]
    rounds = []
    for first in (0, 1)[: max(0, min(2, n - 1))]:
        table = []
        for spot in np.ndindex(*shape):
            mate = spot[index] + 1 if spot[index] % 2 == first else spot[index] - 1
            target = list(spot)
            if 0 <= mate < n:
                target[index] = mate
            elif others:
                target[others[0]] ^= 1
            else:
                continue
            table.append((int(np.ravel_multi_index(spot, shape)), int(np.ravel_multi_index(tuple(target), shape))))
        rounds.append(table)
    return rounds


def exchange(sizes, axis, first, second):
    rounds = pair_swaps(sizes, axis)
    got = [lax.ppermute(v, tuple(sizes), r) for v, r in zip((first, second), rounds)]
    return (got[0], got[-1]) if got else (first, second)


def even(axis):
    return lax.axis_index(axis) % 2 == 0


def from_before(axis, got):
    value = jnp.where(even(axis), got[1], got[0])
    return jnp.where(lax.axis_index(axis) > 0, value, 0.0)


def from_after(axis, n, got):
    value = jnp.where(even(axis), got[0], got[1])
    return jnp.where(lax.axis_index(axis) < n - 1, value, 0.0)


def order(axis, to_after, to_before):
    e = even(axis)
    return jnp.where(e, to_after, to_before), jnp.where(e, to_before, to_after)


def lanes_of(shape):
    return lax.broadcasted_iota(jnp.int32, shape, len(shape) - 1)


def terrain_piece_kernel(elev_hbm, base_hbm, stretch_hbm, out_ref, elev_ref, base_ref, stretch_ref, sems):
    mine = lax.axis_index("gz")
    pairs = ((elev_hbm, elev_ref), (base_hbm, base_ref), (stretch_hbm, stretch_ref))
    copies = [pltpu.make_async_copy(a, b, sems.at[i]) for i, (a, b) in enumerate(pairs)]
    for copy in copies:
        copy.start()
    for copy in copies:
        copy.wait()
    ny, width = elev_ref.shape
    nx = out_ref.shape[1]
    nz = base_ref.shape[1]
    height = elev_ref[...].astype(F32) / 200.0
    wide = jnp.concatenate([height, jnp.zeros((ny, nx - width), F32)], axis=1)
    out_ref[:ny, :] = pltpu.roll(wide, mine * width, 1)
    row = lax.broadcasted_iota(jnp.int32, (SUB, nx), 0)
    fill = jnp.zeros((1, nx - nz), F32)
    base = jnp.concatenate([base_ref[...], fill], axis=1)
    stretch = jnp.concatenate([stretch_ref[...], fill], axis=1)
    both = jnp.where(row == 0, base, jnp.where(row == 1, stretch, 0.0))
    out_ref[ny:, :] = pltpu.roll(both, mine * nz, 1)


def pack_sides(field, nz, ny, nx, low_ref, high_ref, out1_ref, out2_ref):
    tiles = ny // SUB
    lane2 = lanes_of((SUB, nx)) // 2
    for c in range(3):
        lo = jnp.zeros((SUB, nx), F32)
        hi = jnp.zeros((SUB, nx), F32)
        for k in range(nz):
            for t in range(tiles):
                m = k * tiles + t
                turned = pltpu.roll(field(c, k, t), (2 * m + 2) % nx, 1)
                hi = jnp.where(lane2 == m, turned, hi)
                lo = jnp.where(lane2 == (m + 1) % (nx // 2), turned, lo)
        at = slice(SUB * c, SUB * c + SUB)
        low_ref[at, :] = lo
        high_ref[at, :] = hi
        out1_ref[at, :], out2_ref[at, :] = order("gx", hi, lo)


def pack_rows(field, nz, ny, y_refs):
    for c in range(3):
        for k in range(nz):
            j = 2 * (c * nz + k)
            both = order("gy", field(c, k, slice(ny - 2, ny)), field(c, k, slice(0, 2)))
            for ref, rows in zip(y_refs, both):
                ref[j : j + 2, :] = rows


def pack_kernel(
    stress_hbm, stress_ref, low_ref, high_ref, out1_ref, out2_ref, z1_ref, z2_ref, *rest
):
    *y_refs, sems = rest
    comps, nz, ny, nx = stress_ref.shape
    copies = [
        pltpu.make_async_copy(stress_hbm.at[c], stress_ref.at[c], sems.at[c]) for c in range(comps)
    ]
    z_even = even("gz")
    z1_at = jnp.where(z_even, nz - 2, 0)
    z2_at = jnp.where(z_even, 0, nz - 2)
    z_copies = [
        pltpu.make_async_copy(stress_hbm.at[:, pl.ds(z1_at, 2)], z1_ref, sems.at[comps]),
        pltpu.make_async_copy(stress_hbm.at[:, pl.ds(z2_at, 2)], z2_ref, sems.at[comps + 1]),
    ]
    of_x = (0, 3, 4)
    of_y = (3, 1, 5)
    loading = (0, 3, 4, 1, 5, 2)
    for c in loading[:5]:
        copies[c].start()
    for copy in z_copies:
        copy.start()
    copies[2].start()
    for c in of_x:
        copies[c].wait()
    pack_sides(
        lambda c, k, t: stress_ref[of_x[c], k, SUB * t : SUB * t + SUB, :],
        nz, ny, nx, low_ref, high_ref, out1_ref, out2_ref,
    )
    copies[1].wait()
    copies[5].wait()
    pack_rows(lambda c, k, rows: stress_ref[of_y[c], k, rows, :], nz, ny, y_refs)
    copies[2].wait()
    for copy in z_copies:
        copy.wait()


def y_send_kernel(rounds, slab_ref, *refs):
    ny = slab_ref.shape[0] - SUB
    faces = refs[0].shape[0]
    rows = order("gy", slab_ref[ny - 4 : ny, :], slab_ref[0:4, :])
    for i in range(rounds):
        refs[rounds + i][:faces, :] = refs[i][...]
        refs[rounds + i][faces : faces + 4, :] = rows[i]
        refs[rounds + i][faces + 4 :, :] = jnp.zeros_like(rows[i])


def x_send_kernel(n_gy, slab_ref, y1_ref, y2_ref, x1_ref, x2_ref, tall_ref, out1_ref, out2_ref):
    ny = slab_ref.shape[0] - SUB
    nx = slab_ref.shape[1]
    xs = x1_ref.shape[0]
    lane4 = lanes_of((SUB, nx)) // 4
    got = (y1_ref[0:4, :], y2_ref[0:4, :])
    tall_ref[: PAD - 4, :] = jnp.zeros((PAD - 4, nx), F32)
    tall_ref[PAD - 4 : PAD, :] = from_before("gy", got)
    tall_ref[PAD : PAD + ny, :] = slab_ref[:ny, :]
    tall_ref[PAD + ny : PAD + ny + 4, :] = from_after("gy", n_gy, got)
    tall_ref[PAD + ny + 4 :, :] = jnp.zeros((PAD - 4, nx), F32)
    lo = jnp.zeros((SUB, nx), F32)
    hi = jnp.zeros((SUB, nx), F32)
    for j in range((ny + 2 * PAD) // SUB):
        tile = tall_ref[SUB * j : SUB * j + SUB, :]
        lo = jnp.where(lane4 == j, pltpu.roll(tile, 4 * j, 1), lo)
        hi = jnp.where(lane4 == j, pltpu.roll(tile, (4 * j + 4) % nx, 1), hi)
    out1_ref[:xs, :] = x1_ref[...]
    out2_ref[:xs, :] = x2_ref[...]
    out1_ref[xs:, :], out2_ref[xs:, :] = order("gx", hi, lo)


def binomial(at):
    return (at(-2) + at(2) + 4.0 * (at(-1) + at(1)) + 6.0 * at(0)) / 16.0


def centred12(at):
    return 8.0 * (at(1) - at(-1)) - (at(2) - at(-2))


def metric_kernel(
    sizes, layers_ref, own, x1_ref, x2_ref, factor_ref, mz_ref, slope_ref, rim, sown,
):
    n_gx = sizes[0]
    gz = lax.axis_index("gz")
    nz, ny, nx = factor_ref.shape
    lane = lanes_of((SUB, nx))
    got = (x1_ref[...], x2_ref[...])
    left, right = from_before("gx", got), from_after("gx", n_gx, got)
    for j in range((ny + 2 * PAD) // SUB):
        rim[SUB * j : SUB * j + SUB, :] = jnp.where(
            lane < nx // 2,
            pltpu.roll(right, (nx - 4 * j) % nx, 1),
            pltpu.roll(left, nx - 4 - 4 * j, 1),
        )
    rows = ny + 4
    tall_own = binomial(lambda s: own[PAD - 2 + s : PAD - 2 + s + rows, :])
    tall_rim = binomial(lambda s: rim[PAD - 2 + s : PAD - 2 + s + rows, :])

    def shifted(a, b, s):
        ln = lanes_of(a.shape)
        cut = (ln < s) if s > 0 else (ln >= nx + s)
        if s > 0:
            mixed_a, mixed_b = jnp.where(cut, b, a), jnp.where(cut, a, b)
        elif s < 0:
            mixed_a, mixed_b = jnp.where(cut, b, a), jnp.where(cut, a, b)
        else:
            return a, b
        return pltpu.roll(mixed_a, (-s) % nx, 1), pltpu.roll(mixed_b, (-s) % nx, 1)

    def padded_rows(a):
        return jnp.concatenate([a, jnp.zeros((SUB - rows % SUB, nx), F32)], axis=0)

    tall_own, tall_rim = padded_rows(tall_own), padded_rows(tall_rim)
    pairs = {s: shifted(tall_own, tall_rim, s) for s in (-2, -1, 0, 1, 2)}
    surf_own = binomial(lambda s: pairs[s][0])
    surf_rim = binomial(lambda s: pairs[s][1])
    sown[...] = surf_own
    slope_ref[1] = centred12(lambda s: sown[2 + s : 2 + s + ny, :]) / 12.0
    pairs2 = {s: shifted(surf_own, surf_rim, s)[0] for s in (-2, -1, 1, 2)}
    along = centred12(lambda s: pairs2[s]) / 12.0
    surface = sown[2 : 2 + ny, :]
    sown[...] = along
    slope_ref[0] = sown[2 : 2 + ny, :]

    def above(slab, total):
        for k in range(nz):
            s = layers_ref[1, slab * nz + k]
            total = total + (s * layers_ref[0, slab * nz + k]) * jnp.exp(s * surface)
        return total

    total = lax.fori_loop(0, gz, above, jnp.zeros((ny, nx), F32))
    for k in range(nz):
        s = layers_ref[1, gz * nz + k]
        thickness = layers_ref[0, gz * nz + k] * jnp.exp(s * surface)
        weighted = s * thickness
        mz = 1.0 / thickness
        lift = total + 0.5 * weighted
        total = total + weighted
        mz_ref[k] = mz
        factor_ref[k] = (lift - 1.0) * mz

def edge_terms(got_left, got_right, low, high):
    dl = got_left - high
    dr = got_right - low
    nx = dl.shape[-1]
    lane = lanes_of(dl.shape)
    even = lane % 2 == 0
    dl = pltpu.roll(dl, 2, 1)
    dr = pltpu.roll(dr, nx - 2, 1)
    to_low = jnp.where(even, dl - 8.0 * pltpu.roll(dl, nx - 1, 1), dl)
    to_high = jnp.where(even, -dr, 8.0 * pltpu.roll(dr, 1, 1) - dr)
    second = (lane // 2) % 2 == 1
    return jnp.where(second, to_low, to_high), jnp.where(second, to_high, to_low)


def turned_left(edges, m):
    nx = edges.shape[-1]
    shift = (2 * nx - 2 - 2 * m) % nx if isinstance(m, int) else 2 * nx - 2 - 2 * m
    return pltpu.roll(edges, shift, 1)


def sides(lane):
    return (lane < 2) | (lane >= lane.shape[-1] - 2)


def periodic_x(tile):
    nx = tile.shape[-1]
    return 8.0 * (pltpu.roll(tile, nx - 1, 1) - pltpu.roll(tile, 1, 1)) - (
        pltpu.roll(tile, nx - 2, 1) - pltpu.roll(tile, 2, 1)
    )


def lookup(row, tile):
    table = jnp.broadcast_to(row, tile.shape)
    return jnp.take_along_axis(table, tile, axis=1, mode="promise_in_bounds")


def table_rows(refs, nx):
    n = refs[0].shape[1]
    return [jnp.concatenate([r, jnp.zeros((1, nx - n), F32)], axis=1) for r in refs]


def fill_edges(n_gx, edge_ref, x1_ref, x2_ref, low_ref, high_ref):
    for c in range(3):
        at = slice(SUB * c, SUB * c + SUB)
        got = (x1_ref[at, :], x2_ref[at, :])
        first, second = edge_terms(
            from_before("gx", got), from_after("gx", n_gx, got), low_ref[at, :], high_ref[at, :]
        )
        edge_ref[c, 0] = first
        edge_ref[c, 1] = second


def fill_rows(n_gy, tall, field, y1_ref, y2_ref, nz, ny, layers):
    for c in range(3):
        for spot, k in enumerate(layers):
            j = 2 * (c * nz + k)
            got = (y1_ref[j : j + 2, :], y2_ref[j : j + 2, :])
            tall[c, spot, PAD : PAD + ny, :] = field(c, k)
            tall[c, spot, PAD - 2 : PAD, :] = from_before("gy", got)
            tall[c, spot, PAD + ny : PAD + ny + 2, :] = from_after("gy", n_gy, got)


def depth_halos(n_gz, zb, za, z1_ref, z2_ref):
    got = (z1_ref[...], z2_ref[...])
    zb[...] = from_before("gz", got)
    za[...] = from_after("gz", n_gz, got)


def tile_rows(t):
    return slice(SUB * t, SUB * t + SUB)


def row_difference(tall, c, spot, t):
    return centred12(lambda s: tall[c, spot, PAD + SUB * t + s : PAD + SUB * t + s + SUB, :])


def inner_depth(ref, out_ref, comps, k, tiles):
    for t in range(tiles):
        for c in range(comps):
            out_ref[c, k - 2, tile_rows(t), :] = centred12(lambda s: ref[c, k + s, tile_rows(t), :])


def outer_depth(ref, zb, za, out_ref, comps, nz, tiles):
    for spot, k in enumerate((0, 1, nz - 2, nz - 1)):
        for t in range(tiles):
            for c in range(comps):

                def at(s):
                    if k + s < 0:
                        return zb[c, k + s + 2, tile_rows(t), :]
                    if k + s >= nz:
                        return za[c, k + s - nz, tile_rows(t), :]
                    return ref[c, k + s, tile_rows(t), :]

                out_ref[c, spot, tile_rows(t), :] = centred12(at)


def cell_kernel(*refs):
    given, cells_ref, held, sems = refs[:6], refs[6], refs[7:13], refs[13]
    copies = [
        pltpu.make_async_copy(a, b, sems.at[i]) for i, (a, b) in enumerate(zip(given, held))
    ]
    for copy in copies:
        copy.start()
    for copy in copies:
        copy.wait()
    material_ref, buoy_ref, lam_ref, mu_ref, relax_ref, weight_ref = held
    nz, ny, nx = material_ref.shape
    keep = jnp.exp(-step_size / relax_ref[...])
    tables = table_rows(
        [
            buoy_ref[...] * (step_size / 12.0), lam_ref[...] / 12.0, mu_ref[...] / 12.0, keep,
            (1.0 - keep) * weight_ref[...],
        ],
        nx,
    )

    @pl.loop(0, nz)
    def _(k):
        for t in range(ny // SUB):
            kind = material_ref[k, tile_rows(t), :]
            for i, table in enumerate(tables):
                cells_ref[i, k, tile_rows(t), :] = lookup(table, kind)


def depth_kernel(stress_ref, velocity_hbm, depth_ref, along_ref, velocity_ref, sem):
    load = pltpu.make_async_copy(velocity_hbm, velocity_ref, sem)
    load.start()
    _, nz, ny, _ = stress_ref.shape
    tiles = ny // SUB

    def along(k):
        for t in range(tiles):
            for c, comp in enumerate((0, 3, 4)):
                along_ref[c, k, tile_rows(t), :] = periodic_x(stress_ref[comp, k, tile_rows(t), :])

    for k in (0, 1, nz - 2, nz - 1):
        along(k)

    @pl.loop(2, nz - 2)
    def _(k):
        along(k)
        inner_depth(stress_ref, depth_ref, 6, k, tiles)

    load.wait()


def plane_kernel(sizes, stress_ref, along_ref, y1_ref, y2_ref, plane_ref, tall):
    _, nz, ny, nx = stress_ref.shape
    tiles = ny // SUB
    of_y = (3, 1, 5)
    fill_rows(sizes[1], tall, lambda c, k: stress_ref[of_y[c], k], y1_ref, y2_ref, nz, ny, range(nz))

    @pl.loop(0, nz)
    def _(k):
        for t in range(tiles):
            for c in range(3):
                plane_ref[c, k, tile_rows(t), :] = along_ref[
                    c, k, tile_rows(t), :
                ] + row_difference(tall, c, k, t)


def velocity_kernel(
    sizes, velocity_ref, stress_ref, cells_ref, inner_ref, plane_ref, factor_ref, mz_ref, slope_ref,
    x1_ref, x2_ref, z1_ref, z2_ref, low_ref, high_ref, out_ref, vlow_ref, vhigh_ref, vx1_ref, vx2_ref, vz1_ref, vz2_ref,
    *rest,
):
    *vy_refs, edge, zb, za, outer_ref = rest
    _, nz, ny, nx = velocity_ref.shape
    tiles = ny // SUB
    lane = lanes_of((SUB, nx))
    fill_edges(sizes[0], edge, x1_ref, x2_ref, low_ref, high_ref)
    depth_halos(sizes[2], zb, za, z1_ref, z2_ref)
    outer_depth(stress_ref, zb, za, outer_ref, 6, nz, tiles)

    def layer(k, depth_ref, spot):
        for t in range(tiles):
            rows = tile_rows(t)
            b = cells_ref[0, k, rows, :]
            factor = factor_ref[k, rows, :]
            mz = mz_ref[k, rows, :]
            mx = slope_ref[0, rows, :] * factor
            my = slope_ref[1, rows, :] * factor
            gk = [depth_ref[c, spot, rows, :] for c in range(6)]
            beside = [
                plane_ref[c, k, rows, :]
                + jnp.where(sides(lane), turned_left(edge[c, t % 2], k * tiles + t), 0.0)
                for c in range(3)
            ]
            accel = (
                beside[0] - mx * gk[0] - my * gk[3] + mz * gk[4],
                beside[1] - mx * gk[3] - my * gk[1] + mz * gk[5],
                beside[2] - mx * gk[4] - my * gk[5] + mz * gk[2],
            )
            for c in range(3):
                out_ref[c, k, rows, :] = velocity_ref[c, k, rows, :] + b * accel[c]

    for spot, k in enumerate((0, 1, nz - 2, nz - 1)):
        layer(k, outer_ref, spot)

    @pl.loop(2, nz - 2)
    def _(k):
        layer(k, inner_ref, k - 2)

    pack_sides(
        lambda c, k, t: out_ref[c, k, tile_rows(t), :], nz, ny, nx, vlow_ref, vhigh_ref, vx1_ref, vx2_ref
    )
    pack_rows(lambda c, k, rows: out_ref[c, k, rows, :], nz, ny, vy_refs)
    vz1_ref[...], vz2_ref[...] = order("gz", out_ref[:, nz - 2 : nz], out_ref[:, 0:2])


def velocity_inner_kernel(vel_ref, vel_hbm, depth_ref, along_ref, sem):
    store = pltpu.make_async_copy(vel_ref, vel_hbm, sem)
    store.start()
    _, nz, ny, nx = vel_ref.shape
    tiles = ny // SUB

    def along(k):
        for t in range(tiles):
            for c in range(3):
                along_ref[c, k, tile_rows(t), :] = periodic_x(vel_ref[c, k, tile_rows(t), :])

    for k in (0, 1, nz - 2, nz - 1):
        along(k)

    @pl.loop(2, nz - 2)
    def _(k):
        along(k)
        inner_depth(vel_ref, depth_ref, 3, k, tiles)

    store.wait()


def stress_kernel(
    sizes, vel_ref, stress_ref, memory_ref, cells_ref, inner_ref, along_ref, factor_ref, mz_ref, slope_ref,
    x1_ref, x2_ref, low_ref, high_ref, y1_ref, y2_ref, z1_ref, z2_ref,
    stress_hbm, memory_hbm, edge, tall, zb, za, outer, stress_out, memory_out, sems,
):
    n_gx, n_gy, n_gz = sizes
    _, nz, ny, nx = vel_ref.shape
    tiles = ny // SUB
    lane = lanes_of((SUB, nx))
    fill_edges(n_gx, edge, x1_ref, x2_ref, low_ref, high_ref)
    fill_rows(n_gy, tall, lambda c, k: vel_ref[c, k], y1_ref, y2_ref, nz, ny, range(nz))

    def layer(k, depth_ref, spot):
        for t in range(tiles):
            rows = tile_rows(t)
            factor = factor_ref[k, rows, :]
            mz = mz_ref[k, rows, :]
            mx = slope_ref[0, rows, :] * factor
            my = slope_ref[1, rows, :] * factor
            dk = [depth_ref[c, spot, rows, :] for c in range(3)]
            dx = [
                along_ref[c, k, rows, :]
                + jnp.where(sides(lane), turned_left(edge[c, t % 2], k * tiles + t), 0.0)
                - mx * dk[c]
                for c in range(3)
            ]
            dy = [row_difference(tall, c, k, t) - my * dk[c] for c in range(3)]
            dz = [mz * dk[c] for c in range(3)]
            lam, mu, keep, gain = (cells_ref[i, k, rows, :] for i in range(1, 5))
            volume = lam * (dx[0] + dy[1] + dz[2])
            mu2 = mu + mu
            rates = (
                volume + mu2 * dx[0],
                volume + mu2 * dy[1],
                volume + mu2 * dz[2],
                mu * (dy[0] + dx[1]),
                mu * (dz[0] + dx[2]),
                mu * (dz[1] + dy[2]),
            )
            for c in range(6):
                kept = keep * memory_ref[c, k, rows, :] + gain * rates[c]
                memory_out[c, k, rows, :] = kept
                stress_out[c, k, rows, :] = stress_ref[c, k, rows, :] + step_size * (
                    rates[c] - kept
                )

    def out_copies(first, count, spot):
        layers = pl.ds(first, count)
        return [
            pltpu.make_async_copy(a.at[:, layers], b.at[:, layers], sems.at[i, spot])
            for i, (a, b) in enumerate(((stress_out, stress_hbm), (memory_out, memory_hbm)))
        ]

    inner = nz - 4
    step = next(d for d in (4, 3, 2, 1) if inner % d == 0)
    chunks = inner // step

    @pl.loop(0, chunks)
    def _(j):
        @pl.loop(0, step)
        def _(i):
            k = 2 + j * step + i
            layer(k, inner_ref, k - 2)

        for copy in out_copies(2 + j * step, step, 2 + j):
            copy.start()

    depth_halos(n_gz, zb, za, z1_ref, z2_ref)
    outer_depth(vel_ref, zb, za, outer, 3, nz, tiles)
    last = []
    for spot, k in enumerate((0, 1, nz - 2, nz - 1)):
        layer(k, outer, spot)
        if spot % 2 == 1:
            last += out_copies(k - 1, 2, spot // 2)
            for copy in last[-2:]:
                copy.start()

    @pl.loop(0, chunks)
    def _(j):
        for copy in out_copies(2 + j * step, step, 2 + j):
            copy.wait()

    for copy in last:
        copy.wait()


def in_hbm(value):
    return pltpu.with_memory_space_constraint(value, pltpu.HBM)


def call(kernel, outs, in_specs, scratch=(), name=None, out_specs=None, aliases=None):
    return pl.pallas_call(
        kernel,
        out_shape=[jax.ShapeDtypeStruct(s, F32) for s in outs],
        in_specs=in_specs,
        out_specs=out_specs or [VM] * len(outs),
        scratch_shapes=list(scratch),
        compiler_params=params(),
        input_output_aliases=aliases or {},
        name=name,
    )


def local(
    sizes, elevation, layer_base, stretch, material, buoyancy, lame_lambda, shear_modulus,
    relax_time, anelastic_weight, velocity, stress, memory,
):
    n_gx, n_gy, n_gz = counts = tuple(sizes[a] for a in ("gx", "gy", "gz"))
    _, nz, ny, nx = velocity.shape
    rows = ny + SUB
    slab = call(
        terrain_piece_kernel,
        [(rows, nx)],
        [HB] * 3,
        [
            pltpu.VMEM(elevation.shape, jnp.int32),
            pltpu.VMEM((1, nz), F32),
            pltpu.VMEM((1, nz), F32),
            DMA((3,)),
        ],
        name="terrain_piece",
    )(in_hbm(elevation), in_hbm(layer_base[None]), in_hbm(stretch[None]))[0]
    tied = lax.optimization_barrier
    faces = 2 * 3 * nz
    xs = 3 * SUB
    y_rounds = min(2, n_gy - 1) if n_gy > 1 else 1
    z_face = (6, 2, ny, nx)
    slab, material = tied((slab, material))
    tables = (buoyancy, lame_lambda, shear_modulus, relax_time, anelastic_weight)
    cells = call(
        cell_kernel,
        [(5, nz, ny, nx)],
        [HB] * 6,
        [pltpu.VMEM(material.shape, jnp.int32)]
        + [pltpu.VMEM((1, table.shape[0]), F32) for table in tables]
        + [DMA((6,))],
        name="cells",
    )(in_hbm(material), *[in_hbm(table[None]) for table in tables])[0]
    if n_gz & (n_gz - 1):
        slab = lax.psum(slab, "gz")
        slab, stress = tied((slab, stress))
    else:
        bit = 1
        while bit < n_gz:
            slab = slab + lax.ppermute(slab, "gz", [(i, i ^ bit) for i in range(n_gz)])
            if bit == 1:
                slab, stress, cells = tied((slab, stress, cells))
            bit *= 2
    stress_vm, low, high, x1, x2, z1, z2, *ys = call(
        pack_kernel,
        [stress.shape] + [(xs, nx)] * 4 + [z_face] * 2 + [(faces, nx)] * y_rounds,
        [HB],
        [DMA((8,))],
        name="pack_stress",
    )(in_hbm(stress))
    ys = call(
        functools.partial(y_send_kernel, y_rounds),
        [(faces + SUB, nx)] * y_rounds,
        [VM] * (1 + y_rounds),
        name="y_send",
    )(slab, *ys)
    ys, velocity = tied((ys, velocity))
    y1, y2 = exchange(sizes, "gy", ys[0], ys[-1])
    inner_k, along, velocity_vm = call(
        depth_kernel,
        [(6, nz - 4, ny, nx), velocity.shape, velocity.shape],
        [VM, HB],
        [DMA],
        name="depth",
    )(stress_vm, in_hbm(velocity))
    x1, x2, inner_k = tied((x1, x2, inner_k))
    terrain, x1, x2 = call(
        functools.partial(x_send_kernel, n_gy),
        [(ny + 2 * PAD, nx)] + [(xs + SUB, nx)] * 2,
        [VM] * 5,
        name="x_send",
    )(slab, y1[faces:], y2[faces:], x1, x2)
    x1, x2, z1, z2 = tied((x1, x2, z1, z2))
    x1, x2 = exchange(sizes, "gx", x1, x2)
    z1, z2 = exchange(sizes, "gz", z1, z2)
    edge = pltpu.VMEM((3, 2, SUB, nx), F32)
    tall = pltpu.VMEM((3, nz, ny + 2 * PAD, nx), F32)

    def depth(comps):
        return [pltpu.VMEM((comps, 2, ny, nx), F32)] * 2

    plane = call(
        functools.partial(plane_kernel, counts), [velocity.shape], [VM] * 4, [tall], name="planes"
    )(stress_vm, along, y1, y2)[0]
    plane, x1, x2 = tied((plane, x1, x2))
    factor, mz, slope = call(
        functools.partial(metric_kernel, counts),
        [(nz, ny, nx), (nz, ny, nx), (2, ny, nx)],
        [SM] + [VM] * 3,
        [pltpu.VMEM((ny + 2 * PAD, nx), F32), pltpu.VMEM((ny + PAD, nx), F32)],
        name="metrics",
    )(slab[ny:], terrain, x1[xs:], x2[xs:])
    vel, vlow, vhigh, vx1, vx2, vz1, vz2, *vys = call(
        functools.partial(velocity_kernel, counts),
        [velocity.shape] + [(xs, nx)] * 4 + [(3, 2, ny, nx)] * 2 + [(faces, nx)] * y_rounds,
        [VM] * 14,
        [edge] + depth(6) + [pltpu.VMEM((6, 4, ny, nx), F32)],
        name="velocity",
    )(velocity_vm, stress_vm, cells, inner_k, plane, factor, mz, slope, x1, x2, z1, z2, low, high)
    vz1, vz2 = exchange(sizes, "gz", vz1, vz2)
    vy1, vy2 = exchange(sizes, "gy", vys[0], vys[-1])
    vx1, vx2 = exchange(sizes, "gx", vx1, vx2)
    vel_next, vel_k, vel_x = call(
        velocity_inner_kernel,
        [velocity.shape, (3, nz - 4, ny, nx), velocity.shape],
        [VM],
        [DMA],
        name="velocity_inner",
        out_specs=[HB, VM, VM],
    )(vel)
    stress_next, memory_next = call(
        functools.partial(stress_kernel, counts),
        [stress.shape, stress.shape],
        [VM] * 17,
        [edge, tall] + depth(3)
        + [pltpu.VMEM((3, 4, ny, nx), F32), pltpu.VMEM(stress.shape, F32), pltpu.VMEM(stress.shape, F32)]
        + [DMA((2, nz))],
        name="stress",
        out_specs=[HB] * 2,
    )(
        vel, stress_vm, memory, cells, vel_k, vel_x, factor, mz, slope, vx1, vx2, vlow, vhigh, vy1, vy2,
        vz1, vz2,
    )
    return vel_next, stress_next, memory_next


def solution(mesh):
    sizes = {a: mesh.shape[a] for a in ("gx", "gy", "gz")}
    field = P(None, "gz", "gy", "gx")
    return jax.shard_map(
        functools.partial(local, sizes),
        mesh=mesh,
        in_specs=(
            P("gy", ("gx", "gz")), P("gz"), P("gz"), P("gz", "gy", "gx"),
            P(), P(), P(), P(), P(), field, field, field,
        ),
        out_specs=(field, field, field),
        check_vma=False,
    )
```

time: 35.5 us -> 32 us (0.901)
  waiting for transfers between devices: 7.91 us -> 2.36 us
  Pallas kernels: 10.1 us -> 14.8 us
  local copies, waits for them, and re-layouts: 3.49 us -> 0.01 us
  starting transfers between devices: 12.9 us -> 13.7 us
    pallas_call x3 -> x8, Pallas kernels: 5.73 us -> 11.2 us  [the longest x1 2.98 us: local(): call(functools.partial(stress_kernel, counts), [stress.shape, stress.shap...]
    ppermute x10, waiting for transfers between devices: 7.07 us -> 2.12 us  [exchange(): lax.ppermute(v, tuple(sizes), r)]
    unnamed x24 -> x2, local copies, waits for them, and re-layouts: 3.48 us -> 0.01 us
    pallas_call x1, Pallas kernels: 3.28 us -> 1.72 us  [local(): call(functools.partial(velocity_kernel, counts), [velocity.shape] + [(xs,...]
    ppermute x10, starting transfers between devices: 9.48 us -> 10.6 us  [exchange(): lax.ppermute(v, tuple(sizes), r)]
    pallas_call x1, Pallas kernels: 0.11 us -> 0.82 us  [local(): call(terrain_piece_kernel, [(rows, nx)], [HB] * 3, [pltpu.VMEM(elevation....]
    ppermute x2, waiting for transfers between devices: 0.85 us -> 0.24 us  [local(): slab = slab + lax.ppermute(slab, 'gz', [(i, i ^ bit) for i in range(n_gz)])]
  transfers between devices with their start and end apart: 12 -> 12, of which waited for: 4 -> 3; matrix products, arithmetic and copies ran while one was open for 0% -> 0% of each run, Pallas kernels for 8% -> 29%
where the time goes in v3:
time: 32 us; the launch traced here: 31.7 us
  Pallas kernels  14.8 us (46%)
  starting transfers between devices  13.7 us (43%)
  waiting for transfers between devices  2.36 us (7%)
  between operations  0.81 us (3%)
    ppermute x10, starting transfers between devices, exchange(): lax.ppermute(v, tuple(sizes), r)  10.6 us
    ppermute x2, starting transfers between devices, local(): slab = slab + lax.ppermute(slab, 'gz', [(i, i ^ bit) for i in range(n_gz)])  3.12 us
    pallas_call x1, Pallas kernels, local(): call(functools.partial(stress_kernel, counts), [stress.shape, stress.shap...  2.98 us
    pallas_call x1, Pallas kernels, local(): call(cell_kernel, [(5, nz, ny, nx)], [HB] * 6, [pltpu.VMEM(material.shape...  2.63 us
    ppermute x10, waiting for transfers between devices, exchange(): lax.ppermute(v, tuple(sizes), r)  2.12 us
    pallas_call x1, Pallas kernels, local(): call(depth_kernel, [(6, nz - 4, ny, nx), velocity.shape, velocity.shape],...  1.82 us
    pallas_call x1, Pallas kernels, local(): call(velocity_inner_kernel, [velocity.shape, (3, nz - 4, ny, nx), velocit...  1.74 us
    pallas_call x1, Pallas kernels, local(): call(functools.partial(velocity_kernel, counts), [velocity.shape] + [(xs,...  1.72 us
  transfers between devices with their start and end apart: 12, of which 3 were waited for; matrix products, arithmetic and copies ran while one was open for 0% of the time, Pallas kernels for 29%

profile of v3, /device:TPU:0, one launch (start us, length us, event | category | flops | bytes accessed | tf_op | source)
XLA Modules:
  0.0 31.7 jit_solution(11444074994793886345)
XLA Ops:
  0.6 0.8 %terrain_piece.1 = f32[40,128]{1,0:T(8,128)S(1)} custom-call(s32[32,32]{1,0:T(8,128)} %elev_hbm.1, f32[1,16]{1,0:T(1,128)} %bitcast.7, f32[1,16]{1,0:T(1,128)} %bitcast.8), custom_call_target="tpu_custom_call" | custom-call | tf_op jit(solution)/shard_map/terrain_piece/pallas_call | solution.py:604
  1.5 0.5 %collective-permute-start = (f32[40,128]{1,0:T(8,128)S(1)}, f32[40,128]{1,0:T(8,128)S(1)}, u32[]{:S(2)}, u32[]{:S(2)}) collective-permute-start(f32[40,128]{1,0:T(8,128)S(1)} %terrain_piece.1), channel_id=1, source_target_pairs={{0,1},{1,0},{2,3},{3,2},{4,5},{5,4},{6,7},{7,6},{8,9},{9,8},{10,11... | collective-permute-start | bytes 61448 | tf_op jit(solution)/shard_map/ppermute | solution.py:638
  2.0 2.6 %cells.1.cells_ref = f32[5,16,32,128]{3,2,1,0:T(8,128)S(1)} custom-call(s32[16,32,128]{2,1,0:T(8,128)} %refs_0_, f32[1,16]{1,0:T(1,128)} %bitcast.9, f32[1,16]{1,0:T(1,128)} %bitcast.10, f32[1,16]{1,0:T(1,128)} %bitcast.11, f32[1,16]{1,0:T(1,128)} %bitcast.12, f32[1,16]{1,0:T(1,128)} %bitcast.13), custom_call_target="tpu_custom_call" | custom-call | tf_op jit(solution)/shard_map/cells/pallas_call | solution.py:623
  4.6 0.0 collective-permute-done
  4.6 2.6 %collective-permute-start.1 = (f32[40,128]{1,0:T(8,128)S(1)}, f32[40,128]{1,0:T(8,128)S(1)}, u32[]{:S(2)}, u32[]{:S(2)}) collective-permute-start(f32[40,128]{1,0:T(8,128)S(1)} %add.6), channel_id=1, source_target_pairs={{0,2},{1,3},{2,0},{3,1},{4,6},{5,7},{6,4},{7,5},{8,10},{9,11},{10,... | collective-permute-start | bytes 61448 | tf_op jit(solution)/shard_map/ppermute | solution.py:638
  7.2 1.5 %pack_stress.1 = (f32[6,16,32,128]{3,2,1,0:T(8,128)S(1)}, f32[24,128]{1,0:T(8,128)S(1)}, f32[24,128]{1,0:T(8,128)S(1)}, f32[24,128]{1,0:T(8,128)S(1)}, f32[24,12...) custom-call(f32[6,16,32,128]{3,2,1,0:T(8,128)} %stress_hbm), custom_call_target="tpu_custom_call" | custom-call | tf_op jit(solution)/shard_map/pack_stress/pallas_call | solution.py:642
  8.8 0.2 collective-permute-done.1
  9.1 2.0 %collective-permute-start.2 = (f32[104,128]{1,0:T(8,128)S(1)}, f32[104,128]{1,0:T(8,128)S(1)}, u32[]{:S(2)}, u32[]{:S(2)}) collective-permute-start(f32[104,128]{1,0:T(8,128)S(1)} %y_send.1), channel_id=1, source_target_pairs={{0,4},{1,5},{2,6},{3,7},{4,0},{5,1},{6,2},{7,3},{8,12},{9,13},{10,... | collective-permute-start | bytes 159752 | tf_op jit(solution)/shard_map/ppermute | solution.py:46
  11.1 1.8 %depth.1 = (f32[6,12,32,128]{3,2,1,0:T(8,128)S(1)}, f32[3,16,32,128]{3,2,1,0:T(8,128)S(1)}, f32[3,16,32,128]{3,2,1,0:T(8,128)S(1)}) custom-call(f32[6,16,32,128]{3,2,1,0:T(8,128)S(1)} %get-tuple-element.53.stress_ref, f32[3,16,32,128]{3,2,1,0:T(8,128)} %velocity_hbm), custom_call_target="tpu_custom_call" | custom-call | tf_op jit(solution)/shard_map/depth/pallas_call | solution.py:657
  12.9 0.3 %collective-permute-done.2.y1_ref.y2_ref = f32[104,128]{1,0:T(8,128)S(1)} collective-permute-done((f32[104,128]{1,0:T(8,128)S(1)}, f32[104,128]{1,0:T(8,128)S(1)}, u32[]{:S(2)}, u32[]{:S(2)}) %collective-permute-start.2) | collective-permute-done | bytes 53280 | tf_op jit(solution)/shard_map/ppermute | solution.py:46
  13.3 0.1 x_send.1
  13.4 0.1 collective-permute-start.5
  13.4 2.0 %collective-permute-start.6 = (f32[6,2,32,128]{3,2,1,0:T(8,128)S(1)}, f32[6,2,32,128]{3,2,1,0:T(8,128)S(1)}, u32[]{:S(2)}, u32[]{:S(2)}) collective-permute-start(f32[6,2,32,128]{3,2,1,0:T(8,128)S(1)} %get-tuple-element.81), channel_id=1, source_target_pairs={{0,4},{1,2},{2,1},{3,7},{4,0},{5,6},{6,5},{7,3},{8,12},{9,10},{10,... | collective-permute-start | bytes 589832 | tf_op jit(solution)/shard_map/ppermute | solution.py:46
  15.4 1.6 %collective-permute-start.3 = (f32[32,128]{1,0:T(8,128)S(1)}, f32[32,128]{1,0:T(8,128)S(1)}, u32[]{:S(2)}, u32[]{:S(2)}) collective-permute-start(f32[32,128]{1,0:T(8,128)S(1)} %get-tuple-element.71), channel_id=1, source_target_pairs={{0,8},{1,9},{2,10},{3,11},{4,12},{5,13},{6,14},{7,15},{8,0},{9,1},... | collective-permute-start | bytes 49160 | tf_op jit(solution)/shard_map/ppermute | solution.py:46
  17.0 0.0 collective-permute-start.4
  17.0 0.4 %planes.1.plane_ref = f32[3,16,32,128]{3,2,1,0:T(8,128)S(1)} custom-call(f32[6,16,32,128]{3,2,1,0:T(8,128)S(1)} %get-tuple-element.53.stress_ref, f32[3,16,32,128]{3,2,1,0:T(8,128)S(1)} %get-tuple-element.63.along_ref, f32[104,128]{1,0:T(8,128)S(1)} %collective-permute-done.2.y1_ref.y2_ref, f32[104,128]{1,0:T(8,128)S(1)} %collective-permute-done.2.y1_ref.y2_ref), custom_call_target="tpu_custom_call" | custom-call | tf_op jit(solution)/shard_map/planes/pallas_call | solution.py:680
  17.4 1.8 %collective-permute-done.3.x1_ref = f32[32,128]{1,0:T(8,128)S(1)} collective-permute-done((f32[32,128]{1,0:T(8,128)S(1)}, f32[32,128]{1,0:T(8,128)S(1)}, u32[]{:S(2)}, u32[]{:S(2)}) %collective-permute-start.3) | collective-permute-done | bytes 16416 | tf_op jit(solution)/shard_map/ppermute | solution.py:46
  19.2 0.0 collective-permute-done.4.x2_ref
  19.2 1.0 %metrics.1 = (f32[16,32,128]{2,1,0:T(8,128)S(1)}, f32[16,32,128]{2,1,0:T(8,128)S(1)}, f32[2,32,128]{2,1,0:T(8,128)S(1)}) custom-call(f32[8,128]{1,0:T(8,128)S(1)} %slice.18.layers_ref, f32[48,128]{1,0:T(8,128)S(1)} %get-tuple-element.74.own, f32[8,128]{1,0:T(8,128)S(1)} %slice.15.x1_ref, f32[8,128]{1,0:T(8,128)S(1)} %slice.16.x2_ref), custom_call_target="tpu_custom_call" | custom-call | tf_op jit(solution)/shard_map/metrics/pallas_call | solution.py:684
  20.2 0.0 collective-permute-done.5.z1_ref
  20.2 0.0 collective-permute-done.6.z2_ref
  20.2 0.0 copy-start
  20.3 1.7 %velocity.1 = (f32[3,16,32,128]{3,2,1,0:T(8,128)S(1)}, f32[24,128]{1,0:T(8,128)S(1)}, f32[24,128]{1,0:T(8,128)S(1)}, f32[24,128]{1,0:T(8,128)S(1)}, f32[24,128]{...) custom-call(f32[3,16,32,128]{3,2,1,0:T(8,128)S(1)} %get-tuple-element.57.veloc, ...), custom_call_target="tpu_custom_call" | custom-call | tf_op jit(solution)/shard_map/velocity/pallas_call | solution.py:691
  22.0 0.1 collective-permute-start.10
  22.1 1.0 %collective-permute-start.11 = (f32[3,2,32,128]{3,2,1,0:T(8,128)S(1)}, f32[3,2,32,128]{3,2,1,0:T(8,128)S(1)}, u32[]{:S(2)}, u32[]{:S(2)}) collective-permute-start(f32[3,2,32,128]{3,2,1,0:T(8,128)S(1)} %get-tuple-element.94), channel_id=1, source_target_pairs={{0,4},{1,2},{2,1},{3,7},{4,0},{5,6},{6,5},{7,3},{8,12},{9,10},{10,... | collective-permute-start | bytes 294920 | tf_op jit(solution)/shard_map/ppermute | solution.py:46
  23.0 1.1 %collective-permute-start.9 = (f32[96,128]{1,0:T(8,128)S(1)}, f32[96,128]{1,0:T(8,128)S(1)}, u32[]{:S(2)}, u32[]{:S(2)}) collective-permute-start(f32[96,128]{1,0:T(8,128)S(1)} %get-tuple-element.92), channel_id=1, source_target_pairs={{0,4},{1,5},{2,6},{3,7},{4,0},{5,1},{6,2},{7,3},{8,12},{9,13},{10,... | collective-permute-start | bytes 147464 | tf_op jit(solution)/shard_map/ppermute | solution.py:46
  24.2 2.7 %collective-permute-start.7 = (f32[24,128]{1,0:T(8,128)S(1)}, f32[24,128]{1,0:T(8,128)S(1)}, u32[]{:S(2)}, u32[]{:S(2)}) collective-permute-start(f32[24,128]{1,0:T(8,128)S(1)} %get-tuple-element.88), channel_id=1, source_target_pairs={{0,8},{1,9},{2,10},{3,11},{4,12},{5,13},{6,14},{7,15},{8,0},{9,1},... | collective-permute-start | bytes 36872 | tf_op jit(solution)/shard_map/ppermute | solution.py:46
  26.9 0.0 collective-permute-start.8
  26.9 1.7 %velocity_inner.1 = (f32[3,16,32,128]{3,2,1,0:T(8,128)}, f32[3,12,32,128]{3,2,1,0:T(8,128)S(1)}, f32[3,16,32,128]{3,2,1,0:T(8,128)S(1)}) custom-call(f32[3,16,32,128]{3,2,1,0:T(8,128)S(1)} %get-tuple-element.84.vel_ref), custom_call_target="tpu_custom_call" | custom-call | tf_op jit(solution)/shard_map/velocity_inner/pallas_call | solution.py:701
  28.6 0.0 collective-permute-done.7.x1_ref
  28.6 0.0 collective-permute-done.8.x2_ref
  28.6 0.0 collective-permute-done.9.y1_ref.y2_ref
  28.6 0.0 collective-permute-done.10.z1_ref
  28.6 0.0 collective-permute-done.11.z2_ref
  28.7 0.0 copy-done
  28.7 3.0 %stress.1 = (f32[6,16,32,128]{3,2,1,0:T(8,128)}, f32[6,16,32,128]{3,2,1,0:T(8,128)}) custom-call(f32[3,16,32,128]{3,2,1,0:T(8,128)S(1)} %get-tuple-element.84.vel_ref, f32[6,16,32,128]{3,2,1,0:T(8,128)S(1)} %get-tuple-element.53.stress_ref, f32[6,16,32,128]{3,2,1,0:T(8,128)S(1)} %copy-done, f32[5,16,32,128]{3,2,1,0:T(8,128)S(1)} %cells.1.cells_ref, ...), custom_call_target="tpu_custom_call" | custom-call | tf_op jit(solution)/shard_map/stress/pallas_call | solution.py:709
  (7 shorter events, 0.0 us)
Async XLA Ops:
  1.5 3.2 %collective-permute-start = (f32[40,128]{1,0:T(8,128)S(1)}, f32[40,128]{1,0:T(8,128)S(1)}, u32[]{:S(2)}, u32[]{:S(2)}) collective-permute-start(f32[40,128]{1,0:T(8,128)S(1)} %terrain_piece.1), channel_id=1, source_target_pairs={{0,1},{1,0},{2,3},{3,2},{4,5},{5,4},{6,7},{7,6},{8,9},{9,8},{10,11... | collective-permute-start | bytes 61448 | tf_op jit(solution)/shard_map/ppermute | solution.py:638
  4.6 4.4 %collective-permute-start.1 = (f32[40,128]{1,0:T(8,128)S(1)}, f32[40,128]{1,0:T(8,128)S(1)}, u32[]{:S(2)}, u32[]{:S(2)}) collective-permute-start(f32[40,128]{1,0:T(8,128)S(1)} %add.6), channel_id=1, source_target_pairs={{0,2},{1,3},{2,0},{3,1},{4,6},{5,7},{6,4},{7,5},{8,10},{9,11},{10,... | collective-permute-start | bytes 61448 | tf_op jit(solution)/shard_map/ppermute | solution.py:638
  9.1 4.2 %collective-permute-start.2 = (f32[104,128]{1,0:T(8,128)S(1)}, f32[104,128]{1,0:T(8,128)S(1)}, u32[]{:S(2)}, u32[]{:S(2)}) collective-permute-start(f32[104,128]{1,0:T(8,128)S(1)} %y_send.1), channel_id=1, source_target_pairs={{0,4},{1,5},{2,6},{3,7},{4,0},{5,1},{6,2},{7,3},{8,12},{9,13},{10,... | collective-permute-start | bytes 159752 | tf_op jit(solution)/shard_map/ppermute | solution.py:46
  13.4 6.9 %collective-permute-start.5 = (f32[6,2,32,128]{3,2,1,0:T(8,128)S(1)}, f32[6,2,32,128]{3,2,1,0:T(8,128)S(1)}, u32[]{:S(2)}, u32[]{:S(2)}) collective-permute-start(f32[6,2,32,128]{3,2,1,0:T(8,128)S(1)} %get-tuple-element.80), channel_id=1, source_target_pairs={{0,1},{1,0},{2,3},{3,2},{4,5},{5,4},{6,7},{7,6},{8,9},{9,8},{10,11... | collective-permute-start | bytes 589832 | tf_op jit(solution)/shard_map/ppermute | solution.py:46
  13.4 6.8 %collective-permute-start.6 = (f32[6,2,32,128]{3,2,1,0:T(8,128)S(1)}, f32[6,2,32,128]{3,2,1,0:T(8,128)S(1)}, u32[]{:S(2)}, u32[]{:S(2)}) collective-permute-start(f32[6,2,32,128]{3,2,1,0:T(8,128)S(1)} %get-tuple-element.81), channel_id=1, source_target_pairs={{0,4},{1,2},{2,1},{3,7},{4,0},{5,6},{6,5},{7,3},{8,12},{9,10},{10,... | collective-permute-start | bytes 589832 | tf_op jit(solution)/shard_map/ppermute | solution.py:46
  15.4 3.7 %collective-permute-start.3 = (f32[32,128]{1,0:T(8,128)S(1)}, f32[32,128]{1,0:T(8,128)S(1)}, u32[]{:S(2)}, u32[]{:S(2)}) collective-permute-start(f32[32,128]{1,0:T(8,128)S(1)} %get-tuple-element.71), channel_id=1, source_target_pairs={{0,8},{1,9},{2,10},{3,11},{4,12},{5,13},{6,14},{7,15},{8,0},{9,1},... | collective-permute-start | bytes 49160 | tf_op jit(solution)/shard_map/ppermute | solution.py:46
  17.0 2.2 %collective-permute-start.4 = (f32[32,128]{1,0:T(8,128)S(1)}, f32[32,128]{1,0:T(8,128)S(1)}, u32[]{:S(2)}, u32[]{:S(2)}) collective-permute-start(f32[32,128]{1,0:T(8,128)S(1)} %get-tuple-element.72), channel_id=1, source_target_pairs={{0,1},{1,0},{2,3},{3,2},{4,5},{5,4},{6,7},{7,6},{8,16},{9,17},{10,... | collective-permute-start | bytes 49160 | tf_op jit(solution)/shard_map/ppermute | solution.py:46
  20.2 8.4 %copy-start = (f32[6,16,32,128]{3,2,1,0:T(8,128)S(1)}, f32[6,16,32,128]{3,2,1,0:T(8,128)}, u32[]{:S(2)}) copy-start(f32[6,16,32,128]{3,2,1,0:T(8,128)} %memory_ref.1) | copy-start | bytes 4718596
  22.0 6.7 %collective-permute-start.10 = (f32[3,2,32,128]{3,2,1,0:T(8,128)S(1)}, f32[3,2,32,128]{3,2,1,0:T(8,128)S(1)}, u32[]{:S(2)}, u32[]{:S(2)}) collective-permute-start(f32[3,2,32,128]{3,2,1,0:T(8,128)S(1)} %get-tuple-element.93), channel_id=1, source_target_pairs={{0,1},{1,0},{2,3},{3,2},{4,5},{5,4},{6,7},{7,6},{8,9},{9,8},{10,11... | collective-permute-start | bytes 294920 | tf_op jit(solution)/shard_map/ppermute | solution.py:46
  22.1 6.6 %collective-permute-start.11 = (f32[3,2,32,128]{3,2,1,0:T(8,128)S(1)}, f32[3,2,32,128]{3,2,1,0:T(8,128)S(1)}, u32[]{:S(2)}, u32[]{:S(2)}) collective-permute-start(f32[3,2,32,128]{3,2,1,0:T(8,128)S(1)} %get-tuple-element.94), channel_id=1, source_target_pairs={{0,4},{1,2},{2,1},{3,7},{4,0},{5,6},{6,5},{7,3},{8,12},{9,10},{10,... | collective-permute-start | bytes 294920 | tf_op jit(solution)/shard_map/ppermute | solution.py:46
  23.0 5.6 %collective-permute-start.9 = (f32[96,128]{1,0:T(8,128)S(1)}, f32[96,128]{1,0:T(8,128)S(1)}, u32[]{:S(2)}, u32[]{:S(2)}) collective-permute-start(f32[96,128]{1,0:T(8,128)S(1)} %get-tuple-element.92), channel_id=1, source_target_pairs={{0,4},{1,5},{2,6},{3,7},{4,0},{5,1},{6,2},{7,3},{8,12},{9,13},{10,... | collective-permute-start | bytes 147464 | tf_op jit(solution)/shard_map/ppermute | solution.py:46
  24.2 4.5 %collective-permute-start.7 = (f32[24,128]{1,0:T(8,128)S(1)}, f32[24,128]{1,0:T(8,128)S(1)}, u32[]{:S(2)}, u32[]{:S(2)}) collective-permute-start(f32[24,128]{1,0:T(8,128)S(1)} %get-tuple-element.88), channel_id=1, source_target_pairs={{0,8},{1,9},{2,10},{3,11},{4,12},{5,13},{6,14},{7,15},{8,0},{9,1},... | collective-permute-start | bytes 36872 | tf_op jit(solution)/shard_map/ppermute | solution.py:46
  26.9 1.8 %collective-permute-start.8 = (f32[24,128]{1,0:T(8,128)S(1)}, f32[24,128]{1,0:T(8,128)S(1)}, u32[]{:S(2)}, u32[]{:S(2)}) collective-permute-start(f32[24,128]{1,0:T(8,128)S(1)} %get-tuple-element.89), channel_id=1, source_target_pairs={{0,1},{1,0},{2,3},{3,2},{4,5},{5,4},{6,7},{7,6},{8,16},{9,17},{10,... | collective-permute-start | bytes 36872 | tf_op jit(solution)/shard_map/ppermute | solution.py:46

commit v4 on v3

--- a/solution.py
+++ b/solution.py
@@ -326,6 +326,16 @@
     za[...] = from_after("gz", n_gz, got)
 
 
+def over(low, high, most, body):
+    count = high - low
+    group = next(d for d in range(most, 0, -1) if count % d == 0)
+
+    @pl.loop(0, count // group)
+    def _(j):
+        for i in range(group):
+            body(low + j * group + i)
+
+
 def tile_rows(t):
     return slice(SUB * t, SUB * t + SUB)
 
@@ -375,12 +385,13 @@
         nx,
     )
 
-    @pl.loop(0, nz)
-    def _(k):
+    def layer(k):
         for t in range(ny // SUB):
             kind = material_ref[k, tile_rows(t), :]
             for i, table in enumerate(tables):
                 cells_ref[i, k, tile_rows(t), :] = lookup(table, kind)
+
+    over(0, nz, 4, layer)
 
 
 def depth_kernel(stress_ref, velocity_hbm, depth_ref, along_ref, velocity_ref, sem):
@@ -394,14 +405,8 @@
             for c, comp in enumerate((0, 3, 4)):
                 along_ref[c, k, tile_rows(t), :] = periodic_x(stress_ref[comp, k, tile_rows(t), :])
 
-    for k in (0, 1, nz - 2, nz - 1):
-        along(k)
-
-    @pl.loop(2, nz - 2)
-    def _(k):
-        along(k)
-        inner_depth(stress_ref, depth_ref, 6, k, tiles)
-
+    over(0, nz, 4, along)
+    over(2, nz - 2, 4, lambda k: inner_depth(stress_ref, depth_ref, 6, k, tiles))
     load.wait()
 
 
@@ -411,13 +416,14 @@
     of_y = (3, 1, 5)
     fill_rows(sizes[1], tall, lambda c, k: stress_ref[of_y[c], k], y1_ref, y2_ref, nz, ny, range(nz))
 
-    @pl.loop(0, nz)
-    def _(k):
+    def layer(k):
         for t in range(tiles):
             for c in range(3):
                 plane_ref[c, k, tile_rows(t), :] = along_ref[
                     c, k, tile_rows(t), :
                 ] + row_difference(tall, c, k, t)
+
+    over(0, nz, 4, layer)
 
 
 def velocity_kernel(
@@ -458,10 +464,7 @@
     for spot, k in enumerate((0, 1, nz - 2, nz - 1)):
         layer(k, outer_ref, spot)
 
-    @pl.loop(2, nz - 2)
-    def _(k):
-        layer(k, inner_ref, k - 2)
-
+    over(2, nz - 2, 4, lambda k: layer(k, inner_ref, k - 2))
     pack_sides(
         lambda c, k, t: out_ref[c, k, tile_rows(t), :], nz, ny, nx, vlow_ref, vhigh_ref, vx1_ref, vx2_ref
     )
@@ -480,14 +483,8 @@
             for c in range(3):
                 along_ref[c, k, tile_rows(t), :] = periodic_x(vel_ref[c, k, tile_rows(t), :])
 
-    for k in (0, 1, nz - 2, nz - 1):
-        along(k)
-
-    @pl.loop(2, nz - 2)
-    def _(k):
-        along(k)
-        inner_depth(vel_ref, depth_ref, 3, k, tiles)
-
+    over(0, nz, 4, along)
+    over(2, nz - 2, 4, lambda k: inner_depth(vel_ref, depth_ref, 3, k, tiles))
     store.wait()
 
 
@@ -550,8 +547,7 @@
 
     @pl.loop(0, chunks)
     def _(j):
-        @pl.loop(0, step)
-        def _(i):
+        for i in range(step):
             k = 2 + j * step + i
             layer(k, inner_ref, k - 2)
 
@@ -581,7 +577,7 @@
     return pltpu.with_memory_space_constraint(value, pltpu.HBM)
 
 
-def call(kernel, outs, in_specs, scratch=(), name=None, out_specs=None, aliases=None):
+def call(kernel, outs, in_specs, scratch=(), name=None, out_specs=None, cost=0.0):
     return pl.pallas_call(
         kernel,
         out_shape=[jax.ShapeDtypeStruct(s, F32) for s in outs],
@@ -589,7 +585,7 @@
         out_specs=out_specs or [VM] * len(outs),
         scratch_shapes=list(scratch),
         compiler_params=params(),
-        input_output_aliases=aliases or {},
+        cost_estimate=pl.CostEstimate(flops=int(cost * 1e9), transcendentals=0, bytes_accessed=int(cost * 3.5e6)),
         name=name,
     )
 
@@ -611,14 +607,61 @@
             pltpu.VMEM((1, nz), F32),
             DMA((3,)),
         ],
-        name="terrain_piece",
+        name="terrain_piece", cost=0.8,
     )(in_hbm(elevation), in_hbm(layer_base[None]), in_hbm(stretch[None]))[0]
     tied = lax.optimization_barrier
     faces = 2 * 3 * nz
     xs = 3 * SUB
     y_rounds = min(2, n_gy - 1) if n_gy > 1 else 1
     z_face = (6, 2, ny, nx)
-    slab, material = tied((slab, material))
+    slab, stress = tied((slab, stress))
+    stress_vm, low, high, x1, x2, z1, z2, *ys = call(
+        pack_kernel,
+        [stress.shape] + [(xs, nx)] * 4 + [z_face] * 2 + [(faces, nx)] * y_rounds,
+        [HB],
+        [DMA((8,))],
+        name="pack_stress", cost=1.5,
+    )(in_hbm(stress))
+    if n_gz & (n_gz - 1):
+        slab = lax.psum(slab, "gz")
+    else:
+        bit = 1
+        while bit < n_gz:
+            slab = slab + lax.ppermute(slab, "gz", [(i, i ^ bit) for i in range(n_gz)])
+            if bit == 1:
+                slab, z1, z2 = tied((slab, z1, z2))
+            bit *= 2
+    z1, z2 = exchange(sizes, "gz", z1, z2)
+    ys = call(
+        functools.partial(y_send_kernel, y_rounds),
+        [(faces + SUB, nx)] * y_rounds,
+        [VM] * (1 + y_rounds),
+        name="y_send", cost=0.02,
+    )(slab, *ys)
+    ys, stress_vm = tied((ys, stress_vm))
+    y1, y2 = exchange(sizes, "gy", ys[0], ys[-1])
+    inner_k, along, velocity_vm = call(
+        depth_kernel,
+        [(6, nz - 4, ny, nx), velocity.shape, velocity.shape],
+        [VM, HB],
+        [DMA],
+        name="depth", cost=1.0,
+    )(stress_vm, in_hbm(velocity))
+    x1, x2, inner_k = tied((x1, x2, inner_k))
+    terrain, x1, x2 = call(
+        functools.partial(x_send_kernel, n_gy),
+        [(ny + 2 * PAD, nx)] + [(xs + SUB, nx)] * 2,
+        [VM] * 5,
+        name="x_send", cost=0.1,
+    )(slab, y1[faces:], y2[faces:], x1, x2)
+    x1, x2, material = tied((x1, x2, material))
+    x1, x2 = exchange(sizes, "gx", x1, x2)
+    edge = pltpu.VMEM((3, 2, SUB, nx), F32)
+    tall = pltpu.VMEM((3, nz, ny + 2 * PAD, nx), F32)
+
+    def depth(comps):
+        return [pltpu.VMEM((comps, 2, ny, nx), F32)] * 2
+
     tables = (buoyancy, lame_lambda, shear_modulus, relax_time, anelastic_weight)
     cells = call(
         cell_kernel,
@@ -627,73 +670,25 @@
         [pltpu.VMEM(material.shape, jnp.int32)]
         + [pltpu.VMEM((1, table.shape[0]), F32) for table in tables]
         + [DMA((6,))],
-        name="cells",
+        name="cells", cost=1.2,
     )(in_hbm(material), *[in_hbm(table[None]) for table in tables])[0]
-    if n_gz & (n_gz - 1):
-        slab = lax.psum(slab, "gz")
-        slab, stress = tied((slab, stress))
-    else:
-        bit = 1
-        while bit < n_gz:
-            slab = slab + lax.ppermute(slab, "gz", [(i, i ^ bit) for i in range(n_gz)])
-            if bit == 1:
-                slab, stress, cells = tied((slab, stress, cells))
-            bit *= 2
-    stress_vm, low, high, x1, x2, z1, z2, *ys = call(
-        pack_kernel,
-        [stress.shape] + [(xs, nx)] * 4 + [z_face] * 2 + [(faces, nx)] * y_rounds,
-        [HB],
-        [DMA((8,))],
-        name="pack_stress",
-    )(in_hbm(stress))
-    ys = call(
-        functools.partial(y_send_kernel, y_rounds),
-        [(faces + SUB, nx)] * y_rounds,
-        [VM] * (1 + y_rounds),
-        name="y_send",
-    )(slab, *ys)
-    ys, velocity = tied((ys, velocity))
-    y1, y2 = exchange(sizes, "gy", ys[0], ys[-1])
-    inner_k, along, velocity_vm = call(
-        depth_kernel,
-        [(6, nz - 4, ny, nx), velocity.shape, velocity.shape],
-        [VM, HB],
-        [DMA],
-        name="depth",
-    )(stress_vm, in_hbm(velocity))
-    x1, x2, inner_k = tied((x1, x2, inner_k))
-    terrain, x1, x2 = call(
-        functools.partial(x_send_kernel, n_gy),
-        [(ny + 2 * PAD, nx)] + [(xs + SUB, nx)] * 2,
-        [VM] * 5,
-        name="x_send",
-    )(slab, y1[faces:], y2[faces:], x1, x2)
-    x1, x2, z1, z2 = tied((x1, x2, z1, z2))
-    x1, x2 = exchange(sizes, "gx", x1, x2)
-    z1, z2 = exchange(sizes, "gz", z1, z2)
-    edge = pltpu.VMEM((3, 2, SUB, nx), F32)
-    tall = pltpu.VMEM((3, nz, ny + 2 * PAD, nx), F32)
-
-    def depth(comps):
-        return [pltpu.VMEM((comps, 2, ny, nx), F32)] * 2
-
     plane = call(
-        functools.partial(plane_kernel, counts), [velocity.shape], [VM] * 4, [tall], name="planes"
+        functools.partial(plane_kernel, counts), [velocity.shape], [VM] * 4, [tall], name="planes", cost=0.4
     )(stress_vm, along, y1, y2)[0]
-    plane, x1, x2 = tied((plane, x1, x2))
+    plane, cells, x1, x2 = tied((plane, cells, x1, x2))
     factor, mz, slope = call(
         functools.partial(metric_kernel, counts),
         [(nz, ny, nx), (nz, ny, nx), (2, ny, nx)],
         [SM] + [VM] * 3,
         [pltpu.VMEM((ny + 2 * PAD, nx), F32), pltpu.VMEM((ny + PAD, nx), F32)],
-        name="metrics",
+        name="metrics", cost=1.1,
     )(slab[ny:], terrain, x1[xs:], x2[xs:])
     vel, vlow, vhigh, vx1, vx2, vz1, vz2, *vys = call(
         functools.partial(velocity_kernel, counts),
         [velocity.shape] + [(xs, nx)] * 4 + [(3, 2, ny, nx)] * 2 + [(faces, nx)] * y_rounds,
         [VM] * 14,
         [edge] + depth(6) + [pltpu.VMEM((6, 4, ny, nx), F32)],
-        name="velocity",
+        name="velocity", cost=1.5,
     )(velocity_vm, stress_vm, cells, inner_k, plane, factor, mz, slope, x1, x2, z1, z2, low, high)
     vz1, vz2 = exchange(sizes, "gz", vz1, vz2)
     vy1, vy2 = exchange(sizes, "gy", vys[0], vys[-1])
@@ -703,7 +698,7 @@
         [velocity.shape, (3, nz - 4, ny, nx), velocity.shape],
         [VM],
         [DMA],
-        name="velocity_inner",
+        name="velocity_inner", cost=1.0,
         out_specs=[HB, VM, VM],
     )(vel)
     stress_next, memory_next = call(
@@ -713,7 +708,7 @@
         [edge, tall] + depth(3)
         + [pltpu.VMEM((3, 4, ny, nx), F32), pltpu.VMEM(stress.shape, F32), pltpu.VMEM(stress.shape, F32)]
         + [DMA((2, nz))],
-        name="stress",
+        name="stress", cost=2.8,
         out_specs=[HB] * 2,
     )(
         vel, stress_vm, memory, cells, vel_k, vel_x, factor, mz, slope, vx1, vx2, vlow, vhigh, vy1, vy2,

time: 32 us -> 31.1 us (0.972)
  Pallas kernels: 14.8 us -> 11.8 us
  waiting for transfers between devices: 2.36 us -> 3.85 us
  starting transfers between devices: 13.7 us -> 14.3 us
    ppermute x10, waiting for transfers between devices: 2.12 us -> 3.77 us  [exchange(): lax.ppermute(v, tuple(sizes), r)]
    pallas_call x1, Pallas kernels: 2.63 us -> 1.83 us  [local(): call(cell_kernel, [(5, nz, ny, nx)], [HB] * 6, [pltpu.VMEM(material.shape...]
    pallas_call x1, Pallas kernels: 1.72 us -> 1.1 us  [local(): call(functools.partial(velocity_kernel, counts), [velocity.shape] + [(xs,...]
    ppermute x10, starting transfers between devices: 10.6 us -> 11.2 us  [exchange(): lax.ppermute(v, tuple(sizes), r)]
    pallas_call x1, Pallas kernels: 1.74 us -> 1.19 us  [local(): call(velocity_inner_kernel, [velocity.shape, (3, nz - 4, ny, nx), velocit...]
    pallas_call x1, Pallas kernels: 1.82 us -> 1.33 us  [local(): call(depth_kernel, [(6, nz - 4, ny, nx), velocity.shape, velocity.shape],...]
    pallas_call x1, Pallas kernels: 2.98 us -> 2.55 us  [local(): call(functools.partial(stress_kernel, counts), [stress.shape, stress.shap...]
  transfers between devices with their start and end apart: 12 -> 12, of which waited for: 3 -> 3; matrix products, arithmetic and copies ran while one was open for 0% -> 0% of each run, Pallas kernels for 29% -> 24%
where the time goes in v4:
time: 31.1 us; the launch traced here: 30.8 us
  starting transfers between devices  14.3 us (46%)
  Pallas kernels  11.8 us (38%)
  waiting for transfers between devices  3.85 us (12%)
  between operations  0.79 us (3%)
    ppermute x10, starting transfers between devices, exchange(): lax.ppermute(v, tuple(sizes), r)  11.2 us
    ppermute x10, waiting for transfers between devices, exchange(): lax.ppermute(v, tuple(sizes), r)  3.77 us
    ppermute x2, starting transfers between devices, local(): slab = slab + lax.ppermute(slab, 'gz', [(i, i ^ bit) for i in range(n_gz)])  3.12 us
    pallas_call x1, Pallas kernels, local(): call(functools.partial(stress_kernel, counts), [stress.shape, stress.shap...  2.55 us
    pallas_call x1, Pallas kernels, local(): call(cell_kernel, [(5, nz, ny, nx)], [HB] * 6, [pltpu.VMEM(material.shape...  1.83 us
    pallas_call x1, Pallas kernels, local(): call(pack_kernel, [stress.shape] + [(xs, nx)] * 4 + [z_face] * 2 + [(face...  1.53 us
    pallas_call x1, Pallas kernels, local(): call(depth_kernel, [(6, nz - 4, ny, nx), velocity.shape, velocity.shape],...  1.33 us
    pallas_call x1, Pallas kernels, local(): call(velocity_inner_kernel, [velocity.shape, (3, nz - 4, ny, nx), velocit...  1.19 us
  transfers between devices with their start and end apart: 12, of which 3 were waited for; matrix products, arithmetic and copies ran while one was open for 0% of the time, Pallas kernels for 24%

profile of v4, /device:TPU:0, one launch (start us, length us, event | category | flops | bytes accessed | tf_op | source)
XLA Modules:
  0.0 30.8 jit_solution(11190688838334503353)
XLA Ops:
  0.6 0.8 %terrain_piece.1 = f32[40,128]{1,0:T(8,128)S(1)} custom-call(s32[32,32]{1,0:T(8,128)} %elev_hbm.1, f32[1,16]{1,0:T(1,128)} %bitcast.7, f32[1,16]{1,0:T(1,128)} %bitcast.8), custom_call_target="tpu_custom_call" | custom-call | flops 800000000 | bytes 2800000 | tf_op jit(solution)/shard_map/terrain_piece/pallas_call | solution.py:600
  1.5 0.5 %collective-permute-start = (f32[40,128]{1,0:T(8,128)S(1)}, f32[40,128]{1,0:T(8,128)S(1)}, u32[]{:S(2)}, u32[]{:S(2)}) collective-permute-start(f32[40,128]{1,0:T(8,128)S(1)} %terrain_piece.1), channel_id=1, source_target_pairs={{0,1},{1,0},{2,3},{3,2},{4,5},{5,4},{6,7},{7,6},{8,9},{9,8},{10,11... | collective-permute-start | bytes 61448 | tf_op jit(solution)/shard_map/ppermute | solution.py:630
  2.0 1.5 %pack_stress.1 = (f32[6,16,32,128]{3,2,1,0:T(8,128)S(1)}, f32[24,128]{1,0:T(8,128)S(1)}, f32[24,128]{1,0:T(8,128)S(1)}, f32[24,128]{1,0:T(8,128)S(1)}, f32[24,12...) custom-call(f32[6,16,32,128]{3,2,1,0:T(8,128)} %stress_hbm), custom_call_target="tpu_custom_call" | custom-call | flops 1500000000 | bytes 5250000 | tf_op jit(solution)/shard_map/pack_stress/pallas_call | solution.py:618
  3.5 0.0 collective-permute-done
  3.5 2.6 %collective-permute-start.1 = (f32[40,128]{1,0:T(8,128)S(1)}, f32[40,128]{1,0:T(8,128)S(1)}, u32[]{:S(2)}, u32[]{:S(2)}) collective-permute-start(f32[40,128]{1,0:T(8,128)S(1)} %add.6), channel_id=1, source_target_pairs={{0,2},{1,3},{2,0},{3,1},{4,6},{5,7},{6,4},{7,5},{8,10},{9,11},{10,... | collective-permute-start | bytes 61448 | tf_op jit(solution)/shard_map/ppermute | solution.py:630
  6.1 0.2 collective-permute-start.5
  6.4 1.5 %collective-permute-start.6 = (f32[6,2,32,128]{3,2,1,0:T(8,128)S(1)}, f32[6,2,32,128]{3,2,1,0:T(8,128)S(1)}, u32[]{:S(2)}, u32[]{:S(2)}) collective-permute-start(f32[6,2,32,128]{3,2,1,0:T(8,128)S(1)} %get-tuple-element.81), channel_id=1, source_target_pairs={{0,4},{1,2},{2,1},{3,7},{4,0},{5,6},{6,5},{7,3},{8,12},{9,10},{10,... | collective-permute-start | bytes 589832 | tf_op jit(solution)/shard_map/ppermute | solution.py:46
  7.8 0.1 collective-permute-done.1
  8.0 2.0 %collective-permute-start.2 = (f32[104,128]{1,0:T(8,128)S(1)}, f32[104,128]{1,0:T(8,128)S(1)}, u32[]{:S(2)}, u32[]{:S(2)}) collective-permute-start(f32[104,128]{1,0:T(8,128)S(1)} %y_send.1), channel_id=1, source_target_pairs={{0,4},{1,5},{2,6},{3,7},{4,0},{5,1},{6,2},{7,3},{8,12},{9,13},{10,... | collective-permute-start | bytes 159752 | tf_op jit(solution)/shard_map/ppermute | solution.py:46
  10.0 1.3 %depth.1 = (f32[6,12,32,128]{3,2,1,0:T(8,128)S(1)}, f32[3,16,32,128]{3,2,1,0:T(8,128)S(1)}, f32[3,16,32,128]{3,2,1,0:T(8,128)S(1)}) custom-call(f32[6,16,32,128]{3,2,1,0:T(8,128)S(1)} %get-tuple-element.57.stress_ref, f32[3,16,32,128]{3,2,1,0:T(8,128)} %velocity_hbm.1), custom_call_target="tpu_custom_call" | custom-call | flops 1000000000 | bytes 3500000 | tf_op jit(solution)/shard_map/depth/pallas_call | solution.py:643
  11.3 1.8 %collective-permute-done.2.y1_ref.y2_ref = f32[104,128]{1,0:T(8,128)S(1)} collective-permute-done((f32[104,128]{1,0:T(8,128)S(1)}, f32[104,128]{1,0:T(8,128)S(1)}, u32[]{:S(2)}, u32[]{:S(2)}) %collective-permute-start.2) | collective-permute-done | bytes 53280 | tf_op jit(solution)/shard_map/ppermute | solution.py:46
  13.2 0.1 x_send.1
  13.3 1.6 %collective-permute-start.3 = (f32[32,128]{1,0:T(8,128)S(1)}, f32[32,128]{1,0:T(8,128)S(1)}, u32[]{:S(2)}, u32[]{:S(2)}) collective-permute-start(f32[32,128]{1,0:T(8,128)S(1)} %get-tuple-element.69), channel_id=1, source_target_pairs={{0,8},{1,9},{2,10},{3,11},{4,12},{5,13},{6,14},{7,15},{8,0},{9,1},... | collective-permute-start | bytes 49160 | tf_op jit(solution)/shard_map/ppermute | solution.py:46
  14.9 0.0 collective-permute-start.4
  14.9 1.8 %cells.1.cells_ref = f32[5,16,32,128]{3,2,1,0:T(8,128)S(1)} custom-call(s32[16,32,128]{2,1,0:T(8,128)} %refs_0_, f32[1,16]{1,0:T(1,128)} %bitcast.9, f32[1,16]{1,0:T(1,128)} %bitcast.10, f32[1,16]{1,0:T(1,128)} %bitcast.11, f32[1,16]{1,0:T(1,128)} %bitcast.12, f32[1,16]{1,0:T(1,128)} %bitcast.13), custom_call_target="tpu_custom_call" | custom-call | flops 1200000000 | bytes 4200000 | tf_op jit(solution)/shard_map/cells/pallas_call | solution.py:666
  16.7 0.4 %planes.1.plane_ref = f32[3,16,32,128]{3,2,1,0:T(8,128)S(1)} custom-call(f32[6,16,32,128]{3,2,1,0:T(8,128)S(1)} %get-tuple-element.57.stress_ref, f32[3,16,32,128]{3,2,1,0:T(8,128)S(1)} %get-tuple-element.59.along_ref, f32[104,128]{1,0:T(8,128)S(1)} %collective-permute-done.2.y1_ref.y2_ref, f32[104,128]{1,0:T(8,128)S(1)} %collective-permute-done.2.y1_ref.y2_ref), custom_call_target="tpu_custom_call" | custom-call | flops 400000000 | bytes 1400000 | tf_op jit(solution)/shard_map/planes/pallas_call | solution.py:675
  17.1 0.0 collective-permute-done.3.x1_ref
  17.1 0.0 collective-permute-done.4.x2_ref
  17.1 1.0 %metrics.1 = (f32[16,32,128]{2,1,0:T(8,128)S(1)}, f32[16,32,128]{2,1,0:T(8,128)S(1)}, f32[2,32,128]{2,1,0:T(8,128)S(1)}) custom-call(f32[8,128]{1,0:T(8,128)S(1)} %slice.18.layers_ref, f32[48,128]{1,0:T(8,128)S(1)} %get-tuple-element.74.own, f32[8,128]{1,0:T(8,128)S(1)} %slice.15.x1_ref, f32[8,128]{1,0:T(8,128)S(1)} %slice.16.x2_ref), custom_call_target="tpu_custom_call" | custom-call | flops 1100000000 | bytes 3850000 | tf_op jit(solution)/shard_map/metrics/pallas_call | solution.py:679
  18.2 0.0 collective-permute-done.5.z1_ref
  18.2 0.0 collective-permute-done.6.z2_ref
  18.2 1.1 %velocity.1 = (f32[3,16,32,128]{3,2,1,0:T(8,128)S(1)}, f32[24,128]{1,0:T(8,128)S(1)}, f32[24,128]{1,0:T(8,128)S(1)}, f32[24,128]{1,0:T(8,128)S(1)}, f32[24,128]{...) custom-call(f32[3,16,32,128]{3,2,1,0:T(8,128)S(1)} %get-tuple-element.58.veloc, ...), custom_call_target="tpu_custom_call" | custom-call | flops 1500000000 | bytes 5250000 | tf_op jit(solution)/shard_map/velocity/pallas_call | solution.py:686
  19.3 0.6 %collective-permute-start.10 = (f32[3,2,32,128]{3,2,1,0:T(8,128)S(1)}, f32[3,2,32,128]{3,2,1,0:T(8,128)S(1)}, u32[]{:S(2)}, u32[]{:S(2)}) collective-permute-start(f32[3,2,32,128]{3,2,1,0:T(8,128)S(1)} %get-tuple-element.93), channel_id=1, source_target_pairs={{0,1},{1,0},{2,3},{3,2},{4,5},{5,4},{6,7},{7,6},{8,9},{9,8},{10,11... | collective-permute-start | bytes 294920 | tf_op jit(solution)/shard_map/ppermute | solution.py:46
  19.9 1.5 %collective-permute-start.11 = (f32[3,2,32,128]{3,2,1,0:T(8,128)S(1)}, f32[3,2,32,128]{3,2,1,0:T(8,128)S(1)}, u32[]{:S(2)}, u32[]{:S(2)}) collective-permute-start(f32[3,2,32,128]{3,2,1,0:T(8,128)S(1)} %get-tuple-element.94), channel_id=1, source_target_pairs={{0,4},{1,2},{2,1},{3,7},{4,0},{5,6},{6,5},{7,3},{8,12},{9,10},{10,... | collective-permute-start | bytes 294920 | tf_op jit(solution)/shard_map/ppermute | solution.py:46
  21.4 2.7 %collective-permute-start.7 = (f32[24,128]{1,0:T(8,128)S(1)}, f32[24,128]{1,0:T(8,128)S(1)}, u32[]{:S(2)}, u32[]{:S(2)}) collective-permute-start(f32[24,128]{1,0:T(8,128)S(1)} %get-tuple-element.88), channel_id=1, source_target_pairs={{0,8},{1,9},{2,10},{3,11},{4,12},{5,13},{6,14},{7,15},{8,0},{9,1},... | collective-permute-start | bytes 36872 | tf_op jit(solution)/shard_map/ppermute | solution.py:46
  24.1 0.0 collective-permute-start.8
  24.1 1.0 %collective-permute-start.9 = (f32[96,128]{1,0:T(8,128)S(1)}, f32[96,128]{1,0:T(8,128)S(1)}, u32[]{:S(2)}, u32[]{:S(2)}) collective-permute-start(f32[96,128]{1,0:T(8,128)S(1)} %get-tuple-element.92), channel_id=1, source_target_pairs={{0,4},{1,5},{2,6},{3,7},{4,0},{5,1},{6,2},{7,3},{8,12},{9,13},{10,... | collective-permute-start | bytes 147464 | tf_op jit(solution)/shard_map/ppermute | solution.py:46
  25.1 0.0 copy-start
  25.1 1.2 %velocity_inner.1 = (f32[3,16,32,128]{3,2,1,0:T(8,128)}, f32[3,12,32,128]{3,2,1,0:T(8,128)S(1)}, f32[3,16,32,128]{3,2,1,0:T(8,128)S(1)}) custom-call(f32[3,16,32,128]{3,2,1,0:T(8,128)S(1)} %get-tuple-element.84.vel_ref), custom_call_target="tpu_custom_call" | custom-call | flops 1000000000 | bytes 3500000 | tf_op jit(solution)/shard_map/velocity_inner/pallas_call | solution.py:696
  26.3 0.0 collective-permute-done.7.x1_ref
  26.3 0.0 collective-permute-done.8.x2_ref
  26.3 1.9 %collective-permute-done.9.y1_ref.y2_ref = f32[96,128]{1,0:T(8,128)S(1)} collective-permute-done((f32[96,128]{1,0:T(8,128)S(1)}, f32[96,128]{1,0:T(8,128)S(1)}, u32[]{:S(2)}, u32[]{:S(2)}) %collective-permute-start.9) | collective-permute-done | bytes 49184 | tf_op jit(solution)/shard_map/ppermute | solution.py:46
  28.2 0.0 collective-permute-done.10.z1_ref
  28.2 0.0 collective-permute-done.11.z2_ref
  28.2 0.0 copy-done
  28.2 2.5 %stress.1 = (f32[6,16,32,128]{3,2,1,0:T(8,128)}, f32[6,16,32,128]{3,2,1,0:T(8,128)}) custom-call(f32[3,16,32,128]{3,2,1,0:T(8,128)S(1)} %get-tuple-element.84.vel_ref, f32[6,16,32,128]{3,2,1,0:T(8,128)S(1)} %get-tuple-element.57.stress_ref, f32[6,16,32,128]{3,2,1,0:T(8,128)S(1)} %copy-done, f32[5,16,32,128]{3,2,1,0:T(8,128)S(1)} %cells.1.cells_ref, ...), custom_call_target="tpu_custom_call" | custom-call | flops 2800000000 | bytes 9800000 | tf_op jit(solution)/shard_map/stress/pallas_call | solution.py:704
  (7 shorter events, 0.0 us)
Async XLA Ops:
  1.5 2.1 %collective-permute-start = (f32[40,128]{1,0:T(8,128)S(1)}, f32[40,128]{1,0:T(8,128)S(1)}, u32[]{:S(2)}, u32[]{:S(2)}) collective-permute-start(f32[40,128]{1,0:T(8,128)S(1)} %terrain_piece.1), channel_id=1, source_target_pairs={{0,1},{1,0},{2,3},{3,2},{4,5},{5,4},{6,7},{7,6},{8,9},{9,8},{10,11... | collective-permute-start | bytes 61448 | tf_op jit(solution)/shard_map/ppermute | solution.py:630
  3.5 4.4 %collective-permute-start.1 = (f32[40,128]{1,0:T(8,128)S(1)}, f32[40,128]{1,0:T(8,128)S(1)}, u32[]{:S(2)}, u32[]{:S(2)}) collective-permute-start(f32[40,128]{1,0:T(8,128)S(1)} %add.6), channel_id=1, source_target_pairs={{0,2},{1,3},{2,0},{3,1},{4,6},{5,7},{6,4},{7,5},{8,10},{9,11},{10,... | collective-permute-start | bytes 61448 | tf_op jit(solution)/shard_map/ppermute | solution.py:630
  6.1 12.0 %collective-permute-start.5 = (f32[6,2,32,128]{3,2,1,0:T(8,128)S(1)}, f32[6,2,32,128]{3,2,1,0:T(8,128)S(1)}, u32[]{:S(2)}, u32[]{:S(2)}) collective-permute-start(f32[6,2,32,128]{3,2,1,0:T(8,128)S(1)} %get-tuple-element.80), channel_id=1, source_target_pairs={{0,1},{1,0},{2,3},{3,2},{4,5},{5,4},{6,7},{7,6},{8,9},{9,8},{10,11... | collective-permute-start | bytes 589832 | tf_op jit(solution)/shard_map/ppermute | solution.py:46
  6.4 11.8 %collective-permute-start.6 = (f32[6,2,32,128]{3,2,1,0:T(8,128)S(1)}, f32[6,2,32,128]{3,2,1,0:T(8,128)S(1)}, u32[]{:S(2)}, u32[]{:S(2)}) collective-permute-start(f32[6,2,32,128]{3,2,1,0:T(8,128)S(1)} %get-tuple-element.81), channel_id=1, source_target_pairs={{0,4},{1,2},{2,1},{3,7},{4,0},{5,6},{6,5},{7,3},{8,12},{9,10},{10,... | collective-permute-start | bytes 589832 | tf_op jit(solution)/shard_map/ppermute | solution.py:46
  8.0 5.2 %collective-permute-start.2 = (f32[104,128]{1,0:T(8,128)S(1)}, f32[104,128]{1,0:T(8,128)S(1)}, u32[]{:S(2)}, u32[]{:S(2)}) collective-permute-start(f32[104,128]{1,0:T(8,128)S(1)} %y_send.1), channel_id=1, source_target_pairs={{0,4},{1,5},{2,6},{3,7},{4,0},{5,1},{6,2},{7,3},{8,12},{9,13},{10,... | collective-permute-start | bytes 159752 | tf_op jit(solution)/shard_map/ppermute | solution.py:46
  13.3 3.8 %collective-permute-start.3 = (f32[32,128]{1,0:T(8,128)S(1)}, f32[32,128]{1,0:T(8,128)S(1)}, u32[]{:S(2)}, u32[]{:S(2)}) collective-permute-start(f32[32,128]{1,0:T(8,128)S(1)} %get-tuple-element.69), channel_id=1, source_target_pairs={{0,8},{1,9},{2,10},{3,11},{4,12},{5,13},{6,14},{7,15},{8,0},{9,1},... | collective-permute-start | bytes 49160 | tf_op jit(solution)/shard_map/ppermute | solution.py:46
  14.9 2.2 %collective-permute-start.4 = (f32[32,128]{1,0:T(8,128)S(1)}, f32[32,128]{1,0:T(8,128)S(1)}, u32[]{:S(2)}, u32[]{:S(2)}) collective-permute-start(f32[32,128]{1,0:T(8,128)S(1)} %get-tuple-element.70), channel_id=1, source_target_pairs={{0,1},{1,0},{2,3},{3,2},{4,5},{5,4},{6,7},{7,6},{8,16},{9,17},{10,... | collective-permute-start | bytes 49160 | tf_op jit(solution)/shard_map/ppermute | solution.py:46
  19.3 8.9 %collective-permute-start.10 = (f32[3,2,32,128]{3,2,1,0:T(8,128)S(1)}, f32[3,2,32,128]{3,2,1,0:T(8,128)S(1)}, u32[]{:S(2)}, u32[]{:S(2)}) collective-permute-start(f32[3,2,32,128]{3,2,1,0:T(8,128)S(1)} %get-tuple-element.93), channel_id=1, source_target_pairs={{0,1},{1,0},{2,3},{3,2},{4,5},{5,4},{6,7},{7,6},{8,9},{9,8},{10,11... | collective-permute-start | bytes 294920 | tf_op jit(solution)/shard_map/ppermute | solution.py:46
  19.9 8.3 %collective-permute-start.11 = (f32[3,2,32,128]{3,2,1,0:T(8,128)S(1)}, f32[3,2,32,128]{3,2,1,0:T(8,128)S(1)}, u32[]{:S(2)}, u32[]{:S(2)}) collective-permute-start(f32[3,2,32,128]{3,2,1,0:T(8,128)S(1)} %get-tuple-element.94), channel_id=1, source_target_pairs={{0,4},{1,2},{2,1},{3,7},{4,0},{5,6},{6,5},{7,3},{8,12},{9,10},{10,... | collective-permute-start | bytes 294920 | tf_op jit(solution)/shard_map/ppermute | solution.py:46
  21.4 4.9 %collective-permute-start.7 = (f32[24,128]{1,0:T(8,128)S(1)}, f32[24,128]{1,0:T(8,128)S(1)}, u32[]{:S(2)}, u32[]{:S(2)}) collective-permute-start(f32[24,128]{1,0:T(8,128)S(1)} %get-tuple-element.88), channel_id=1, source_target_pairs={{0,8},{1,9},{2,10},{3,11},{4,12},{5,13},{6,14},{7,15},{8,0},{9,1},... | collective-permute-start | bytes 36872 | tf_op jit(solution)/shard_map/ppermute | solution.py:46
  24.1 2.2 %collective-permute-start.8 = (f32[24,128]{1,0:T(8,128)S(1)}, f32[24,128]{1,0:T(8,128)S(1)}, u32[]{:S(2)}, u32[]{:S(2)}) collective-permute-start(f32[24,128]{1,0:T(8,128)S(1)} %get-tuple-element.89), channel_id=1, source_target_pairs={{0,1},{1,0},{2,3},{3,2},{4,5},{5,4},{6,7},{7,6},{8,16},{9,17},{10,... | collective-permute-start | bytes 36872 | tf_op jit(solution)/shard_map/ppermute | solution.py:46
  24.1 4.2 %collective-permute-start.9 = (f32[96,128]{1,0:T(8,128)S(1)}, f32[96,128]{1,0:T(8,128)S(1)}, u32[]{:S(2)}, u32[]{:S(2)}) collective-permute-start(f32[96,128]{1,0:T(8,128)S(1)} %get-tuple-element.92), channel_id=1, source_target_pairs={{0,4},{1,5},{2,6},{3,7},{4,0},{5,1},{6,2},{7,3},{8,12},{9,13},{10,... | collective-permute-start | bytes 147464 | tf_op jit(solution)/shard_map/ppermute | solution.py:46
  25.1 3.1 %copy-start = (f32[6,16,32,128]{3,2,1,0:T(8,128)S(1)}, f32[6,16,32,128]{3,2,1,0:T(8,128)}, u32[]{:S(2)}) copy-start(f32[6,16,32,128]{3,2,1,0:T(8,128)} %memory_ref.1) | copy-start | bytes 4718596

commit v5 on v4

--- a/solution.py
+++ b/solution.py
@@ -30,8 +30,8 @@
         for spot in np.ndindex(*shape):
             mate = spot[index] + 1 if spot[index] % 2 == first else spot[index] - 1
             target = list(spot)
-            if 0 <= mate < n:
-                target[index] = mate
+            if 0 <= mate < n or axis == "gz":
+                target[index] = mate % n
             elif others:
                 target[others[0]] ^= 1
             else:
@@ -119,51 +119,24 @@
                 ref[j : j + 2, :] = rows
 
 
-def pack_kernel(
-    stress_hbm, stress_ref, low_ref, high_ref, out1_ref, out2_ref, z1_ref, z2_ref, *rest
-):
-    *y_refs, sems = rest
-    comps, nz, ny, nx = stress_ref.shape
-    copies = [
-        pltpu.make_async_copy(stress_hbm.at[c], stress_ref.at[c], sems.at[c]) for c in range(comps)
-    ]
-    z_even = even("gz")
-    z1_at = jnp.where(z_even, nz - 2, 0)
-    z2_at = jnp.where(z_even, 0, nz - 2)
-    z_copies = [
-        pltpu.make_async_copy(stress_hbm.at[:, pl.ds(z1_at, 2)], z1_ref, sems.at[comps]),
-        pltpu.make_async_copy(stress_hbm.at[:, pl.ds(z2_at, 2)], z2_ref, sems.at[comps + 1]),
-    ]
+def pack_kernel(stress_ref, low_ref, high_ref, out1_ref, out2_ref, z1_ref, z2_ref, *y_refs):
+    _, nz, ny, nx = stress_ref.shape
     of_x = (0, 3, 4)
     of_y = (3, 1, 5)
-    loading = (0, 3, 4, 1, 5, 2)
-    for c in loading[:5]:
-        copies[c].start()
-    for copy in z_copies:
-        copy.start()
-    copies[2].start()
-    for c in of_x:
-        copies[c].wait()
+    z1_ref[...], z2_ref[...] = order("gz", stress_ref[:, nz - 2 : nz], stress_ref[:, 0:2])
     pack_sides(
         lambda c, k, t: stress_ref[of_x[c], k, SUB * t : SUB * t + SUB, :],
         nz, ny, nx, low_ref, high_ref, out1_ref, out2_ref,
     )
-    copies[1].wait()
-    copies[5].wait()
     pack_rows(lambda c, k, rows: stress_ref[of_y[c], k, rows, :], nz, ny, y_refs)
-    copies[2].wait()
-    for copy in z_copies:
-        copy.wait()
-
-
-def y_send_kernel(rounds, slab_ref, *refs):
+
+
+def y_send_kernel(slab_ref, *out_refs):
     ny = slab_ref.shape[0] - SUB
-    faces = refs[0].shape[0]
-    rows = order("gy", slab_ref[ny - 4 : ny, :], slab_ref[0:4, :])
-    for i in range(rounds):
-        refs[rounds + i][:faces, :] = refs[i][...]
-        refs[rounds + i][faces : faces + 4, :] = rows[i]
-        refs[rounds + i][faces + 4 :, :] = jnp.zeros_like(rows[i])
+    both = order("gy", slab_ref[ny - 4 : ny, :], slab_ref[0:4, :])
+    for ref, rows in zip(out_refs, both):
+        ref[0:4, :] = rows
+        ref[4:, :] = jnp.zeros_like(rows)
 
 
 def x_send_kernel(n_gy, slab_ref, y1_ref, y2_ref, x1_ref, x2_ref, tall_ref, out1_ref, out2_ref):
@@ -243,14 +216,16 @@
 
     def above(slab, total):
         for k in range(nz):
-            s = layers_ref[1, slab * nz + k]
-            total = total + (s * layers_ref[0, slab * nz + k]) * jnp.exp(s * surface)
+            at = pl.ds(slab * nz + k, 1)
+            s = layers_ref[1, at, :]
+            total = total + (s * layers_ref[0, at, :]) * jnp.exp(s * surface)
         return total
 
     total = lax.fori_loop(0, gz, above, jnp.zeros((ny, nx), F32))
     for k in range(nz):
-        s = layers_ref[1, gz * nz + k]
-        thickness = layers_ref[0, gz * nz + k] * jnp.exp(s * surface)
+        at = pl.ds(gz * nz + k, 1)
+        s = layers_ref[1, at, :]
+        thickness = layers_ref[0, at, :] * jnp.exp(s * surface)
         weighted = s * thickness
         mz = 1.0 / thickness
         lift = total + 0.5 * weighted
@@ -365,16 +340,16 @@
                 out_ref[c, spot, tile_rows(t), :] = centred12(at)
 
 
-def cell_kernel(*refs):
-    given, cells_ref, held, sems = refs[:6], refs[6], refs[7:13], refs[13]
-    copies = [
-        pltpu.make_async_copy(a, b, sems.at[i]) for i, (a, b) in enumerate(zip(given, held))
-    ]
-    for copy in copies:
-        copy.start()
-    for copy in copies:
-        copy.wait()
-    material_ref, buoy_ref, lam_ref, mu_ref, relax_ref, weight_ref = held
+def cell_kernel(
+    layers_ref, material_ref, buoy_ref, lam_ref, mu_ref, relax_ref, weight_ref, cells_ref, spread_ref
+):
+    lane = lanes_of((SUB, layers_ref.shape[1]))
+    sub = lax.broadcasted_iota(jnp.int32, lane.shape, 0)
+    for i in range(2):
+        row = jnp.broadcast_to(layers_ref[i : i + 1, :], lane.shape)
+        for g in range(spread_ref.shape[1] // SUB):
+            one = jnp.sum(jnp.where(lane == SUB * g + sub, row, 0.0), axis=1, keepdims=True)
+            spread_ref[i, tile_rows(g), :] = jnp.broadcast_to(one, lane.shape)
     nz, ny, nx = material_ref.shape
     keep = jnp.exp(-step_size / relax_ref[...])
     tables = table_rows(
@@ -394,9 +369,7 @@
     over(0, nz, 4, layer)
 
 
-def depth_kernel(stress_ref, velocity_hbm, depth_ref, along_ref, velocity_ref, sem):
-    load = pltpu.make_async_copy(velocity_hbm, velocity_ref, sem)
-    load.start()
+def depth_kernel(stress_ref, depth_ref, along_ref):
     _, nz, ny, _ = stress_ref.shape
     tiles = ny // SUB
 
@@ -407,7 +380,6 @@
 
     over(0, nz, 4, along)
     over(2, nz - 2, 4, lambda k: inner_depth(stress_ref, depth_ref, 6, k, tiles))
-    load.wait()
 
 
 def plane_kernel(sizes, stress_ref, along_ref, y1_ref, y2_ref, plane_ref, tall):
@@ -585,7 +557,7 @@
         out_specs=out_specs or [VM] * len(outs),
         scratch_shapes=list(scratch),
         compiler_params=params(),
-        cost_estimate=pl.CostEstimate(flops=int(cost * 1e9), transcendentals=0, bytes_accessed=int(cost * 3.5e6)),
+        cost_estimate=pl.CostEstimate(flops=int(cost * 6e8), transcendentals=0, bytes_accessed=int(cost * 3.5e6)),
         name=name,
     )
 
@@ -615,13 +587,13 @@
     y_rounds = min(2, n_gy - 1) if n_gy > 1 else 1
     z_face = (6, 2, ny, nx)
     slab, stress = tied((slab, stress))
-    stress_vm, low, high, x1, x2, z1, z2, *ys = call(
+    stress_vm = stress
+    low, high, x1, x2, z1, z2, *ys = call(
         pack_kernel,
-        [stress.shape] + [(xs, nx)] * 4 + [z_face] * 2 + [(faces, nx)] * y_rounds,
-        [HB],
-        [DMA((8,))],
-        name="pack_stress", cost=1.5,
-    )(in_hbm(stress))
+        [(xs, nx)] * 4 + [z_face] * 2 + [(faces, nx)] * y_rounds,
+        [VM],
+        name="pack_stress", cost=0.5,
+    )(stress)
     if n_gz & (n_gz - 1):
         slab = lax.psum(slab, "gz")
     else:
@@ -632,29 +604,17 @@
                 slab, z1, z2 = tied((slab, z1, z2))
             bit *= 2
     z1, z2 = exchange(sizes, "gz", z1, z2)
-    ys = call(
-        functools.partial(y_send_kernel, y_rounds),
-        [(faces + SUB, nx)] * y_rounds,
-        [VM] * (1 + y_rounds),
-        name="y_send", cost=0.02,
-    )(slab, *ys)
-    ys, stress_vm = tied((ys, stress_vm))
+    ts = call(y_send_kernel, [(SUB, nx)] * y_rounds, [VM], name="y_send", cost=0.02)(slab)
+    ts, ys = tied((ts, ys))
+    t1, t2 = exchange(sizes, "gy", ts[0], ts[-1])
     y1, y2 = exchange(sizes, "gy", ys[0], ys[-1])
-    inner_k, along, velocity_vm = call(
-        depth_kernel,
-        [(6, nz - 4, ny, nx), velocity.shape, velocity.shape],
-        [VM, HB],
-        [DMA],
-        name="depth", cost=1.0,
-    )(stress_vm, in_hbm(velocity))
-    x1, x2, inner_k = tied((x1, x2, inner_k))
     terrain, x1, x2 = call(
         functools.partial(x_send_kernel, n_gy),
         [(ny + 2 * PAD, nx)] + [(xs + SUB, nx)] * 2,
         [VM] * 5,
         name="x_send", cost=0.1,
-    )(slab, y1[faces:], y2[faces:], x1, x2)
-    x1, x2, material = tied((x1, x2, material))
+    )(slab, t1, t2, x1, x2)
+    x1, x2, material, stress_vm = tied((x1, x2, material, stress_vm))
     x1, x2 = exchange(sizes, "gx", x1, x2)
     edge = pltpu.VMEM((3, 2, SUB, nx), F32)
     tall = pltpu.VMEM((3, nz, ny + 2 * PAD, nx), F32)
@@ -663,15 +623,13 @@
         return [pltpu.VMEM((comps, 2, ny, nx), F32)] * 2
 
     tables = (buoyancy, lame_lambda, shear_modulus, relax_time, anelastic_weight)
-    cells = call(
-        cell_kernel,
-        [(5, nz, ny, nx)],
-        [HB] * 6,
-        [pltpu.VMEM(material.shape, jnp.int32)]
-        + [pltpu.VMEM((1, table.shape[0]), F32) for table in tables]
-        + [DMA((6,))],
-        name="cells", cost=1.2,
-    )(in_hbm(material), *[in_hbm(table[None]) for table in tables])[0]
+    all_layers = -(-n_gz * nz // SUB) * SUB
+    cells, spread = call(
+        cell_kernel, [(5, nz, ny, nx), (2, all_layers, nx)], [VM] * 7, name="cells", cost=0.8
+    )(slab[ny:], material, *[table[None] for table in tables])
+    inner_k, along = call(
+        depth_kernel, [(6, nz - 4, ny, nx), velocity.shape], [VM], name="depth", cost=0.9
+    )(stress_vm)
     plane = call(
         functools.partial(plane_kernel, counts), [velocity.shape], [VM] * 4, [tall], name="planes", cost=0.4
     )(stress_vm, along, y1, y2)[0]
@@ -679,17 +637,17 @@
     factor, mz, slope = call(
         functools.partial(metric_kernel, counts),
         [(nz, ny, nx), (nz, ny, nx), (2, ny, nx)],
-        [SM] + [VM] * 3,
+        [VM] * 4,
         [pltpu.VMEM((ny + 2 * PAD, nx), F32), pltpu.VMEM((ny + PAD, nx), F32)],
         name="metrics", cost=1.1,
-    )(slab[ny:], terrain, x1[xs:], x2[xs:])
+    )(spread, terrain, x1[xs:], x2[xs:])
     vel, vlow, vhigh, vx1, vx2, vz1, vz2, *vys = call(
         functools.partial(velocity_kernel, counts),
         [velocity.shape] + [(xs, nx)] * 4 + [(3, 2, ny, nx)] * 2 + [(faces, nx)] * y_rounds,
         [VM] * 14,
         [edge] + depth(6) + [pltpu.VMEM((6, 4, ny, nx), F32)],
         name="velocity", cost=1.5,
-    )(velocity_vm, stress_vm, cells, inner_k, plane, factor, mz, slope, x1, x2, z1, z2, low, high)
+    )(velocity, stress_vm, cells, inner_k, plane, factor, mz, slope, x1, x2, z1, z2, low, high)
     vz1, vz2 = exchange(sizes, "gz", vz1, vz2)
     vy1, vy2 = exchange(sizes, "gy", vys[0], vys[-1])
     vx1, vx2 = exchange(sizes, "gx", vx1, vx2)
@@ -698,7 +656,7 @@
         [velocity.shape, (3, nz - 4, ny, nx), velocity.shape],
         [VM],
         [DMA],
-        name="velocity_inner", cost=1.0,
+        name="velocity_inner", cost=0.1,
         out_specs=[HB, VM, VM],
     )(vel)
     stress_next, memory_next = call(

time: 31.1 us -> 29.3 us (0.942)
  Pallas kernels: 11.8 us -> 9.02 us
  local copies, waits for them, and re-layouts: 0.02 us -> 0.68 us
  waiting for transfers between devices: 3.85 us -> 4.17 us
    pallas_call x4, Pallas kernels: 4.7 us -> 2.51 us  [the longest x1 1.32 us: local(): call(depth_kernel, [(6, nz - 4, ny, nx), velocity.shape], [VM], name='dep...]
    ppermute x2, waiting for transfers between devices: 0.08 us -> 2.12 us  [local(): slab = slab + lax.ppermute(slab, 'gz', [(i, i ^ bit) for i in range(n_gz)])]
    ppermute x10 -> x11, waiting for transfers between devices: 3.77 us -> 2.06 us  [exchange(): lax.ppermute(v, tuple(sizes), r)]
    unnamed x2 -> x18, local copies, waits for them, and re-layouts: 0.01 us -> 0.67 us
    pallas_call x1, Pallas kernels: 1.02 us -> 0.42 us  [local(): call(functools.partial(metric_kernel, counts), [(nz, ny, nx), (nz, ny, nx...]
    ppermute x10 -> x11, starting transfers between devices: 11.2 us -> 11 us  [exchange(): lax.ppermute(v, tuple(sizes), r)]
  transfers between devices with their start and end apart: 12 -> 13, of which waited for: 3 -> 4; matrix products, arithmetic and copies ran while one was open for 0% -> 0% of each run, Pallas kernels for 24% -> 16%
where the time goes in v5:
time: 29.3 us; the launch traced here: 29.1 us
  starting transfers between devices  14.4 us (49%)
  Pallas kernels  9.02 us (31%)
  waiting for transfers between devices  4.17 us (14%)
  between operations  0.88 us (3%)
  local copies, waits for them, and re-layouts  0.68 us (2%)
    ppermute x11, starting transfers between devices, exchange(): lax.ppermute(v, tuple(sizes), r)  11 us
    ppermute x2, starting transfers between devices, local(): slab = slab + lax.ppermute(slab, 'gz', [(i, i ^ bit) for i in range(n_gz)])  3.38 us
    pallas_call x1, Pallas kernels, local(): call(functools.partial(stress_kernel, counts), [stress.shape, stress.shap...  2.49 us
    ppermute x2, waiting for transfers between devices, local(): slab = slab + lax.ppermute(slab, 'gz', [(i, i ^ bit) for i in range(n_gz)])  2.12 us
    ppermute x11, waiting for transfers between devices, exchange(): lax.ppermute(v, tuple(sizes), r)  2.06 us
    pallas_call x1, Pallas kernels, local(): call(depth_kernel, [(6, nz - 4, ny, nx), velocity.shape], [VM], name='dep...  1.32 us
    pallas_call x1, Pallas kernels, local(): call(velocity_inner_kernel, [velocity.shape, (3, nz - 4, ny, nx), velocit...  1.19 us
    pallas_call x1, Pallas kernels, local(): call(functools.partial(velocity_kernel, counts), [velocity.shape] + [(xs,...  1.07 us
  transfers between devices with their start and end apart: 13, of which 4 were waited for; matrix products, arithmetic and copies ran while one was open for 0% of the time, Pallas kernels for 16%

profile of v5, /device:TPU:0, one launch (start us, length us, event | category | flops | bytes accessed | tf_op | source)
XLA Modules:
  0.0 29.1 jit_solution(2084172596893332769)
XLA Ops:
  0.6 0.0 copy-start
  0.6 0.0 copy-start.3
  0.7 0.0 copy-start.4
  0.7 0.0 copy-start.5
  0.7 0.0 copy-start.6
  0.7 0.0 copy-start.7
  0.7 0.0 copy-start.8
  0.7 0.9 %terrain_piece.1 = f32[40,128]{1,0:T(8,128)S(1)} custom-call(s32[32,32]{1,0:T(8,128)} %elev_hbm.1, f32[1,16]{1,0:T(1,128)} %bitcast.12, f32[1,16]{1,0:T(1,128)} %bitcast.13), custom_call_target="tpu_custom_call" | custom-call | flops 480000000 | bytes 2800000 | tf_op jit(solution)/shard_map/terrain_piece/pallas_call | solution.py:572
  1.7 0.5 %collective-permute-start = (f32[40,128]{1,0:T(8,128)S(1)}, f32[40,128]{1,0:T(8,128)S(1)}, u32[]{:S(2)}, u32[]{:S(2)}) collective-permute-start(f32[40,128]{1,0:T(8,128)S(1)} %terrain_piece.1), channel_id=1, source_target_pairs={{0,1},{1,0},{2,3},{3,2},{4,5},{5,4},{6,7},{7,6},{8,9},{9,8},{10,11... | collective-permute-start | bytes 61448 | tf_op jit(solution)/shard_map/ppermute | solution.py:602
  2.2 0.0 copy-done
  2.2 0.3 %pack_stress.1 = (f32[24,128]{1,0:T(8,128)S(1)}, f32[24,128]{1,0:T(8,128)S(1)}, f32[24,128]{1,0:T(8,128)S(1)}, f32[24,128]{1,0:T(8,128)S(1)}, f32[6,2,32,128]{3,...) custom-call(f32[6,16,32,128]{3,2,1,0:T(8,128)S(1)} %copy-done), custom_call_target="tpu_custom_call" | custom-call | flops 300000000 | bytes 1750000 | tf_op jit(solution)/shard_map/pack_stress/pallas_call | solution.py:591
  2.5 0.5 %collective-permute-done = f32[40,128]{1,0:T(8,128)S(1)} collective-permute-done((f32[40,128]{1,0:T(8,128)S(1)}, f32[40,128]{1,0:T(8,128)S(1)}, u32[]{:S(2)}, u32[]{:S(2)}) %collective-permute-start) | collective-permute-done | bytes 20512 | tf_op jit(solution)/shard_map/ppermute | solution.py:602
  3.0 2.9 %collective-permute-start.1 = (f32[40,128]{1,0:T(8,128)S(1)}, f32[40,128]{1,0:T(8,128)S(1)}, u32[]{:S(2)}, u32[]{:S(2)}) collective-permute-start(f32[40,128]{1,0:T(8,128)S(1)} %add.6), channel_id=1, source_target_pairs={{0,2},{1,3},{2,0},{3,1},{4,6},{5,7},{6,4},{7,5},{8,10},{9,11},{10,... | collective-permute-start | bytes 61448 | tf_op jit(solution)/shard_map/ppermute | solution.py:602
  5.9 0.0 collective-permute-start.6
  5.9 0.2 collective-permute-start.7
  6.1 1.6 %collective-permute-done.1 = f32[40,128]{1,0:T(8,128)S(1)} collective-permute-done((f32[40,128]{1,0:T(8,128)S(1)}, f32[40,128]{1,0:T(8,128)S(1)}, u32[]{:S(2)}, u32[]{:S(2)}) %collective-permute-start.1) | collective-permute-done | bytes 20512 | tf_op jit(solution)/shard_map/ppermute | solution.py:602
  7.7 2.1 %collective-permute-start.2 = (f32[8,128]{1,0:T(8,128)S(1)}, f32[8,128]{1,0:T(8,128)S(1)}, u32[]{:S(2)}, u32[]{:S(2)}) collective-permute-start(f32[8,128]{1,0:T(8,128)S(1)} %y_send.1), channel_id=1, source_target_pairs={{0,4},{1,5},{2,6},{3,7},{4,0},{5,1},{6,2},{7,3},{8,12},{9,13},{10,... | collective-permute-start | bytes 12296 | tf_op jit(solution)/shard_map/ppermute | solution.py:46
  9.7 0.1 collective-permute-start.3
  9.8 1.6 %collective-permute-done.2.y1_ref.y2_ref = f32[8,128]{1,0:T(8,128)S(1)} collective-permute-done((f32[8,128]{1,0:T(8,128)S(1)}, f32[8,128]{1,0:T(8,128)S(1)}, u32[]{:S(2)}, u32[]{:S(2)}) %collective-permute-start.2) | collective-permute-done | bytes 4128 | tf_op jit(solution)/shard_map/ppermute | solution.py:46
  11.4 0.1 x_send.1
  11.5 2.1 %collective-permute-start.4 = (f32[32,128]{1,0:T(8,128)S(1)}, f32[32,128]{1,0:T(8,128)S(1)}, u32[]{:S(2)}, u32[]{:S(2)}) collective-permute-start(f32[32,128]{1,0:T(8,128)S(1)} %get-tuple-element.64), channel_id=1, source_target_pairs={{0,8},{1,9},{2,10},{3,11},{4,12},{5,13},{6,14},{7,15},{8,0},{9,1},... | collective-permute-start | bytes 49160 | tf_op jit(solution)/shard_map/ppermute | solution.py:46
  13.5 0.0 collective-permute-start.5
  13.6 0.0 copy-done.3
  13.6 0.0 copy-done.4
  13.6 0.0 copy-done.5
  13.6 0.0 copy-done.6
  13.6 0.0 copy-done.7
  13.6 0.0 copy-done.8
  13.6 0.9 %cells.1 = (f32[5,16,32,128]{3,2,1,0:T(8,128)S(1)}, f32[2,64,128]{2,1,0:T(8,128)S(1)}) custom-call(f32[8,128]{1,0:T(8,128)S(1)} %slice.12.layers_ref, s32[16,32,128]{2,1,0:T(8,128)S(1)} %copy-done.3, f32[1,16]{1,0:T(1,128)S(1)} %bitcast.7, f32[1,16]{1,0:T(1,128)S(1)} %bitcast.8, f32[1,16]{1,0:T(1,128)S(1)} %bitcast.9, f32[1,16]{1,0:T(1,128)S(1)} %bitcast.10, ...), custom_call_target="tpu_custom_call" | custom-call | flops 480000000 | bytes 2800000 | tf_op jit(solution)/shard_map/cells/pallas_call | solution.py:627
  14.5 1.3 %depth.1 = (f32[6,12,32,128]{3,2,1,0:T(8,128)S(1)}, f32[3,16,32,128]{3,2,1,0:T(8,128)S(1)}) custom-call(f32[6,16,32,128]{3,2,1,0:T(8,128)S(1)} %copy-done), custom_call_target="tpu_custom_call" | custom-call | flops 540000000 | bytes 3150000 | tf_op jit(solution)/shard_map/depth/pallas_call | solution.py:630
  15.8 0.0 collective-permute-done.3.y1_ref.y2_ref
  15.8 0.3 %planes.1.plane_ref = f32[3,16,32,128]{3,2,1,0:T(8,128)S(1)} custom-call(f32[6,16,32,128]{3,2,1,0:T(8,128)S(1)} %copy-done, f32[3,16,32,128]{3,2,1,0:T(8,128)S(1)} %get-tuple-element.60.along_ref, f32[96,128]{1,0:T(8,128)S(1)} %collective-permute-done.3.y1_ref.y2_ref, f32[96,128]{1,0:T(8,128)S(1)} %collective-permute-done.3.y1_ref.y2_ref), custom_call_target="tpu_custom_call" | custom-call | flops 240000000 | bytes 1400000 | tf_op jit(solution)/shard_map/planes/pallas_call | solution.py:633
  16.1 0.0 copy-start.2
  16.2 0.0 collective-permute-done.4.x1_ref
  16.2 0.0 collective-permute-done.5.x2_ref
  16.2 0.4 %metrics.1 = (f32[16,32,128]{2,1,0:T(8,128)S(1)}, f32[16,32,128]{2,1,0:T(8,128)S(1)}, f32[2,32,128]{2,1,0:T(8,128)S(1)}) custom-call(f32[2,64,128]{2,1,0:T(8,128)S(1)} %get-tuple-element.69.layers_ref, f32[48,128]{1,0:T(8,128)S(1)} %get-tuple-element.70.own, f32[8,128]{1,0:T(8,128)S(1)} %slice.10.x1_ref, f32[8,128]{1,0:T(8,128)S(1)} %slice.11.x2_ref), custom_call_target="tpu_custom_call" | custom-call | flops 660000000 | bytes 3850000 | tf_op jit(solution)/shard_map/metrics/pallas_call | solution.py:637
  16.6 0.0 collective-permute-done.6.z1_ref
  16.6 0.0 collective-permute-done.7.z2_ref
  16.6 0.6 %copy-done.2 = f32[3,16,32,128]{3,2,1,0:T(8,128)S(1)} copy-done((f32[3,16,32,128]{3,2,1,0:T(8,128)S(1)}, f32[3,16,32,128]{3,2,1,0:T(8,128)}, u32[]{:S(2)}) %copy-start.2) | copy-done | bytes 786456
  17.3 0.0 copy-start.1
  17.3 1.1 %velocity.1 = (f32[3,16,32,128]{3,2,1,0:T(8,128)S(1)}, f32[24,128]{1,0:T(8,128)S(1)}, f32[24,128]{1,0:T(8,128)S(1)}, f32[24,128]{1,0:T(8,128)S(1)}, f32[24,128]{...) custom-call(f32[3,16,32,128]{3,2,1,0:T(8,128)S(1)} %copy-done.2, ...), custom_call_target="tpu_custom_call" | custom-call | flops 900000000 | bytes 5250000 | tf_op jit(solution)/shard_map/velocity/pallas_call | solution.py:644
  18.4 0.6 %collective-permute-start.11 = (f32[3,2,32,128]{3,2,1,0:T(8,128)S(1)}, f32[3,2,32,128]{3,2,1,0:T(8,128)S(1)}, u32[]{:S(2)}, u32[]{:S(2)}) collective-permute-start(f32[3,2,32,128]{3,2,1,0:T(8,128)S(1)} %get-tuple-element.89), channel_id=1, source_target_pairs={{0,1},{1,0},{2,3},{3,2},{4,5},{5,4},{6,7},{7,6},{8,9},{9,8},{10,11... | collective-permute-start | bytes 294920 | tf_op jit(solution)/shard_map/ppermute | solution.py:46
  18.9 1.4 %collective-permute-start.12 = (f32[3,2,32,128]{3,2,1,0:T(8,128)S(1)}, f32[3,2,32,128]{3,2,1,0:T(8,128)S(1)}, u32[]{:S(2)}, u32[]{:S(2)}) collective-permute-start(f32[3,2,32,128]{3,2,1,0:T(8,128)S(1)} %get-tuple-element.90), channel_id=1, source_target_pairs={{0,3},{1,2},{2,1},{3,0},{4,7},{5,6},{6,5},{7,4},{8,11},{9,10},{10,... | collective-permute-start | bytes 294920 | tf_op jit(solution)/shard_map/ppermute | solution.py:46
  20.3 1.5 %collective-permute-start.10 = (f32[96,128]{1,0:T(8,128)S(1)}, f32[96,128]{1,0:T(8,128)S(1)}, u32[]{:S(2)}, u32[]{:S(2)}) collective-permute-start(f32[96,128]{1,0:T(8,128)S(1)} %get-tuple-element.88), channel_id=1, source_target_pairs={{0,4},{1,5},{2,6},{3,7},{4,0},{5,1},{6,2},{7,3},{8,12},{9,13},{10,... | collective-permute-start | bytes 147464 | tf_op jit(solution)/shard_map/ppermute | solution.py:46
  21.8 3.1 %collective-permute-start.8 = (f32[24,128]{1,0:T(8,128)S(1)}, f32[24,128]{1,0:T(8,128)S(1)}, u32[]{:S(2)}, u32[]{:S(2)}) collective-permute-start(f32[24,128]{1,0:T(8,128)S(1)} %get-tuple-element.84), channel_id=1, source_target_pairs={{0,8},{1,9},{2,10},{3,11},{4,12},{5,13},{6,14},{7,15},{8,0},{9,1},... | collective-permute-start | bytes 36872 | tf_op jit(solution)/shard_map/ppermute | solution.py:46
  24.9 0.0 collective-permute-start.9
  24.9 1.2 %velocity_inner.1 = (f32[3,16,32,128]{3,2,1,0:T(8,128)}, f32[3,12,32,128]{3,2,1,0:T(8,128)S(1)}, f32[3,16,32,128]{3,2,1,0:T(8,128)S(1)}) custom-call(f32[3,16,32,128]{3,2,1,0:T(8,128)S(1)} %get-tuple-element.80.vel_ref), custom_call_target="tpu_custom_call" | custom-call | flops 60000000 | bytes 350000 | tf_op jit(solution)/shard_map/velocity_inner/pallas_call | solution.py:654
  26.1 0.5 %collective-permute-done.8.x1_ref = f32[24,128]{1,0:T(8,128)S(1)} collective-permute-done((f32[24,128]{1,0:T(8,128)S(1)}, f32[24,128]{1,0:T(8,128)S(1)}, u32[]{:S(2)}, u32[]{:S(2)}) %collective-permute-start.8) | collective-permute-done | bytes 12320 | tf_op jit(solution)/shard_map/ppermute | solution.py:46
  26.6 0.0 collective-permute-done.9.x2_ref
  26.6 0.0 collective-permute-done.10.y1_ref.y2_ref
  26.6 0.0 collective-permute-done.11.z1_ref
  26.6 0.0 collective-permute-done.12.z2_ref
  26.6 0.0 copy-done.1
  26.6 2.5 %stress.1 = (f32[6,16,32,128]{3,2,1,0:T(8,128)}, f32[6,16,32,128]{3,2,1,0:T(8,128)}) custom-call(f32[3,16,32,128]{3,2,1,0:T(8,128)S(1)} %get-tuple-element.80.vel_ref, f32[6,16,32,128]{3,2,1,0:T(8,128)S(1)} %copy-done, f32[6,16,32,128]{3,2,1,0:T(8,128)S(1)} %copy-done.1, f32[5,16,32,128]{3,2,1,0:T(8,128)S(1)} %get-tuple-element.66.cells_ref, ...), custom_call_target="tpu_custom_call" | custom-call | flops 1680000000 | bytes 9800000 | tf_op jit(solution)/shard_map/stress/pallas_call | solution.py:662
  (6 shorter events, 0.0 us)
Async XLA Ops:
  0.6 1.5 %copy-start = (f32[6,16,32,128]{3,2,1,0:T(8,128)S(1)}, f32[6,16,32,128]{3,2,1,0:T(8,128)}, u32[]{:S(2)}) copy-start(f32[6,16,32,128]{3,2,1,0:T(8,128)} %stress_ref.4) | copy-start | bytes 4718596
  0.6 12.9 %copy-start.3 = (s32[16,32,128]{2,1,0:T(8,128)S(1)}, s32[16,32,128]{2,1,0:T(8,128)}, u32[]{:S(2)}) copy-start(s32[16,32,128]{2,1,0:T(8,128)} %material_ref) | copy-start | bytes 786436
  0.7 12.9 %copy-start.4 = (f32[16]{0:T(128)S(1)}, f32[16]{0:T(128)}, u32[]{:S(2)}) copy-start(f32[16]{0:T(128)} %param.16) | copy-start | bytes 196
  0.7 12.9 %copy-start.5 = (f32[16]{0:T(128)S(1)}, f32[16]{0:T(128)}, u32[]{:S(2)}) copy-start(f32[16]{0:T(128)} %param.17) | copy-start | bytes 196
  0.7 12.9 %copy-start.6 = (f32[16]{0:T(128)S(1)}, f32[16]{0:T(128)}, u32[]{:S(2)}) copy-start(f32[16]{0:T(128)} %param.18) | copy-start | bytes 196
  0.7 12.9 %copy-start.7 = (f32[16]{0:T(128)S(1)}, f32[16]{0:T(128)}, u32[]{:S(2)}) copy-start(f32[16]{0:T(128)} %param.19) | copy-start | bytes 196
  0.7 12.9 %copy-start.8 = (f32[16]{0:T(128)S(1)}, f32[16]{0:T(128)}, u32[]{:S(2)}) copy-start(f32[16]{0:T(128)} %param.20) | copy-start | bytes 196
  1.7 1.4 %collective-permute-start = (f32[40,128]{1,0:T(8,128)S(1)}, f32[40,128]{1,0:T(8,128)S(1)}, u32[]{:S(2)}, u32[]{:S(2)}) collective-permute-start(f32[40,128]{1,0:T(8,128)S(1)} %terrain_piece.1), channel_id=1, source_target_pairs={{0,1},{1,0},{2,3},{3,2},{4,5},{5,4},{6,7},{7,6},{8,9},{9,8},{10,11... | collective-permute-start | bytes 61448 | tf_op jit(solution)/shard_map/ppermute | solution.py:602
  3.0 4.6 %collective-permute-start.1 = (f32[40,128]{1,0:T(8,128)S(1)}, f32[40,128]{1,0:T(8,128)S(1)}, u32[]{:S(2)}, u32[]{:S(2)}) collective-permute-start(f32[40,128]{1,0:T(8,128)S(1)} %add.6), channel_id=1, source_target_pairs={{0,2},{1,3},{2,0},{3,1},{4,6},{5,7},{6,4},{7,5},{8,10},{9,11},{10,... | collective-permute-start | bytes 61448 | tf_op jit(solution)/shard_map/ppermute | solution.py:602
  5.9 10.7 %collective-permute-start.6 = (f32[6,2,32,128]{3,2,1,0:T(8,128)S(1)}, f32[6,2,32,128]{3,2,1,0:T(8,128)S(1)}, u32[]{:S(2)}, u32[]{:S(2)}) collective-permute-start(f32[6,2,32,128]{3,2,1,0:T(8,128)S(1)} %get-tuple-element.76), channel_id=1, source_target_pairs={{0,1},{1,0},{2,3},{3,2},{4,5},{5,4},{6,7},{7,6},{8,9},{9,8},{10,11... | collective-permute-start | bytes 589832 | tf_op jit(solution)/shard_map/ppermute | solution.py:46
  5.9 10.8 %collective-permute-start.7 = (f32[6,2,32,128]{3,2,1,0:T(8,128)S(1)}, f32[6,2,32,128]{3,2,1,0:T(8,128)S(1)}, u32[]{:S(2)}, u32[]{:S(2)}) collective-permute-start(f32[6,2,32,128]{3,2,1,0:T(8,128)S(1)} %get-tuple-element.77), channel_id=1, source_target_pairs={{0,3},{1,2},{2,1},{3,0},{4,7},{5,6},{6,5},{7,4},{8,11},{9,10},{10,... | collective-permute-start | bytes 589832 | tf_op jit(solution)/shard_map/ppermute | solution.py:46
  7.7 3.7 %collective-permute-start.2 = (f32[8,128]{1,0:T(8,128)S(1)}, f32[8,128]{1,0:T(8,128)S(1)}, u32[]{:S(2)}, u32[]{:S(2)}) collective-permute-start(f32[8,128]{1,0:T(8,128)S(1)} %y_send.1), channel_id=1, source_target_pairs={{0,4},{1,5},{2,6},{3,7},{4,0},{5,1},{6,2},{7,3},{8,12},{9,13},{10,... | collective-permute-start | bytes 12296 | tf_op jit(solution)/shard_map/ppermute | solution.py:46
  9.7 6.1 %collective-permute-start.3 = (f32[96,128]{1,0:T(8,128)S(1)}, f32[96,128]{1,0:T(8,128)S(1)}, u32[]{:S(2)}, u32[]{:S(2)}) collective-permute-start(f32[96,128]{1,0:T(8,128)S(1)} %get-tuple-element.61), channel_id=1, source_target_pairs={{0,4},{1,5},{2,6},{3,7},{4,0},{5,1},{6,2},{7,3},{8,12},{9,13},{10,... | collective-permute-start | bytes 147464 | tf_op jit(solution)/shard_map/ppermute | solution.py:46
  11.5 4.7 %collective-permute-start.4 = (f32[32,128]{1,0:T(8,128)S(1)}, f32[32,128]{1,0:T(8,128)S(1)}, u32[]{:S(2)}, u32[]{:S(2)}) collective-permute-start(f32[32,128]{1,0:T(8,128)S(1)} %get-tuple-element.64), channel_id=1, source_target_pairs={{0,8},{1,9},{2,10},{3,11},{4,12},{5,13},{6,14},{7,15},{8,0},{9,1},... | collective-permute-start | bytes 49160 | tf_op jit(solution)/shard_map/ppermute | solution.py:46
  13.5 2.6 %collective-permute-start.5 = (f32[32,128]{1,0:T(8,128)S(1)}, f32[32,128]{1,0:T(8,128)S(1)}, u32[]{:S(2)}, u32[]{:S(2)}) collective-permute-start(f32[32,128]{1,0:T(8,128)S(1)} %get-tuple-element.65), channel_id=1, source_target_pairs={{0,1},{1,0},{2,3},{3,2},{4,5},{5,4},{6,7},{7,6},{8,16},{9,17},{10,... | collective-permute-start | bytes 49160 | tf_op jit(solution)/shard_map/ppermute | solution.py:46
  16.1 1.1 %copy-start.2 = (f32[3,16,32,128]{3,2,1,0:T(8,128)S(1)}, f32[3,16,32,128]{3,2,1,0:T(8,128)}, u32[]{:S(2)}) copy-start(f32[3,16,32,128]{3,2,1,0:T(8,128)} %velocity_ref.1) | copy-start | bytes 2359300
  17.3 9.3 %copy-start.1 = (f32[6,16,32,128]{3,2,1,0:T(8,128)S(1)}, f32[6,16,32,128]{3,2,1,0:T(8,128)}, u32[]{:S(2)}) copy-start(f32[6,16,32,128]{3,2,1,0:T(8,128)} %memory_ref.1) | copy-start | bytes 4718596
  18.4 8.2 %collective-permute-start.11 = (f32[3,2,32,128]{3,2,1,0:T(8,128)S(1)}, f32[3,2,32,128]{3,2,1,0:T(8,128)S(1)}, u32[]{:S(2)}, u32[]{:S(2)}) collective-permute-start(f32[3,2,32,128]{3,2,1,0:T(8,128)S(1)} %get-tuple-element.89), channel_id=1, source_target_pairs={{0,1},{1,0},{2,3},{3,2},{4,5},{5,4},{6,7},{7,6},{8,9},{9,8},{10,11... | collective-permute-start | bytes 294920 | tf_op jit(solution)/shard_map/ppermute | solution.py:46
  18.9 7.7 %collective-permute-start.12 = (f32[3,2,32,128]{3,2,1,0:T(8,128)S(1)}, f32[3,2,32,128]{3,2,1,0:T(8,128)S(1)}, u32[]{:S(2)}, u32[]{:S(2)}) collective-permute-start(f32[3,2,32,128]{3,2,1,0:T(8,128)S(1)} %get-tuple-element.90), channel_id=1, source_target_pairs={{0,3},{1,2},{2,1},{3,0},{4,7},{5,6},{6,5},{7,4},{8,11},{9,10},{10,... | collective-permute-start | bytes 294920 | tf_op jit(solution)/shard_map/ppermute | solution.py:46
  20.3 6.3 %collective-permute-start.10 = (f32[96,128]{1,0:T(8,128)S(1)}, f32[96,128]{1,0:T(8,128)S(1)}, u32[]{:S(2)}, u32[]{:S(2)}) collective-permute-start(f32[96,128]{1,0:T(8,128)S(1)} %get-tuple-element.88), channel_id=1, source_target_pairs={{0,4},{1,5},{2,6},{3,7},{4,0},{5,1},{6,2},{7,3},{8,12},{9,13},{10,... | collective-permute-start | bytes 147464 | tf_op jit(solution)/shard_map/ppermute | solution.py:46
  21.8 4.8 %collective-permute-start.8 = (f32[24,128]{1,0:T(8,128)S(1)}, f32[24,128]{1,0:T(8,128)S(1)}, u32[]{:S(2)}, u32[]{:S(2)}) collective-permute-start(f32[24,128]{1,0:T(8,128)S(1)} %get-tuple-element.84), channel_id=1, source_target_pairs={{0,8},{1,9},{2,10},{3,11},{4,12},{5,13},{6,14},{7,15},{8,0},{9,1},... | collective-permute-start | bytes 36872 | tf_op jit(solution)/shard_map/ppermute | solution.py:46
  24.9 1.7 %collective-permute-start.9 = (f32[24,128]{1,0:T(8,128)S(1)}, f32[24,128]{1,0:T(8,128)S(1)}, u32[]{:S(2)}, u32[]{:S(2)}) collective-permute-start(f32[24,128]{1,0:T(8,128)S(1)} %get-tuple-element.85), channel_id=1, source_target_pairs={{0,1},{1,0},{2,3},{3,2},{4,5},{5,4},{6,7},{7,6},{8,16},{9,17},{10,... | collective-permute-start | bytes 36872 | tf_op jit(solution)/shard_map/ppermute | solution.py:46

commit v6 on v5

--- a/solution.py
+++ b/solution.py
@@ -257,11 +257,40 @@
     return (lane < 2) | (lane >= lane.shape[-1] - 2)
 
 
-def periodic_x(tile):
-    nx = tile.shape[-1]
-    return 8.0 * (pltpu.roll(tile, nx - 1, 1) - pltpu.roll(tile, 1, 1)) - (
-        pltpu.roll(tile, nx - 2, 1) - pltpu.roll(tile, 2, 1)
+def x_weights(nx):
+    ahead = (
+        lax.broadcasted_iota(jnp.int32, (nx, nx), 0) - lax.broadcasted_iota(jnp.int32, (nx, nx), 1)
     )
+    weights = jnp.zeros((nx, nx), F32)
+    for offset, weight in ((1, 8.0), (-1, -8.0), (2, -1.0), (-2, 1.0)):
+        weights = jnp.where((ahead == offset) | (ahead == offset + nx) | (ahead == offset - nx), weight, weights)
+    weights = weights.astype(jnp.bfloat16)
+    return jnp.concatenate([weights] * 3, axis=0)
+
+
+def periodic_x(value, weights):
+    high = value.astype(jnp.bfloat16)
+    rest = value - high.astype(F32)
+    middle = rest.astype(jnp.bfloat16)
+    low = (rest - middle.astype(F32)).astype(jnp.bfloat16)
+    return jnp.dot(
+        jnp.concatenate([high, middle, low], axis=1), weights, preferred_element_type=F32
+    )
+
+
+def along_all(ref, comps, out_ref, group=16):
+    _, nz, ny, nx = out_ref.shape
+    group = next(d for d in range(group, 0, -1) if nz % d == 0)
+    weights = x_weights(nx)
+
+    @pl.loop(0, nz // group)
+    def _(j):
+        layers = pl.ds(j * group, group)
+        rows = [ref[c, layers].reshape(group * ny, nx) for c in comps]
+        result = periodic_x(jnp.concatenate(rows, axis=0), weights)
+        for i in range(len(comps)):
+            part = result[i * group * ny : (i + 1) * group * ny]
+            out_ref[i, layers] = part.reshape(group, ny, nx)
 
 
 def lookup(row, tile):
@@ -369,20 +398,20 @@
     over(0, nz, 4, layer)
 
 
-def depth_kernel(stress_ref, depth_ref, along_ref):
+def depth_kernel(stress_ref, velocity_hbm, depth_ref, along_ref, velocity_ref, sem):
+    load = pltpu.make_async_copy(velocity_hbm, velocity_ref, sem)
+    load.start()
     _, nz, ny, _ = stress_ref.shape
-    tiles = ny // SUB
-
-    def along(k):
-        for t in range(tiles):
-            for c, comp in enumerate((0, 3, 4)):
-                along_ref[c, k, tile_rows(t), :] = periodic_x(stress_ref[comp, k, tile_rows(t), :])
-
-    over(0, nz, 4, along)
-    over(2, nz - 2, 4, lambda k: inner_depth(stress_ref, depth_ref, 6, k, tiles))
-
-
-def plane_kernel(sizes, stress_ref, along_ref, y1_ref, y2_ref, plane_ref, tall):
+    along_all(stress_ref, (0, 3, 4), along_ref)
+    over(2, nz - 2, 4, lambda k: inner_depth(stress_ref, depth_ref, 6, k, ny // SUB))
+    load.wait()
+
+
+def plane_kernel(
+    sizes, stress_ref, along_ref, y1_ref, y2_ref, z1_ref, z2_ref, plane_ref, outer_ref, tall, zb, za
+):
+    depth_halos(sizes[2], zb, za, z1_ref, z2_ref)
+    outer_depth(stress_ref, zb, za, outer_ref, 6, stress_ref.shape[1], stress_ref.shape[2] // SUB)
     _, nz, ny, nx = stress_ref.shape
     tiles = ny // SUB
     of_y = (3, 1, 5)
@@ -399,17 +428,15 @@
 
 
 def velocity_kernel(
-    sizes, velocity_ref, stress_ref, cells_ref, inner_ref, plane_ref, factor_ref, mz_ref, slope_ref,
-    x1_ref, x2_ref, z1_ref, z2_ref, low_ref, high_ref, out_ref, vlow_ref, vhigh_ref, vx1_ref, vx2_ref, vz1_ref, vz2_ref,
+    sizes, velocity_ref, cells_ref, inner_ref, outer_ref, plane_ref, factor_ref, mz_ref, slope_ref,
+    x1_ref, x2_ref, low_ref, high_ref, out_ref, vlow_ref, vhigh_ref, vx1_ref, vx2_ref, vz1_ref, vz2_ref,
     *rest,
 ):
-    *vy_refs, edge, zb, za, outer_ref = rest
+    *vy_refs, edge = rest
     _, nz, ny, nx = velocity_ref.shape
     tiles = ny // SUB
     lane = lanes_of((SUB, nx))
     fill_edges(sizes[0], edge, x1_ref, x2_ref, low_ref, high_ref)
-    depth_halos(sizes[2], zb, za, z1_ref, z2_ref)
-    outer_depth(stress_ref, zb, za, outer_ref, 6, nz, tiles)
 
     def layer(k, depth_ref, spot):
         for t in range(tiles):
@@ -450,12 +477,7 @@
     _, nz, ny, nx = vel_ref.shape
     tiles = ny // SUB
 
-    def along(k):
-        for t in range(tiles):
-            for c in range(3):
-                along_ref[c, k, tile_rows(t), :] = periodic_x(vel_ref[c, k, tile_rows(t), :])
-
-    over(0, nz, 4, along)
+    along_all(vel_ref, (0, 1, 2), along_ref)
     over(2, nz - 2, 4, lambda k: inner_depth(vel_ref, depth_ref, 3, k, tiles))
     store.wait()
 
@@ -598,8 +620,12 @@
         slab = lax.psum(slab, "gz")
     else:
         bit = 1
+        rounds = pair_swaps(sizes, "gz")
         while bit < n_gz:
-            slab = slab + lax.ppermute(slab, "gz", [(i, i ^ bit) for i in range(n_gz)])
+            if n_gz == 4:
+                slab = slab + lax.ppermute(slab, tuple(sizes), rounds[bit - 1])
+            else:
+                slab = slab + lax.ppermute(slab, "gz", [(i, i ^ bit) for i in range(n_gz)])
             if bit == 1:
                 slab, z1, z2 = tied((slab, z1, z2))
             bit *= 2
@@ -627,12 +653,20 @@
     cells, spread = call(
         cell_kernel, [(5, nz, ny, nx), (2, all_layers, nx)], [VM] * 7, name="cells", cost=0.8
     )(slab[ny:], material, *[table[None] for table in tables])
-    inner_k, along = call(
-        depth_kernel, [(6, nz - 4, ny, nx), velocity.shape], [VM], name="depth", cost=0.9
-    )(stress_vm)
-    plane = call(
-        functools.partial(plane_kernel, counts), [velocity.shape], [VM] * 4, [tall], name="planes", cost=0.4
-    )(stress_vm, along, y1, y2)[0]
+    inner_k, along, velocity_vm = call(
+        depth_kernel,
+        [(6, nz - 4, ny, nx), velocity.shape, velocity.shape],
+        [VM, HB],
+        [DMA],
+        name="depth", cost=2.2,
+    )(stress_vm, in_hbm(velocity))
+    plane, outer_k = call(
+        functools.partial(plane_kernel, counts),
+        [velocity.shape, (6, 4, ny, nx)],
+        [VM] * 6,
+        [tall] + depth(6),
+        name="planes", cost=0.6,
+    )(stress_vm, along, y1, y2, z1, z2)
     plane, cells, x1, x2 = tied((plane, cells, x1, x2))
     factor, mz, slope = call(
         functools.partial(metric_kernel, counts),
@@ -644,10 +678,10 @@
     vel, vlow, vhigh, vx1, vx2, vz1, vz2, *vys = call(
         functools.partial(velocity_kernel, counts),
         [velocity.shape] + [(xs, nx)] * 4 + [(3, 2, ny, nx)] * 2 + [(faces, nx)] * y_rounds,
-        [VM] * 14,
-        [edge] + depth(6) + [pltpu.VMEM((6, 4, ny, nx), F32)],
+        [VM] * 12,
+        [edge],
         name="velocity", cost=1.5,
-    )(velocity, stress_vm, cells, inner_k, plane, factor, mz, slope, x1, x2, z1, z2, low, high)
+    )(velocity_vm, cells, inner_k, outer_k, plane, factor, mz, slope, x1, x2, low, high)
     vz1, vz2 = exchange(sizes, "gz", vz1, vz2)
     vy1, vy2 = exchange(sizes, "gy", vys[0], vys[-1])
     vx1, vx2 = exchange(sizes, "gx", vx1, vx2)

time: 29.3 us -> 27.9 us (0.952)
  local copies, waits for them, and re-layouts: 0.68 us -> 0.05 us
  Pallas kernels: 9.02 us -> 8.64 us
    unnamed x18 -> x16, local copies, waits for them, and re-layouts: 0.67 us -> 0.04 us
    ppermute x2, waiting for transfers between devices: 2.12 us -> 1.64 us  [local(): slab = slab + lax.ppermute(slab, tuple(sizes), rounds[bit - 1])]
    ppermute x11, waiting for transfers between devices: 2.06 us -> 2.37 us  [exchange(): lax.ppermute(v, tuple(sizes), r)]
    pallas_call x1, Pallas kernels: 1.19 us -> 0.89 us  [local(): call(velocity_inner_kernel, [velocity.shape, (3, nz - 4, ny, nx), velocit...]
  transfers between devices with their start and end apart: 13 -> 13, of which waited for: 4 -> 4; matrix products, arithmetic and copies ran while one was open for 0% -> 0% of each run, Pallas kernels for 16% -> 13%
where the time goes in v6:
time: 27.9 us; the launch traced here: 27.7 us
  starting transfers between devices  14.2 us (51%)
  Pallas kernels  8.64 us (31%)
  waiting for transfers between devices  4.02 us (14%)
  between operations  0.87 us (3%)
    ppermute x11, starting transfers between devices, exchange(): lax.ppermute(v, tuple(sizes), r)  11 us
    ppermute x2, starting transfers between devices, local(): slab = slab + lax.ppermute(slab, tuple(sizes), rounds[bit - 1])  3.15 us
    pallas_call x1, Pallas kernels, local(): call(functools.partial(stress_kernel, counts), [stress.shape, stress.shap...  2.53 us
    ppermute x11, waiting for transfers between devices, exchange(): lax.ppermute(v, tuple(sizes), r)  2.37 us
    ppermute x2, waiting for transfers between devices, local(): slab = slab + lax.ppermute(slab, tuple(sizes), rounds[bit - 1])  1.64 us
    pallas_call x1, Pallas kernels, local(): call(depth_kernel, [(6, nz - 4, ny, nx), velocity.shape, velocity.shape],...  1.14 us
    pallas_call x1, Pallas kernels, local(): call(functools.partial(velocity_kernel, counts), [velocity.shape] + [(xs,...  1.02 us
    pallas_call x1, Pallas kernels, local(): call(terrain_piece_kernel, [(rows, nx)], [HB] * 3, [pltpu.VMEM(elevation....  0.94 us
  transfers between devices with their start and end apart: 13, of which 4 were waited for; matrix products, arithmetic and copies ran while one was open for 0% of the time, Pallas kernels for 13%

profile of v6, /device:TPU:0, one launch (start us, length us, event | category | flops | bytes accessed | tf_op | source)
XLA Modules:
  0.0 27.7 jit_solution(4413835893167427920)
XLA Ops:
  0.6 0.0 copy-start
  0.6 0.9 %terrain_piece.1 = f32[40,128]{1,0:T(8,128)S(1)} custom-call(s32[32,32]{1,0:T(8,128)} %elev_hbm.1, f32[1,16]{1,0:T(1,128)} %bitcast.12, f32[1,16]{1,0:T(1,128)} %bitcast.13), custom_call_target="tpu_custom_call" | custom-call | flops 480000000 | bytes 2800000 | tf_op jit(solution)/shard_map/terrain_piece/pallas_call | solution.py:594
  1.6 0.5 %collective-permute-start = (f32[40,128]{1,0:T(8,128)S(1)}, f32[40,128]{1,0:T(8,128)S(1)}, u32[]{:S(2)}, u32[]{:S(2)}) collective-permute-start(f32[40,128]{1,0:T(8,128)S(1)} %terrain_piece.1), channel_id=1, source_target_pairs={{0,1},{1,0},{2,3},{3,2},{4,5},{5,4},{6,7},{7,6},{8,9},{9,8},{10,11... | collective-permute-start | bytes 61448 | tf_op jit(solution)/shard_map/ppermute | solution.py:626
  2.1 0.0 copy-done
  2.1 0.3 %pack_stress.1 = (f32[24,128]{1,0:T(8,128)S(1)}, f32[24,128]{1,0:T(8,128)S(1)}, f32[24,128]{1,0:T(8,128)S(1)}, f32[24,128]{1,0:T(8,128)S(1)}, f32[6,2,32,128]{3,...) custom-call(f32[6,16,32,128]{3,2,1,0:T(8,128)S(1)} %copy-done), custom_call_target="tpu_custom_call" | custom-call | flops 300000000 | bytes 1750000 | tf_op jit(solution)/shard_map/pack_stress/pallas_call | solution.py:613
  2.4 0.5 %collective-permute-done = f32[40,128]{1,0:T(8,128)S(1)} collective-permute-done((f32[40,128]{1,0:T(8,128)S(1)}, f32[40,128]{1,0:T(8,128)S(1)}, u32[]{:S(2)}, u32[]{:S(2)}) %collective-permute-start) | collective-permute-done | bytes 20512 | tf_op jit(solution)/shard_map/ppermute | solution.py:626
  3.0 2.6 %collective-permute-start.1 = (f32[40,128]{1,0:T(8,128)S(1)}, f32[40,128]{1,0:T(8,128)S(1)}, u32[]{:S(2)}, u32[]{:S(2)}) collective-permute-start(f32[40,128]{1,0:T(8,128)S(1)} %add.6), channel_id=1, source_target_pairs={{0,3},{1,2},{2,1},{3,0},{4,7},{5,6},{6,5},{7,4},{8,11},{9,10},{10,... | collective-permute-start | bytes 61448 | tf_op jit(solution)/shard_map/ppermute | solution.py:626
  5.6 0.3 %collective-permute-start.4 = (f32[6,2,32,128]{3,2,1,0:T(8,128)S(1)}, f32[6,2,32,128]{3,2,1,0:T(8,128)S(1)}, u32[]{:S(2)}, u32[]{:S(2)}) collective-permute-start(f32[6,2,32,128]{3,2,1,0:T(8,128)S(1)} %get-tuple-element.66), channel_id=1, source_target_pairs={{0,1},{1,0},{2,3},{3,2},{4,5},{5,4},{6,7},{7,6},{8,9},{9,8},{10,11... | collective-permute-start | bytes 589832 | tf_op jit(solution)/shard_map/ppermute | solution.py:46
  5.9 0.1 collective-permute-start.5
  6.0 1.1 %collective-permute-done.1 = f32[40,128]{1,0:T(8,128)S(1)} collective-permute-done((f32[40,128]{1,0:T(8,128)S(1)}, f32[40,128]{1,0:T(8,128)S(1)}, u32[]{:S(2)}, u32[]{:S(2)}) %collective-permute-start.1) | collective-permute-done | bytes 20512 | tf_op jit(solution)/shard_map/ppermute | solution.py:626
  7.1 2.0 %collective-permute-start.2 = (f32[8,128]{1,0:T(8,128)S(1)}, f32[8,128]{1,0:T(8,128)S(1)}, u32[]{:S(2)}, u32[]{:S(2)}) collective-permute-start(f32[8,128]{1,0:T(8,128)S(1)} %y_send.1), channel_id=1, source_target_pairs={{0,4},{1,5},{2,6},{3,7},{4,0},{5,1},{6,2},{7,3},{8,12},{9,13},{10,... | collective-permute-start | bytes 12296 | tf_op jit(solution)/shard_map/ppermute | solution.py:46
  9.1 0.1 collective-permute-start.3
  9.2 1.6 %collective-permute-done.2.y1_ref.y2_ref = f32[8,128]{1,0:T(8,128)S(1)} collective-permute-done((f32[8,128]{1,0:T(8,128)S(1)}, f32[8,128]{1,0:T(8,128)S(1)}, u32[]{:S(2)}, u32[]{:S(2)}) %collective-permute-start.2) | collective-permute-done | bytes 4128 | tf_op jit(solution)/shard_map/ppermute | solution.py:46
  10.8 0.1 x_send.1
  10.9 0.0 copy-start.2
  10.9 0.0 copy-start.3
  10.9 0.0 copy-start.4
  10.9 0.0 copy-start.5
  10.9 0.0 copy-start.6
  10.9 0.0 copy-start.7
  10.9 2.0 %collective-permute-start.6 = (f32[32,128]{1,0:T(8,128)S(1)}, f32[32,128]{1,0:T(8,128)S(1)}, u32[]{:S(2)}, u32[]{:S(2)}) collective-permute-start(f32[32,128]{1,0:T(8,128)S(1)} %get-tuple-element.71), channel_id=1, source_target_pairs={{0,8},{1,9},{2,10},{3,11},{4,12},{5,13},{6,14},{7,15},{8,0},{9,1},... | collective-permute-start | bytes 49160 | tf_op jit(solution)/shard_map/ppermute | solution.py:46
  13.0 0.0 collective-permute-start.7
  13.0 1.1 %depth.1 = (f32[6,12,32,128]{3,2,1,0:T(8,128)S(1)}, f32[3,16,32,128]{3,2,1,0:T(8,128)S(1)}, f32[3,16,32,128]{3,2,1,0:T(8,128)S(1)}) custom-call(f32[6,16,32,128]{3,2,1,0:T(8,128)S(1)} %copy-done, f32[3,16,32,128]{3,2,1,0:T(8,128)} %velocity_hbm.1), custom_call_target="tpu_custom_call" | custom-call | flops 1320000000 | bytes 7700000 | tf_op jit(solution)/shard_map/depth/pallas_call | solution.py:656
  14.1 0.0 copy-done.2
  14.1 0.0 copy-done.3
  14.2 0.0 copy-done.4
  14.2 0.0 copy-done.5
  14.2 0.0 copy-done.6
  14.2 0.0 copy-done.7
  14.2 0.9 %cells.1 = (f32[5,16,32,128]{3,2,1,0:T(8,128)S(1)}, f32[2,64,128]{2,1,0:T(8,128)S(1)}) custom-call(f32[8,128]{1,0:T(8,128)S(1)} %slice.12.layers_ref, s32[16,32,128]{2,1,0:T(8,128)S(1)} %copy-done.2, f32[1,16]{1,0:T(1,128)S(1)} %bitcast.7, f32[1,16]{1,0:T(1,128)S(1)} %bitcast.8, f32[1,16]{1,0:T(1,128)S(1)} %bitcast.9, f32[1,16]{1,0:T(1,128)S(1)} %bitcast.10, ...), custom_call_target="tpu_custom_call" | custom-call | flops 480000000 | bytes 2800000 | tf_op jit(solution)/shard_map/cells/pallas_call | solution.py:653
  15.1 0.0 collective-permute-done.3.y1_ref.y2_ref
  15.1 0.0 collective-permute-done.4.z1_ref
  15.1 0.0 collective-permute-done.5.z2_ref
  15.1 0.4 %planes.1 = (f32[3,16,32,128]{3,2,1,0:T(8,128)S(1)}, f32[6,4,32,128]{3,2,1,0:T(8,128)S(1)}) custom-call(f32[6,16,32,128]{3,2,1,0:T(8,128)S(1)} %copy-done, f32[3,16,32,128]{3,2,1,0:T(8,128)S(1)} %get-tuple-element.64.along_ref, f32[96,128]{1,0:T(8,128)S(1)} %collective-permute-done.3.y1_ref.y2_ref, f32[96,128]{1,0:T(8,128)S(1)} %collective-permute-done.3.y1_ref.y2_ref, ...), custom_call_target="tpu_custom_call" | custom-call | flops 360000000 | bytes 2100000 | tf_op jit(solution)/shard_map/planes/pallas_call | solution.py:663
  15.5 0.0 collective-permute-done.6.x1_ref
  15.6 0.0 collective-permute-done.7.x2_ref
  15.6 0.4 %metrics.1 = (f32[16,32,128]{2,1,0:T(8,128)S(1)}, f32[16,32,128]{2,1,0:T(8,128)S(1)}, f32[2,32,128]{2,1,0:T(8,128)S(1)}) custom-call(f32[2,64,128]{2,1,0:T(8,128)S(1)} %get-tuple-element.77.layers_ref, f32[48,128]{1,0:T(8,128)S(1)} %get-tuple-element.78.own, f32[8,128]{1,0:T(8,128)S(1)} %slice.10.x1_ref, f32[8,128]{1,0:T(8,128)S(1)} %slice.11.x2_ref), custom_call_target="tpu_custom_call" | custom-call | flops 660000000 | bytes 3850000 | tf_op jit(solution)/shard_map/metrics/pallas_call | solution.py:671
  16.0 0.0 copy-start.1
  16.0 1.0 %velocity.1 = (f32[3,16,32,128]{3,2,1,0:T(8,128)S(1)}, f32[24,128]{1,0:T(8,128)S(1)}, f32[24,128]{1,0:T(8,128)S(1)}, f32[24,128]{1,0:T(8,128)S(1)}, f32[24,128]{...) custom-call(f32[3,16,32,128]{3,2,1,0:T(8,128)S(1)} %get-tuple-element.63.veloc, ...), custom_call_target="tpu_custom_call" | custom-call | flops 900000000 | bytes 5250000 | tf_op jit(solution)/shard_map/velocity/pallas_call | solution.py:678
  17.1 0.6 %collective-permute-start.11 = (f32[3,2,32,128]{3,2,1,0:T(8,128)S(1)}, f32[3,2,32,128]{3,2,1,0:T(8,128)S(1)}, u32[]{:S(2)}, u32[]{:S(2)}) collective-permute-start(f32[3,2,32,128]{3,2,1,0:T(8,128)S(1)} %get-tuple-element.95), channel_id=1, source_target_pairs={{0,1},{1,0},{2,3},{3,2},{4,5},{5,4},{6,7},{7,6},{8,9},{9,8},{10,11... | collective-permute-start | bytes 294920 | tf_op jit(solution)/shard_map/ppermute | solution.py:46
  17.7 1.3 %collective-permute-start.12 = (f32[3,2,32,128]{3,2,1,0:T(8,128)S(1)}, f32[3,2,32,128]{3,2,1,0:T(8,128)S(1)}, u32[]{:S(2)}, u32[]{:S(2)}) collective-permute-start(f32[3,2,32,128]{3,2,1,0:T(8,128)S(1)} %get-tuple-element.96), channel_id=1, source_target_pairs={{0,3},{1,2},{2,1},{3,0},{4,7},{5,6},{6,5},{7,4},{8,11},{9,10},{10,... | collective-permute-start | bytes 294920 | tf_op jit(solution)/shard_map/ppermute | solution.py:46
  19.0 1.5 %collective-permute-start.10 = (f32[96,128]{1,0:T(8,128)S(1)}, f32[96,128]{1,0:T(8,128)S(1)}, u32[]{:S(2)}, u32[]{:S(2)}) collective-permute-start(f32[96,128]{1,0:T(8,128)S(1)} %get-tuple-element.94), channel_id=1, source_target_pairs={{0,4},{1,5},{2,6},{3,7},{4,0},{5,1},{6,2},{7,3},{8,12},{9,13},{10,... | collective-permute-start | bytes 147464 | tf_op jit(solution)/shard_map/ppermute | solution.py:46
  20.5 3.0 %collective-permute-start.8 = (f32[24,128]{1,0:T(8,128)S(1)}, f32[24,128]{1,0:T(8,128)S(1)}, u32[]{:S(2)}, u32[]{:S(2)}) collective-permute-start(f32[24,128]{1,0:T(8,128)S(1)} %get-tuple-element.90), channel_id=1, source_target_pairs={{0,8},{1,9},{2,10},{3,11},{4,12},{5,13},{6,14},{7,15},{8,0},{9,1},... | collective-permute-start | bytes 36872 | tf_op jit(solution)/shard_map/ppermute | solution.py:46
  23.5 0.0 collective-permute-start.9
  23.5 0.9 %velocity_inner.1 = (f32[3,16,32,128]{3,2,1,0:T(8,128)}, f32[3,12,32,128]{3,2,1,0:T(8,128)S(1)}, f32[3,16,32,128]{3,2,1,0:T(8,128)S(1)}) custom-call(f32[3,16,32,128]{3,2,1,0:T(8,128)S(1)} %get-tuple-element.86.vel_ref), custom_call_target="tpu_custom_call" | custom-call | flops 60000000 | bytes 350000 | tf_op jit(solution)/shard_map/velocity_inner/pallas_call | solution.py:688
  24.4 0.8 %collective-permute-done.8.x1_ref = f32[24,128]{1,0:T(8,128)S(1)} collective-permute-done((f32[24,128]{1,0:T(8,128)S(1)}, f32[24,128]{1,0:T(8,128)S(1)}, u32[]{:S(2)}, u32[]{:S(2)}) %collective-permute-start.8) | collective-permute-done | bytes 12320 | tf_op jit(solution)/shard_map/ppermute | solution.py:46
  25.2 0.0 collective-permute-done.9.x2_ref
  25.2 0.0 collective-permute-done.10.y1_ref.y2_ref
  25.2 0.0 collective-permute-done.11.z1_ref
  25.2 0.0 collective-permute-done.12.z2_ref
  25.2 0.0 copy-done.1
  25.2 2.5 %stress.1 = (f32[6,16,32,128]{3,2,1,0:T(8,128)}, f32[6,16,32,128]{3,2,1,0:T(8,128)}) custom-call(f32[3,16,32,128]{3,2,1,0:T(8,128)S(1)} %get-tuple-element.86.vel_ref, f32[6,16,32,128]{3,2,1,0:T(8,128)S(1)} %copy-done, f32[6,16,32,128]{3,2,1,0:T(8,128)S(1)} %copy-done.1, f32[5,16,32,128]{3,2,1,0:T(8,128)S(1)} %get-tuple-element.73.cells_ref, ...), custom_call_target="tpu_custom_call" | custom-call | flops 1680000000 | bytes 9800000 | tf_op jit(solution)/shard_map/stress/pallas_call | solution.py:696
  (6 shorter events, 0.0 us)
Async XLA Ops:
  0.6 1.5 %copy-start = (f32[6,16,32,128]{3,2,1,0:T(8,128)S(1)}, f32[6,16,32,128]{3,2,1,0:T(8,128)}, u32[]{:S(2)}) copy-start(f32[6,16,32,128]{3,2,1,0:T(8,128)} %stress_ref.3) | copy-start | bytes 4718596
  1.6 1.4 %collective-permute-start = (f32[40,128]{1,0:T(8,128)S(1)}, f32[40,128]{1,0:T(8,128)S(1)}, u32[]{:S(2)}, u32[]{:S(2)}) collective-permute-start(f32[40,128]{1,0:T(8,128)S(1)} %terrain_piece.1), channel_id=1, source_target_pairs={{0,1},{1,0},{2,3},{3,2},{4,5},{5,4},{6,7},{7,6},{8,9},{9,8},{10,11... | collective-permute-start | bytes 61448 | tf_op jit(solution)/shard_map/ppermute | solution.py:626
  3.0 4.1 %collective-permute-start.1 = (f32[40,128]{1,0:T(8,128)S(1)}, f32[40,128]{1,0:T(8,128)S(1)}, u32[]{:S(2)}, u32[]{:S(2)}) collective-permute-start(f32[40,128]{1,0:T(8,128)S(1)} %add.6), channel_id=1, source_target_pairs={{0,3},{1,2},{2,1},{3,0},{4,7},{5,6},{6,5},{7,4},{8,11},{9,10},{10,... | collective-permute-start | bytes 61448 | tf_op jit(solution)/shard_map/ppermute | solution.py:626
  5.6 9.5 %collective-permute-start.4 = (f32[6,2,32,128]{3,2,1,0:T(8,128)S(1)}, f32[6,2,32,128]{3,2,1,0:T(8,128)S(1)}, u32[]{:S(2)}, u32[]{:S(2)}) collective-permute-start(f32[6,2,32,128]{3,2,1,0:T(8,128)S(1)} %get-tuple-element.66), channel_id=1, source_target_pairs={{0,1},{1,0},{2,3},{3,2},{4,5},{5,4},{6,7},{7,6},{8,9},{9,8},{10,11... | collective-permute-start | bytes 589832 | tf_op jit(solution)/shard_map/ppermute | solution.py:46
  5.9 9.2 %collective-permute-start.5 = (f32[6,2,32,128]{3,2,1,0:T(8,128)S(1)}, f32[6,2,32,128]{3,2,1,0:T(8,128)S(1)}, u32[]{:S(2)}, u32[]{:S(2)}) collective-permute-start(f32[6,2,32,128]{3,2,1,0:T(8,128)S(1)} %get-tuple-element.67), channel_id=1, source_target_pairs={{0,3},{1,2},{2,1},{3,0},{4,7},{5,6},{6,5},{7,4},{8,11},{9,10},{10,... | collective-permute-start | bytes 589832 | tf_op jit(solution)/shard_map/ppermute | solution.py:46
  7.1 3.7 %collective-permute-start.2 = (f32[8,128]{1,0:T(8,128)S(1)}, f32[8,128]{1,0:T(8,128)S(1)}, u32[]{:S(2)}, u32[]{:S(2)}) collective-permute-start(f32[8,128]{1,0:T(8,128)S(1)} %y_send.1), channel_id=1, source_target_pairs={{0,4},{1,5},{2,6},{3,7},{4,0},{5,1},{6,2},{7,3},{8,12},{9,13},{10,... | collective-permute-start | bytes 12296 | tf_op jit(solution)/shard_map/ppermute | solution.py:46
  9.1 6.0 %collective-permute-start.3 = (f32[96,128]{1,0:T(8,128)S(1)}, f32[96,128]{1,0:T(8,128)S(1)}, u32[]{:S(2)}, u32[]{:S(2)}) collective-permute-start(f32[96,128]{1,0:T(8,128)S(1)} %get-tuple-element.65), channel_id=1, source_target_pairs={{0,4},{1,5},{2,6},{3,7},{4,0},{5,1},{6,2},{7,3},{8,12},{9,13},{10,... | collective-permute-start | bytes 147464 | tf_op jit(solution)/shard_map/ppermute | solution.py:46
  10.9 3.3 %copy-start.2 = (s32[16,32,128]{2,1,0:T(8,128)S(1)}, s32[16,32,128]{2,1,0:T(8,128)}, u32[]{:S(2)}) copy-start(s32[16,32,128]{2,1,0:T(8,128)} %material_ref) | copy-start | bytes 786436
  10.9 3.3 %copy-start.3 = (f32[16]{0:T(128)S(1)}, f32[16]{0:T(128)}, u32[]{:S(2)}) copy-start(f32[16]{0:T(128)} %param.16) | copy-start | bytes 196
  10.9 3.3 %copy-start.4 = (f32[16]{0:T(128)S(1)}, f32[16]{0:T(128)}, u32[]{:S(2)}) copy-start(f32[16]{0:T(128)} %param.17) | copy-start | bytes 196
  10.9 3.3 %copy-start.5 = (f32[16]{0:T(128)S(1)}, f32[16]{0:T(128)}, u32[]{:S(2)}) copy-start(f32[16]{0:T(128)} %param.18) | copy-start | bytes 196
  10.9 3.3 %copy-start.6 = (f32[16]{0:T(128)S(1)}, f32[16]{0:T(128)}, u32[]{:S(2)}) copy-start(f32[16]{0:T(128)} %param.19) | copy-start | bytes 196
  10.9 3.3 %copy-start.7 = (f32[16]{0:T(128)S(1)}, f32[16]{0:T(128)}, u32[]{:S(2)}) copy-start(f32[16]{0:T(128)} %param.20) | copy-start | bytes 196
  10.9 4.6 %collective-permute-start.6 = (f32[32,128]{1,0:T(8,128)S(1)}, f32[32,128]{1,0:T(8,128)S(1)}, u32[]{:S(2)}, u32[]{:S(2)}) collective-permute-start(f32[32,128]{1,0:T(8,128)S(1)} %get-tuple-element.71), channel_id=1, source_target_pairs={{0,8},{1,9},{2,10},{3,11},{4,12},{5,13},{6,14},{7,15},{8,0},{9,1},... | collective-permute-start | bytes 49160 | tf_op jit(solution)/shard_map/ppermute | solution.py:46
  13.0 2.6 %collective-permute-start.7 = (f32[32,128]{1,0:T(8,128)S(1)}, f32[32,128]{1,0:T(8,128)S(1)}, u32[]{:S(2)}, u32[]{:S(2)}) collective-permute-start(f32[32,128]{1,0:T(8,128)S(1)} %get-tuple-element.72), channel_id=1, source_target_pairs={{0,1},{1,0},{2,3},{3,2},{4,5},{5,4},{6,7},{7,6},{8,16},{9,17},{10,... | collective-permute-start | bytes 49160 | tf_op jit(solution)/shard_map/ppermute | solution.py:46
  16.0 9.2 %copy-start.1 = (f32[6,16,32,128]{3,2,1,0:T(8,128)S(1)}, f32[6,16,32,128]{3,2,1,0:T(8,128)}, u32[]{:S(2)}) copy-start(f32[6,16,32,128]{3,2,1,0:T(8,128)} %memory_ref.1) | copy-start | bytes 4718596
  17.1 8.1 %collective-permute-start.11 = (f32[3,2,32,128]{3,2,1,0:T(8,128)S(1)}, f32[3,2,32,128]{3,2,1,0:T(8,128)S(1)}, u32[]{:S(2)}, u32[]{:S(2)}) collective-permute-start(f32[3,2,32,128]{3,2,1,0:T(8,128)S(1)} %get-tuple-element.95), channel_id=1, source_target_pairs={{0,1},{1,0},{2,3},{3,2},{4,5},{5,4},{6,7},{7,6},{8,9},{9,8},{10,11... | collective-permute-start | bytes 294920 | tf_op jit(solution)/shard_map/ppermute | solution.py:46
  17.7 7.5 %collective-permute-start.12 = (f32[3,2,32,128]{3,2,1,0:T(8,128)S(1)}, f32[3,2,32,128]{3,2,1,0:T(8,128)S(1)}, u32[]{:S(2)}, u32[]{:S(2)}) collective-permute-start(f32[3,2,32,128]{3,2,1,0:T(8,128)S(1)} %get-tuple-element.96), channel_id=1, source_target_pairs={{0,3},{1,2},{2,1},{3,0},{4,7},{5,6},{6,5},{7,4},{8,11},{9,10},{10,... | collective-permute-start | bytes 294920 | tf_op jit(solution)/shard_map/ppermute | solution.py:46
  19.0 6.2 %collective-permute-start.10 = (f32[96,128]{1,0:T(8,128)S(1)}, f32[96,128]{1,0:T(8,128)S(1)}, u32[]{:S(2)}, u32[]{:S(2)}) collective-permute-start(f32[96,128]{1,0:T(8,128)S(1)} %get-tuple-element.94), channel_id=1, source_target_pairs={{0,4},{1,5},{2,6},{3,7},{4,0},{5,1},{6,2},{7,3},{8,12},{9,13},{10,... | collective-permute-start | bytes 147464 | tf_op jit(solution)/shard_map/ppermute | solution.py:46
  20.5 4.7 %collective-permute-start.8 = (f32[24,128]{1,0:T(8,128)S(1)}, f32[24,128]{1,0:T(8,128)S(1)}, u32[]{:S(2)}, u32[]{:S(2)}) collective-permute-start(f32[24,128]{1,0:T(8,128)S(1)} %get-tuple-element.90), channel_id=1, source_target_pairs={{0,8},{1,9},{2,10},{3,11},{4,12},{5,13},{6,14},{7,15},{8,0},{9,1},... | collective-permute-start | bytes 36872 | tf_op jit(solution)/shard_map/ppermute | solution.py:46
  23.5 1.7 %collective-permute-start.9 = (f32[24,128]{1,0:T(8,128)S(1)}, f32[24,128]{1,0:T(8,128)S(1)}, u32[]{:S(2)}, u32[]{:S(2)}) collective-permute-start(f32[24,128]{1,0:T(8,128)S(1)} %get-tuple-element.91), channel_id=1, source_target_pairs={{0,1},{1,0},{2,3},{3,2},{4,5},{5,4},{6,7},{7,6},{8,16},{9,17},{10,... | collective-permute-start | bytes 36872 | tf_op jit(solution)/shard_map/ppermute | solution.py:46

commit v7 on v6

--- a/solution.py
+++ b/solution.py
@@ -41,9 +41,13 @@
     return rounds
 
 
-def exchange(sizes, axis, first, second):
-    rounds = pair_swaps(sizes, axis)
-    got = [lax.ppermute(v, tuple(sizes), r) for v, r in zip((first, second), rounds)]
+def exchange(sizes, axis, first, second, second_first=False):
+    rounds = list(zip((first, second), pair_swaps(sizes, axis)))
+    if second_first:
+        rounds = rounds[::-1]
+    got = [lax.ppermute(v, tuple(sizes), r) for v, r in rounds]
+    if second_first:
+        got = got[::-1]
     return (got[0], got[-1]) if got else (first, second)
 
 
@@ -631,28 +635,9 @@
             bit *= 2
     z1, z2 = exchange(sizes, "gz", z1, z2)
     ts = call(y_send_kernel, [(SUB, nx)] * y_rounds, [VM], name="y_send", cost=0.02)(slab)
-    ts, ys = tied((ts, ys))
+    ts, ys, stress_vm = tied((ts, ys, stress_vm))
     t1, t2 = exchange(sizes, "gy", ts[0], ts[-1])
     y1, y2 = exchange(sizes, "gy", ys[0], ys[-1])
-    terrain, x1, x2 = call(
-        functools.partial(x_send_kernel, n_gy),
-        [(ny + 2 * PAD, nx)] + [(xs + SUB, nx)] * 2,
-        [VM] * 5,
-        name="x_send", cost=0.1,
-    )(slab, t1, t2, x1, x2)
-    x1, x2, material, stress_vm = tied((x1, x2, material, stress_vm))
-    x1, x2 = exchange(sizes, "gx", x1, x2)
-    edge = pltpu.VMEM((3, 2, SUB, nx), F32)
-    tall = pltpu.VMEM((3, nz, ny + 2 * PAD, nx), F32)
-
-    def depth(comps):
-        return [pltpu.VMEM((comps, 2, ny, nx), F32)] * 2
-
-    tables = (buoyancy, lame_lambda, shear_modulus, relax_time, anelastic_weight)
-    all_layers = -(-n_gz * nz // SUB) * SUB
-    cells, spread = call(
-        cell_kernel, [(5, nz, ny, nx), (2, all_layers, nx)], [VM] * 7, name="cells", cost=0.8
-    )(slab[ny:], material, *[table[None] for table in tables])
     inner_k, along, velocity_vm = call(
         depth_kernel,
         [(6, nz - 4, ny, nx), velocity.shape, velocity.shape],
@@ -660,6 +645,26 @@
         [DMA],
         name="depth", cost=2.2,
     )(stress_vm, in_hbm(velocity))
+    x1, x2, inner_k = tied((x1, x2, inner_k))
+    terrain, x1, x2 = call(
+        functools.partial(x_send_kernel, n_gy),
+        [(ny + 2 * PAD, nx)] + [(xs + SUB, nx)] * 2,
+        [VM] * 5,
+        name="x_send", cost=0.1,
+    )(slab, t1, t2, x1, x2)
+    x1, x2, material = tied((x1, x2, material))
+    x1, x2 = exchange(sizes, "gx", x1, x2, True)
+    edge = pltpu.VMEM((3, 2, SUB, nx), F32)
+    tall = pltpu.VMEM((3, nz, ny + 2 * PAD, nx), F32)
+
+    def depth(comps):
+        return [pltpu.VMEM((comps, 2, ny, nx), F32)] * 2
+
+    tables = (buoyancy, lame_lambda, shear_modulus, relax_time, anelastic_weight)
+    all_layers = -(-n_gz * nz // SUB) * SUB
+    cells, spread = call(
+        cell_kernel, [(5, nz, ny, nx), (2, all_layers, nx)], [VM] * 7, name="cells", cost=0.8
+    )(slab[ny:], material, *[table[None] for table in tables])
     plane, outer_k = call(
         functools.partial(plane_kernel, counts),
         [velocity.shape, (6, 4, ny, nx)],

time: 27.9 us -> 27.1 us (0.971)
  waiting for transfers between devices: 4.02 us -> 3.22 us
    ppermute x11, waiting for transfers between devices: 2.37 us -> 1.57 us  [exchange(): got = [lax.ppermute(v, tuple(sizes), r) for v, r in rounds]]
  transfers between devices with their start and end apart: 13 -> 13, of which waited for: 4 -> 5; matrix products, arithmetic and copies ran while one was open for 0% -> 0% of each run, Pallas kernels for 13% -> 14%
where the time goes in v7:
time: 27.1 us; the launch traced here: 26.9 us
  starting transfers between devices  14.1 us (52%)
  Pallas kernels  8.63 us (32%)
  waiting for transfers between devices  3.22 us (12%)
  between operations  0.85 us (3%)
    ppermute x11, starting transfers between devices, exchange(): got = [lax.ppermute(v, tuple(sizes), r) for v, r in rounds]  11 us
    ppermute x2, starting transfers between devices, local(): slab = slab + lax.ppermute(slab, tuple(sizes), rounds[bit - 1])  3.15 us
    pallas_call x1, Pallas kernels, local(): call(functools.partial(stress_kernel, counts), [stress.shape, stress.shap...  2.53 us
    ppermute x2, waiting for transfers between devices, local(): slab = slab + lax.ppermute(slab, tuple(sizes), rounds[bit - 1])  1.64 us
    ppermute x11, waiting for transfers between devices, exchange(): got = [lax.ppermute(v, tuple(sizes), r) for v, r in rounds]  1.57 us
    pallas_call x1, Pallas kernels, local(): call(depth_kernel, [(6, nz - 4, ny, nx), velocity.shape, velocity.shape],...  1.14 us
    pallas_call x1, Pallas kernels, local(): call(functools.partial(velocity_kernel, counts), [velocity.shape] + [(xs,...  1.02 us
    pallas_call x1, Pallas kernels, local(): call(terrain_piece_kernel, [(rows, nx)], [HB] * 3, [pltpu.VMEM(elevation....  0.94 us
  transfers between devices with their start and end apart: 13, of which 5 were waited for; matrix products, arithmetic and copies ran while one was open for 0% of the time, Pallas kernels for 14%

profile of v7, /device:TPU:0, one launch (start us, length us, event | category | flops | bytes accessed | tf_op | source)
XLA Modules:
  0.0 26.9 jit_solution(12379614126590456066)
XLA Ops:
  0.6 0.0 copy-start
  0.6 0.9 %terrain_piece.1 = f32[40,128]{1,0:T(8,128)S(1)} custom-call(s32[32,32]{1,0:T(8,128)} %elev_hbm.1, f32[1,16]{1,0:T(1,128)} %bitcast.12, f32[1,16]{1,0:T(1,128)} %bitcast.13), custom_call_target="tpu_custom_call" | custom-call | flops 480000000 | bytes 2800000 | tf_op jit(solution)/shard_map/terrain_piece/pallas_call | solution.py:598
  1.6 0.5 %collective-permute-start = (f32[40,128]{1,0:T(8,128)S(1)}, f32[40,128]{1,0:T(8,128)S(1)}, u32[]{:S(2)}, u32[]{:S(2)}) collective-permute-start(f32[40,128]{1,0:T(8,128)S(1)} %terrain_piece.1), channel_id=1, source_target_pairs={{0,1},{1,0},{2,3},{3,2},{4,5},{5,4},{6,7},{7,6},{8,9},{9,8},{10,11... | collective-permute-start | bytes 61448 | tf_op jit(solution)/shard_map/ppermute | solution.py:630
  2.1 0.0 copy-done
  2.1 0.3 %pack_stress.1 = (f32[24,128]{1,0:T(8,128)S(1)}, f32[24,128]{1,0:T(8,128)S(1)}, f32[24,128]{1,0:T(8,128)S(1)}, f32[24,128]{1,0:T(8,128)S(1)}, f32[6,2,32,128]{3,...) custom-call(f32[6,16,32,128]{3,2,1,0:T(8,128)S(1)} %copy-done), custom_call_target="tpu_custom_call" | custom-call | flops 300000000 | bytes 1750000 | tf_op jit(solution)/shard_map/pack_stress/pallas_call | solution.py:617
  2.4 0.5 %collective-permute-done = f32[40,128]{1,0:T(8,128)S(1)} collective-permute-done((f32[40,128]{1,0:T(8,128)S(1)}, f32[40,128]{1,0:T(8,128)S(1)}, u32[]{:S(2)}, u32[]{:S(2)}) %collective-permute-start) | collective-permute-done | bytes 20512 | tf_op jit(solution)/shard_map/ppermute | solution.py:630
  3.0 2.6 %collective-permute-start.1 = (f32[40,128]{1,0:T(8,128)S(1)}, f32[40,128]{1,0:T(8,128)S(1)}, u32[]{:S(2)}, u32[]{:S(2)}) collective-permute-start(f32[40,128]{1,0:T(8,128)S(1)} %add.6), channel_id=1, source_target_pairs={{0,3},{1,2},{2,1},{3,0},{4,7},{5,6},{6,5},{7,4},{8,11},{9,10},{10,... | collective-permute-start | bytes 61448 | tf_op jit(solution)/shard_map/ppermute | solution.py:630
  5.6 0.3 %collective-permute-start.3 = (f32[6,2,32,128]{3,2,1,0:T(8,128)S(1)}, f32[6,2,32,128]{3,2,1,0:T(8,128)S(1)}, u32[]{:S(2)}, u32[]{:S(2)}) collective-permute-start(f32[6,2,32,128]{3,2,1,0:T(8,128)S(1)} %get-tuple-element.64), channel_id=1, source_target_pairs={{0,1},{1,0},{2,3},{3,2},{4,5},{5,4},{6,7},{7,6},{8,9},{9,8},{10,11... | collective-permute-start | bytes 589832 | tf_op jit(solution)/shard_map/ppermute | solution.py:48
  5.9 0.1 collective-permute-start.4
  6.0 1.1 %collective-permute-done.1 = f32[40,128]{1,0:T(8,128)S(1)} collective-permute-done((f32[40,128]{1,0:T(8,128)S(1)}, f32[40,128]{1,0:T(8,128)S(1)}, u32[]{:S(2)}, u32[]{:S(2)}) %collective-permute-start.1) | collective-permute-done | bytes 20512 | tf_op jit(solution)/shard_map/ppermute | solution.py:630
  7.1 0.0 copy-start.2
  7.1 0.0 copy-start.3
  7.1 0.0 copy-start.4
  7.2 0.0 copy-start.5
  7.2 0.0 copy-start.6
  7.2 0.0 copy-start.7
  7.2 2.0 %collective-permute-start.5 = (f32[8,128]{1,0:T(8,128)S(1)}, f32[8,128]{1,0:T(8,128)S(1)}, u32[]{:S(2)}, u32[]{:S(2)}) collective-permute-start(f32[8,128]{1,0:T(8,128)S(1)} %y_send.1), channel_id=1, source_target_pairs={{0,4},{1,5},{2,6},{3,7},{4,0},{5,1},{6,2},{7,3},{8,12},{9,13},{10,... | collective-permute-start | bytes 12296 | tf_op jit(solution)/shard_map/ppermute | solution.py:48
  9.2 0.1 collective-permute-start.2
  9.3 1.1 %depth.1 = (f32[6,12,32,128]{3,2,1,0:T(8,128)S(1)}, f32[3,16,32,128]{3,2,1,0:T(8,128)S(1)}, f32[3,16,32,128]{3,2,1,0:T(8,128)S(1)}) custom-call(f32[6,16,32,128]{3,2,1,0:T(8,128)S(1)} %copy-done, f32[3,16,32,128]{3,2,1,0:T(8,128)} %velocity_hbm.1), custom_call_target="tpu_custom_call" | custom-call | flops 1320000000 | bytes 7700000 | tf_op jit(solution)/shard_map/depth/pallas_call | solution.py:641
  10.4 0.4 %collective-permute-done.5.y1_ref.y2_ref = f32[8,128]{1,0:T(8,128)S(1)} collective-permute-done((f32[8,128]{1,0:T(8,128)S(1)}, f32[8,128]{1,0:T(8,128)S(1)}, u32[]{:S(2)}, u32[]{:S(2)}) %collective-permute-start.5) | collective-permute-done | bytes 4128 | tf_op jit(solution)/shard_map/ppermute | solution.py:48
  10.9 0.1 x_send.1
  11.0 2.0 %collective-permute-start.6 = (f32[32,128]{1,0:T(8,128)S(1)}, f32[32,128]{1,0:T(8,128)S(1)}, u32[]{:S(2)}, u32[]{:S(2)}) collective-permute-start(f32[32,128]{1,0:T(8,128)S(1)} %get-tuple-element.77), channel_id=1, source_target_pairs={{0,8},{1,9},{2,10},{3,11},{4,12},{5,13},{6,14},{7,15},{8,0},{9,1},... | collective-permute-start | bytes 49160 | tf_op jit(solution)/shard_map/ppermute | solution.py:48
  13.0 0.0 collective-permute-start.7
  13.0 0.0 copy-done.2
  13.0 0.0 copy-done.3
  13.0 0.0 copy-done.4
  13.0 0.0 copy-done.5
  13.0 0.0 copy-done.6
  13.0 0.0 copy-done.7
  13.0 0.9 %cells.1 = (f32[5,16,32,128]{3,2,1,0:T(8,128)S(1)}, f32[2,64,128]{2,1,0:T(8,128)S(1)}) custom-call(f32[8,128]{1,0:T(8,128)S(1)} %slice.12.layers_ref, s32[16,32,128]{2,1,0:T(8,128)S(1)} %copy-done.2, f32[1,16]{1,0:T(1,128)S(1)} %bitcast.7, f32[1,16]{1,0:T(1,128)S(1)} %bitcast.8, f32[1,16]{1,0:T(1,128)S(1)} %bitcast.9, f32[1,16]{1,0:T(1,128)S(1)} %bitcast.10, ...), custom_call_target="tpu_custom_call" | custom-call | flops 480000000 | bytes 2800000 | tf_op jit(solution)/shard_map/cells/pallas_call | solution.py:665
  13.9 0.0 collective-permute-done.2.y1_ref.y2_ref
  14.0 0.0 collective-permute-done.3.z1_ref
  14.0 0.0 collective-permute-done.4.z2_ref
  14.0 0.4 %planes.1 = (f32[3,16,32,128]{3,2,1,0:T(8,128)S(1)}, f32[6,4,32,128]{3,2,1,0:T(8,128)S(1)}) custom-call(f32[6,16,32,128]{3,2,1,0:T(8,128)S(1)} %copy-done, f32[3,16,32,128]{3,2,1,0:T(8,128)S(1)} %get-tuple-element.62.along_ref, f32[96,128]{1,0:T(8,128)S(1)} %collective-permute-done.2.y1_ref.y2_ref, f32[96,128]{1,0:T(8,128)S(1)} %collective-permute-done.2.y1_ref.y2_ref, ...), custom_call_target="tpu_custom_call" | custom-call | flops 360000000 | bytes 2100000 | tf_op jit(solution)/shard_map/planes/pallas_call | solution.py:668
  14.4 0.3 %collective-permute-done.6.x1_ref = f32[32,128]{1,0:T(8,128)S(1)} collective-permute-done((f32[32,128]{1,0:T(8,128)S(1)}, f32[32,128]{1,0:T(8,128)S(1)}, u32[]{:S(2)}, u32[]{:S(2)}) %collective-permute-start.6) | collective-permute-done | bytes 16416 | tf_op jit(solution)/shard_map/ppermute | solution.py:48
  14.7 0.0 collective-permute-done.7.x2_ref
  14.8 0.4 %metrics.1 = (f32[16,32,128]{2,1,0:T(8,128)S(1)}, f32[16,32,128]{2,1,0:T(8,128)S(1)}, f32[2,32,128]{2,1,0:T(8,128)S(1)}) custom-call(f32[2,64,128]{2,1,0:T(8,128)S(1)} %get-tuple-element.83.layers_ref, f32[48,128]{1,0:T(8,128)S(1)} %get-tuple-element.84.own, f32[8,128]{1,0:T(8,128)S(1)} %slice.10.x1_ref, f32[8,128]{1,0:T(8,128)S(1)} %slice.11.x2_ref), custom_call_target="tpu_custom_call" | custom-call | flops 660000000 | bytes 3850000 | tf_op jit(solution)/shard_map/metrics/pallas_call | solution.py:676
  15.2 0.0 copy-start.1
  15.2 1.0 %velocity.1 = (f32[3,16,32,128]{3,2,1,0:T(8,128)S(1)}, f32[24,128]{1,0:T(8,128)S(1)}, f32[24,128]{1,0:T(8,128)S(1)}, f32[24,128]{1,0:T(8,128)S(1)}, f32[24,128]{...) custom-call(f32[3,16,32,128]{3,2,1,0:T(8,128)S(1)} %get-tuple-element.61.veloc, ...), custom_call_target="tpu_custom_call" | custom-call | flops 900000000 | bytes 5250000 | tf_op jit(solution)/shard_map/velocity/pallas_call | solution.py:683
  16.2 0.3 %collective-permute-start.11 = (f32[3,2,32,128]{3,2,1,0:T(8,128)S(1)}, f32[3,2,32,128]{3,2,1,0:T(8,128)S(1)}, u32[]{:S(2)}, u32[]{:S(2)}) collective-permute-start(f32[3,2,32,128]{3,2,1,0:T(8,128)S(1)} %get-tuple-element.101), channel_id=1, source_target_pairs={{0,1},{1,0},{2,3},{3,2},{4,5},{5,4},{6,7},{7,6},{8,9},{9,8},{10,11... | collective-permute-start | bytes 294920 | tf_op jit(solution)/shard_map/ppermute | solution.py:48
  16.5 1.9 %collective-permute-start.12 = (f32[3,2,32,128]{3,2,1,0:T(8,128)S(1)}, f32[3,2,32,128]{3,2,1,0:T(8,128)S(1)}, u32[]{:S(2)}, u32[]{:S(2)}) collective-permute-start(f32[3,2,32,128]{3,2,1,0:T(8,128)S(1)} %get-tuple-element.102), channel_id=1, source_target_pairs={{0,3},{1,2},{2,1},{3,0},{4,7},{5,6},{6,5},{7,4},{8,11},{9,10},{10,... | collective-permute-start | bytes 294920 | tf_op jit(solution)/shard_map/ppermute | solution.py:48
  18.5 1.5 %collective-permute-start.10 = (f32[96,128]{1,0:T(8,128)S(1)}, f32[96,128]{1,0:T(8,128)S(1)}, u32[]{:S(2)}, u32[]{:S(2)}) collective-permute-start(f32[96,128]{1,0:T(8,128)S(1)} %get-tuple-element.100), channel_id=1, source_target_pairs={{0,4},{1,5},{2,6},{3,7},{4,0},{5,1},{6,2},{7,3},{8,12},{9,13},{10,... | collective-permute-start | bytes 147464 | tf_op jit(solution)/shard_map/ppermute | solution.py:48
  20.0 2.7 %collective-permute-start.8 = (f32[24,128]{1,0:T(8,128)S(1)}, f32[24,128]{1,0:T(8,128)S(1)}, u32[]{:S(2)}, u32[]{:S(2)}) collective-permute-start(f32[24,128]{1,0:T(8,128)S(1)} %get-tuple-element.96), channel_id=1, source_target_pairs={{0,8},{1,9},{2,10},{3,11},{4,12},{5,13},{6,14},{7,15},{8,0},{9,1},... | collective-permute-start | bytes 36872 | tf_op jit(solution)/shard_map/ppermute | solution.py:48
  22.6 0.0 collective-permute-start.9
  22.6 0.9 %velocity_inner.1 = (f32[3,16,32,128]{3,2,1,0:T(8,128)}, f32[3,12,32,128]{3,2,1,0:T(8,128)S(1)}, f32[3,16,32,128]{3,2,1,0:T(8,128)S(1)}) custom-call(f32[3,16,32,128]{3,2,1,0:T(8,128)S(1)} %get-tuple-element.92.vel_ref), custom_call_target="tpu_custom_call" | custom-call | flops 60000000 | bytes 350000 | tf_op jit(solution)/shard_map/velocity_inner/pallas_call | solution.py:693
  23.5 0.8 %collective-permute-done.8.x1_ref = f32[24,128]{1,0:T(8,128)S(1)} collective-permute-done((f32[24,128]{1,0:T(8,128)S(1)}, f32[24,128]{1,0:T(8,128)S(1)}, u32[]{:S(2)}, u32[]{:S(2)}) %collective-permute-start.8) | collective-permute-done | bytes 12320 | tf_op jit(solution)/shard_map/ppermute | solution.py:48
  24.3 0.0 collective-permute-done.9.x2_ref
  24.3 0.0 collective-permute-done.10.y1_ref.y2_ref
  24.3 0.0 collective-permute-done.11.z1_ref
  24.3 0.0 collective-permute-done.12.z2_ref
  24.3 0.0 copy-done.1
  24.4 2.5 %stress.1 = (f32[6,16,32,128]{3,2,1,0:T(8,128)}, f32[6,16,32,128]{3,2,1,0:T(8,128)}) custom-call(f32[3,16,32,128]{3,2,1,0:T(8,128)S(1)} %get-tuple-element.92.vel_ref, f32[6,16,32,128]{3,2,1,0:T(8,128)S(1)} %copy-done, f32[6,16,32,128]{3,2,1,0:T(8,128)S(1)} %copy-done.1, f32[5,16,32,128]{3,2,1,0:T(8,128)S(1)} %get-tuple-element.79.cells_ref, ...), custom_call_target="tpu_custom_call" | custom-call | flops 1680000000 | bytes 9800000 | tf_op jit(solution)/shard_map/stress/pallas_call | solution.py:701
  (6 shorter events, 0.0 us)
Async XLA Ops:
  0.6 1.5 %copy-start = (f32[6,16,32,128]{3,2,1,0:T(8,128)S(1)}, f32[6,16,32,128]{3,2,1,0:T(8,128)}, u32[]{:S(2)}) copy-start(f32[6,16,32,128]{3,2,1,0:T(8,128)} %stress_ref.3) | copy-start | bytes 4718596
  1.6 1.4 %collective-permute-start = (f32[40,128]{1,0:T(8,128)S(1)}, f32[40,128]{1,0:T(8,128)S(1)}, u32[]{:S(2)}, u32[]{:S(2)}) collective-permute-start(f32[40,128]{1,0:T(8,128)S(1)} %terrain_piece.1), channel_id=1, source_target_pairs={{0,1},{1,0},{2,3},{3,2},{4,5},{5,4},{6,7},{7,6},{8,9},{9,8},{10,11... | collective-permute-start | bytes 61448 | tf_op jit(solution)/shard_map/ppermute | solution.py:630
  3.0 4.1 %collective-permute-start.1 = (f32[40,128]{1,0:T(8,128)S(1)}, f32[40,128]{1,0:T(8,128)S(1)}, u32[]{:S(2)}, u32[]{:S(2)}) collective-permute-start(f32[40,128]{1,0:T(8,128)S(1)} %add.6), channel_id=1, source_target_pairs={{0,3},{1,2},{2,1},{3,0},{4,7},{5,6},{6,5},{7,4},{8,11},{9,10},{10,... | collective-permute-start | bytes 61448 | tf_op jit(solution)/shard_map/ppermute | solution.py:630
  5.6 8.4 %collective-permute-start.3 = (f32[6,2,32,128]{3,2,1,0:T(8,128)S(1)}, f32[6,2,32,128]{3,2,1,0:T(8,128)S(1)}, u32[]{:S(2)}, u32[]{:S(2)}) collective-permute-start(f32[6,2,32,128]{3,2,1,0:T(8,128)S(1)} %get-tuple-element.64), channel_id=1, source_target_pairs={{0,1},{1,0},{2,3},{3,2},{4,5},{5,4},{6,7},{7,6},{8,9},{9,8},{10,11... | collective-permute-start | bytes 589832 | tf_op jit(solution)/shard_map/ppermute | solution.py:48
  5.9 8.0 %collective-permute-start.4 = (f32[6,2,32,128]{3,2,1,0:T(8,128)S(1)}, f32[6,2,32,128]{3,2,1,0:T(8,128)S(1)}, u32[]{:S(2)}, u32[]{:S(2)}) collective-permute-start(f32[6,2,32,128]{3,2,1,0:T(8,128)S(1)} %get-tuple-element.65), channel_id=1, source_target_pairs={{0,3},{1,2},{2,1},{3,0},{4,7},{5,6},{6,5},{7,4},{8,11},{9,10},{10,... | collective-permute-start | bytes 589832 | tf_op jit(solution)/shard_map/ppermute | solution.py:48
  7.1 5.9 %copy-start.2 = (s32[16,32,128]{2,1,0:T(8,128)S(1)}, s32[16,32,128]{2,1,0:T(8,128)}, u32[]{:S(2)}) copy-start(s32[16,32,128]{2,1,0:T(8,128)} %material_ref) | copy-start | bytes 786436
  7.1 5.9 %copy-start.3 = (f32[16]{0:T(128)S(1)}, f32[16]{0:T(128)}, u32[]{:S(2)}) copy-start(f32[16]{0:T(128)} %param.16) | copy-start | bytes 196
  7.1 5.9 %copy-start.4 = (f32[16]{0:T(128)S(1)}, f32[16]{0:T(128)}, u32[]{:S(2)}) copy-start(f32[16]{0:T(128)} %param.17) | copy-start | bytes 196
  7.2 5.9 %copy-start.5 = (f32[16]{0:T(128)S(1)}, f32[16]{0:T(128)}, u32[]{:S(2)}) copy-start(f32[16]{0:T(128)} %param.18) | copy-start | bytes 196
  7.2 5.9 %copy-start.6 = (f32[16]{0:T(128)S(1)}, f32[16]{0:T(128)}, u32[]{:S(2)}) copy-start(f32[16]{0:T(128)} %param.19) | copy-start | bytes 196
  7.2 5.9 %copy-start.7 = (f32[16]{0:T(128)S(1)}, f32[16]{0:T(128)}, u32[]{:S(2)}) copy-start(f32[16]{0:T(128)} %param.20) | copy-start | bytes 196
  7.2 3.7 %collective-permute-start.5 = (f32[8,128]{1,0:T(8,128)S(1)}, f32[8,128]{1,0:T(8,128)S(1)}, u32[]{:S(2)}, u32[]{:S(2)}) collective-permute-start(f32[8,128]{1,0:T(8,128)S(1)} %y_send.1), channel_id=1, source_target_pairs={{0,4},{1,5},{2,6},{3,7},{4,0},{5,1},{6,2},{7,3},{8,12},{9,13},{10,... | collective-permute-start | bytes 12296 | tf_op jit(solution)/shard_map/ppermute | solution.py:48
  9.2 4.8 %collective-permute-start.2 = (f32[96,128]{1,0:T(8,128)S(1)}, f32[96,128]{1,0:T(8,128)S(1)}, u32[]{:S(2)}, u32[]{:S(2)}) collective-permute-start(f32[96,128]{1,0:T(8,128)S(1)} %get-tuple-element.63), channel_id=1, source_target_pairs={{0,4},{1,5},{2,6},{3,7},{4,0},{5,1},{6,2},{7,3},{8,12},{9,13},{10,... | collective-permute-start | bytes 147464 | tf_op jit(solution)/shard_map/ppermute | solution.py:48
  11.0 3.8 %collective-permute-start.6 = (f32[32,128]{1,0:T(8,128)S(1)}, f32[32,128]{1,0:T(8,128)S(1)}, u32[]{:S(2)}, u32[]{:S(2)}) collective-permute-start(f32[32,128]{1,0:T(8,128)S(1)} %get-tuple-element.77), channel_id=1, source_target_pairs={{0,8},{1,9},{2,10},{3,11},{4,12},{5,13},{6,14},{7,15},{8,0},{9,1},... | collective-permute-start | bytes 49160 | tf_op jit(solution)/shard_map/ppermute | solution.py:48
  13.0 1.8 %collective-permute-start.7 = (f32[32,128]{1,0:T(8,128)S(1)}, f32[32,128]{1,0:T(8,128)S(1)}, u32[]{:S(2)}, u32[]{:S(2)}) collective-permute-start(f32[32,128]{1,0:T(8,128)S(1)} %get-tuple-element.78), channel_id=1, source_target_pairs={{0,1},{1,0},{2,3},{3,2},{4,5},{5,4},{6,7},{7,6},{8,16},{9,17},{10,... | collective-permute-start | bytes 49160 | tf_op jit(solution)/shard_map/ppermute | solution.py:48
  15.2 9.2 %copy-start.1 = (f32[6,16,32,128]{3,2,1,0:T(8,128)S(1)}, f32[6,16,32,128]{3,2,1,0:T(8,128)}, u32[]{:S(2)}) copy-start(f32[6,16,32,128]{3,2,1,0:T(8,128)} %memory_ref.1) | copy-start | bytes 4718596
  16.2 8.1 %collective-permute-start.11 = (f32[3,2,32,128]{3,2,1,0:T(8,128)S(1)}, f32[3,2,32,128]{3,2,1,0:T(8,128)S(1)}, u32[]{:S(2)}, u32[]{:S(2)}) collective-permute-start(f32[3,2,32,128]{3,2,1,0:T(8,128)S(1)} %get-tuple-element.101), channel_id=1, source_target_pairs={{0,1},{1,0},{2,3},{3,2},{4,5},{5,4},{6,7},{7,6},{8,9},{9,8},{10,11... | collective-permute-start | bytes 294920 | tf_op jit(solution)/shard_map/ppermute | solution.py:48
  16.5 7.8 %collective-permute-start.12 = (f32[3,2,32,128]{3,2,1,0:T(8,128)S(1)}, f32[3,2,32,128]{3,2,1,0:T(8,128)S(1)}, u32[]{:S(2)}, u32[]{:S(2)}) collective-permute-start(f32[3,2,32,128]{3,2,1,0:T(8,128)S(1)} %get-tuple-element.102), channel_id=1, source_target_pairs={{0,3},{1,2},{2,1},{3,0},{4,7},{5,6},{6,5},{7,4},{8,11},{9,10},{10,... | collective-permute-start | bytes 294920 | tf_op jit(solution)/shard_map/ppermute | solution.py:48
  18.5 5.9 %collective-permute-start.10 = (f32[96,128]{1,0:T(8,128)S(1)}, f32[96,128]{1,0:T(8,128)S(1)}, u32[]{:S(2)}, u32[]{:S(2)}) collective-permute-start(f32[96,128]{1,0:T(8,128)S(1)} %get-tuple-element.100), channel_id=1, source_target_pairs={{0,4},{1,5},{2,6},{3,7},{4,0},{5,1},{6,2},{7,3},{8,12},{9,13},{10,... | collective-permute-start | bytes 147464 | tf_op jit(solution)/shard_map/ppermute | solution.py:48
  20.0 4.3 %collective-permute-start.8 = (f32[24,128]{1,0:T(8,128)S(1)}, f32[24,128]{1,0:T(8,128)S(1)}, u32[]{:S(2)}, u32[]{:S(2)}) collective-permute-start(f32[24,128]{1,0:T(8,128)S(1)} %get-tuple-element.96), channel_id=1, source_target_pairs={{0,8},{1,9},{2,10},{3,11},{4,12},{5,13},{6,14},{7,15},{8,0},{9,1},... | collective-permute-start | bytes 36872 | tf_op jit(solution)/shard_map/ppermute | solution.py:48
  22.6 1.7 %collective-permute-start.9 = (f32[24,128]{1,0:T(8,128)S(1)}, f32[24,128]{1,0:T(8,128)S(1)}, u32[]{:S(2)}, u32[]{:S(2)}) collective-permute-start(f32[24,128]{1,0:T(8,128)S(1)} %get-tuple-element.97), channel_id=1, source_target_pairs={{0,1},{1,0},{2,3},{3,2},{4,5},{5,4},{6,7},{7,6},{8,16},{9,17},{10,... | collective-permute-start | bytes 36872 | tf_op jit(solution)/shard_map/ppermute | solution.py:48

commit v8 on v7

--- a/solution.py
+++ b/solution.py
@@ -94,6 +94,16 @@
     stretch = jnp.concatenate([stretch_ref[...], fill], axis=1)
     both = jnp.where(row == 0, base, jnp.where(row == 1, stretch, 0.0))
     out_ref[ny:, :] = pltpu.roll(both, mine * nz, 1)
+
+
+def merge_kernel(first_ref, elev_ref, out_ref):
+    ny, width = elev_ref.shape
+    nx = out_ref.shape[1]
+    height = elev_ref[...].astype(F32) / 200.0
+    wide = jnp.concatenate([height, jnp.zeros((ny, nx - width), F32)], axis=1)
+    mate = lax.axis_index("gz") + jnp.where(even("gz"), 1, -1)
+    out_ref[:ny, :] = first_ref[:ny, :] + pltpu.roll(wide, mate * width, 1)
+    out_ref[ny:, :] = first_ref[ny:, :]
 
 
 def pack_sides(field, nz, ny, nx, low_ref, high_ref, out1_ref, out2_ref):
@@ -595,6 +605,9 @@
     n_gx, n_gy, n_gz = counts = tuple(sizes[a] for a in ("gx", "gy", "gz"))
     _, nz, ny, nx = velocity.shape
     rows = ny + SUB
+    rounds = pair_swaps(sizes, "gz")
+    if n_gz == 4:
+        piece = lax.ppermute(elevation, tuple(sizes), rounds[0])
     slab = call(
         terrain_piece_kernel,
         [(rows, nx)],
@@ -612,7 +625,22 @@
     xs = 3 * SUB
     y_rounds = min(2, n_gy - 1) if n_gy > 1 else 1
     z_face = (6, 2, ny, nx)
-    slab, stress = tied((slab, stress))
+    if n_gz == 4:
+        slab = call(merge_kernel, [(rows, nx)], [VM] * 2, name="merge", cost=0.1)(slab, piece)[0]
+        slab, stress = tied((slab, stress))
+        slab = slab + lax.ppermute(slab, tuple(sizes), rounds[1])
+        layers = slab[ny:]
+    elif n_gz & (n_gz - 1):
+        slab = lax.psum(slab, "gz")
+        layers = slab[ny:]
+    else:
+        bit = 1
+        while bit < n_gz:
+            slab = slab + lax.ppermute(slab, "gz", [(i, i ^ bit) for i in range(n_gz)])
+            if bit == 1:
+                slab, stress = tied((slab, stress))
+            bit *= 2
+        layers = slab[ny:]
     stress_vm = stress
     low, high, x1, x2, z1, z2, *ys = call(
         pack_kernel,
@@ -620,24 +648,13 @@
         [VM],
         name="pack_stress", cost=0.5,
     )(stress)
-    if n_gz & (n_gz - 1):
-        slab = lax.psum(slab, "gz")
-    else:
-        bit = 1
-        rounds = pair_swaps(sizes, "gz")
-        while bit < n_gz:
-            if n_gz == 4:
-                slab = slab + lax.ppermute(slab, tuple(sizes), rounds[bit - 1])
-            else:
-                slab = slab + lax.ppermute(slab, "gz", [(i, i ^ bit) for i in range(n_gz)])
-            if bit == 1:
-                slab, z1, z2 = tied((slab, z1, z2))
-            bit *= 2
     z1, z2 = exchange(sizes, "gz", z1, z2)
     ts = call(y_send_kernel, [(SUB, nx)] * y_rounds, [VM], name="y_send", cost=0.02)(slab)
-    ts, ys, stress_vm = tied((ts, ys, stress_vm))
+    ts, ys, stress_vm, layers = tied((ts, ys, stress_vm, layers))
     t1, t2 = exchange(sizes, "gy", ts[0], ts[-1])
     y1, y2 = exchange(sizes, "gy", ys[0], ys[-1])
+    if n_gz == 4:
+        layers = layers + lax.ppermute(layers, tuple(sizes), rounds[0])
     inner_k, along, velocity_vm = call(
         depth_kernel,
         [(6, nz - 4, ny, nx), velocity.shape, velocity.shape],
@@ -664,7 +681,7 @@
     all_layers = -(-n_gz * nz // SUB) * SUB
     cells, spread = call(
         cell_kernel, [(5, nz, ny, nx), (2, all_layers, nx)], [VM] * 7, name="cells", cost=0.8
-    )(slab[ny:], material, *[table[None] for table in tables])
+    )(layers, material, *[table[None] for table in tables])
     plane, outer_k = call(
         functools.partial(plane_kernel, counts),
         [velocity.shape, (6, 4, ny, nx)],

time: 27.1 us -> 26.4 us (0.974)
  waiting for transfers between devices: 3.22 us -> 2.33 us
  starting transfers between devices: 14.1 us -> 14.4 us
    ppermute x2 -> x3, waiting for transfers between devices: 1.64 us -> 0.97 us  [the longest x1 0.75 us: local(): slab = slab + lax.ppermute(slab, tuple(sizes), rounds[1])]
    ppermute x2 -> x3, starting transfers between devices: 3.15 us -> 3.15 us  [the longest x1 2.63 us: local(): slab = slab + lax.ppermute(slab, tuple(sizes), rounds[1])]
  transfers between devices with their start and end apart: 13 -> 14, of which waited for: 5 -> 5; matrix products, arithmetic and copies ran while one was open for 0% -> 0% of each run, Pallas kernels for 14% -> 17%
where the time goes in v8:
time: 26.4 us; the launch traced here: 26.2 us
  starting transfers between devices  14.4 us (55%)
  Pallas kernels  8.58 us (32%)
  waiting for transfers between devices  2.33 us (9%)
  between operations  0.87 us (3%)
    ppermute x11, starting transfers between devices, exchange(): got = [lax.ppermute(v, tuple(sizes), r) for v, r in rounds]  11.2 us
    ppermute x1, starting transfers between devices, local(): slab = slab + lax.ppermute(slab, tuple(sizes), rounds[1])  2.63 us
    pallas_call x1, Pallas kernels, local(): call(functools.partial(stress_kernel, counts), [stress.shape, stress.shap...  2.53 us
    ppermute x11, waiting for transfers between devices, exchange(): got = [lax.ppermute(v, tuple(sizes), r) for v, r in rounds]  1.36 us
    pallas_call x1, Pallas kernels, local(): call(depth_kernel, [(6, nz - 4, ny, nx), velocity.shape, velocity.shape],...  1.14 us
    pallas_call x1, Pallas kernels, local(): call(functools.partial(velocity_kernel, counts), [velocity.shape] + [(xs,...  1.02 us
    pallas_call x1, Pallas kernels, local(): call(cell_kernel, [(5, nz, ny, nx), (2, all_layers, nx)], [VM] * 7, name=...  0.89 us
    pallas_call x1, Pallas kernels, local(): call(velocity_inner_kernel, [velocity.shape, (3, nz - 4, ny, nx), velocit...  0.89 us
  transfers between devices with their start and end apart: 14, of which 5 were waited for; matrix products, arithmetic and copies ran while one was open for 0% of the time, Pallas kernels for 17%

profile of v8, /device:TPU:0, one launch (start us, length us, event | category | flops | bytes accessed | tf_op | source)
XLA Modules:
  0.0 26.2 jit_solution(402480882360270554)
XLA Ops:
  0.6 0.0 copy-start
  0.6 0.5 %collective-permute-start = (s32[32,32]{1,0:T(8,128)}, s32[32,32]{1,0:T(8,128)S(1)}, u32[]{:S(2)}, u32[]{:S(2)}) collective-permute-start(s32[32,32]{1,0:T(8,128)} %elev_hbm.1), channel_id=1, source_target_pairs={{0,1},{1,0},{2,3},{3,2},{4,5},{5,4},{6,7},{7,6},{8,9},{9,8},{10,11... | collective-permute-start | bytes 12296 | tf_op jit(solution)/shard_map/ppermute | solution.py:610
  1.2 0.8 %terrain_piece.1.first_ref = f32[40,128]{1,0:T(8,128)S(1)} custom-call(s32[32,32]{1,0:T(8,128)} %elev_hbm.1, f32[1,16]{1,0:T(1,128)} %bitcast.12, f32[1,16]{1,0:T(1,128)} %bitcast.13), custom_call_target="tpu_custom_call" | custom-call | flops 480000000 | bytes 2800000 | tf_op jit(solution)/shard_map/terrain_piece/pallas_call | solution.py:611
  2.0 0.2 collective-permute-done.elev_ref
  2.2 0.1 merge.1
  2.3 2.6 %collective-permute-start.1 = (f32[40,128]{1,0:T(8,128)S(1)}, f32[40,128]{1,0:T(8,128)S(1)}, u32[]{:S(2)}, u32[]{:S(2)}) collective-permute-start(f32[40,128]{1,0:T(8,128)S(1)} %merge.1), channel_id=1, source_target_pairs={{0,3},{1,2},{2,1},{3,0},{4,7},{5,6},{6,5},{7,4},{8,11},{9,10},{10,... | collective-permute-start | bytes 61448 | tf_op jit(solution)/shard_map/ppermute | solution.py:631
  4.9 0.0 copy-done
  4.9 0.3 %pack_stress.1 = (f32[24,128]{1,0:T(8,128)S(1)}, f32[24,128]{1,0:T(8,128)S(1)}, f32[24,128]{1,0:T(8,128)S(1)}, f32[24,128]{1,0:T(8,128)S(1)}, f32[6,2,32,128]{3,...) custom-call(f32[6,16,32,128]{3,2,1,0:T(8,128)S(1)} %copy-done), custom_call_target="tpu_custom_call" | custom-call | flops 300000000 | bytes 1750000 | tf_op jit(solution)/shard_map/pack_stress/pallas_call | solution.py:645
  5.2 0.4 %collective-permute-start.3 = (f32[6,2,32,128]{3,2,1,0:T(8,128)S(1)}, f32[6,2,32,128]{3,2,1,0:T(8,128)S(1)}, u32[]{:S(2)}, u32[]{:S(2)}) collective-permute-start(f32[6,2,32,128]{3,2,1,0:T(8,128)S(1)} %get-tuple-element.59), channel_id=1, source_target_pairs={{0,1},{1,0},{2,3},{3,2},{4,5},{5,4},{6,7},{7,6},{8,9},{9,8},{10,11... | collective-permute-start | bytes 589832 | tf_op jit(solution)/shard_map/ppermute | solution.py:48
  5.6 0.0 collective-permute-start.4
  5.7 0.7 %collective-permute-done.1 = f32[40,128]{1,0:T(8,128)S(1)} collective-permute-done((f32[40,128]{1,0:T(8,128)S(1)}, f32[40,128]{1,0:T(8,128)S(1)}, u32[]{:S(2)}, u32[]{:S(2)}) %collective-permute-start.1) | collective-permute-done | bytes 20512 | tf_op jit(solution)/shard_map/ppermute | solution.py:631
  6.4 0.0 copy-start.2
  6.4 0.0 copy-start.3
  6.4 0.0 copy-start.4
  6.5 0.0 copy-start.5
  6.5 0.0 copy-start.6
  6.5 0.0 copy-start.7
  6.5 2.0 %collective-permute-start.6 = (f32[8,128]{1,0:T(8,128)S(1)}, f32[8,128]{1,0:T(8,128)S(1)}, u32[]{:S(2)}, u32[]{:S(2)}) collective-permute-start(f32[8,128]{1,0:T(8,128)S(1)} %y_send.1), channel_id=1, source_target_pairs={{0,4},{1,5},{2,6},{3,7},{4,0},{5,1},{6,2},{7,3},{8,12},{9,13},{10,... | collective-permute-start | bytes 12296 | tf_op jit(solution)/shard_map/ppermute | solution.py:48
  8.5 0.0 collective-permute-start.5
  8.5 0.3 collective-permute-start.2
  8.8 1.1 %depth.1 = (f32[6,12,32,128]{3,2,1,0:T(8,128)S(1)}, f32[3,16,32,128]{3,2,1,0:T(8,128)S(1)}, f32[3,16,32,128]{3,2,1,0:T(8,128)S(1)}) custom-call(f32[6,16,32,128]{3,2,1,0:T(8,128)S(1)} %copy-done, f32[3,16,32,128]{3,2,1,0:T(8,128)} %velocity_hbm.1), custom_call_target="tpu_custom_call" | custom-call | flops 1320000000 | bytes 7700000 | tf_op jit(solution)/shard_map/depth/pallas_call | solution.py:658
  9.9 0.3 %collective-permute-done.6.y1_ref.y2_ref = f32[8,128]{1,0:T(8,128)S(1)} collective-permute-done((f32[8,128]{1,0:T(8,128)S(1)}, f32[8,128]{1,0:T(8,128)S(1)}, u32[]{:S(2)}, u32[]{:S(2)}) %collective-permute-start.6) | collective-permute-done | bytes 4128 | tf_op jit(solution)/shard_map/ppermute | solution.py:48
  10.2 0.1 x_send.1
  10.3 2.1 %collective-permute-start.7 = (f32[32,128]{1,0:T(8,128)S(1)}, f32[32,128]{1,0:T(8,128)S(1)}, u32[]{:S(2)}, u32[]{:S(2)}) collective-permute-start(f32[32,128]{1,0:T(8,128)S(1)} %get-tuple-element.73), channel_id=1, source_target_pairs={{0,8},{1,9},{2,10},{3,11},{4,12},{5,13},{6,14},{7,15},{8,0},{9,1},... | collective-permute-start | bytes 49160 | tf_op jit(solution)/shard_map/ppermute | solution.py:48
  12.3 0.0 collective-permute-done.5
  12.3 0.0 collective-permute-start.8
  12.3 0.0 copy-done.2
  12.3 0.0 copy-done.3
  12.4 0.0 copy-done.4
  12.4 0.0 copy-done.5
  12.4 0.0 copy-done.6
  12.4 0.0 copy-done.7
  12.4 0.9 %cells.1 = (f32[5,16,32,128]{3,2,1,0:T(8,128)S(1)}, f32[2,64,128]{2,1,0:T(8,128)S(1)}) custom-call(f32[8,128]{1,0:T(8,128)S(1)} %add.7.layers_ref, s32[16,32,128]{2,1,0:T(8,128)S(1)} %copy-done.2, f32[1,16]{1,0:T(1,128)S(1)} %bitcast.7, f32[1,16]{1,0:T(1,128)S(1)} %bitcast.8, f32[1,16]{1,0:T(1,128)S(1)} %bitcast.9, f32[1,16]{1,0:T(1,128)S(1)} %bitcast.10, ...), custom_call_target="tpu_custom_call" | custom-call | flops 480000000 | bytes 2800000 | tf_op jit(solution)/shard_map/cells/pallas_call | solution.py:682
  13.3 0.0 collective-permute-done.2.y1_ref.y2_ref
  13.3 0.0 collective-permute-done.3.z1_ref
  13.3 0.0 collective-permute-done.4.z2_ref
  13.3 0.4 %planes.1 = (f32[3,16,32,128]{3,2,1,0:T(8,128)S(1)}, f32[6,4,32,128]{3,2,1,0:T(8,128)S(1)}) custom-call(f32[6,16,32,128]{3,2,1,0:T(8,128)S(1)} %copy-done, f32[3,16,32,128]{3,2,1,0:T(8,128)S(1)} %get-tuple-element.57.along_ref, f32[96,128]{1,0:T(8,128)S(1)} %collective-permute-done.2.y1_ref.y2_ref, f32[96,128]{1,0:T(8,128)S(1)} %collective-permute-done.2.y1_ref.y2_ref, ...), custom_call_target="tpu_custom_call" | custom-call | flops 360000000 | bytes 2100000 | tf_op jit(solution)/shard_map/planes/pallas_call | solution.py:685
  13.7 0.3 %collective-permute-done.7.x1_ref = f32[32,128]{1,0:T(8,128)S(1)} collective-permute-done((f32[32,128]{1,0:T(8,128)S(1)}, f32[32,128]{1,0:T(8,128)S(1)}, u32[]{:S(2)}, u32[]{:S(2)}) %collective-permute-start.7) | collective-permute-done | bytes 16416 | tf_op jit(solution)/shard_map/ppermute | solution.py:48
  14.0 0.0 collective-permute-done.8.x2_ref
  14.1 0.4 %metrics.1 = (f32[16,32,128]{2,1,0:T(8,128)S(1)}, f32[16,32,128]{2,1,0:T(8,128)S(1)}, f32[2,32,128]{2,1,0:T(8,128)S(1)}) custom-call(f32[2,64,128]{2,1,0:T(8,128)S(1)} %get-tuple-element.79.layers_ref, f32[48,128]{1,0:T(8,128)S(1)} %get-tuple-element.80.own, f32[8,128]{1,0:T(8,128)S(1)} %slice.10.x1_ref, f32[8,128]{1,0:T(8,128)S(1)} %slice.11.x2_ref), custom_call_target="tpu_custom_call" | custom-call | flops 660000000 | bytes 3850000 | tf_op jit(solution)/shard_map/metrics/pallas_call | solution.py:693
  14.5 0.0 copy-start.1
  14.5 1.0 %velocity.1 = (f32[3,16,32,128]{3,2,1,0:T(8,128)S(1)}, f32[24,128]{1,0:T(8,128)S(1)}, f32[24,128]{1,0:T(8,128)S(1)}, f32[24,128]{1,0:T(8,128)S(1)}, f32[24,128]{...) custom-call(f32[3,16,32,128]{3,2,1,0:T(8,128)S(1)} %get-tuple-element.56.veloc, ...), custom_call_target="tpu_custom_call" | custom-call | flops 900000000 | bytes 5250000 | tf_op jit(solution)/shard_map/velocity/pallas_call | solution.py:700
  15.5 0.3 %collective-permute-start.12 = (f32[3,2,32,128]{3,2,1,0:T(8,128)S(1)}, f32[3,2,32,128]{3,2,1,0:T(8,128)S(1)}, u32[]{:S(2)}, u32[]{:S(2)}) collective-permute-start(f32[3,2,32,128]{3,2,1,0:T(8,128)S(1)} %get-tuple-element.97), channel_id=1, source_target_pairs={{0,1},{1,0},{2,3},{3,2},{4,5},{5,4},{6,7},{7,6},{8,9},{9,8},{10,11... | collective-permute-start | bytes 294920 | tf_op jit(solution)/shard_map/ppermute | solution.py:48
  15.9 1.9 %collective-permute-start.13 = (f32[3,2,32,128]{3,2,1,0:T(8,128)S(1)}, f32[3,2,32,128]{3,2,1,0:T(8,128)S(1)}, u32[]{:S(2)}, u32[]{:S(2)}) collective-permute-start(f32[3,2,32,128]{3,2,1,0:T(8,128)S(1)} %get-tuple-element.98), channel_id=1, source_target_pairs={{0,3},{1,2},{2,1},{3,0},{4,7},{5,6},{6,5},{7,4},{8,11},{9,10},{10,... | collective-permute-start | bytes 294920 | tf_op jit(solution)/shard_map/ppermute | solution.py:48
  17.8 1.5 %collective-permute-start.11 = (f32[96,128]{1,0:T(8,128)S(1)}, f32[96,128]{1,0:T(8,128)S(1)}, u32[]{:S(2)}, u32[]{:S(2)}) collective-permute-start(f32[96,128]{1,0:T(8,128)S(1)} %get-tuple-element.96), channel_id=1, source_target_pairs={{0,4},{1,5},{2,6},{3,7},{4,0},{5,1},{6,2},{7,3},{8,12},{9,13},{10,... | collective-permute-start | bytes 147464 | tf_op jit(solution)/shard_map/ppermute | solution.py:48
  19.3 2.7 %collective-permute-start.9 = (f32[24,128]{1,0:T(8,128)S(1)}, f32[24,128]{1,0:T(8,128)S(1)}, u32[]{:S(2)}, u32[]{:S(2)}) collective-permute-start(f32[24,128]{1,0:T(8,128)S(1)} %get-tuple-element.92), channel_id=1, source_target_pairs={{0,8},{1,9},{2,10},{3,11},{4,12},{5,13},{6,14},{7,15},{8,0},{9,1},... | collective-permute-start | bytes 36872 | tf_op jit(solution)/shard_map/ppermute | solution.py:48
  22.0 0.0 collective-permute-start.10
  22.0 0.9 %velocity_inner.1 = (f32[3,16,32,128]{3,2,1,0:T(8,128)}, f32[3,12,32,128]{3,2,1,0:T(8,128)S(1)}, f32[3,16,32,128]{3,2,1,0:T(8,128)S(1)}) custom-call(f32[3,16,32,128]{3,2,1,0:T(8,128)S(1)} %get-tuple-element.88.vel_ref), custom_call_target="tpu_custom_call" | custom-call | flops 60000000 | bytes 350000 | tf_op jit(solution)/shard_map/velocity_inner/pallas_call | solution.py:710
  22.9 0.8 %collective-permute-done.9.x1_ref = f32[24,128]{1,0:T(8,128)S(1)} collective-permute-done((f32[24,128]{1,0:T(8,128)S(1)}, f32[24,128]{1,0:T(8,128)S(1)}, u32[]{:S(2)}, u32[]{:S(2)}) %collective-permute-start.9) | collective-permute-done | bytes 12320 | tf_op jit(solution)/shard_map/ppermute | solution.py:48
  23.7 0.0 collective-permute-done.10.x2_ref
  23.7 0.0 collective-permute-done.11.y1_ref.y2_ref
  23.7 0.0 collective-permute-done.12.z1_ref
  23.7 0.0 collective-permute-done.13.z2_ref
  23.7 0.0 copy-done.1
  23.7 2.5 %stress.1 = (f32[6,16,32,128]{3,2,1,0:T(8,128)}, f32[6,16,32,128]{3,2,1,0:T(8,128)}) custom-call(f32[3,16,32,128]{3,2,1,0:T(8,128)S(1)} %get-tuple-element.88.vel_ref, f32[6,16,32,128]{3,2,1,0:T(8,128)S(1)} %copy-done, f32[6,16,32,128]{3,2,1,0:T(8,128)S(1)} %copy-done.1, f32[5,16,32,128]{3,2,1,0:T(8,128)S(1)} %get-tuple-element.75.cells_ref, ...), custom_call_target="tpu_custom_call" | custom-call | flops 1680000000 | bytes 9800000 | tf_op jit(solution)/shard_map/stress/pallas_call | solution.py:718
  (6 shorter events, 0.0 us)
Async XLA Ops:
  0.6 4.3 %copy-start = (f32[6,16,32,128]{3,2,1,0:T(8,128)S(1)}, f32[6,16,32,128]{3,2,1,0:T(8,128)}, u32[]{:S(2)}) copy-start(f32[6,16,32,128]{3,2,1,0:T(8,128)} %stress_ref.3) | copy-start | bytes 4718596
  0.6 1.6 %collective-permute-start = (s32[32,32]{1,0:T(8,128)}, s32[32,32]{1,0:T(8,128)S(1)}, u32[]{:S(2)}, u32[]{:S(2)}) collective-permute-start(s32[32,32]{1,0:T(8,128)} %elev_hbm.1), channel_id=1, source_target_pairs={{0,1},{1,0},{2,3},{3,2},{4,5},{5,4},{6,7},{7,6},{8,9},{9,8},{10,11... | collective-permute-start | bytes 12296 | tf_op jit(solution)/shard_map/ppermute | solution.py:610
  2.3 4.1 %collective-permute-start.1 = (f32[40,128]{1,0:T(8,128)S(1)}, f32[40,128]{1,0:T(8,128)S(1)}, u32[]{:S(2)}, u32[]{:S(2)}) collective-permute-start(f32[40,128]{1,0:T(8,128)S(1)} %merge.1), channel_id=1, source_target_pairs={{0,3},{1,2},{2,1},{3,0},{4,7},{5,6},{6,5},{7,4},{8,11},{9,10},{10,... | collective-permute-start | bytes 61448 | tf_op jit(solution)/shard_map/ppermute | solution.py:631
  5.2 8.1 %collective-permute-start.3 = (f32[6,2,32,128]{3,2,1,0:T(8,128)S(1)}, f32[6,2,32,128]{3,2,1,0:T(8,128)S(1)}, u32[]{:S(2)}, u32[]{:S(2)}) collective-permute-start(f32[6,2,32,128]{3,2,1,0:T(8,128)S(1)} %get-tuple-element.59), channel_id=1, source_target_pairs={{0,1},{1,0},{2,3},{3,2},{4,5},{5,4},{6,7},{7,6},{8,9},{9,8},{10,11... | collective-permute-start | bytes 589832 | tf_op jit(solution)/shard_map/ppermute | solution.py:48
  5.6 7.7 %collective-permute-start.4 = (f32[6,2,32,128]{3,2,1,0:T(8,128)S(1)}, f32[6,2,32,128]{3,2,1,0:T(8,128)S(1)}, u32[]{:S(2)}, u32[]{:S(2)}) collective-permute-start(f32[6,2,32,128]{3,2,1,0:T(8,128)S(1)} %get-tuple-element.60), channel_id=1, source_target_pairs={{0,3},{1,2},{2,1},{3,0},{4,7},{5,6},{6,5},{7,4},{8,11},{9,10},{10,... | collective-permute-start | bytes 589832 | tf_op jit(solution)/shard_map/ppermute | solution.py:48
  6.4 5.9 %copy-start.2 = (s32[16,32,128]{2,1,0:T(8,128)S(1)}, s32[16,32,128]{2,1,0:T(8,128)}, u32[]{:S(2)}) copy-start(s32[16,32,128]{2,1,0:T(8,128)} %material_ref) | copy-start | bytes 786436
  6.4 5.9 %copy-start.3 = (f32[16]{0:T(128)S(1)}, f32[16]{0:T(128)}, u32[]{:S(2)}) copy-start(f32[16]{0:T(128)} %param.16) | copy-start | bytes 196
  6.4 5.9 %copy-start.4 = (f32[16]{0:T(128)S(1)}, f32[16]{0:T(128)}, u32[]{:S(2)}) copy-start(f32[16]{0:T(128)} %param.17) | copy-start | bytes 196
  6.5 5.9 %copy-start.5 = (f32[16]{0:T(128)S(1)}, f32[16]{0:T(128)}, u32[]{:S(2)}) copy-start(f32[16]{0:T(128)} %param.18) | copy-start | bytes 196
  6.5 5.9 %copy-start.6 = (f32[16]{0:T(128)S(1)}, f32[16]{0:T(128)}, u32[]{:S(2)}) copy-start(f32[16]{0:T(128)} %param.19) | copy-start | bytes 196
  6.5 5.9 %copy-start.7 = (f32[16]{0:T(128)S(1)}, f32[16]{0:T(128)}, u32[]{:S(2)}) copy-start(f32[16]{0:T(128)} %param.20) | copy-start | bytes 196
  6.5 3.7 %collective-permute-start.6 = (f32[8,128]{1,0:T(8,128)S(1)}, f32[8,128]{1,0:T(8,128)S(1)}, u32[]{:S(2)}, u32[]{:S(2)}) collective-permute-start(f32[8,128]{1,0:T(8,128)S(1)} %y_send.1), channel_id=1, source_target_pairs={{0,4},{1,5},{2,6},{3,7},{4,0},{5,1},{6,2},{7,3},{8,12},{9,13},{10,... | collective-permute-start | bytes 12296 | tf_op jit(solution)/shard_map/ppermute | solution.py:48
  8.5 3.8 %collective-permute-start.5 = (f32[8,128]{1,0:T(8,128)S(1)}, f32[8,128]{1,0:T(8,128)S(1)}, u32[]{:S(2)}, u32[]{:S(2)}) collective-permute-start(f32[8,128]{1,0:T(8,128)S(1)} %slice.12), channel_id=1, source_target_pairs={{0,1},{1,0},{2,3},{3,2},{4,5},{5,4},{6,7},{7,6},{8,9},{9,8},{10,11... | collective-permute-start | bytes 12296 | tf_op jit(solution)/shard_map/ppermute | solution.py:657
  8.5 4.8 %collective-permute-start.2 = (f32[96,128]{1,0:T(8,128)S(1)}, f32[96,128]{1,0:T(8,128)S(1)}, u32[]{:S(2)}, u32[]{:S(2)}) collective-permute-start(f32[96,128]{1,0:T(8,128)S(1)} %get-tuple-element.58), channel_id=1, source_target_pairs={{0,4},{1,5},{2,6},{3,7},{4,0},{5,1},{6,2},{7,3},{8,12},{9,13},{10,... | collective-permute-start | bytes 147464 | tf_op jit(solution)/shard_map/ppermute | solution.py:48
  10.3 3.8 %collective-permute-start.7 = (f32[32,128]{1,0:T(8,128)S(1)}, f32[32,128]{1,0:T(8,128)S(1)}, u32[]{:S(2)}, u32[]{:S(2)}) collective-permute-start(f32[32,128]{1,0:T(8,128)S(1)} %get-tuple-element.73), channel_id=1, source_target_pairs={{0,8},{1,9},{2,10},{3,11},{4,12},{5,13},{6,14},{7,15},{8,0},{9,1},... | collective-permute-start | bytes 49160 | tf_op jit(solution)/shard_map/ppermute | solution.py:48
  12.3 1.7 %collective-permute-start.8 = (f32[32,128]{1,0:T(8,128)S(1)}, f32[32,128]{1,0:T(8,128)S(1)}, u32[]{:S(2)}, u32[]{:S(2)}) collective-permute-start(f32[32,128]{1,0:T(8,128)S(1)} %get-tuple-element.74), channel_id=1, source_target_pairs={{0,1},{1,0},{2,3},{3,2},{4,5},{5,4},{6,7},{7,6},{8,16},{9,17},{10,... | collective-permute-start | bytes 49160 | tf_op jit(solution)/shard_map/ppermute | solution.py:48
  14.5 9.2 %copy-start.1 = (f32[6,16,32,128]{3,2,1,0:T(8,128)S(1)}, f32[6,16,32,128]{3,2,1,0:T(8,128)}, u32[]{:S(2)}) copy-start(f32[6,16,32,128]{3,2,1,0:T(8,128)} %memory_ref.1) | copy-start | bytes 4718596
  15.5 8.1 %collective-permute-start.12 = (f32[3,2,32,128]{3,2,1,0:T(8,128)S(1)}, f32[3,2,32,128]{3,2,1,0:T(8,128)S(1)}, u32[]{:S(2)}, u32[]{:S(2)}) collective-permute-start(f32[3,2,32,128]{3,2,1,0:T(8,128)S(1)} %get-tuple-element.97), channel_id=1, source_target_pairs={{0,1},{1,0},{2,3},{3,2},{4,5},{5,4},{6,7},{7,6},{8,9},{9,8},{10,11... | collective-permute-start | bytes 294920 | tf_op jit(solution)/shard_map/ppermute | solution.py:48
  15.9 7.8 %collective-permute-start.13 = (f32[3,2,32,128]{3,2,1,0:T(8,128)S(1)}, f32[3,2,32,128]{3,2,1,0:T(8,128)S(1)}, u32[]{:S(2)}, u32[]{:S(2)}) collective-permute-start(f32[3,2,32,128]{3,2,1,0:T(8,128)S(1)} %get-tuple-element.98), channel_id=1, source_target_pairs={{0,3},{1,2},{2,1},{3,0},{4,7},{5,6},{6,5},{7,4},{8,11},{9,10},{10,... | collective-permute-start | bytes 294920 | tf_op jit(solution)/shard_map/ppermute | solution.py:48
  17.8 5.9 %collective-permute-start.11 = (f32[96,128]{1,0:T(8,128)S(1)}, f32[96,128]{1,0:T(8,128)S(1)}, u32[]{:S(2)}, u32[]{:S(2)}) collective-permute-start(f32[96,128]{1,0:T(8,128)S(1)} %get-tuple-element.96), channel_id=1, source_target_pairs={{0,4},{1,5},{2,6},{3,7},{4,0},{5,1},{6,2},{7,3},{8,12},{9,13},{10,... | collective-permute-start | bytes 147464 | tf_op jit(solution)/shard_map/ppermute | solution.py:48
  19.3 4.4 %collective-permute-start.9 = (f32[24,128]{1,0:T(8,128)S(1)}, f32[24,128]{1,0:T(8,128)S(1)}, u32[]{:S(2)}, u32[]{:S(2)}) collective-permute-start(f32[24,128]{1,0:T(8,128)S(1)} %get-tuple-element.92), channel_id=1, source_target_pairs={{0,8},{1,9},{2,10},{3,11},{4,12},{5,13},{6,14},{7,15},{8,0},{9,1},... | collective-permute-start | bytes 36872 | tf_op jit(solution)/shard_map/ppermute | solution.py:48
  22.0 1.7 %collective-permute-start.10 = (f32[24,128]{1,0:T(8,128)S(1)}, f32[24,128]{1,0:T(8,128)S(1)}, u32[]{:S(2)}, u32[]{:S(2)}) collective-permute-start(f32[24,128]{1,0:T(8,128)S(1)} %get-tuple-element.93), channel_id=1, source_target_pairs={{0,1},{1,0},{2,3},{3,2},{4,5},{5,4},{6,7},{7,6},{8,16},{9,17},{10,... | collective-permute-start | bytes 36872 | tf_op jit(solution)/shard_map/ppermute | solution.py:48

commit v9 on v8

--- a/solution.py
+++ b/solution.py
@@ -485,7 +485,7 @@
     vz1_ref[...], vz2_ref[...] = order("gz", out_ref[:, nz - 2 : nz], out_ref[:, 0:2])
 
 
-def velocity_inner_kernel(vel_ref, vel_hbm, depth_ref, along_ref, sem):
+def velocity_inner_kernel(vel_ref, vel_hbm, depth_ref, along_ref, across_ref, tall, sem):
     store = pltpu.make_async_copy(vel_ref, vel_hbm, sem)
     store.start()
     _, nz, ny, nx = vel_ref.shape
@@ -493,20 +493,58 @@
 
     along_all(vel_ref, (0, 1, 2), along_ref)
     over(2, nz - 2, 4, lambda k: inner_depth(vel_ref, depth_ref, 3, k, tiles))
+    nothing = jnp.zeros((2, nx), F32)
+    for c in range(3):
+        for k in range(nz):
+            tall[c, k, PAD : PAD + ny, :] = vel_ref[c, k]
+            tall[c, k, PAD - 2 : PAD, :] = nothing
+            tall[c, k, PAD + ny : PAD + ny + 2, :] = nothing
+
+    def across(k):
+        for t in range(tiles):
+            for c in range(3):
+                across_ref[c, k, tile_rows(t), :] = row_difference(tall, c, k, t)
+
+    over(0, nz, 4, across)
     store.wait()
 
 
+def fill_sides(n_gy, top, bottom, y1_ref, y2_ref):
+    count = y1_ref.shape[0]
+    got = (y1_ref[...], y2_ref[...])
+    even_row = lax.broadcasted_iota(jnp.int32, got[0].shape, 0) % 2 == 0
+    empty = jnp.zeros((SUB, y1_ref.shape[1]), F32)
+    before, after = from_before("gy", got), from_after("gy", n_gy, got)
+    top[:count, :] = before
+    top[count:, :] = empty
+    bottom[:SUB, :] = empty
+    bottom[SUB:, :] = after
+    top[:count, :] = jnp.where(even_row, before - 8.0 * top[1 : count + 1, :], before)
+    bottom[SUB:, :] = jnp.where(even_row, -after, 8.0 * bottom[SUB - 1 : SUB + count - 1, :] - after)
+
+
+def beside_rows(top, bottom, c, k, t, nz, tiles):
+    j = 2 * (c * nz + k)
+    row = lax.broadcasted_iota(jnp.int32, (SUB, top.shape[1]), 0)
+    added = 0.0
+    if t == 0:
+        added = jnp.where(row < 2, top[pl.ds(j, SUB), :], 0.0)
+    if t == tiles - 1:
+        added = added + jnp.where(row >= SUB - 2, bottom[pl.ds(j + 2, SUB), :], 0.0)
+    return added
+
+
 def stress_kernel(
-    sizes, vel_ref, stress_ref, memory_ref, cells_ref, inner_ref, along_ref, factor_ref, mz_ref, slope_ref,
-    x1_ref, x2_ref, low_ref, high_ref, y1_ref, y2_ref, z1_ref, z2_ref,
-    stress_hbm, memory_hbm, edge, tall, zb, za, outer, stress_out, memory_out, sems,
+    sizes, vel_ref, stress_ref, memory_ref, cells_ref, inner_ref, along_ref, across_ref, factor_ref, mz_ref,
+    slope_ref, x1_ref, x2_ref, low_ref, high_ref, y1_ref, y2_ref, z1_ref, z2_ref,
+    stress_hbm, memory_hbm, edge, top, bottom, zb, za, outer, stress_out, memory_out, sems,
 ):
     n_gx, n_gy, n_gz = sizes
     _, nz, ny, nx = vel_ref.shape
     tiles = ny // SUB
     lane = lanes_of((SUB, nx))
     fill_edges(n_gx, edge, x1_ref, x2_ref, low_ref, high_ref)
-    fill_rows(n_gy, tall, lambda c, k: vel_ref[c, k], y1_ref, y2_ref, nz, ny, range(nz))
+    fill_sides(n_gy, top, bottom, y1_ref, y2_ref)
 
     def layer(k, depth_ref, spot):
         for t in range(tiles):
@@ -522,7 +560,10 @@
                 - mx * dk[c]
                 for c in range(3)
             ]
-            dy = [row_difference(tall, c, k, t) - my * dk[c] for c in range(3)]
+            dy = [
+                across_ref[c, k, rows, :] + beside_rows(top, bottom, c, k, t, nz, tiles) - my * dk[c]
+                for c in range(3)
+            ]
             dz = [mz * dk[c] for c in range(3)]
             lam, mu, keep, gain = (cells_ref[i, k, rows, :] for i in range(1, 5))
             volume = lam * (dx[0] + dy[1] + dz[2])
@@ -542,43 +583,31 @@
                     rates[c] - kept
                 )
 
-    def out_copies(first, count, spot):
+    pairs = ((stress_out, stress_hbm), (memory_out, memory_hbm))
+
+    def send(first, count):
         layers = pl.ds(first, count)
-        return [
-            pltpu.make_async_copy(a.at[:, layers], b.at[:, layers], sems.at[i, spot])
-            for i, (a, b) in enumerate(((stress_out, stress_hbm), (memory_out, memory_hbm)))
-        ]
+        for i, (a, b) in enumerate(pairs):
+            pltpu.make_async_copy(a.at[:, layers], b.at[:, layers], sems.at[i]).start()
 
     inner = nz - 4
     step = next(d for d in (4, 3, 2, 1) if inner % d == 0)
-    chunks = inner // step
-
-    @pl.loop(0, chunks)
+
+    @pl.loop(0, inner // step)
     def _(j):
         for i in range(step):
             k = 2 + j * step + i
             layer(k, inner_ref, k - 2)
-
-        for copy in out_copies(2 + j * step, step, 2 + j):
-            copy.start()
+        send(2 + j * step, step)
 
     depth_halos(n_gz, zb, za, z1_ref, z2_ref)
     outer_depth(vel_ref, zb, za, outer, 3, nz, tiles)
-    last = []
     for spot, k in enumerate((0, 1, nz - 2, nz - 1)):
         layer(k, outer, spot)
         if spot % 2 == 1:
-            last += out_copies(k - 1, 2, spot // 2)
-            for copy in last[-2:]:
-                copy.start()
-
-    @pl.loop(0, chunks)
-    def _(j):
-        for copy in out_copies(2 + j * step, step, 2 + j):
-            copy.wait()
-
-    for copy in last:
-        copy.wait()
+            send(k - 1, 2)
+    for i, (a, b) in enumerate(pairs):
+        pltpu.make_async_copy(a, b, sems.at[i]).wait()
 
 
 def in_hbm(value):
@@ -707,25 +736,26 @@
     vz1, vz2 = exchange(sizes, "gz", vz1, vz2)
     vy1, vy2 = exchange(sizes, "gy", vys[0], vys[-1])
     vx1, vx2 = exchange(sizes, "gx", vx1, vx2)
-    vel_next, vel_k, vel_x = call(
+    vel_next, vel_k, vel_x, vel_y = call(
         velocity_inner_kernel,
-        [velocity.shape, (3, nz - 4, ny, nx), velocity.shape],
+        [velocity.shape, (3, nz - 4, ny, nx), velocity.shape, velocity.shape],
         [VM],
-        [DMA],
+        [tall, DMA],
         name="velocity_inner", cost=0.1,
-        out_specs=[HB, VM, VM],
+        out_specs=[HB, VM, VM, VM],
     )(vel)
     stress_next, memory_next = call(
         functools.partial(stress_kernel, counts),
         [stress.shape, stress.shape],
-        [VM] * 17,
-        [edge, tall] + depth(3)
+        [VM] * 18,
+        [edge, pltpu.VMEM((faces + SUB, nx), F32), pltpu.VMEM((faces + SUB, nx), F32)]
+        + depth(3)
         + [pltpu.VMEM((3, 4, ny, nx), F32), pltpu.VMEM(stress.shape, F32), pltpu.VMEM(stress.shape, F32)]
-        + [DMA((2, nz))],
+        + [DMA((2,))],
         name="stress", cost=2.8,
         out_specs=[HB] * 2,
     )(
-        vel, stress_vm, memory, cells, vel_k, vel_x, factor, mz, slope, vx1, vx2, vlow, vhigh, vy1, vy2,
+        vel, stress_vm, memory, cells, vel_k, vel_x, vel_y, factor, mz, slope, vx1, vx2, vlow, vhigh, vy1, vy2,
         vz1, vz2,
     )
     return vel_next, stress_next, memory_next

time: 26.4 us -> 25.9 us (0.981)
  Pallas kernels: 8.58 us -> 8.08 us
    pallas_call x1, Pallas kernels: 2.53 us -> 2.06 us  [local(): call(functools.partial(stress_kernel, counts), [stress.shape, stress.shap...]
  transfers between devices with their start and end apart: 14 -> 14, of which waited for: 5 -> 5; matrix products, arithmetic and copies ran while one was open for 0% -> 0% of each run, Pallas kernels for 17% -> 18%
where the time goes in v9:
time: 25.9 us; the launch traced here: 25.7 us
  starting transfers between devices  14.4 us (56%)
  Pallas kernels  8.08 us (31%)
  waiting for transfers between devices  2.33 us (9%)
  between operations  0.87 us (3%)
    ppermute x11, starting transfers between devices, exchange(): got = [lax.ppermute(v, tuple(sizes), r) for v, r in rounds]  11.2 us
    ppermute x1, starting transfers between devices, local(): slab = slab + lax.ppermute(slab, tuple(sizes), rounds[1])  2.63 us
    pallas_call x1, Pallas kernels, local(): call(functools.partial(stress_kernel, counts), [stress.shape, stress.shap...  2.06 us
    ppermute x11, waiting for transfers between devices, exchange(): got = [lax.ppermute(v, tuple(sizes), r) for v, r in rounds]  1.36 us
    pallas_call x1, Pallas kernels, local(): call(depth_kernel, [(6, nz - 4, ny, nx), velocity.shape, velocity.shape],...  1.14 us
    pallas_call x1, Pallas kernels, local(): call(functools.partial(velocity_kernel, counts), [velocity.shape] + [(xs,...  0.99 us
    pallas_call x1, Pallas kernels, local(): call(cell_kernel, [(5, nz, ny, nx), (2, all_layers, nx)], [VM] * 7, name=...  0.89 us
    pallas_call x1, Pallas kernels, local(): call(velocity_inner_kernel, [velocity.shape, (3, nz - 4, ny, nx), velocit...  0.89 us
  transfers between devices with their start and end apart: 14, of which 5 were waited for; matrix products, arithmetic and copies ran while one was open for 0% of the time, Pallas kernels for 18%

profile of v9, /device:TPU:0, one launch (start us, length us, event | category | flops | bytes accessed | tf_op | source)
XLA Modules:
  0.0 25.7 jit_solution(13111993565627607977)
XLA Ops:
  0.6 0.0 copy-start
  0.6 0.5 %collective-permute-start = (s32[32,32]{1,0:T(8,128)}, s32[32,32]{1,0:T(8,128)S(1)}, u32[]{:S(2)}, u32[]{:S(2)}) collective-permute-start(s32[32,32]{1,0:T(8,128)} %elev_hbm.1), channel_id=1, source_target_pairs={{0,1},{1,0},{2,3},{3,2},{4,5},{5,4},{6,7},{7,6},{8,9},{9,8},{10,11... | collective-permute-start | bytes 12296 | tf_op jit(solution)/shard_map/ppermute | solution.py:639
  1.2 0.8 %terrain_piece.1.first_ref = f32[40,128]{1,0:T(8,128)S(1)} custom-call(s32[32,32]{1,0:T(8,128)} %elev_hbm.1, f32[1,16]{1,0:T(1,128)} %bitcast.12, f32[1,16]{1,0:T(1,128)} %bitcast.13), custom_call_target="tpu_custom_call" | custom-call | flops 480000000 | bytes 2800000 | tf_op jit(solution)/shard_map/terrain_piece/pallas_call | solution.py:640
  2.0 0.2 collective-permute-done.elev_ref
  2.2 0.1 merge.1
  2.3 2.6 %collective-permute-start.1 = (f32[40,128]{1,0:T(8,128)S(1)}, f32[40,128]{1,0:T(8,128)S(1)}, u32[]{:S(2)}, u32[]{:S(2)}) collective-permute-start(f32[40,128]{1,0:T(8,128)S(1)} %merge.1), channel_id=1, source_target_pairs={{0,3},{1,2},{2,1},{3,0},{4,7},{5,6},{6,5},{7,4},{8,11},{9,10},{10,... | collective-permute-start | bytes 61448 | tf_op jit(solution)/shard_map/ppermute | solution.py:660
  4.9 0.0 copy-done
  4.9 0.3 %pack_stress.1 = (f32[24,128]{1,0:T(8,128)S(1)}, f32[24,128]{1,0:T(8,128)S(1)}, f32[24,128]{1,0:T(8,128)S(1)}, f32[24,128]{1,0:T(8,128)S(1)}, f32[6,2,32,128]{3,...) custom-call(f32[6,16,32,128]{3,2,1,0:T(8,128)S(1)} %copy-done), custom_call_target="tpu_custom_call" | custom-call | flops 300000000 | bytes 1750000 | tf_op jit(solution)/shard_map/pack_stress/pallas_call | solution.py:674
  5.2 0.4 %collective-permute-start.3 = (f32[6,2,32,128]{3,2,1,0:T(8,128)S(1)}, f32[6,2,32,128]{3,2,1,0:T(8,128)S(1)}, u32[]{:S(2)}, u32[]{:S(2)}) collective-permute-start(f32[6,2,32,128]{3,2,1,0:T(8,128)S(1)} %get-tuple-element.60), channel_id=1, source_target_pairs={{0,1},{1,0},{2,3},{3,2},{4,5},{5,4},{6,7},{7,6},{8,9},{9,8},{10,11... | collective-permute-start | bytes 589832 | tf_op jit(solution)/shard_map/ppermute | solution.py:48
  5.6 0.0 collective-permute-start.4
  5.7 0.7 %collective-permute-done.1 = f32[40,128]{1,0:T(8,128)S(1)} collective-permute-done((f32[40,128]{1,0:T(8,128)S(1)}, f32[40,128]{1,0:T(8,128)S(1)}, u32[]{:S(2)}, u32[]{:S(2)}) %collective-permute-start.1) | collective-permute-done | bytes 20512 | tf_op jit(solution)/shard_map/ppermute | solution.py:660
  6.4 0.0 copy-start.2
  6.4 0.0 copy-start.3
  6.4 0.0 copy-start.4
  6.5 0.0 copy-start.5
  6.5 0.0 copy-start.6
  6.5 0.0 copy-start.7
  6.5 2.0 %collective-permute-start.6 = (f32[8,128]{1,0:T(8,128)S(1)}, f32[8,128]{1,0:T(8,128)S(1)}, u32[]{:S(2)}, u32[]{:S(2)}) collective-permute-start(f32[8,128]{1,0:T(8,128)S(1)} %y_send.1), channel_id=1, source_target_pairs={{0,4},{1,5},{2,6},{3,7},{4,0},{5,1},{6,2},{7,3},{8,12},{9,13},{10,... | collective-permute-start | bytes 12296 | tf_op jit(solution)/shard_map/ppermute | solution.py:48
  8.5 0.0 collective-permute-start.5
  8.5 0.3 collective-permute-start.2
  8.8 1.1 %depth.1 = (f32[6,12,32,128]{3,2,1,0:T(8,128)S(1)}, f32[3,16,32,128]{3,2,1,0:T(8,128)S(1)}, f32[3,16,32,128]{3,2,1,0:T(8,128)S(1)}) custom-call(f32[6,16,32,128]{3,2,1,0:T(8,128)S(1)} %copy-done, f32[3,16,32,128]{3,2,1,0:T(8,128)} %velocity_hbm.1), custom_call_target="tpu_custom_call" | custom-call | flops 1320000000 | bytes 7700000 | tf_op jit(solution)/shard_map/depth/pallas_call | solution.py:687
  9.9 0.3 %collective-permute-done.6.y1_ref.y2_ref = f32[8,128]{1,0:T(8,128)S(1)} collective-permute-done((f32[8,128]{1,0:T(8,128)S(1)}, f32[8,128]{1,0:T(8,128)S(1)}, u32[]{:S(2)}, u32[]{:S(2)}) %collective-permute-start.6) | collective-permute-done | bytes 4128 | tf_op jit(solution)/shard_map/ppermute | solution.py:48
  10.2 0.1 x_send.1
  10.3 2.1 %collective-permute-start.7 = (f32[32,128]{1,0:T(8,128)S(1)}, f32[32,128]{1,0:T(8,128)S(1)}, u32[]{:S(2)}, u32[]{:S(2)}) collective-permute-start(f32[32,128]{1,0:T(8,128)S(1)} %get-tuple-element.74), channel_id=1, source_target_pairs={{0,8},{1,9},{2,10},{3,11},{4,12},{5,13},{6,14},{7,15},{8,0},{9,1},... | collective-permute-start | bytes 49160 | tf_op jit(solution)/shard_map/ppermute | solution.py:48
  12.3 0.0 collective-permute-done.5
  12.3 0.0 collective-permute-start.8
  12.3 0.0 copy-done.2
  12.3 0.0 copy-done.3
  12.4 0.0 copy-done.4
  12.4 0.0 copy-done.5
  12.4 0.0 copy-done.6
  12.4 0.0 copy-done.7
  12.4 0.9 %cells.1 = (f32[5,16,32,128]{3,2,1,0:T(8,128)S(1)}, f32[2,64,128]{2,1,0:T(8,128)S(1)}) custom-call(f32[8,128]{1,0:T(8,128)S(1)} %add.7.layers_ref, s32[16,32,128]{2,1,0:T(8,128)S(1)} %copy-done.2, f32[1,16]{1,0:T(1,128)S(1)} %bitcast.7, f32[1,16]{1,0:T(1,128)S(1)} %bitcast.8, f32[1,16]{1,0:T(1,128)S(1)} %bitcast.9, f32[1,16]{1,0:T(1,128)S(1)} %bitcast.10, ...), custom_call_target="tpu_custom_call" | custom-call | flops 480000000 | bytes 2800000 | tf_op jit(solution)/shard_map/cells/pallas_call | solution.py:711
  13.3 0.0 collective-permute-done.2.y1_ref.y2_ref
  13.3 0.0 collective-permute-done.3.z1_ref
  13.3 0.0 collective-permute-done.4.z2_ref
  13.3 0.4 %planes.1 = (f32[3,16,32,128]{3,2,1,0:T(8,128)S(1)}, f32[6,4,32,128]{3,2,1,0:T(8,128)S(1)}) custom-call(f32[6,16,32,128]{3,2,1,0:T(8,128)S(1)} %copy-done, f32[3,16,32,128]{3,2,1,0:T(8,128)S(1)} %get-tuple-element.58.along_ref, f32[96,128]{1,0:T(8,128)S(1)} %collective-permute-done.2.y1_ref.y2_ref, f32[96,128]{1,0:T(8,128)S(1)} %collective-permute-done.2.y1_ref.y2_ref, ...), custom_call_target="tpu_custom_call" | custom-call | flops 360000000 | bytes 2100000 | tf_op jit(solution)/shard_map/planes/pallas_call | solution.py:714
  13.7 0.3 %collective-permute-done.7.x1_ref = f32[32,128]{1,0:T(8,128)S(1)} collective-permute-done((f32[32,128]{1,0:T(8,128)S(1)}, f32[32,128]{1,0:T(8,128)S(1)}, u32[]{:S(2)}, u32[]{:S(2)}) %collective-permute-start.7) | collective-permute-done | bytes 16416 | tf_op jit(solution)/shard_map/ppermute | solution.py:48
  14.0 0.0 collective-permute-done.8.x2_ref
  14.1 0.4 %metrics.1 = (f32[16,32,128]{2,1,0:T(8,128)S(1)}, f32[16,32,128]{2,1,0:T(8,128)S(1)}, f32[2,32,128]{2,1,0:T(8,128)S(1)}) custom-call(f32[2,64,128]{2,1,0:T(8,128)S(1)} %get-tuple-element.80.layers_ref, f32[48,128]{1,0:T(8,128)S(1)} %get-tuple-element.81.own, f32[8,128]{1,0:T(8,128)S(1)} %slice.10.x1_ref, f32[8,128]{1,0:T(8,128)S(1)} %slice.11.x2_ref), custom_call_target="tpu_custom_call" | custom-call | flops 660000000 | bytes 3850000 | tf_op jit(solution)/shard_map/metrics/pallas_call | solution.py:722
  14.5 0.0 copy-start.1
  14.5 1.0 %velocity.1 = (f32[3,16,32,128]{3,2,1,0:T(8,128)S(1)}, f32[24,128]{1,0:T(8,128)S(1)}, f32[24,128]{1,0:T(8,128)S(1)}, f32[24,128]{1,0:T(8,128)S(1)}, f32[24,128]{...) custom-call(f32[3,16,32,128]{3,2,1,0:T(8,128)S(1)} %get-tuple-element.57.veloc, ...), custom_call_target="tpu_custom_call" | custom-call | flops 900000000 | bytes 5250000 | tf_op jit(solution)/shard_map/velocity/pallas_call | solution.py:729
  15.5 0.3 %collective-permute-start.12 = (f32[3,2,32,128]{3,2,1,0:T(8,128)S(1)}, f32[3,2,32,128]{3,2,1,0:T(8,128)S(1)}, u32[]{:S(2)}, u32[]{:S(2)}) collective-permute-start(f32[3,2,32,128]{3,2,1,0:T(8,128)S(1)} %get-tuple-element.99), channel_id=1, source_target_pairs={{0,1},{1,0},{2,3},{3,2},{4,5},{5,4},{6,7},{7,6},{8,9},{9,8},{10,11... | collective-permute-start | bytes 294920 | tf_op jit(solution)/shard_map/ppermute | solution.py:48
  15.8 1.9 %collective-permute-start.13 = (f32[3,2,32,128]{3,2,1,0:T(8,128)S(1)}, f32[3,2,32,128]{3,2,1,0:T(8,128)S(1)}, u32[]{:S(2)}, u32[]{:S(2)}) collective-permute-start(f32[3,2,32,128]{3,2,1,0:T(8,128)S(1)} %get-tuple-element.100), channel_id=1, source_target_pairs={{0,3},{1,2},{2,1},{3,0},{4,7},{5,6},{6,5},{7,4},{8,11},{9,10},{10,... | collective-permute-start | bytes 294920 | tf_op jit(solution)/shard_map/ppermute | solution.py:48
  17.7 1.5 %collective-permute-start.11 = (f32[96,128]{1,0:T(8,128)S(1)}, f32[96,128]{1,0:T(8,128)S(1)}, u32[]{:S(2)}, u32[]{:S(2)}) collective-permute-start(f32[96,128]{1,0:T(8,128)S(1)} %get-tuple-element.98), channel_id=1, source_target_pairs={{0,4},{1,5},{2,6},{3,7},{4,0},{5,1},{6,2},{7,3},{8,12},{9,13},{10,... | collective-permute-start | bytes 147464 | tf_op jit(solution)/shard_map/ppermute | solution.py:48
  19.2 2.7 %collective-permute-start.9 = (f32[24,128]{1,0:T(8,128)S(1)}, f32[24,128]{1,0:T(8,128)S(1)}, u32[]{:S(2)}, u32[]{:S(2)}) collective-permute-start(f32[24,128]{1,0:T(8,128)S(1)} %get-tuple-element.94), channel_id=1, source_target_pairs={{0,8},{1,9},{2,10},{3,11},{4,12},{5,13},{6,14},{7,15},{8,0},{9,1},... | collective-permute-start | bytes 36872 | tf_op jit(solution)/shard_map/ppermute | solution.py:48
  21.9 0.0 collective-permute-start.10
  21.9 0.9 %velocity_inner.1 = (f32[3,16,32,128]{3,2,1,0:T(8,128)}, f32[3,12,32,128]{3,2,1,0:T(8,128)S(1)}, f32[3,16,32,128]{3,2,1,0:T(8,128)S(1)}, f32[3,16,32,128]{3,2,1,0:T(8,128)S(1)}) custom-call(f32[3,16,32,128]{3,2,1,0:T(8,128)S(1)} %get-tuple-element.89.vel_ref), custom_call_target="tpu_custom_call" | custom-call | flops 60000000 | bytes 350000 | tf_op jit(solution)/shard_map/velocity_inner/pallas_call | solution.py:739
  22.8 0.8 %collective-permute-done.9.x1_ref = f32[24,128]{1,0:T(8,128)S(1)} collective-permute-done((f32[24,128]{1,0:T(8,128)S(1)}, f32[24,128]{1,0:T(8,128)S(1)}, u32[]{:S(2)}, u32[]{:S(2)}) %collective-permute-start.9) | collective-permute-done | bytes 12320 | tf_op jit(solution)/shard_map/ppermute | solution.py:48
  23.6 0.0 collective-permute-done.10.x2_ref
  23.6 0.0 collective-permute-done.11.y1_ref.y2_ref
  23.6 0.0 collective-permute-done.12.z1_ref
  23.6 0.0 collective-permute-done.13.z2_ref
  23.6 0.0 copy-done.1
  23.7 2.1 %stress.1 = (f32[6,16,32,128]{3,2,1,0:T(8,128)}, f32[6,16,32,128]{3,2,1,0:T(8,128)}) custom-call(f32[3,16,32,128]{3,2,1,0:T(8,128)S(1)} %get-tuple-element.89.vel_ref, f32[6,16,32,128]{3,2,1,0:T(8,128)S(1)} %copy-done, f32[6,16,32,128]{3,2,1,0:T(8,128)S(1)} %copy-done.1, f32[5,16,32,128]{3,2,1,0:T(8,128)S(1)} %get-tuple-element.76.cells_ref, ...), custom_call_target="tpu_custom_call" | custom-call | flops 1680000000 | bytes 9800000 | tf_op jit(solution)/shard_map/stress/pallas_call | solution.py:747
  (6 shorter events, 0.0 us)
Async XLA Ops:
  0.6 4.3 %copy-start = (f32[6,16,32,128]{3,2,1,0:T(8,128)S(1)}, f32[6,16,32,128]{3,2,1,0:T(8,128)}, u32[]{:S(2)}) copy-start(f32[6,16,32,128]{3,2,1,0:T(8,128)} %stress_ref.3) | copy-start | bytes 4718596
  0.6 1.6 %collective-permute-start = (s32[32,32]{1,0:T(8,128)}, s32[32,32]{1,0:T(8,128)S(1)}, u32[]{:S(2)}, u32[]{:S(2)}) collective-permute-start(s32[32,32]{1,0:T(8,128)} %elev_hbm.1), channel_id=1, source_target_pairs={{0,1},{1,0},{2,3},{3,2},{4,5},{5,4},{6,7},{7,6},{8,9},{9,8},{10,11... | collective-permute-start | bytes 12296 | tf_op jit(solution)/shard_map/ppermute | solution.py:639
  2.3 4.1 %collective-permute-start.1 = (f32[40,128]{1,0:T(8,128)S(1)}, f32[40,128]{1,0:T(8,128)S(1)}, u32[]{:S(2)}, u32[]{:S(2)}) collective-permute-start(f32[40,128]{1,0:T(8,128)S(1)} %merge.1), channel_id=1, source_target_pairs={{0,3},{1,2},{2,1},{3,0},{4,7},{5,6},{6,5},{7,4},{8,11},{9,10},{10,... | collective-permute-start | bytes 61448 | tf_op jit(solution)/shard_map/ppermute | solution.py:660
  5.2 8.1 %collective-permute-start.3 = (f32[6,2,32,128]{3,2,1,0:T(8,128)S(1)}, f32[6,2,32,128]{3,2,1,0:T(8,128)S(1)}, u32[]{:S(2)}, u32[]{:S(2)}) collective-permute-start(f32[6,2,32,128]{3,2,1,0:T(8,128)S(1)} %get-tuple-element.60), channel_id=1, source_target_pairs={{0,1},{1,0},{2,3},{3,2},{4,5},{5,4},{6,7},{7,6},{8,9},{9,8},{10,11... | collective-permute-start | bytes 589832 | tf_op jit(solution)/shard_map/ppermute | solution.py:48
  5.6 7.7 %collective-permute-start.4 = (f32[6,2,32,128]{3,2,1,0:T(8,128)S(1)}, f32[6,2,32,128]{3,2,1,0:T(8,128)S(1)}, u32[]{:S(2)}, u32[]{:S(2)}) collective-permute-start(f32[6,2,32,128]{3,2,1,0:T(8,128)S(1)} %get-tuple-element.61), channel_id=1, source_target_pairs={{0,3},{1,2},{2,1},{3,0},{4,7},{5,6},{6,5},{7,4},{8,11},{9,10},{10,... | collective-permute-start | bytes 589832 | tf_op jit(solution)/shard_map/ppermute | solution.py:48
  6.4 5.9 %copy-start.2 = (s32[16,32,128]{2,1,0:T(8,128)S(1)}, s32[16,32,128]{2,1,0:T(8,128)}, u32[]{:S(2)}) copy-start(s32[16,32,128]{2,1,0:T(8,128)} %material_ref) | copy-start | bytes 786436
  6.4 5.9 %copy-start.3 = (f32[16]{0:T(128)S(1)}, f32[16]{0:T(128)}, u32[]{:S(2)}) copy-start(f32[16]{0:T(128)} %param.16) | copy-start | bytes 196
  6.4 5.9 %copy-start.4 = (f32[16]{0:T(128)S(1)}, f32[16]{0:T(128)}, u32[]{:S(2)}) copy-start(f32[16]{0:T(128)} %param.17) | copy-start | bytes 196
  6.5 5.9 %copy-start.5 = (f32[16]{0:T(128)S(1)}, f32[16]{0:T(128)}, u32[]{:S(2)}) copy-start(f32[16]{0:T(128)} %param.18) | copy-start | bytes 196
  6.5 5.9 %copy-start.6 = (f32[16]{0:T(128)S(1)}, f32[16]{0:T(128)}, u32[]{:S(2)}) copy-start(f32[16]{0:T(128)} %param.19) | copy-start | bytes 196
  6.5 5.9 %copy-start.7 = (f32[16]{0:T(128)S(1)}, f32[16]{0:T(128)}, u32[]{:S(2)}) copy-start(f32[16]{0:T(128)} %param.20) | copy-start | bytes 196
  6.5 3.7 %collective-permute-start.6 = (f32[8,128]{1,0:T(8,128)S(1)}, f32[8,128]{1,0:T(8,128)S(1)}, u32[]{:S(2)}, u32[]{:S(2)}) collective-permute-start(f32[8,128]{1,0:T(8,128)S(1)} %y_send.1), channel_id=1, source_target_pairs={{0,4},{1,5},{2,6},{3,7},{4,0},{5,1},{6,2},{7,3},{8,12},{9,13},{10,... | collective-permute-start | bytes 12296 | tf_op jit(solution)/shard_map/ppermute | solution.py:48
  8.5 3.8 %collective-permute-start.5 = (f32[8,128]{1,0:T(8,128)S(1)}, f32[8,128]{1,0:T(8,128)S(1)}, u32[]{:S(2)}, u32[]{:S(2)}) collective-permute-start(f32[8,128]{1,0:T(8,128)S(1)} %slice.12), channel_id=1, source_target_pairs={{0,1},{1,0},{2,3},{3,2},{4,5},{5,4},{6,7},{7,6},{8,9},{9,8},{10,11... | collective-permute-start | bytes 12296 | tf_op jit(solution)/shard_map/ppermute | solution.py:686
  8.5 4.8 %collective-permute-start.2 = (f32[96,128]{1,0:T(8,128)S(1)}, f32[96,128]{1,0:T(8,128)S(1)}, u32[]{:S(2)}, u32[]{:S(2)}) collective-permute-start(f32[96,128]{1,0:T(8,128)S(1)} %get-tuple-element.59), channel_id=1, source_target_pairs={{0,4},{1,5},{2,6},{3,7},{4,0},{5,1},{6,2},{7,3},{8,12},{9,13},{10,... | collective-permute-start | bytes 147464 | tf_op jit(solution)/shard_map/ppermute | solution.py:48
  10.3 3.8 %collective-permute-start.7 = (f32[32,128]{1,0:T(8,128)S(1)}, f32[32,128]{1,0:T(8,128)S(1)}, u32[]{:S(2)}, u32[]{:S(2)}) collective-permute-start(f32[32,128]{1,0:T(8,128)S(1)} %get-tuple-element.74), channel_id=1, source_target_pairs={{0,8},{1,9},{2,10},{3,11},{4,12},{5,13},{6,14},{7,15},{8,0},{9,1},... | collective-permute-start | bytes 49160 | tf_op jit(solution)/shard_map/ppermute | solution.py:48
  12.3 1.7 %collective-permute-start.8 = (f32[32,128]{1,0:T(8,128)S(1)}, f32[32,128]{1,0:T(8,128)S(1)}, u32[]{:S(2)}, u32[]{:S(2)}) collective-permute-start(f32[32,128]{1,0:T(8,128)S(1)} %get-tuple-element.75), channel_id=1, source_target_pairs={{0,1},{1,0},{2,3},{3,2},{4,5},{5,4},{6,7},{7,6},{8,16},{9,17},{10,... | collective-permute-start | bytes 49160 | tf_op jit(solution)/shard_map/ppermute | solution.py:48
  14.5 9.2 %copy-start.1 = (f32[6,16,32,128]{3,2,1,0:T(8,128)S(1)}, f32[6,16,32,128]{3,2,1,0:T(8,128)}, u32[]{:S(2)}) copy-start(f32[6,16,32,128]{3,2,1,0:T(8,128)} %memory_ref.1) | copy-start | bytes 4718596
  15.5 8.1 %collective-permute-start.12 = (f32[3,2,32,128]{3,2,1,0:T(8,128)S(1)}, f32[3,2,32,128]{3,2,1,0:T(8,128)S(1)}, u32[]{:S(2)}, u32[]{:S(2)}) collective-permute-start(f32[3,2,32,128]{3,2,1,0:T(8,128)S(1)} %get-tuple-element.99), channel_id=1, source_target_pairs={{0,1},{1,0},{2,3},{3,2},{4,5},{5,4},{6,7},{7,6},{8,9},{9,8},{10,11... | collective-permute-start | bytes 294920 | tf_op jit(solution)/shard_map/ppermute | solution.py:48
  15.8 7.8 %collective-permute-start.13 = (f32[3,2,32,128]{3,2,1,0:T(8,128)S(1)}, f32[3,2,32,128]{3,2,1,0:T(8,128)S(1)}, u32[]{:S(2)}, u32[]{:S(2)}) collective-permute-start(f32[3,2,32,128]{3,2,1,0:T(8,128)S(1)} %get-tuple-element.100), channel_id=1, source_target_pairs={{0,3},{1,2},{2,1},{3,0},{4,7},{5,6},{6,5},{7,4},{8,11},{9,10},{10,... | collective-permute-start | bytes 294920 | tf_op jit(solution)/shard_map/ppermute | solution.py:48
  17.7 5.9 %collective-permute-start.11 = (f32[96,128]{1,0:T(8,128)S(1)}, f32[96,128]{1,0:T(8,128)S(1)}, u32[]{:S(2)}, u32[]{:S(2)}) collective-permute-start(f32[96,128]{1,0:T(8,128)S(1)} %get-tuple-element.98), channel_id=1, source_target_pairs={{0,4},{1,5},{2,6},{3,7},{4,0},{5,1},{6,2},{7,3},{8,12},{9,13},{10,... | collective-permute-start | bytes 147464 | tf_op jit(solution)/shard_map/ppermute | solution.py:48
  19.2 4.4 %collective-permute-start.9 = (f32[24,128]{1,0:T(8,128)S(1)}, f32[24,128]{1,0:T(8,128)S(1)}, u32[]{:S(2)}, u32[]{:S(2)}) collective-permute-start(f32[24,128]{1,0:T(8,128)S(1)} %get-tuple-element.94), channel_id=1, source_target_pairs={{0,8},{1,9},{2,10},{3,11},{4,12},{5,13},{6,14},{7,15},{8,0},{9,1},... | collective-permute-start | bytes 36872 | tf_op jit(solution)/shard_map/ppermute | solution.py:48
  21.9 1.7 %collective-permute-start.10 = (f32[24,128]{1,0:T(8,128)S(1)}, f32[24,128]{1,0:T(8,128)S(1)}, u32[]{:S(2)}, u32[]{:S(2)}) collective-permute-start(f32[24,128]{1,0:T(8,128)S(1)} %get-tuple-element.95), channel_id=1, source_target_pairs={{0,1},{1,0},{2,3},{3,2},{4,5},{5,4},{6,7},{7,6},{8,16},{9,17},{10,... | collective-permute-start | bytes 36872 | tf_op jit(solution)/shard_map/ppermute | solution.py:48

commit v10 on v9

--- a/solution.py
+++ b/solution.py
@@ -409,7 +409,7 @@
             for i, table in enumerate(tables):
                 cells_ref[i, k, tile_rows(t), :] = lookup(table, kind)
 
-    over(0, nz, 4, layer)
+    over(0, nz, 8, layer)
 
 
 def depth_kernel(stress_ref, velocity_hbm, depth_ref, along_ref, velocity_ref, sem):
@@ -477,7 +477,7 @@
     for spot, k in enumerate((0, 1, nz - 2, nz - 1)):
         layer(k, outer_ref, spot)
 
-    over(2, nz - 2, 4, lambda k: layer(k, inner_ref, k - 2))
+    over(2, nz - 2, 12, lambda k: layer(k, inner_ref, k - 2))
     pack_sides(
         lambda c, k, t: out_ref[c, k, tile_rows(t), :], nz, ny, nx, vlow_ref, vhigh_ref, vx1_ref, vx2_ref
     )
@@ -593,12 +593,11 @@
     inner = nz - 4
     step = next(d for d in (4, 3, 2, 1) if inner % d == 0)
 
-    @pl.loop(0, inner // step)
-    def _(j):
-        for i in range(step):
-            k = 2 + j * step + i
-            layer(k, inner_ref, k - 2)
-        send(2 + j * step, step)
+    for k in range(2, nz - 2):
+        layer(k, inner_ref, k - 2)
+        if (k - 1) % 2 == 0 or k == nz - 3:
+            count = (k - 2) % 2 + 1
+            send(k + 1 - count, count)
 
     depth_halos(n_gz, zb, za, z1_ref, z2_ref)
     outer_depth(vel_ref, zb, za, outer, 3, nz, tiles)

time: 25.9 us -> 25.6 us (0.988)
  Pallas kernels: 8.08 us -> 7.65 us
  transfers between devices with their start and end apart: 14 -> 14, of which waited for: 5 -> 5; matrix products, arithmetic and copies ran while one was open for 0% -> 0% of each run, Pallas kernels for 18% -> 17%
where the time goes in v10:
time: 25.6 us; the launch traced here: 25.4 us
  starting transfers between devices  14.4 us (56%)
  Pallas kernels  7.65 us (30%)
  waiting for transfers between devices  2.46 us (10%)
  between operations  0.87 us (3%)
    ppermute x11, starting transfers between devices, exchange(): got = [lax.ppermute(v, tuple(sizes), r) for v, r in rounds]  11.2 us
    ppermute x1, starting transfers between devices, local(): slab = slab + lax.ppermute(slab, tuple(sizes), rounds[1])  2.63 us
    pallas_call x1, Pallas kernels, local(): call(functools.partial(stress_kernel, counts), [stress.shape, stress.shap...  1.97 us
    ppermute x11, waiting for transfers between devices, exchange(): got = [lax.ppermute(v, tuple(sizes), r) for v, r in rounds]  1.49 us
    pallas_call x1, Pallas kernels, local(): call(depth_kernel, [(6, nz - 4, ny, nx), velocity.shape, velocity.shape],...  1.14 us
    pallas_call x1, Pallas kernels, local(): call(velocity_inner_kernel, [velocity.shape, (3, nz - 4, ny, nx), velocit...  0.89 us
    pallas_call x1, Pallas kernels, local(): call(terrain_piece_kernel, [(rows, nx)], [HB] * 3, [pltpu.VMEM(elevation....  0.82 us
    pallas_call x1, Pallas kernels, local(): call(functools.partial(velocity_kernel, counts), [velocity.shape] + [(xs,...  0.78 us
  transfers between devices with their start and end apart: 14, of which 5 were waited for; matrix products, arithmetic and copies ran while one was open for 0% of the time, Pallas kernels for 17%

profile of v10, /device:TPU:0, one launch (start us, length us, event | category | flops | bytes accessed | tf_op | source)
XLA Modules:
  0.0 25.4 jit_solution(10815088223733199770)
XLA Ops:
  0.6 0.0 copy-start
  0.6 0.5 %collective-permute-start = (s32[32,32]{1,0:T(8,128)}, s32[32,32]{1,0:T(8,128)S(1)}, u32[]{:S(2)}, u32[]{:S(2)}) collective-permute-start(s32[32,32]{1,0:T(8,128)} %elev_hbm.1), channel_id=1, source_target_pairs={{0,1},{1,0},{2,3},{3,2},{4,5},{5,4},{6,7},{7,6},{8,9},{9,8},{10,11... | collective-permute-start | bytes 12296 | tf_op jit(solution)/shard_map/ppermute | solution.py:638
  1.2 0.8 %terrain_piece.1.first_ref = f32[40,128]{1,0:T(8,128)S(1)} custom-call(s32[32,32]{1,0:T(8,128)} %elev_hbm.1, f32[1,16]{1,0:T(1,128)} %bitcast.12, f32[1,16]{1,0:T(1,128)} %bitcast.13), custom_call_target="tpu_custom_call" | custom-call | flops 480000000 | bytes 2800000 | tf_op jit(solution)/shard_map/terrain_piece/pallas_call | solution.py:639
  2.0 0.2 collective-permute-done.elev_ref
  2.2 0.1 merge.1
  2.3 2.6 %collective-permute-start.1 = (f32[40,128]{1,0:T(8,128)S(1)}, f32[40,128]{1,0:T(8,128)S(1)}, u32[]{:S(2)}, u32[]{:S(2)}) collective-permute-start(f32[40,128]{1,0:T(8,128)S(1)} %merge.1), channel_id=1, source_target_pairs={{0,3},{1,2},{2,1},{3,0},{4,7},{5,6},{6,5},{7,4},{8,11},{9,10},{10,... | collective-permute-start | bytes 61448 | tf_op jit(solution)/shard_map/ppermute | solution.py:659
  4.9 0.0 copy-done
  4.9 0.3 %pack_stress.1 = (f32[24,128]{1,0:T(8,128)S(1)}, f32[24,128]{1,0:T(8,128)S(1)}, f32[24,128]{1,0:T(8,128)S(1)}, f32[24,128]{1,0:T(8,128)S(1)}, f32[6,2,32,128]{3,...) custom-call(f32[6,16,32,128]{3,2,1,0:T(8,128)S(1)} %copy-done), custom_call_target="tpu_custom_call" | custom-call | flops 300000000 | bytes 1750000 | tf_op jit(solution)/shard_map/pack_stress/pallas_call | solution.py:673
  5.2 0.4 %collective-permute-start.3 = (f32[6,2,32,128]{3,2,1,0:T(8,128)S(1)}, f32[6,2,32,128]{3,2,1,0:T(8,128)S(1)}, u32[]{:S(2)}, u32[]{:S(2)}) collective-permute-start(f32[6,2,32,128]{3,2,1,0:T(8,128)S(1)} %get-tuple-element.60), channel_id=1, source_target_pairs={{0,1},{1,0},{2,3},{3,2},{4,5},{5,4},{6,7},{7,6},{8,9},{9,8},{10,11... | collective-permute-start | bytes 589832 | tf_op jit(solution)/shard_map/ppermute | solution.py:48
  5.6 0.0 collective-permute-start.4
  5.7 0.7 %collective-permute-done.1 = f32[40,128]{1,0:T(8,128)S(1)} collective-permute-done((f32[40,128]{1,0:T(8,128)S(1)}, f32[40,128]{1,0:T(8,128)S(1)}, u32[]{:S(2)}, u32[]{:S(2)}) %collective-permute-start.1) | collective-permute-done | bytes 20512 | tf_op jit(solution)/shard_map/ppermute | solution.py:659
  6.4 0.0 copy-start.2
  6.4 0.0 copy-start.3
  6.4 0.0 copy-start.4
  6.5 0.0 copy-start.5
  6.5 0.0 copy-start.6
  6.5 0.0 copy-start.7
  6.5 2.0 %collective-permute-start.6 = (f32[8,128]{1,0:T(8,128)S(1)}, f32[8,128]{1,0:T(8,128)S(1)}, u32[]{:S(2)}, u32[]{:S(2)}) collective-permute-start(f32[8,128]{1,0:T(8,128)S(1)} %y_send.1), channel_id=1, source_target_pairs={{0,4},{1,5},{2,6},{3,7},{4,0},{5,1},{6,2},{7,3},{8,12},{9,13},{10,... | collective-permute-start | bytes 12296 | tf_op jit(solution)/shard_map/ppermute | solution.py:48
  8.5 0.0 collective-permute-start.5
  8.5 0.3 %collective-permute-start.2 = (f32[96,128]{1,0:T(8,128)S(1)}, f32[96,128]{1,0:T(8,128)S(1)}, u32[]{:S(2)}, u32[]{:S(2)}) collective-permute-start(f32[96,128]{1,0:T(8,128)S(1)} %get-tuple-element.59), channel_id=1, source_target_pairs={{0,4},{1,5},{2,6},{3,7},{4,0},{5,1},{6,2},{7,3},{8,12},{9,13},{10,... | collective-permute-start | bytes 147464 | tf_op jit(solution)/shard_map/ppermute | solution.py:48
  8.8 1.1 %depth.1 = (f32[6,12,32,128]{3,2,1,0:T(8,128)S(1)}, f32[3,16,32,128]{3,2,1,0:T(8,128)S(1)}, f32[3,16,32,128]{3,2,1,0:T(8,128)S(1)}) custom-call(f32[6,16,32,128]{3,2,1,0:T(8,128)S(1)} %copy-done, f32[3,16,32,128]{3,2,1,0:T(8,128)} %velocity_hbm.1), custom_call_target="tpu_custom_call" | custom-call | flops 1320000000 | bytes 7700000 | tf_op jit(solution)/shard_map/depth/pallas_call | solution.py:686
  9.9 0.3 %collective-permute-done.6.y1_ref.y2_ref = f32[8,128]{1,0:T(8,128)S(1)} collective-permute-done((f32[8,128]{1,0:T(8,128)S(1)}, f32[8,128]{1,0:T(8,128)S(1)}, u32[]{:S(2)}, u32[]{:S(2)}) %collective-permute-start.6) | collective-permute-done | bytes 4128 | tf_op jit(solution)/shard_map/ppermute | solution.py:48
  10.2 0.1 x_send.1
  10.3 2.1 %collective-permute-start.7 = (f32[32,128]{1,0:T(8,128)S(1)}, f32[32,128]{1,0:T(8,128)S(1)}, u32[]{:S(2)}, u32[]{:S(2)}) collective-permute-start(f32[32,128]{1,0:T(8,128)S(1)} %get-tuple-element.74), channel_id=1, source_target_pairs={{0,8},{1,9},{2,10},{3,11},{4,12},{5,13},{6,14},{7,15},{8,0},{9,1},... | collective-permute-start | bytes 49160 | tf_op jit(solution)/shard_map/ppermute | solution.py:48
  12.3 0.0 collective-permute-done.5
  12.3 0.0 collective-permute-start.8
  12.3 0.0 copy-done.2
  12.3 0.0 copy-done.3
  12.4 0.0 copy-done.4
  12.4 0.0 copy-done.5
  12.4 0.0 copy-done.6
  12.4 0.0 copy-done.7
  12.4 0.8 %cells.1 = (f32[5,16,32,128]{3,2,1,0:T(8,128)S(1)}, f32[2,64,128]{2,1,0:T(8,128)S(1)}) custom-call(f32[8,128]{1,0:T(8,128)S(1)} %add.7.layers_ref, s32[16,32,128]{2,1,0:T(8,128)S(1)} %copy-done.2, f32[1,16]{1,0:T(1,128)S(1)} %bitcast.7, f32[1,16]{1,0:T(1,128)S(1)} %bitcast.8, f32[1,16]{1,0:T(1,128)S(1)} %bitcast.9, f32[1,16]{1,0:T(1,128)S(1)} %bitcast.10, ...), custom_call_target="tpu_custom_call" | custom-call | flops 480000000 | bytes 2800000 | tf_op jit(solution)/shard_map/cells/pallas_call | solution.py:710
  13.2 0.0 collective-permute-done.2.y1_ref.y2_ref
  13.2 0.0 collective-permute-done.3.z1_ref
  13.2 0.0 collective-permute-done.4.z2_ref
  13.2 0.4 %planes.1 = (f32[3,16,32,128]{3,2,1,0:T(8,128)S(1)}, f32[6,4,32,128]{3,2,1,0:T(8,128)S(1)}) custom-call(f32[6,16,32,128]{3,2,1,0:T(8,128)S(1)} %copy-done, f32[3,16,32,128]{3,2,1,0:T(8,128)S(1)} %get-tuple-element.58.along_ref, f32[96,128]{1,0:T(8,128)S(1)} %collective-permute-done.2.y1_ref.y2_ref, f32[96,128]{1,0:T(8,128)S(1)} %collective-permute-done.2.y1_ref.y2_ref, ...), custom_call_target="tpu_custom_call" | custom-call | flops 360000000 | bytes 2100000 | tf_op jit(solution)/shard_map/planes/pallas_call | solution.py:713
  13.6 0.4 %collective-permute-done.7.x1_ref = f32[32,128]{1,0:T(8,128)S(1)} collective-permute-done((f32[32,128]{1,0:T(8,128)S(1)}, f32[32,128]{1,0:T(8,128)S(1)}, u32[]{:S(2)}, u32[]{:S(2)}) %collective-permute-start.7) | collective-permute-done | bytes 16416 | tf_op jit(solution)/shard_map/ppermute | solution.py:48
  14.0 0.0 collective-permute-done.8.x2_ref
  14.1 0.4 %metrics.1 = (f32[16,32,128]{2,1,0:T(8,128)S(1)}, f32[16,32,128]{2,1,0:T(8,128)S(1)}, f32[2,32,128]{2,1,0:T(8,128)S(1)}) custom-call(f32[2,64,128]{2,1,0:T(8,128)S(1)} %get-tuple-element.80.layers_ref, f32[48,128]{1,0:T(8,128)S(1)} %get-tuple-element.81.own, f32[8,128]{1,0:T(8,128)S(1)} %slice.10.x1_ref, f32[8,128]{1,0:T(8,128)S(1)} %slice.11.x2_ref), custom_call_target="tpu_custom_call" | custom-call | flops 660000000 | bytes 3850000 | tf_op jit(solution)/shard_map/metrics/pallas_call | solution.py:721
  14.5 0.0 copy-start.1
  14.5 0.8 %velocity.1 = (f32[3,16,32,128]{3,2,1,0:T(8,128)S(1)}, f32[24,128]{1,0:T(8,128)S(1)}, f32[24,128]{1,0:T(8,128)S(1)}, f32[24,128]{1,0:T(8,128)S(1)}, f32[24,128]{...) custom-call(f32[3,16,32,128]{3,2,1,0:T(8,128)S(1)} %get-tuple-element.57.veloc, ...), custom_call_target="tpu_custom_call" | custom-call | flops 900000000 | bytes 5250000 | tf_op jit(solution)/shard_map/velocity/pallas_call | solution.py:728
  15.3 0.2 collective-permute-start.12
  15.5 2.0 %collective-permute-start.13 = (f32[3,2,32,128]{3,2,1,0:T(8,128)S(1)}, f32[3,2,32,128]{3,2,1,0:T(8,128)S(1)}, u32[]{:S(2)}, u32[]{:S(2)}) collective-permute-start(f32[3,2,32,128]{3,2,1,0:T(8,128)S(1)} %get-tuple-element.100), channel_id=1, source_target_pairs={{0,3},{1,2},{2,1},{3,0},{4,7},{5,6},{6,5},{7,4},{8,11},{9,10},{10,... | collective-permute-start | bytes 294920 | tf_op jit(solution)/shard_map/ppermute | solution.py:48
  17.5 1.5 %collective-permute-start.11 = (f32[96,128]{1,0:T(8,128)S(1)}, f32[96,128]{1,0:T(8,128)S(1)}, u32[]{:S(2)}, u32[]{:S(2)}) collective-permute-start(f32[96,128]{1,0:T(8,128)S(1)} %get-tuple-element.98), channel_id=1, source_target_pairs={{0,4},{1,5},{2,6},{3,7},{4,0},{5,1},{6,2},{7,3},{8,12},{9,13},{10,... | collective-permute-start | bytes 147464 | tf_op jit(solution)/shard_map/ppermute | solution.py:48
  19.0 2.7 %collective-permute-start.9 = (f32[24,128]{1,0:T(8,128)S(1)}, f32[24,128]{1,0:T(8,128)S(1)}, u32[]{:S(2)}, u32[]{:S(2)}) collective-permute-start(f32[24,128]{1,0:T(8,128)S(1)} %get-tuple-element.94), channel_id=1, source_target_pairs={{0,8},{1,9},{2,10},{3,11},{4,12},{5,13},{6,14},{7,15},{8,0},{9,1},... | collective-permute-start | bytes 36872 | tf_op jit(solution)/shard_map/ppermute | solution.py:48
  21.7 0.0 collective-permute-start.10
  21.7 0.9 %velocity_inner.1 = (f32[3,16,32,128]{3,2,1,0:T(8,128)}, f32[3,12,32,128]{3,2,1,0:T(8,128)S(1)}, f32[3,16,32,128]{3,2,1,0:T(8,128)S(1)}, f32[3,16,32,128]{3,2,1,0:T(8,128)S(1)}) custom-call(f32[3,16,32,128]{3,2,1,0:T(8,128)S(1)} %get-tuple-element.89.vel_ref), custom_call_target="tpu_custom_call" | custom-call | flops 60000000 | bytes 350000 | tf_op jit(solution)/shard_map/velocity_inner/pallas_call | solution.py:738
  22.6 0.8 %collective-permute-done.9.x1_ref = f32[24,128]{1,0:T(8,128)S(1)} collective-permute-done((f32[24,128]{1,0:T(8,128)S(1)}, f32[24,128]{1,0:T(8,128)S(1)}, u32[]{:S(2)}, u32[]{:S(2)}) %collective-permute-start.9) | collective-permute-done | bytes 12320 | tf_op jit(solution)/shard_map/ppermute | solution.py:48
  23.4 0.0 collective-permute-done.10.x2_ref
  23.4 0.0 collective-permute-done.11.y1_ref.y2_ref
  23.4 0.0 collective-permute-done.12.z1_ref
  23.4 0.0 collective-permute-done.13.z2_ref
  23.4 0.0 copy-done.1
  23.4 2.0 %stress.1 = (f32[6,16,32,128]{3,2,1,0:T(8,128)}, f32[6,16,32,128]{3,2,1,0:T(8,128)}) custom-call(f32[3,16,32,128]{3,2,1,0:T(8,128)S(1)} %get-tuple-element.89.vel_ref, f32[6,16,32,128]{3,2,1,0:T(8,128)S(1)} %copy-done, f32[6,16,32,128]{3,2,1,0:T(8,128)S(1)} %copy-done.1, f32[5,16,32,128]{3,2,1,0:T(8,128)S(1)} %get-tuple-element.76.cells_ref, ...), custom_call_target="tpu_custom_call" | custom-call | flops 1680000000 | bytes 9800000 | tf_op jit(solution)/shard_map/stress/pallas_call | solution.py:746
  (6 shorter events, 0.0 us)
Async XLA Ops:
  0.6 4.3 %copy-start = (f32[6,16,32,128]{3,2,1,0:T(8,128)S(1)}, f32[6,16,32,128]{3,2,1,0:T(8,128)}, u32[]{:S(2)}) copy-start(f32[6,16,32,128]{3,2,1,0:T(8,128)} %stress_ref.3) | copy-start | bytes 4718596
  0.6 1.6 %collective-permute-start = (s32[32,32]{1,0:T(8,128)}, s32[32,32]{1,0:T(8,128)S(1)}, u32[]{:S(2)}, u32[]{:S(2)}) collective-permute-start(s32[32,32]{1,0:T(8,128)} %elev_hbm.1), channel_id=1, source_target_pairs={{0,1},{1,0},{2,3},{3,2},{4,5},{5,4},{6,7},{7,6},{8,9},{9,8},{10,11... | collective-permute-start | bytes 12296 | tf_op jit(solution)/shard_map/ppermute | solution.py:638
  2.3 4.1 %collective-permute-start.1 = (f32[40,128]{1,0:T(8,128)S(1)}, f32[40,128]{1,0:T(8,128)S(1)}, u32[]{:S(2)}, u32[]{:S(2)}) collective-permute-start(f32[40,128]{1,0:T(8,128)S(1)} %merge.1), channel_id=1, source_target_pairs={{0,3},{1,2},{2,1},{3,0},{4,7},{5,6},{6,5},{7,4},{8,11},{9,10},{10,... | collective-permute-start | bytes 61448 | tf_op jit(solution)/shard_map/ppermute | solution.py:659
  5.2 8.0 %collective-permute-start.3 = (f32[6,2,32,128]{3,2,1,0:T(8,128)S(1)}, f32[6,2,32,128]{3,2,1,0:T(8,128)S(1)}, u32[]{:S(2)}, u32[]{:S(2)}) collective-permute-start(f32[6,2,32,128]{3,2,1,0:T(8,128)S(1)} %get-tuple-element.60), channel_id=1, source_target_pairs={{0,1},{1,0},{2,3},{3,2},{4,5},{5,4},{6,7},{7,6},{8,9},{9,8},{10,11... | collective-permute-start | bytes 589832 | tf_op jit(solution)/shard_map/ppermute | solution.py:48
  5.6 7.6 %collective-permute-start.4 = (f32[6,2,32,128]{3,2,1,0:T(8,128)S(1)}, f32[6,2,32,128]{3,2,1,0:T(8,128)S(1)}, u32[]{:S(2)}, u32[]{:S(2)}) collective-permute-start(f32[6,2,32,128]{3,2,1,0:T(8,128)S(1)} %get-tuple-element.61), channel_id=1, source_target_pairs={{0,3},{1,2},{2,1},{3,0},{4,7},{5,6},{6,5},{7,4},{8,11},{9,10},{10,... | collective-permute-start | bytes 589832 | tf_op jit(solution)/shard_map/ppermute | solution.py:48
  6.4 5.9 %copy-start.2 = (s32[16,32,128]{2,1,0:T(8,128)S(1)}, s32[16,32,128]{2,1,0:T(8,128)}, u32[]{:S(2)}) copy-start(s32[16,32,128]{2,1,0:T(8,128)} %material_ref) | copy-start | bytes 786436
  6.4 5.9 %copy-start.3 = (f32[16]{0:T(128)S(1)}, f32[16]{0:T(128)}, u32[]{:S(2)}) copy-start(f32[16]{0:T(128)} %param.16) | copy-start | bytes 196
  6.4 5.9 %copy-start.4 = (f32[16]{0:T(128)S(1)}, f32[16]{0:T(128)}, u32[]{:S(2)}) copy-start(f32[16]{0:T(128)} %param.17) | copy-start | bytes 196
  6.5 5.9 %copy-start.5 = (f32[16]{0:T(128)S(1)}, f32[16]{0:T(128)}, u32[]{:S(2)}) copy-start(f32[16]{0:T(128)} %param.18) | copy-start | bytes 196
  6.5 5.9 %copy-start.6 = (f32[16]{0:T(128)S(1)}, f32[16]{0:T(128)}, u32[]{:S(2)}) copy-start(f32[16]{0:T(128)} %param.19) | copy-start | bytes 196
  6.5 5.9 %copy-start.7 = (f32[16]{0:T(128)S(1)}, f32[16]{0:T(128)}, u32[]{:S(2)}) copy-start(f32[16]{0:T(128)} %param.20) | copy-start | bytes 196
  6.5 3.7 %collective-permute-start.6 = (f32[8,128]{1,0:T(8,128)S(1)}, f32[8,128]{1,0:T(8,128)S(1)}, u32[]{:S(2)}, u32[]{:S(2)}) collective-permute-start(f32[8,128]{1,0:T(8,128)S(1)} %y_send.1), channel_id=1, source_target_pairs={{0,4},{1,5},{2,6},{3,7},{4,0},{5,1},{6,2},{7,3},{8,12},{9,13},{10,... | collective-permute-start | bytes 12296 | tf_op jit(solution)/shard_map/ppermute | solution.py:48
  8.5 3.8 %collective-permute-start.5 = (f32[8,128]{1,0:T(8,128)S(1)}, f32[8,128]{1,0:T(8,128)S(1)}, u32[]{:S(2)}, u32[]{:S(2)}) collective-permute-start(f32[8,128]{1,0:T(8,128)S(1)} %slice.12), channel_id=1, source_target_pairs={{0,1},{1,0},{2,3},{3,2},{4,5},{5,4},{6,7},{7,6},{8,9},{9,8},{10,11... | collective-permute-start | bytes 12296 | tf_op jit(solution)/shard_map/ppermute | solution.py:685
  8.5 4.7 %collective-permute-start.2 = (f32[96,128]{1,0:T(8,128)S(1)}, f32[96,128]{1,0:T(8,128)S(1)}, u32[]{:S(2)}, u32[]{:S(2)}) collective-permute-start(f32[96,128]{1,0:T(8,128)S(1)} %get-tuple-element.59), channel_id=1, source_target_pairs={{0,4},{1,5},{2,6},{3,7},{4,0},{5,1},{6,2},{7,3},{8,12},{9,13},{10,... | collective-permute-start | bytes 147464 | tf_op jit(solution)/shard_map/ppermute | solution.py:48
  10.3 3.8 %collective-permute-start.7 = (f32[32,128]{1,0:T(8,128)S(1)}, f32[32,128]{1,0:T(8,128)S(1)}, u32[]{:S(2)}, u32[]{:S(2)}) collective-permute-start(f32[32,128]{1,0:T(8,128)S(1)} %get-tuple-element.74), channel_id=1, source_target_pairs={{0,8},{1,9},{2,10},{3,11},{4,12},{5,13},{6,14},{7,15},{8,0},{9,1},... | collective-permute-start | bytes 49160 | tf_op jit(solution)/shard_map/ppermute | solution.py:48
  12.3 1.7 %collective-permute-start.8 = (f32[32,128]{1,0:T(8,128)S(1)}, f32[32,128]{1,0:T(8,128)S(1)}, u32[]{:S(2)}, u32[]{:S(2)}) collective-permute-start(f32[32,128]{1,0:T(8,128)S(1)} %get-tuple-element.75), channel_id=1, source_target_pairs={{0,1},{1,0},{2,3},{3,2},{4,5},{5,4},{6,7},{7,6},{8,16},{9,17},{10,... | collective-permute-start | bytes 49160 | tf_op jit(solution)/shard_map/ppermute | solution.py:48
  14.5 9.0 %copy-start.1 = (f32[6,16,32,128]{3,2,1,0:T(8,128)S(1)}, f32[6,16,32,128]{3,2,1,0:T(8,128)}, u32[]{:S(2)}) copy-start(f32[6,16,32,128]{3,2,1,0:T(8,128)} %memory_ref.1) | copy-start | bytes 4718596
  15.3 8.1 %collective-permute-start.12 = (f32[3,2,32,128]{3,2,1,0:T(8,128)S(1)}, f32[3,2,32,128]{3,2,1,0:T(8,128)S(1)}, u32[]{:S(2)}, u32[]{:S(2)}) collective-permute-start(f32[3,2,32,128]{3,2,1,0:T(8,128)S(1)} %get-tuple-element.99), channel_id=1, source_target_pairs={{0,1},{1,0},{2,3},{3,2},{4,5},{5,4},{6,7},{7,6},{8,9},{9,8},{10,11... | collective-permute-start | bytes 294920 | tf_op jit(solution)/shard_map/ppermute | solution.py:48
  15.5 7.9 %collective-permute-start.13 = (f32[3,2,32,128]{3,2,1,0:T(8,128)S(1)}, f32[3,2,32,128]{3,2,1,0:T(8,128)S(1)}, u32[]{:S(2)}, u32[]{:S(2)}) collective-permute-start(f32[3,2,32,128]{3,2,1,0:T(8,128)S(1)} %get-tuple-element.100), channel_id=1, source_target_pairs={{0,3},{1,2},{2,1},{3,0},{4,7},{5,6},{6,5},{7,4},{8,11},{9,10},{10,... | collective-permute-start | bytes 294920 | tf_op jit(solution)/shard_map/ppermute | solution.py:48
  17.5 5.9 %collective-permute-start.11 = (f32[96,128]{1,0:T(8,128)S(1)}, f32[96,128]{1,0:T(8,128)S(1)}, u32[]{:S(2)}, u32[]{:S(2)}) collective-permute-start(f32[96,128]{1,0:T(8,128)S(1)} %get-tuple-element.98), channel_id=1, source_target_pairs={{0,4},{1,5},{2,6},{3,7},{4,0},{5,1},{6,2},{7,3},{8,12},{9,13},{10,... | collective-permute-start | bytes 147464 | tf_op jit(solution)/shard_map/ppermute | solution.py:48
  19.0 4.4 %collective-permute-start.9 = (f32[24,128]{1,0:T(8,128)S(1)}, f32[24,128]{1,0:T(8,128)S(1)}, u32[]{:S(2)}, u32[]{:S(2)}) collective-permute-start(f32[24,128]{1,0:T(8,128)S(1)} %get-tuple-element.94), channel_id=1, source_target_pairs={{0,8},{1,9},{2,10},{3,11},{4,12},{5,13},{6,14},{7,15},{8,0},{9,1},... | collective-permute-start | bytes 36872 | tf_op jit(solution)/shard_map/ppermute | solution.py:48
  21.7 1.7 %collective-permute-start.10 = (f32[24,128]{1,0:T(8,128)S(1)}, f32[24,128]{1,0:T(8,128)S(1)}, u32[]{:S(2)}, u32[]{:S(2)}) collective-permute-start(f32[24,128]{1,0:T(8,128)S(1)} %get-tuple-element.95), channel_id=1, source_target_pairs={{0,1},{1,0},{2,3},{3,2},{4,5},{5,4},{6,7},{7,6},{8,16},{9,17},{10,... | collective-permute-start | bytes 36872 | tf_op jit(solution)/shard_map/ppermute | solution.py:48

commit v11 on v10

--- a/solution.py
+++ b/solution.py
@@ -595,16 +595,13 @@
 
     for k in range(2, nz - 2):
         layer(k, inner_ref, k - 2)
-        if (k - 1) % 2 == 0 or k == nz - 3:
-            count = (k - 2) % 2 + 1
-            send(k + 1 - count, count)
+        send(k, 1)
 
     depth_halos(n_gz, zb, za, z1_ref, z2_ref)
     outer_depth(vel_ref, zb, za, outer, 3, nz, tiles)
     for spot, k in enumerate((0, 1, nz - 2, nz - 1)):
         layer(k, outer, spot)
-        if spot % 2 == 1:
-            send(k - 1, 2)
+        send(k, 1)
     for i, (a, b) in enumerate(pairs):
         pltpu.make_async_copy(a, b, sems.at[i]).wait()
 

time: 25.6 us -> 25.6 us (level)
  no operation moved by 1% of the time
where the time goes in v11:
time: 25.6 us; the launch traced here: 25.4 us
  starting transfers between devices  14.4 us (56%)
  Pallas kernels  7.62 us (30%)
  waiting for transfers between devices  2.46 us (10%)
  between operations  0.87 us (3%)
    ppermute x11, starting transfers between devices, exchange(): got = [lax.ppermute(v, tuple(sizes), r) for v, r in rounds]  11.2 us
    ppermute x1, starting transfers between devices, local(): slab = slab + lax.ppermute(slab, tuple(sizes), rounds[1])  2.63 us
    pallas_call x1, Pallas kernels, local(): call(functools.partial(stress_kernel, counts), [stress.shape, stress.shap...  1.94 us
    ppermute x11, waiting for transfers between devices, exchange(): got = [lax.ppermute(v, tuple(sizes), r) for v, r in rounds]  1.49 us
    pallas_call x1, Pallas kernels, local(): call(depth_kernel, [(6, nz - 4, ny, nx), velocity.shape, velocity.shape],...  1.14 us
    pallas_call x1, Pallas kernels, local(): call(velocity_inner_kernel, [velocity.shape, (3, nz - 4, ny, nx), velocit...  0.89 us
    pallas_call x1, Pallas kernels, local(): call(terrain_piece_kernel, [(rows, nx)], [HB] * 3, [pltpu.VMEM(elevation....  0.82 us
    pallas_call x1, Pallas kernels, local(): call(functools.partial(velocity_kernel, counts), [velocity.shape] + [(xs,...  0.78 us
  transfers between devices with their start and end apart: 14, of which 5 were waited for; matrix products, arithmetic and copies ran while one was open for 0% of the time, Pallas kernels for 17%

profile of v11, /device:TPU:0, one launch (start us, length us, event | category | flops | bytes accessed | tf_op | source)
XLA Modules:
  0.0 25.4 jit_solution(4381522302941198940)
XLA Ops:
  0.6 0.0 copy-start
  0.6 0.5 %collective-permute-start = (s32[32,32]{1,0:T(8,128)}, s32[32,32]{1,0:T(8,128)S(1)}, u32[]{:S(2)}, u32[]{:S(2)}) collective-permute-start(s32[32,32]{1,0:T(8,128)} %elev_hbm.1), channel_id=1, source_target_pairs={{0,1},{1,0},{2,3},{3,2},{4,5},{5,4},{6,7},{7,6},{8,9},{9,8},{10,11... | collective-permute-start | bytes 12296 | tf_op jit(solution)/shard_map/ppermute | solution.py:635
  1.2 0.8 %terrain_piece.1.first_ref = f32[40,128]{1,0:T(8,128)S(1)} custom-call(s32[32,32]{1,0:T(8,128)} %elev_hbm.1, f32[1,16]{1,0:T(1,128)} %bitcast.12, f32[1,16]{1,0:T(1,128)} %bitcast.13), custom_call_target="tpu_custom_call" | custom-call | flops 480000000 | bytes 2800000 | tf_op jit(solution)/shard_map/terrain_piece/pallas_call | solution.py:636
  2.0 0.2 collective-permute-done.elev_ref
  2.2 0.1 merge.1
  2.3 2.6 %collective-permute-start.1 = (f32[40,128]{1,0:T(8,128)S(1)}, f32[40,128]{1,0:T(8,128)S(1)}, u32[]{:S(2)}, u32[]{:S(2)}) collective-permute-start(f32[40,128]{1,0:T(8,128)S(1)} %merge.1), channel_id=1, source_target_pairs={{0,3},{1,2},{2,1},{3,0},{4,7},{5,6},{6,5},{7,4},{8,11},{9,10},{10,... | collective-permute-start | bytes 61448 | tf_op jit(solution)/shard_map/ppermute | solution.py:656
  4.9 0.0 copy-done
  4.9 0.3 %pack_stress.1 = (f32[24,128]{1,0:T(8,128)S(1)}, f32[24,128]{1,0:T(8,128)S(1)}, f32[24,128]{1,0:T(8,128)S(1)}, f32[24,128]{1,0:T(8,128)S(1)}, f32[6,2,32,128]{3,...) custom-call(f32[6,16,32,128]{3,2,1,0:T(8,128)S(1)} %copy-done), custom_call_target="tpu_custom_call" | custom-call | flops 300000000 | bytes 1750000 | tf_op jit(solution)/shard_map/pack_stress/pallas_call | solution.py:670
  5.2 0.4 %collective-permute-start.3 = (f32[6,2,32,128]{3,2,1,0:T(8,128)S(1)}, f32[6,2,32,128]{3,2,1,0:T(8,128)S(1)}, u32[]{:S(2)}, u32[]{:S(2)}) collective-permute-start(f32[6,2,32,128]{3,2,1,0:T(8,128)S(1)} %get-tuple-element.60), channel_id=1, source_target_pairs={{0,1},{1,0},{2,3},{3,2},{4,5},{5,4},{6,7},{7,6},{8,9},{9,8},{10,11... | collective-permute-start | bytes 589832 | tf_op jit(solution)/shard_map/ppermute | solution.py:48
  5.6 0.0 collective-permute-start.4
  5.7 0.7 %collective-permute-done.1 = f32[40,128]{1,0:T(8,128)S(1)} collective-permute-done((f32[40,128]{1,0:T(8,128)S(1)}, f32[40,128]{1,0:T(8,128)S(1)}, u32[]{:S(2)}, u32[]{:S(2)}) %collective-permute-start.1) | collective-permute-done | bytes 20512 | tf_op jit(solution)/shard_map/ppermute | solution.py:656
  6.4 0.0 copy-start.2
  6.4 0.0 copy-start.3
  6.4 0.0 copy-start.4
  6.5 0.0 copy-start.5
  6.5 0.0 copy-start.6
  6.5 0.0 copy-start.7
  6.5 2.0 %collective-permute-start.6 = (f32[8,128]{1,0:T(8,128)S(1)}, f32[8,128]{1,0:T(8,128)S(1)}, u32[]{:S(2)}, u32[]{:S(2)}) collective-permute-start(f32[8,128]{1,0:T(8,128)S(1)} %y_send.1), channel_id=1, source_target_pairs={{0,4},{1,5},{2,6},{3,7},{4,0},{5,1},{6,2},{7,3},{8,12},{9,13},{10,... | collective-permute-start | bytes 12296 | tf_op jit(solution)/shard_map/ppermute | solution.py:48
  8.5 0.0 collective-permute-start.5
  8.5 0.3 %collective-permute-start.2 = (f32[96,128]{1,0:T(8,128)S(1)}, f32[96,128]{1,0:T(8,128)S(1)}, u32[]{:S(2)}, u32[]{:S(2)}) collective-permute-start(f32[96,128]{1,0:T(8,128)S(1)} %get-tuple-element.59), channel_id=1, source_target_pairs={{0,4},{1,5},{2,6},{3,7},{4,0},{5,1},{6,2},{7,3},{8,12},{9,13},{10,... | collective-permute-start | bytes 147464 | tf_op jit(solution)/shard_map/ppermute | solution.py:48
  8.8 1.1 %depth.1 = (f32[6,12,32,128]{3,2,1,0:T(8,128)S(1)}, f32[3,16,32,128]{3,2,1,0:T(8,128)S(1)}, f32[3,16,32,128]{3,2,1,0:T(8,128)S(1)}) custom-call(f32[6,16,32,128]{3,2,1,0:T(8,128)S(1)} %copy-done, f32[3,16,32,128]{3,2,1,0:T(8,128)} %velocity_hbm.1), custom_call_target="tpu_custom_call" | custom-call | flops 1320000000 | bytes 7700000 | tf_op jit(solution)/shard_map/depth/pallas_call | solution.py:683
  9.9 0.3 %collective-permute-done.6.y1_ref.y2_ref = f32[8,128]{1,0:T(8,128)S(1)} collective-permute-done((f32[8,128]{1,0:T(8,128)S(1)}, f32[8,128]{1,0:T(8,128)S(1)}, u32[]{:S(2)}, u32[]{:S(2)}) %collective-permute-start.6) | collective-permute-done | bytes 4128 | tf_op jit(solution)/shard_map/ppermute | solution.py:48
  10.2 0.1 x_send.1
  10.3 2.1 %collective-permute-start.7 = (f32[32,128]{1,0:T(8,128)S(1)}, f32[32,128]{1,0:T(8,128)S(1)}, u32[]{:S(2)}, u32[]{:S(2)}) collective-permute-start(f32[32,128]{1,0:T(8,128)S(1)} %get-tuple-element.74), channel_id=1, source_target_pairs={{0,8},{1,9},{2,10},{3,11},{4,12},{5,13},{6,14},{7,15},{8,0},{9,1},... | collective-permute-start | bytes 49160 | tf_op jit(solution)/shard_map/ppermute | solution.py:48
  12.3 0.0 collective-permute-done.5
  12.3 0.0 collective-permute-start.8
  12.3 0.0 copy-done.2
  12.3 0.0 copy-done.3
  12.4 0.0 copy-done.4
  12.4 0.0 copy-done.5
  12.4 0.0 copy-done.6
  12.4 0.0 copy-done.7
  12.4 0.8 %cells.1 = (f32[5,16,32,128]{3,2,1,0:T(8,128)S(1)}, f32[2,64,128]{2,1,0:T(8,128)S(1)}) custom-call(f32[8,128]{1,0:T(8,128)S(1)} %add.7.layers_ref, s32[16,32,128]{2,1,0:T(8,128)S(1)} %copy-done.2, f32[1,16]{1,0:T(1,128)S(1)} %bitcast.7, f32[1,16]{1,0:T(1,128)S(1)} %bitcast.8, f32[1,16]{1,0:T(1,128)S(1)} %bitcast.9, f32[1,16]{1,0:T(1,128)S(1)} %bitcast.10, ...), custom_call_target="tpu_custom_call" | custom-call | flops 480000000 | bytes 2800000 | tf_op jit(solution)/shard_map/cells/pallas_call | solution.py:707
  13.2 0.0 collective-permute-done.2.y1_ref.y2_ref
  13.2 0.0 collective-permute-done.3.z1_ref
  13.2 0.0 collective-permute-done.4.z2_ref
  13.2 0.4 %planes.1 = (f32[3,16,32,128]{3,2,1,0:T(8,128)S(1)}, f32[6,4,32,128]{3,2,1,0:T(8,128)S(1)}) custom-call(f32[6,16,32,128]{3,2,1,0:T(8,128)S(1)} %copy-done, f32[3,16,32,128]{3,2,1,0:T(8,128)S(1)} %get-tuple-element.58.along_ref, f32[96,128]{1,0:T(8,128)S(1)} %collective-permute-done.2.y1_ref.y2_ref, f32[96,128]{1,0:T(8,128)S(1)} %collective-permute-done.2.y1_ref.y2_ref, ...), custom_call_target="tpu_custom_call" | custom-call | flops 360000000 | bytes 2100000 | tf_op jit(solution)/shard_map/planes/pallas_call | solution.py:710
  13.6 0.4 %collective-permute-done.7.x1_ref = f32[32,128]{1,0:T(8,128)S(1)} collective-permute-done((f32[32,128]{1,0:T(8,128)S(1)}, f32[32,128]{1,0:T(8,128)S(1)}, u32[]{:S(2)}, u32[]{:S(2)}) %collective-permute-start.7) | collective-permute-done | bytes 16416 | tf_op jit(solution)/shard_map/ppermute | solution.py:48
  14.0 0.0 collective-permute-done.8.x2_ref
  14.1 0.4 %metrics.1 = (f32[16,32,128]{2,1,0:T(8,128)S(1)}, f32[16,32,128]{2,1,0:T(8,128)S(1)}, f32[2,32,128]{2,1,0:T(8,128)S(1)}) custom-call(f32[2,64,128]{2,1,0:T(8,128)S(1)} %get-tuple-element.80.layers_ref, f32[48,128]{1,0:T(8,128)S(1)} %get-tuple-element.81.own, f32[8,128]{1,0:T(8,128)S(1)} %slice.10.x1_ref, f32[8,128]{1,0:T(8,128)S(1)} %slice.11.x2_ref), custom_call_target="tpu_custom_call" | custom-call | flops 660000000 | bytes 3850000 | tf_op jit(solution)/shard_map/metrics/pallas_call | solution.py:718
  14.5 0.0 copy-start.1
  14.5 0.8 %velocity.1 = (f32[3,16,32,128]{3,2,1,0:T(8,128)S(1)}, f32[24,128]{1,0:T(8,128)S(1)}, f32[24,128]{1,0:T(8,128)S(1)}, f32[24,128]{1,0:T(8,128)S(1)}, f32[24,128]{...) custom-call(f32[3,16,32,128]{3,2,1,0:T(8,128)S(1)} %get-tuple-element.57.veloc, ...), custom_call_target="tpu_custom_call" | custom-call | flops 900000000 | bytes 5250000 | tf_op jit(solution)/shard_map/velocity/pallas_call | solution.py:725
  15.3 0.2 collective-permute-start.12
  15.5 2.0 %collective-permute-start.13 = (f32[3,2,32,128]{3,2,1,0:T(8,128)S(1)}, f32[3,2,32,128]{3,2,1,0:T(8,128)S(1)}, u32[]{:S(2)}, u32[]{:S(2)}) collective-permute-start(f32[3,2,32,128]{3,2,1,0:T(8,128)S(1)} %get-tuple-element.100), channel_id=1, source_target_pairs={{0,3},{1,2},{2,1},{3,0},{4,7},{5,6},{6,5},{7,4},{8,11},{9,10},{10,... | collective-permute-start | bytes 294920 | tf_op jit(solution)/shard_map/ppermute | solution.py:48
  17.5 1.5 %collective-permute-start.11 = (f32[96,128]{1,0:T(8,128)S(1)}, f32[96,128]{1,0:T(8,128)S(1)}, u32[]{:S(2)}, u32[]{:S(2)}) collective-permute-start(f32[96,128]{1,0:T(8,128)S(1)} %get-tuple-element.98), channel_id=1, source_target_pairs={{0,4},{1,5},{2,6},{3,7},{4,0},{5,1},{6,2},{7,3},{8,12},{9,13},{10,... | collective-permute-start | bytes 147464 | tf_op jit(solution)/shard_map/ppermute | solution.py:48
  19.0 2.7 %collective-permute-start.9 = (f32[24,128]{1,0:T(8,128)S(1)}, f32[24,128]{1,0:T(8,128)S(1)}, u32[]{:S(2)}, u32[]{:S(2)}) collective-permute-start(f32[24,128]{1,0:T(8,128)S(1)} %get-tuple-element.94), channel_id=1, source_target_pairs={{0,8},{1,9},{2,10},{3,11},{4,12},{5,13},{6,14},{7,15},{8,0},{9,1},... | collective-permute-start | bytes 36872 | tf_op jit(solution)/shard_map/ppermute | solution.py:48
  21.7 0.0 collective-permute-start.10
  21.7 0.9 %velocity_inner.1 = (f32[3,16,32,128]{3,2,1,0:T(8,128)}, f32[3,12,32,128]{3,2,1,0:T(8,128)S(1)}, f32[3,16,32,128]{3,2,1,0:T(8,128)S(1)}, f32[3,16,32,128]{3,2,1,0:T(8,128)S(1)}) custom-call(f32[3,16,32,128]{3,2,1,0:T(8,128)S(1)} %get-tuple-element.89.vel_ref), custom_call_target="tpu_custom_call" | custom-call | flops 60000000 | bytes 350000 | tf_op jit(solution)/shard_map/velocity_inner/pallas_call | solution.py:735
  22.6 0.8 %collective-permute-done.9.x1_ref = f32[24,128]{1,0:T(8,128)S(1)} collective-permute-done((f32[24,128]{1,0:T(8,128)S(1)}, f32[24,128]{1,0:T(8,128)S(1)}, u32[]{:S(2)}, u32[]{:S(2)}) %collective-permute-start.9) | collective-permute-done | bytes 12320 | tf_op jit(solution)/shard_map/ppermute | solution.py:48
  23.4 0.0 collective-permute-done.10.x2_ref
  23.4 0.0 collective-permute-done.11.y1_ref.y2_ref
  23.4 0.0 collective-permute-done.12.z1_ref
  23.4 0.0 collective-permute-done.13.z2_ref
  23.4 0.0 copy-done.1
  23.4 1.9 %stress.1 = (f32[6,16,32,128]{3,2,1,0:T(8,128)}, f32[6,16,32,128]{3,2,1,0:T(8,128)}) custom-call(f32[3,16,32,128]{3,2,1,0:T(8,128)S(1)} %get-tuple-element.89.vel_ref, f32[6,16,32,128]{3,2,1,0:T(8,128)S(1)} %copy-done, f32[6,16,32,128]{3,2,1,0:T(8,128)S(1)} %copy-done.1, f32[5,16,32,128]{3,2,1,0:T(8,128)S(1)} %get-tuple-element.76.cells_ref, ...), custom_call_target="tpu_custom_call" | custom-call | flops 1680000000 | bytes 9800000 | tf_op jit(solution)/shard_map/stress/pallas_call | solution.py:743
  (6 shorter events, 0.0 us)
Async XLA Ops:
  0.6 4.3 %copy-start = (f32[6,16,32,128]{3,2,1,0:T(8,128)S(1)}, f32[6,16,32,128]{3,2,1,0:T(8,128)}, u32[]{:S(2)}) copy-start(f32[6,16,32,128]{3,2,1,0:T(8,128)} %stress_ref.3) | copy-start | bytes 4718596
  0.6 1.6 %collective-permute-start = (s32[32,32]{1,0:T(8,128)}, s32[32,32]{1,0:T(8,128)S(1)}, u32[]{:S(2)}, u32[]{:S(2)}) collective-permute-start(s32[32,32]{1,0:T(8,128)} %elev_hbm.1), channel_id=1, source_target_pairs={{0,1},{1,0},{2,3},{3,2},{4,5},{5,4},{6,7},{7,6},{8,9},{9,8},{10,11... | collective-permute-start | bytes 12296 | tf_op jit(solution)/shard_map/ppermute | solution.py:635
  2.3 4.1 %collective-permute-start.1 = (f32[40,128]{1,0:T(8,128)S(1)}, f32[40,128]{1,0:T(8,128)S(1)}, u32[]{:S(2)}, u32[]{:S(2)}) collective-permute-start(f32[40,128]{1,0:T(8,128)S(1)} %merge.1), channel_id=1, source_target_pairs={{0,3},{1,2},{2,1},{3,0},{4,7},{5,6},{6,5},{7,4},{8,11},{9,10},{10,... | collective-permute-start | bytes 61448 | tf_op jit(solution)/shard_map/ppermute | solution.py:656
  5.2 8.0 %collective-permute-start.3 = (f32[6,2,32,128]{3,2,1,0:T(8,128)S(1)}, f32[6,2,32,128]{3,2,1,0:T(8,128)S(1)}, u32[]{:S(2)}, u32[]{:S(2)}) collective-permute-start(f32[6,2,32,128]{3,2,1,0:T(8,128)S(1)} %get-tuple-element.60), channel_id=1, source_target_pairs={{0,1},{1,0},{2,3},{3,2},{4,5},{5,4},{6,7},{7,6},{8,9},{9,8},{10,11... | collective-permute-start | bytes 589832 | tf_op jit(solution)/shard_map/ppermute | solution.py:48
  5.6 7.6 %collective-permute-start.4 = (f32[6,2,32,128]{3,2,1,0:T(8,128)S(1)}, f32[6,2,32,128]{3,2,1,0:T(8,128)S(1)}, u32[]{:S(2)}, u32[]{:S(2)}) collective-permute-start(f32[6,2,32,128]{3,2,1,0:T(8,128)S(1)} %get-tuple-element.61), channel_id=1, source_target_pairs={{0,3},{1,2},{2,1},{3,0},{4,7},{5,6},{6,5},{7,4},{8,11},{9,10},{10,... | collective-permute-start | bytes 589832 | tf_op jit(solution)/shard_map/ppermute | solution.py:48
  6.4 5.9 %copy-start.2 = (s32[16,32,128]{2,1,0:T(8,128)S(1)}, s32[16,32,128]{2,1,0:T(8,128)}, u32[]{:S(2)}) copy-start(s32[16,32,128]{2,1,0:T(8,128)} %material_ref) | copy-start | bytes 786436
  6.4 5.9 %copy-start.3 = (f32[16]{0:T(128)S(1)}, f32[16]{0:T(128)}, u32[]{:S(2)}) copy-start(f32[16]{0:T(128)} %param.16) | copy-start | bytes 196
  6.4 5.9 %copy-start.4 = (f32[16]{0:T(128)S(1)}, f32[16]{0:T(128)}, u32[]{:S(2)}) copy-start(f32[16]{0:T(128)} %param.17) | copy-start | bytes 196
  6.5 5.9 %copy-start.5 = (f32[16]{0:T(128)S(1)}, f32[16]{0:T(128)}, u32[]{:S(2)}) copy-start(f32[16]{0:T(128)} %param.18) | copy-start | bytes 196
  6.5 5.9 %copy-start.6 = (f32[16]{0:T(128)S(1)}, f32[16]{0:T(128)}, u32[]{:S(2)}) copy-start(f32[16]{0:T(128)} %param.19) | copy-start | bytes 196
  6.5 5.9 %copy-start.7 = (f32[16]{0:T(128)S(1)}, f32[16]{0:T(128)}, u32[]{:S(2)}) copy-start(f32[16]{0:T(128)} %param.20) | copy-start | bytes 196
  6.5 3.7 %collective-permute-start.6 = (f32[8,128]{1,0:T(8,128)S(1)}, f32[8,128]{1,0:T(8,128)S(1)}, u32[]{:S(2)}, u32[]{:S(2)}) collective-permute-start(f32[8,128]{1,0:T(8,128)S(1)} %y_send.1), channel_id=1, source_target_pairs={{0,4},{1,5},{2,6},{3,7},{4,0},{5,1},{6,2},{7,3},{8,12},{9,13},{10,... | collective-permute-start | bytes 12296 | tf_op jit(solution)/shard_map/ppermute | solution.py:48
  8.5 3.8 %collective-permute-start.5 = (f32[8,128]{1,0:T(8,128)S(1)}, f32[8,128]{1,0:T(8,128)S(1)}, u32[]{:S(2)}, u32[]{:S(2)}) collective-permute-start(f32[8,128]{1,0:T(8,128)S(1)} %slice.12), channel_id=1, source_target_pairs={{0,1},{1,0},{2,3},{3,2},{4,5},{5,4},{6,7},{7,6},{8,9},{9,8},{10,11... | collective-permute-start | bytes 12296 | tf_op jit(solution)/shard_map/ppermute | solution.py:682
  8.5 4.7 %collective-permute-start.2 = (f32[96,128]{1,0:T(8,128)S(1)}, f32[96,128]{1,0:T(8,128)S(1)}, u32[]{:S(2)}, u32[]{:S(2)}) collective-permute-start(f32[96,128]{1,0:T(8,128)S(1)} %get-tuple-element.59), channel_id=1, source_target_pairs={{0,4},{1,5},{2,6},{3,7},{4,0},{5,1},{6,2},{7,3},{8,12},{9,13},{10,... | collective-permute-start | bytes 147464 | tf_op jit(solution)/shard_map/ppermute | solution.py:48
  10.3 3.8 %collective-permute-start.7 = (f32[32,128]{1,0:T(8,128)S(1)}, f32[32,128]{1,0:T(8,128)S(1)}, u32[]{:S(2)}, u32[]{:S(2)}) collective-permute-start(f32[32,128]{1,0:T(8,128)S(1)} %get-tuple-element.74), channel_id=1, source_target_pairs={{0,8},{1,9},{2,10},{3,11},{4,12},{5,13},{6,14},{7,15},{8,0},{9,1},... | collective-permute-start | bytes 49160 | tf_op jit(solution)/shard_map/ppermute | solution.py:48
  12.3 1.7 %collective-permute-start.8 = (f32[32,128]{1,0:T(8,128)S(1)}, f32[32,128]{1,0:T(8,128)S(1)}, u32[]{:S(2)}, u32[]{:S(2)}) collective-permute-start(f32[32,128]{1,0:T(8,128)S(1)} %get-tuple-element.75), channel_id=1, source_target_pairs={{0,1},{1,0},{2,3},{3,2},{4,5},{5,4},{6,7},{7,6},{8,16},{9,17},{10,... | collective-permute-start | bytes 49160 | tf_op jit(solution)/shard_map/ppermute | solution.py:48
  14.5 9.0 %copy-start.1 = (f32[6,16,32,128]{3,2,1,0:T(8,128)S(1)}, f32[6,16,32,128]{3,2,1,0:T(8,128)}, u32[]{:S(2)}) copy-start(f32[6,16,32,128]{3,2,1,0:T(8,128)} %memory_ref.1) | copy-start | bytes 4718596
  15.3 8.1 %collective-permute-start.12 = (f32[3,2,32,128]{3,2,1,0:T(8,128)S(1)}, f32[3,2,32,128]{3,2,1,0:T(8,128)S(1)}, u32[]{:S(2)}, u32[]{:S(2)}) collective-permute-start(f32[3,2,32,128]{3,2,1,0:T(8,128)S(1)} %get-tuple-element.99), channel_id=1, source_target_pairs={{0,1},{1,0},{2,3},{3,2},{4,5},{5,4},{6,7},{7,6},{8,9},{9,8},{10,11... | collective-permute-start | bytes 294920 | tf_op jit(solution)/shard_map/ppermute | solution.py:48
  15.5 7.9 %collective-permute-start.13 = (f32[3,2,32,128]{3,2,1,0:T(8,128)S(1)}, f32[3,2,32,128]{3,2,1,0:T(8,128)S(1)}, u32[]{:S(2)}, u32[]{:S(2)}) collective-permute-start(f32[3,2,32,128]{3,2,1,0:T(8,128)S(1)} %get-tuple-element.100), channel_id=1, source_target_pairs={{0,3},{1,2},{2,1},{3,0},{4,7},{5,6},{6,5},{7,4},{8,11},{9,10},{10,... | collective-permute-start | bytes 294920 | tf_op jit(solution)/shard_map/ppermute | solution.py:48
  17.5 5.9 %collective-permute-start.11 = (f32[96,128]{1,0:T(8,128)S(1)}, f32[96,128]{1,0:T(8,128)S(1)}, u32[]{:S(2)}, u32[]{:S(2)}) collective-permute-start(f32[96,128]{1,0:T(8,128)S(1)} %get-tuple-element.98), channel_id=1, source_target_pairs={{0,4},{1,5},{2,6},{3,7},{4,0},{5,1},{6,2},{7,3},{8,12},{9,13},{10,... | collective-permute-start | bytes 147464 | tf_op jit(solution)/shard_map/ppermute | solution.py:48
  19.0 4.4 %collective-permute-start.9 = (f32[24,128]{1,0:T(8,128)S(1)}, f32[24,128]{1,0:T(8,128)S(1)}, u32[]{:S(2)}, u32[]{:S(2)}) collective-permute-start(f32[24,128]{1,0:T(8,128)S(1)} %get-tuple-element.94), channel_id=1, source_target_pairs={{0,8},{1,9},{2,10},{3,11},{4,12},{5,13},{6,14},{7,15},{8,0},{9,1},... | collective-permute-start | bytes 36872 | tf_op jit(solution)/shard_map/ppermute | solution.py:48
  21.7 1.7 %collective-permute-start.10 = (f32[24,128]{1,0:T(8,128)S(1)}, f32[24,128]{1,0:T(8,128)S(1)}, u32[]{:S(2)}, u32[]{:S(2)}) collective-permute-start(f32[24,128]{1,0:T(8,128)S(1)} %get-tuple-element.95), channel_id=1, source_target_pairs={{0,1},{1,0},{2,3},{3,2},{4,5},{5,4},{6,7},{7,6},{8,16},{9,17},{10,... | collective-permute-start | bytes 36872 | tf_op jit(solution)/shard_map/ppermute | solution.py:48

commit v12 on v11

--- a/solution.py
+++ b/solution.py
@@ -438,7 +438,7 @@
                     c, k, tile_rows(t), :
                 ] + row_difference(tall, c, k, t)
 
-    over(0, nz, 4, layer)
+    over(0, nz, 16, layer)
 
 
 def velocity_kernel(

time: 25.6 us -> 25.6 us (level)
  no operation moved by 1% of the time
where the time goes in v12:
time: 25.6 us; the launch traced here: 25.4 us
  starting transfers between devices  14.4 us (56%)
  Pallas kernels  7.6 us (30%)
  waiting for transfers between devices  2.49 us (10%)
  between operations  0.86 us (3%)
    ppermute x11, starting transfers between devices, exchange(): got = [lax.ppermute(v, tuple(sizes), r) for v, r in rounds]  11.2 us
    ppermute x1, starting transfers between devices, local(): slab = slab + lax.ppermute(slab, tuple(sizes), rounds[1])  2.63 us
    pallas_call x1, Pallas kernels, local(): call(functools.partial(stress_kernel, counts), [stress.shape, stress.shap...  1.94 us
    ppermute x11, waiting for transfers between devices, exchange(): got = [lax.ppermute(v, tuple(sizes), r) for v, r in rounds]  1.52 us
    pallas_call x1, Pallas kernels, local(): call(depth_kernel, [(6, nz - 4, ny, nx), velocity.shape, velocity.shape],...  1.14 us
    pallas_call x1, Pallas kernels, local(): call(velocity_inner_kernel, [velocity.shape, (3, nz - 4, ny, nx), velocit...  0.89 us
    pallas_call x1, Pallas kernels, local(): call(terrain_piece_kernel, [(rows, nx)], [HB] * 3, [pltpu.VMEM(elevation....  0.82 us
    pallas_call x1, Pallas kernels, local(): call(functools.partial(velocity_kernel, counts), [velocity.shape] + [(xs,...  0.78 us
  transfers between devices with their start and end apart: 14, of which 5 were waited for; matrix products, arithmetic and copies ran while one was open for 0% of the time, Pallas kernels for 17%

profile of v12, /device:TPU:0, one launch (start us, length us, event | category | flops | bytes accessed | tf_op | source)
XLA Modules:
  0.0 25.4 jit_solution(6212978565096229392)
XLA Ops:
  0.6 0.0 copy-start
  0.6 0.5 %collective-permute-start = (s32[32,32]{1,0:T(8,128)}, s32[32,32]{1,0:T(8,128)S(1)}, u32[]{:S(2)}, u32[]{:S(2)}) collective-permute-start(s32[32,32]{1,0:T(8,128)} %elev_hbm.1), channel_id=1, source_target_pairs={{0,1},{1,0},{2,3},{3,2},{4,5},{5,4},{6,7},{7,6},{8,9},{9,8},{10,11... | collective-permute-start | bytes 12296 | tf_op jit(solution)/shard_map/ppermute | solution.py:635
  1.2 0.8 %terrain_piece.1.first_ref = f32[40,128]{1,0:T(8,128)S(1)} custom-call(s32[32,32]{1,0:T(8,128)} %elev_hbm.1, f32[1,16]{1,0:T(1,128)} %bitcast.12, f32[1,16]{1,0:T(1,128)} %bitcast.13), custom_call_target="tpu_custom_call" | custom-call | flops 480000000 | bytes 2800000 | tf_op jit(solution)/shard_map/terrain_piece/pallas_call | solution.py:636
  2.0 0.2 collective-permute-done.elev_ref
  2.2 0.1 merge.1
  2.3 2.6 %collective-permute-start.1 = (f32[40,128]{1,0:T(8,128)S(1)}, f32[40,128]{1,0:T(8,128)S(1)}, u32[]{:S(2)}, u32[]{:S(2)}) collective-permute-start(f32[40,128]{1,0:T(8,128)S(1)} %merge.1), channel_id=1, source_target_pairs={{0,3},{1,2},{2,1},{3,0},{4,7},{5,6},{6,5},{7,4},{8,11},{9,10},{10,... | collective-permute-start | bytes 61448 | tf_op jit(solution)/shard_map/ppermute | solution.py:656
  4.9 0.0 copy-done
  4.9 0.3 %pack_stress.1 = (f32[24,128]{1,0:T(8,128)S(1)}, f32[24,128]{1,0:T(8,128)S(1)}, f32[24,128]{1,0:T(8,128)S(1)}, f32[24,128]{1,0:T(8,128)S(1)}, f32[6,2,32,128]{3,...) custom-call(f32[6,16,32,128]{3,2,1,0:T(8,128)S(1)} %copy-done), custom_call_target="tpu_custom_call" | custom-call | flops 300000000 | bytes 1750000 | tf_op jit(solution)/shard_map/pack_stress/pallas_call | solution.py:670
  5.2 0.4 %collective-permute-start.3 = (f32[6,2,32,128]{3,2,1,0:T(8,128)S(1)}, f32[6,2,32,128]{3,2,1,0:T(8,128)S(1)}, u32[]{:S(2)}, u32[]{:S(2)}) collective-permute-start(f32[6,2,32,128]{3,2,1,0:T(8,128)S(1)} %get-tuple-element.60), channel_id=1, source_target_pairs={{0,1},{1,0},{2,3},{3,2},{4,5},{5,4},{6,7},{7,6},{8,9},{9,8},{10,11... | collective-permute-start | bytes 589832 | tf_op jit(solution)/shard_map/ppermute | solution.py:48
  5.6 0.0 collective-permute-start.4
  5.7 0.7 %collective-permute-done.1 = f32[40,128]{1,0:T(8,128)S(1)} collective-permute-done((f32[40,128]{1,0:T(8,128)S(1)}, f32[40,128]{1,0:T(8,128)S(1)}, u32[]{:S(2)}, u32[]{:S(2)}) %collective-permute-start.1) | collective-permute-done | bytes 20512 | tf_op jit(solution)/shard_map/ppermute | solution.py:656
  6.4 0.0 copy-start.2
  6.4 0.0 copy-start.3
  6.4 0.0 copy-start.4
  6.5 0.0 copy-start.5
  6.5 0.0 copy-start.6
  6.5 0.0 copy-start.7
  6.5 2.0 %collective-permute-start.6 = (f32[8,128]{1,0:T(8,128)S(1)}, f32[8,128]{1,0:T(8,128)S(1)}, u32[]{:S(2)}, u32[]{:S(2)}) collective-permute-start(f32[8,128]{1,0:T(8,128)S(1)} %y_send.1), channel_id=1, source_target_pairs={{0,4},{1,5},{2,6},{3,7},{4,0},{5,1},{6,2},{7,3},{8,12},{9,13},{10,... | collective-permute-start | bytes 12296 | tf_op jit(solution)/shard_map/ppermute | solution.py:48
  8.5 0.0 collective-permute-start.5
  8.5 0.3 %collective-permute-start.2 = (f32[96,128]{1,0:T(8,128)S(1)}, f32[96,128]{1,0:T(8,128)S(1)}, u32[]{:S(2)}, u32[]{:S(2)}) collective-permute-start(f32[96,128]{1,0:T(8,128)S(1)} %get-tuple-element.59), channel_id=1, source_target_pairs={{0,4},{1,5},{2,6},{3,7},{4,0},{5,1},{6,2},{7,3},{8,12},{9,13},{10,... | collective-permute-start | bytes 147464 | tf_op jit(solution)/shard_map/ppermute | solution.py:48
  8.8 1.1 %depth.1 = (f32[6,12,32,128]{3,2,1,0:T(8,128)S(1)}, f32[3,16,32,128]{3,2,1,0:T(8,128)S(1)}, f32[3,16,32,128]{3,2,1,0:T(8,128)S(1)}) custom-call(f32[6,16,32,128]{3,2,1,0:T(8,128)S(1)} %copy-done, f32[3,16,32,128]{3,2,1,0:T(8,128)} %velocity_hbm.1), custom_call_target="tpu_custom_call" | custom-call | flops 1320000000 | bytes 7700000 | tf_op jit(solution)/shard_map/depth/pallas_call | solution.py:683
  9.9 0.3 %collective-permute-done.6.y1_ref.y2_ref = f32[8,128]{1,0:T(8,128)S(1)} collective-permute-done((f32[8,128]{1,0:T(8,128)S(1)}, f32[8,128]{1,0:T(8,128)S(1)}, u32[]{:S(2)}, u32[]{:S(2)}) %collective-permute-start.6) | collective-permute-done | bytes 4128 | tf_op jit(solution)/shard_map/ppermute | solution.py:48
  10.2 0.1 x_send.1
  10.3 2.1 %collective-permute-start.7 = (f32[32,128]{1,0:T(8,128)S(1)}, f32[32,128]{1,0:T(8,128)S(1)}, u32[]{:S(2)}, u32[]{:S(2)}) collective-permute-start(f32[32,128]{1,0:T(8,128)S(1)} %get-tuple-element.74), channel_id=1, source_target_pairs={{0,8},{1,9},{2,10},{3,11},{4,12},{5,13},{6,14},{7,15},{8,0},{9,1},... | collective-permute-start | bytes 49160 | tf_op jit(solution)/shard_map/ppermute | solution.py:48
  12.3 0.0 collective-permute-done.5
  12.3 0.0 collective-permute-start.8
  12.3 0.0 copy-done.2
  12.3 0.0 copy-done.3
  12.4 0.0 copy-done.4
  12.4 0.0 copy-done.5
  12.4 0.0 copy-done.6
  12.4 0.0 copy-done.7
  12.4 0.8 %cells.1 = (f32[5,16,32,128]{3,2,1,0:T(8,128)S(1)}, f32[2,64,128]{2,1,0:T(8,128)S(1)}) custom-call(f32[8,128]{1,0:T(8,128)S(1)} %add.7.layers_ref, s32[16,32,128]{2,1,0:T(8,128)S(1)} %copy-done.2, f32[1,16]{1,0:T(1,128)S(1)} %bitcast.7, f32[1,16]{1,0:T(1,128)S(1)} %bitcast.8, f32[1,16]{1,0:T(1,128)S(1)} %bitcast.9, f32[1,16]{1,0:T(1,128)S(1)} %bitcast.10, ...), custom_call_target="tpu_custom_call" | custom-call | flops 480000000 | bytes 2800000 | tf_op jit(solution)/shard_map/cells/pallas_call | solution.py:707
  13.2 0.0 collective-permute-done.2.y1_ref.y2_ref
  13.2 0.0 collective-permute-done.3.z1_ref
  13.2 0.0 collective-permute-done.4.z2_ref
  13.2 0.4 %planes.1 = (f32[3,16,32,128]{3,2,1,0:T(8,128)S(1)}, f32[6,4,32,128]{3,2,1,0:T(8,128)S(1)}) custom-call(f32[6,16,32,128]{3,2,1,0:T(8,128)S(1)} %copy-done, f32[3,16,32,128]{3,2,1,0:T(8,128)S(1)} %get-tuple-element.58.along_ref, f32[96,128]{1,0:T(8,128)S(1)} %collective-permute-done.2.y1_ref.y2_ref, f32[96,128]{1,0:T(8,128)S(1)} %collective-permute-done.2.y1_ref.y2_ref, ...), custom_call_target="tpu_custom_call" | custom-call | flops 360000000 | bytes 2100000 | tf_op jit(solution)/shard_map/planes/pallas_call | solution.py:710
  13.6 0.5 %collective-permute-done.7.x1_ref = f32[32,128]{1,0:T(8,128)S(1)} collective-permute-done((f32[32,128]{1,0:T(8,128)S(1)}, f32[32,128]{1,0:T(8,128)S(1)}, u32[]{:S(2)}, u32[]{:S(2)}) %collective-permute-start.7) | collective-permute-done | bytes 16416 | tf_op jit(solution)/shard_map/ppermute | solution.py:48
  14.0 0.0 collective-permute-done.8.x2_ref
  14.1 0.4 %metrics.1 = (f32[16,32,128]{2,1,0:T(8,128)S(1)}, f32[16,32,128]{2,1,0:T(8,128)S(1)}, f32[2,32,128]{2,1,0:T(8,128)S(1)}) custom-call(f32[2,64,128]{2,1,0:T(8,128)S(1)} %get-tuple-element.80.layers_ref, f32[48,128]{1,0:T(8,128)S(1)} %get-tuple-element.81.own, f32[8,128]{1,0:T(8,128)S(1)} %slice.10.x1_ref, f32[8,128]{1,0:T(8,128)S(1)} %slice.11.x2_ref), custom_call_target="tpu_custom_call" | custom-call | flops 660000000 | bytes 3850000 | tf_op jit(solution)/shard_map/metrics/pallas_call | solution.py:718
  14.5 0.0 copy-start.1
  14.5 0.8 %velocity.1 = (f32[3,16,32,128]{3,2,1,0:T(8,128)S(1)}, f32[24,128]{1,0:T(8,128)S(1)}, f32[24,128]{1,0:T(8,128)S(1)}, f32[24,128]{1,0:T(8,128)S(1)}, f32[24,128]{...) custom-call(f32[3,16,32,128]{3,2,1,0:T(8,128)S(1)} %get-tuple-element.57.veloc, ...), custom_call_target="tpu_custom_call" | custom-call | flops 900000000 | bytes 5250000 | tf_op jit(solution)/shard_map/velocity/pallas_call | solution.py:725
  15.3 0.2 collective-permute-start.12
  15.5 2.1 %collective-permute-start.13 = (f32[3,2,32,128]{3,2,1,0:T(8,128)S(1)}, f32[3,2,32,128]{3,2,1,0:T(8,128)S(1)}, u32[]{:S(2)}, u32[]{:S(2)}) collective-permute-start(f32[3,2,32,128]{3,2,1,0:T(8,128)S(1)} %get-tuple-element.100), channel_id=1, source_target_pairs={{0,3},{1,2},{2,1},{3,0},{4,7},{5,6},{6,5},{7,4},{8,11},{9,10},{10,... | collective-permute-start | bytes 294920 | tf_op jit(solution)/shard_map/ppermute | solution.py:48
  17.5 1.5 %collective-permute-start.11 = (f32[96,128]{1,0:T(8,128)S(1)}, f32[96,128]{1,0:T(8,128)S(1)}, u32[]{:S(2)}, u32[]{:S(2)}) collective-permute-start(f32[96,128]{1,0:T(8,128)S(1)} %get-tuple-element.98), channel_id=1, source_target_pairs={{0,4},{1,5},{2,6},{3,7},{4,0},{5,1},{6,2},{7,3},{8,12},{9,13},{10,... | collective-permute-start | bytes 147464 | tf_op jit(solution)/shard_map/ppermute | solution.py:48
  19.0 2.7 %collective-permute-start.9 = (f32[24,128]{1,0:T(8,128)S(1)}, f32[24,128]{1,0:T(8,128)S(1)}, u32[]{:S(2)}, u32[]{:S(2)}) collective-permute-start(f32[24,128]{1,0:T(8,128)S(1)} %get-tuple-element.94), channel_id=1, source_target_pairs={{0,8},{1,9},{2,10},{3,11},{4,12},{5,13},{6,14},{7,15},{8,0},{9,1},... | collective-permute-start | bytes 36872 | tf_op jit(solution)/shard_map/ppermute | solution.py:48
  21.7 0.0 collective-permute-start.10
  21.7 0.9 %velocity_inner.1 = (f32[3,16,32,128]{3,2,1,0:T(8,128)}, f32[3,12,32,128]{3,2,1,0:T(8,128)S(1)}, f32[3,16,32,128]{3,2,1,0:T(8,128)S(1)}, f32[3,16,32,128]{3,2,1,0:T(8,128)S(1)}) custom-call(f32[3,16,32,128]{3,2,1,0:T(8,128)S(1)} %get-tuple-element.89.vel_ref), custom_call_target="tpu_custom_call" | custom-call | flops 60000000 | bytes 350000 | tf_op jit(solution)/shard_map/velocity_inner/pallas_call | solution.py:735
  22.6 0.8 %collective-permute-done.9.x1_ref = f32[24,128]{1,0:T(8,128)S(1)} collective-permute-done((f32[24,128]{1,0:T(8,128)S(1)}, f32[24,128]{1,0:T(8,128)S(1)}, u32[]{:S(2)}, u32[]{:S(2)}) %collective-permute-start.9) | collective-permute-done | bytes 12320 | tf_op jit(solution)/shard_map/ppermute | solution.py:48
  23.4 0.0 collective-permute-done.10.x2_ref
  23.4 0.0 collective-permute-done.11.y1_ref.y2_ref
  23.4 0.0 collective-permute-done.12.z1_ref
  23.4 0.0 collective-permute-done.13.z2_ref
  23.4 0.0 copy-done.1
  23.4 1.9 %stress.1 = (f32[6,16,32,128]{3,2,1,0:T(8,128)}, f32[6,16,32,128]{3,2,1,0:T(8,128)}) custom-call(f32[3,16,32,128]{3,2,1,0:T(8,128)S(1)} %get-tuple-element.89.vel_ref, f32[6,16,32,128]{3,2,1,0:T(8,128)S(1)} %copy-done, f32[6,16,32,128]{3,2,1,0:T(8,128)S(1)} %copy-done.1, f32[5,16,32,128]{3,2,1,0:T(8,128)S(1)} %get-tuple-element.76.cells_ref, ...), custom_call_target="tpu_custom_call" | custom-call | flops 1680000000 | bytes 9800000 | tf_op jit(solution)/shard_map/stress/pallas_call | solution.py:743
  (6 shorter events, 0.0 us)
Async XLA Ops:
  0.6 4.3 %copy-start = (f32[6,16,32,128]{3,2,1,0:T(8,128)S(1)}, f32[6,16,32,128]{3,2,1,0:T(8,128)}, u32[]{:S(2)}) copy-start(f32[6,16,32,128]{3,2,1,0:T(8,128)} %stress_ref.3) | copy-start | bytes 4718596
  0.6 1.6 %collective-permute-start = (s32[32,32]{1,0:T(8,128)}, s32[32,32]{1,0:T(8,128)S(1)}, u32[]{:S(2)}, u32[]{:S(2)}) collective-permute-start(s32[32,32]{1,0:T(8,128)} %elev_hbm.1), channel_id=1, source_target_pairs={{0,1},{1,0},{2,3},{3,2},{4,5},{5,4},{6,7},{7,6},{8,9},{9,8},{10,11... | collective-permute-start | bytes 12296 | tf_op jit(solution)/shard_map/ppermute | solution.py:635
  2.3 4.1 %collective-permute-start.1 = (f32[40,128]{1,0:T(8,128)S(1)}, f32[40,128]{1,0:T(8,128)S(1)}, u32[]{:S(2)}, u32[]{:S(2)}) collective-permute-start(f32[40,128]{1,0:T(8,128)S(1)} %merge.1), channel_id=1, source_target_pairs={{0,3},{1,2},{2,1},{3,0},{4,7},{5,6},{6,5},{7,4},{8,11},{9,10},{10,... | collective-permute-start | bytes 61448 | tf_op jit(solution)/shard_map/ppermute | solution.py:656
  5.2 8.0 %collective-permute-start.3 = (f32[6,2,32,128]{3,2,1,0:T(8,128)S(1)}, f32[6,2,32,128]{3,2,1,0:T(8,128)S(1)}, u32[]{:S(2)}, u32[]{:S(2)}) collective-permute-start(f32[6,2,32,128]{3,2,1,0:T(8,128)S(1)} %get-tuple-element.60), channel_id=1, source_target_pairs={{0,1},{1,0},{2,3},{3,2},{4,5},{5,4},{6,7},{7,6},{8,9},{9,8},{10,11... | collective-permute-start | bytes 589832 | tf_op jit(solution)/shard_map/ppermute | solution.py:48
  5.6 7.6 %collective-permute-start.4 = (f32[6,2,32,128]{3,2,1,0:T(8,128)S(1)}, f32[6,2,32,128]{3,2,1,0:T(8,128)S(1)}, u32[]{:S(2)}, u32[]{:S(2)}) collective-permute-start(f32[6,2,32,128]{3,2,1,0:T(8,128)S(1)} %get-tuple-element.61), channel_id=1, source_target_pairs={{0,3},{1,2},{2,1},{3,0},{4,7},{5,6},{6,5},{7,4},{8,11},{9,10},{10,... | collective-permute-start | bytes 589832 | tf_op jit(solution)/shard_map/ppermute | solution.py:48
  6.4 5.9 %copy-start.2 = (s32[16,32,128]{2,1,0:T(8,128)S(1)}, s32[16,32,128]{2,1,0:T(8,128)}, u32[]{:S(2)}) copy-start(s32[16,32,128]{2,1,0:T(8,128)} %material_ref) | copy-start | bytes 786436
  6.4 5.9 %copy-start.3 = (f32[16]{0:T(128)S(1)}, f32[16]{0:T(128)}, u32[]{:S(2)}) copy-start(f32[16]{0:T(128)} %param.16) | copy-start | bytes 196
  6.4 5.9 %copy-start.4 = (f32[16]{0:T(128)S(1)}, f32[16]{0:T(128)}, u32[]{:S(2)}) copy-start(f32[16]{0:T(128)} %param.17) | copy-start | bytes 196
  6.5 5.9 %copy-start.5 = (f32[16]{0:T(128)S(1)}, f32[16]{0:T(128)}, u32[]{:S(2)}) copy-start(f32[16]{0:T(128)} %param.18) | copy-start | bytes 196
  6.5 5.9 %copy-start.6 = (f32[16]{0:T(128)S(1)}, f32[16]{0:T(128)}, u32[]{:S(2)}) copy-start(f32[16]{0:T(128)} %param.19) | copy-start | bytes 196
  6.5 5.9 %copy-start.7 = (f32[16]{0:T(128)S(1)}, f32[16]{0:T(128)}, u32[]{:S(2)}) copy-start(f32[16]{0:T(128)} %param.20) | copy-start | bytes 196
  6.5 3.7 %collective-permute-start.6 = (f32[8,128]{1,0:T(8,128)S(1)}, f32[8,128]{1,0:T(8,128)S(1)}, u32[]{:S(2)}, u32[]{:S(2)}) collective-permute-start(f32[8,128]{1,0:T(8,128)S(1)} %y_send.1), channel_id=1, source_target_pairs={{0,4},{1,5},{2,6},{3,7},{4,0},{5,1},{6,2},{7,3},{8,12},{9,13},{10,... | collective-permute-start | bytes 12296 | tf_op jit(solution)/shard_map/ppermute | solution.py:48
  8.5 3.8 %collective-permute-start.5 = (f32[8,128]{1,0:T(8,128)S(1)}, f32[8,128]{1,0:T(8,128)S(1)}, u32[]{:S(2)}, u32[]{:S(2)}) collective-permute-start(f32[8,128]{1,0:T(8,128)S(1)} %slice.12), channel_id=1, source_target_pairs={{0,1},{1,0},{2,3},{3,2},{4,5},{5,4},{6,7},{7,6},{8,9},{9,8},{10,11... | collective-permute-start | bytes 12296 | tf_op jit(solution)/shard_map/ppermute | solution.py:682
  8.5 4.7 %collective-permute-start.2 = (f32[96,128]{1,0:T(8,128)S(1)}, f32[96,128]{1,0:T(8,128)S(1)}, u32[]{:S(2)}, u32[]{:S(2)}) collective-permute-start(f32[96,128]{1,0:T(8,128)S(1)} %get-tuple-element.59), channel_id=1, source_target_pairs={{0,4},{1,5},{2,6},{3,7},{4,0},{5,1},{6,2},{7,3},{8,12},{9,13},{10,... | collective-permute-start | bytes 147464 | tf_op jit(solution)/shard_map/ppermute | solution.py:48
  10.3 3.8 %collective-permute-start.7 = (f32[32,128]{1,0:T(8,128)S(1)}, f32[32,128]{1,0:T(8,128)S(1)}, u32[]{:S(2)}, u32[]{:S(2)}) collective-permute-start(f32[32,128]{1,0:T(8,128)S(1)} %get-tuple-element.74), channel_id=1, source_target_pairs={{0,8},{1,9},{2,10},{3,11},{4,12},{5,13},{6,14},{7,15},{8,0},{9,1},... | collective-permute-start | bytes 49160 | tf_op jit(solution)/shard_map/ppermute | solution.py:48
  12.3 1.7 %collective-permute-start.8 = (f32[32,128]{1,0:T(8,128)S(1)}, f32[32,128]{1,0:T(8,128)S(1)}, u32[]{:S(2)}, u32[]{:S(2)}) collective-permute-start(f32[32,128]{1,0:T(8,128)S(1)} %get-tuple-element.75), channel_id=1, source_target_pairs={{0,1},{1,0},{2,3},{3,2},{4,5},{5,4},{6,7},{7,6},{8,16},{9,17},{10,... | collective-permute-start | bytes 49160 | tf_op jit(solution)/shard_map/ppermute | solution.py:48
  14.5 9.0 %copy-start.1 = (f32[6,16,32,128]{3,2,1,0:T(8,128)S(1)}, f32[6,16,32,128]{3,2,1,0:T(8,128)}, u32[]{:S(2)}) copy-start(f32[6,16,32,128]{3,2,1,0:T(8,128)} %memory_ref.1) | copy-start | bytes 4718596
  15.3 8.1 %collective-permute-start.12 = (f32[3,2,32,128]{3,2,1,0:T(8,128)S(1)}, f32[3,2,32,128]{3,2,1,0:T(8,128)S(1)}, u32[]{:S(2)}, u32[]{:S(2)}) collective-permute-start(f32[3,2,32,128]{3,2,1,0:T(8,128)S(1)} %get-tuple-element.99), channel_id=1, source_target_pairs={{0,1},{1,0},{2,3},{3,2},{4,5},{5,4},{6,7},{7,6},{8,9},{9,8},{10,11... | collective-permute-start | bytes 294920 | tf_op jit(solution)/shard_map/ppermute | solution.py:48
  15.5 8.0 %collective-permute-start.13 = (f32[3,2,32,128]{3,2,1,0:T(8,128)S(1)}, f32[3,2,32,128]{3,2,1,0:T(8,128)S(1)}, u32[]{:S(2)}, u32[]{:S(2)}) collective-permute-start(f32[3,2,32,128]{3,2,1,0:T(8,128)S(1)} %get-tuple-element.100), channel_id=1, source_target_pairs={{0,3},{1,2},{2,1},{3,0},{4,7},{5,6},{6,5},{7,4},{8,11},{9,10},{10,... | collective-permute-start | bytes 294920 | tf_op jit(solution)/shard_map/ppermute | solution.py:48
  17.5 5.9 %collective-permute-start.11 = (f32[96,128]{1,0:T(8,128)S(1)}, f32[96,128]{1,0:T(8,128)S(1)}, u32[]{:S(2)}, u32[]{:S(2)}) collective-permute-start(f32[96,128]{1,0:T(8,128)S(1)} %get-tuple-element.98), channel_id=1, source_target_pairs={{0,4},{1,5},{2,6},{3,7},{4,0},{5,1},{6,2},{7,3},{8,12},{9,13},{10,... | collective-permute-start | bytes 147464 | tf_op jit(solution)/shard_map/ppermute | solution.py:48
  19.0 4.4 %collective-permute-start.9 = (f32[24,128]{1,0:T(8,128)S(1)}, f32[24,128]{1,0:T(8,128)S(1)}, u32[]{:S(2)}, u32[]{:S(2)}) collective-permute-start(f32[24,128]{1,0:T(8,128)S(1)} %get-tuple-element.94), channel_id=1, source_target_pairs={{0,8},{1,9},{2,10},{3,11},{4,12},{5,13},{6,14},{7,15},{8,0},{9,1},... | collective-permute-start | bytes 36872 | tf_op jit(solution)/shard_map/ppermute | solution.py:48
  21.7 1.7 %collective-permute-start.10 = (f32[24,128]{1,0:T(8,128)S(1)}, f32[24,128]{1,0:T(8,128)S(1)}, u32[]{:S(2)}, u32[]{:S(2)}) collective-permute-start(f32[24,128]{1,0:T(8,128)S(1)} %get-tuple-element.95), channel_id=1, source_target_pairs={{0,1},{1,0},{2,3},{3,2},{4,5},{5,4},{6,7},{7,6},{8,16},{9,17},{10,... | collective-permute-start | bytes 36872 | tf_op jit(solution)/shard_map/ppermute | solution.py:48
